TPU v7x, 32 devices: a whole 2x2x4 slice. The times are simulated.
32 devices in a mesh: strip: 16 (over z, y, core), canvas: 2 (over x).
Axes of the slice: x: 2, y: 2, z: 4, core: 2. Of those that a mesh axis runs over, the one named last changes fastest.
Arguments:
- latent_in: bfloat16 [8, 64, 176, 256], P('canvas', 'strip'), may hold values from -6 to 6
- crop_code: int32 [8, 64, 176], P('canvas', 'strip'), may hold values from 0 to 255, as said below
- code_index: int32 [8, 64, 176], P('canvas', 'strip'), may hold values from 0 to 511
- conv_weight: bfloat16 [3, 3, 256, 256], replicated, may hold values from -0.25 to 0.25
- conv_bias: bfloat16 [256], replicated, may hold values from -3 to 3
- mix_weight: bfloat16 [256, 256], replicated, may hold values from -1 to 1
- mix_bias: bfloat16 [256], replicated, may hold values from -3 to 3
- proj_weight: bfloat16 [256, 64], replicated, may hold values from -0.375 to 0.375
- proj_bias: bfloat16 [64], replicated, may hold values from -3 to 3
- codebook: bfloat16 [512, 64], replicated, may hold values from -6 to 6
- decode_weight: bfloat16 [64, 256], replicated, may hold values from -0.75 to 0.75
- decode_bias: bfloat16 [256], replicated, may hold values from -3 to 3
- out_grad: bfloat16 [8, 64, 176, 256], P('canvas', 'strip'), may hold values from -6 to 6
Outputs:
- decoded: bfloat16 [8, 64, 176, 256], P('canvas', 'strip')
- latent_grad: bfloat16 [8, 64, 176, 256], P('canvas', 'strip')
- conv_weight_grad: float32 [3, 3, 256, 256], replicated
- conv_bias_grad: float32 [256], replicated
- mix_weight_grad: float32 [256, 256], replicated
- mix_bias_grad: float32 [256], replicated
- proj_weight_grad: float32 [256, 64], replicated
- proj_bias_grad: float32 [64], replicated
- codebook_grad: float32 [512, 64], replicated
- decode_weight_grad: float32 [64, 256], replicated
- decode_bias_grad: float32 [256], replicated
Inputs may be any that keep to these rules, and one draw needn't show every extreme that they name: Crops are rectangles of a canvas. Bit b of crop_code (b = 0 to 7, for the neighbours (a, b') in row-major order over the finite set (-1, 0, 1) x the finite set (-1, 0, 1) without (0, 0)) is 1 exactly when that neighbour lies inside the canvas and in the same crop; higher bits are 0.
All inputs are finite; a program needn't handle non-finite values.
Results may differ from a plain program's by a relative error of at most 0.0068.
Values may be sent and summed in bfloat16 or wider, within the bound.
No kernel may reach another device: no remote copies, remote signals or barrier semaphores. Data moves between devices by JAX's collectives and lax.ppermute only.
A program may use at most 128 MiB of HBM per device.

v0:
```python
import jax
import jax.numpy as jnp
from jax import lax
from jax.sharding import PartitionSpec as P

commit_weight = 0.25


def padded(block, sides, width):
    for axis, dim in sides:
        count = lax.axis_size(axis)
        forward = [(i, i + 1) for i in range(count - 1)]
        backward = [(target, source) for source, target in forward]
        low = lax.ppermute(
            lax.slice_in_dim(block, block.shape[dim] - width, None, axis=dim), axis, forward
        )
        high = lax.ppermute(lax.slice_in_dim(block, 0, width, axis=dim), axis, backward)
        block = jnp.concatenate([low, block, high], axis=dim)
    return block


def silu_slope(values):
    logistic = jax.nn.sigmoid(values)
    return logistic * (1.0 + values * (1.0 - logistic))


def mask_columns(crop_code):
    planes = []
    for offset in range(9):
        if offset == 4:
            planes.append(jnp.ones(crop_code.shape, jnp.bfloat16))
        else:
            bit_place = offset if offset < 4 else offset - 1
            planes.append((crop_code // 2**bit_place % 2).astype(jnp.bfloat16))
    return jnp.stack(planes, axis=3)


def row_slab(framed, mask_set, row_step):
    count_rows = mask_set.shape[1]
    across = mask_set.shape[2]
    pieces = []
    for col_step in range(3):
        offset = row_step * 3 + col_step
        window = framed[:, row_step : row_step + count_rows, col_step : col_step + across, :]
        pieces.append(window * mask_set[:, :, :, offset : offset + 1])
    return jnp.concatenate(pieces, axis=3)


def per_device(
    latent_in,
    crop_code,
    code_index,
    conv_weight,
    conv_bias,
    mix_weight,
    mix_bias,
    proj_weight,
    proj_bias,
    codebook,
    decode_weight,
    decode_bias,
    out_grad,
):
    channels = latent_in.shape[3]
    count_rows = latent_in.shape[1]
    across = latent_in.shape[2]
    mask_set = mask_columns(crop_code)
    latent_wide = latent_in.astype(jnp.float32)
    activated = jax.nn.silu(latent_wide).astype(jnp.bfloat16)
    framed = padded(activated, (("strip", 1),), 1)
    framed = jnp.pad(framed, ((0, 0), (0, 0), (1, 1), (0, 0)))
    slab_list = []
    conv_out = conv_bias.astype(jnp.float32)
    for row_step in range(3):
        slab_now = row_slab(framed, mask_set, row_step)
        slab_list.append(slab_now)
        flat_weight = conv_weight[row_step].reshape(3 * channels, channels)
        conv_out = conv_out + jnp.einsum(
            "brwk,kd->brwd", slab_now, flat_weight, preferred_element_type=jnp.float32
        )
    second = jax.nn.silu(conv_out).astype(jnp.bfloat16)
    branch = jnp.einsum(
        "brwc,cd->brwd", second, mix_weight, preferred_element_type=jnp.float32
    ) + mix_bias.astype(jnp.float32)
    stream = (latent_wide + branch).astype(jnp.bfloat16)
    encoded = jnp.einsum(
        "brwc,ce->brwe", stream, proj_weight, preferred_element_type=jnp.float32
    ) + proj_bias.astype(jnp.float32)
    entries = codebook.shape[0]
    matches = code_index[:, :, :, None] == jnp.arange(entries, dtype=jnp.int32)
    quantized = jnp.einsum(
        "brwk,ke->brwe", matches.astype(jnp.bfloat16), codebook, preferred_element_type=jnp.float32
    )
    quant_low = quantized.astype(jnp.bfloat16)
    decoded = (
        jnp.einsum("brwe,ec->brwc", quant_low, decode_weight, preferred_element_type=jnp.float32)
        + decode_bias.astype(jnp.float32)
    ).astype(jnp.bfloat16)
    decode_weight_grad = jnp.einsum(
        "brwe,brwc->ec", quant_low, out_grad, preferred_element_type=jnp.float32
    )
    decode_bias_grad = jnp.sum(out_grad, axis=(0, 1, 2), dtype=jnp.float32)
    back_code = jnp.einsum(
        "brwc,ec->brwe", out_grad, decode_weight, preferred_element_type=jnp.float32
    )
    encoded_grad = (back_code + 2.0 * commit_weight * (encoded - quantized)).astype(jnp.bfloat16)
    proj_weight_grad = jnp.einsum(
        "brwc,brwe->ce", stream, encoded_grad, preferred_element_type=jnp.float32
    )
    proj_bias_grad = jnp.sum(encoded_grad, axis=(0, 1, 2), dtype=jnp.float32)
    codebook_grad = jnp.einsum(
        "brwk,brwe->ke",
        matches.astype(jnp.float32),
        2.0 * (quantized - encoded),
        precision=lax.Precision.HIGHEST,
    )
    stream_grad = jnp.einsum(
        "brwe,ce->brwc", encoded_grad, proj_weight, preferred_element_type=jnp.float32
    )
    branch_grad = stream_grad.astype(jnp.bfloat16)
    mix_weight_grad = jnp.einsum(
        "brwc,brwd->cd", second, branch_grad, preferred_element_type=jnp.float32
    )
    mix_bias_grad = jnp.sum(branch_grad, axis=(0, 1, 2), dtype=jnp.float32)
    second_grad = jnp.einsum(
        "brwd,cd->brwc", branch_grad, mix_weight, preferred_element_type=jnp.float32
    )
    conv_grad = (second_grad * silu_slope(conv_out)).astype(jnp.bfloat16)
    conv_bias_grad = jnp.sum(conv_grad, axis=(0, 1, 2), dtype=jnp.float32)
    weight_rows = []
    for row_step in range(3):
        weight_rows.append(
            jnp.einsum(
                "brwk,brwd->kd", slab_list[row_step], conv_grad, preferred_element_type=jnp.float32
            )
        )
    conv_flat = jnp.stack(weight_rows, axis=0).reshape(9 * channels, channels)
    spread_sum = None
    for row_step in range(3):
        flat_weight = conv_weight[row_step].reshape(3 * channels, channels)
        spread = jnp.einsum(
            "brwd,kd->brwk", conv_grad, flat_weight, preferred_element_type=jnp.float32
        )
        row_total = None
        for col_step in range(3):
            offset = row_step * 3 + col_step
            spread_part = (
                spread[:, :, :, col_step * channels : (col_step + 1) * channels]
                * mask_set[:, :, :, offset : offset + 1]
            )
            placed = jnp.pad(spread_part, ((0, 0), (0, 0), (col_step, 2 - col_step), (0, 0)))
            row_total = placed if row_total is None else row_total + placed
        placed_rows = jnp.pad(row_total, ((0, 0), (row_step, 2 - row_step), (0, 0), (0, 0)))
        spread_sum = placed_rows if spread_sum is None else spread_sum + placed_rows
    rim_sums = jnp.concatenate(
        (
            spread_sum[:, 0:1, 1 : across + 1],
            spread_sum[:, count_rows + 1 : count_rows + 2, 1 : across + 1],
        ),
        axis=1,
    )
    returned = padded(rim_sums.astype(jnp.bfloat16), (("strip", 1),), 1).astype(rim_sums.dtype)
    activated_grad = spread_sum[:, 1 : count_rows + 1, 1 : across + 1]
    activated_grad = activated_grad.at[:, 0].add(returned[:, 0])
    activated_grad = activated_grad.at[:, count_rows - 1].add(returned[:, 3])
    latent_grad = (stream_grad + activated_grad * silu_slope(latent_wide)).astype(jnp.bfloat16)
    summed = lax.psum(
        (
            conv_flat,
            conv_bias_grad,
            mix_weight_grad,
            mix_bias_grad,
            proj_weight_grad,
            proj_bias_grad,
            codebook_grad,
            decode_weight_grad,
            decode_bias_grad,
        ),
        ("strip", "canvas"),
    )
    return (
        decoded,
        latent_grad,
        summed[0].reshape(3, 3, channels, channels),
        summed[1],
        summed[2],
        summed[3],
        summed[4],
        summed[5],
        summed[6],
        summed[7],
        summed[8],
    )


def solution(mesh):
    return jax.shard_map(
        per_device,
        mesh=mesh,
        in_specs=(
            P("canvas", "strip", None, None),
            P("canvas", "strip", None),
            P("canvas", "strip", None),
            P(),
            P(),
            P(),
            P(),
            P(),
            P(),
            P(),
            P(),
            P(),
            P("canvas", "strip", None, None),
        ),
        out_specs=(
            P("canvas", "strip", None, None),
            P("canvas", "strip", None, None),
            P(),
            P(),
            P(),
            P(),
            P(),
            P(),
            P(),
            P(),
            P(),
        ),
        check_vma=False,
    )
```

profile of v0, /device:TPU:1, one launch (start us, length us, event | category | flops | bytes accessed | tf_op | source)
XLA Modules:
  0.0 229.4 jit_solution(9778918154631509219)
XLA Ops:
  7.3 2.3 fusion.6
  9.7 4.7 %collective-permute-start = (bf16[4,1,176,256]{3,2,1,0:T(8,128)(2,1)S(1)}, bf16[4,1,176,256]{3,2,1,0:T(8,128)(2,1)S(1)}, u32[]{:S(2)}, u32[]{:S(2)}) collective-permute-start(bf16[4,1,176,256]{3,2,1,0:T(8,128)(2,1)S(1)} %get-tuple-element.84), channel_id=1, source_target_pairs={{0,2},{2,4},{4,6},{6,8},{8,10},{10,12},{12,14},{14,16},{16,18},{18... | collective-permute-start | bytes 1081352 | tf_op jit(solution)/shard_map/ppermute | solution.py:14
  14.4 1.9 collective-permute-start.1
  16.6 2.0 fusion.1
  18.6 1.1 convolution_bitcast_fusion.2
  19.8 3.3 %collective-permute-done.1 = bf16[4,1,176,256]{3,2,1,0:T(8,128)(2,1)S(1)} collective-permute-done((bf16[4,1,176,256]{3,2,1,0:T(8,128)(2,1)S(1)}, bf16[4,1,176,256]{3,2,1,0:T(8,128)(2,1)S(1)}, u32[]{:S(2)}, u32[]{:S(2)}) %collective-permute-start.1) | collective-permute-done | bytes 360480 | tf_op jit(solution)/shard_map/ppermute | solution.py:17
  23.1 0.8 fusion.19
  23.9 3.0 %slice_multiply_fusion.9 = (bf16[4,4,176,256]{3,2,1,0:T(8,128)(2,1)S(1)}, bf16[4,4,176,256]{3,2,1,0:T(8,128)(2,1)S(1)}, bf16[4,4,176,256]{3,2,1,0:T(8,128)(2,1)S...) fusion(bf16[4,6,178,256]{3,2,1,0:T(8,128)(2,1)S(1)} %fusion.19,, ...), kind=kLoop, calls=%fused_computation.60 | loop fusion | flops 4325376 | bytes 17335296 | tf_op jit(solution)/shard_map/mul | solution.py:45
  26.9 1.6 fusion.23
  28.5 0.9 fusion.26
  29.4 1.8 fusion.25
  31.3 1.4 add_add_fusion
  32.7 1.0 fusion.7
  34.3 3.0 %fusion.32 = f32[512,64]{0,1:T(8,128)} fusion(s32[4,4,176]{2,1,0:T(4,128)S(1)} %copy-done.21, f32[4,4,176,64]{2,3,1,0:T(8,128)S(1)} %fusion.1, f32[4,4,176,64]{2,3,1,0:T(8,128)S(1)} %convolution_add_fusion), kind=kOutput, calls=%fused_computation.74 | convolution fusion | flops 1109098496 | bytes 1584128 | tf_op jit(solution)/shard_map/brwk,brwe->ke/dot_general | solution.py:111
  37.4 0.7 convert_reduce_fusion.3
  38.1 1.1 convolution_bitcast_fusion.1
  39.7 1.7 convolution_bitcast_fusion
  41.4 1.3 convert_reduce_fusion.2
  42.7 2.2 fusion.30
  45.0 2.2 fusion.29
  47.2 2.4 %fusion.28 = f32[1,768,256]{2,1,0:T(8,128)} fusion(bf16[4,4,176,256]{3,2,1,0:T(8,128)(2,1)S(1)} %get-tuple-element.102, bf16[4,4,176,256]{3,2,1,0:T(8,128)(2,1)S(1)} %get-tuple-element.79, bf16[4,4,176,256]{3,2,1,0:T(8,128)(2,1)S(1)} %get-tuple-element.83, bf16[4,4,176,256]{3,2,1,0:T(8,128)(2,1)S(1)} %get-tuple-element.80), kind=kOutput, calls=%fused_computation.69 | convolution fusion | flops 1120272384 | bytes 6553600 | tf_op jit(solution)/shard_map/brwk,brwd->kd/dot_general | solution.py:133
  49.6 1.3 fusion.101
  51.0 1.3 fusion.100
  52.3 1.3 fusion.99
  53.6 5.9 %slice_multiply_fusion.2 = (f32[4,4,176,256]{3,2,1,0:T(8,128)}, f32[4,4,176,256]{3,2,1,0:T(8,128)}, f32[4,4,176,256]{3,2,1,0:T(8,128)}, f32[4,4,176,256]{3,2,1,0...) fusion(f32[4,4,176,768]{3,2,1,0:T(8,128)S(1)} %fusion.101, f32[4,4,176]{2,1,0:T(4,128)S(1)} %get-tuple-element.57, ...), kind=kLoop, calls=%fused_computation.29 | loop fusion | flops 3604480 | bytes 34659328 | tf_op jit(solution)/shard_map/mul | solution.py:148
  59.5 4.3 %pad_add_fusion.1 = f32[4,4,178,256]{3,2,1,0:T(8,128)S(1)} fusion(f32[4,4,176,256]{3,2,1,0:T(8,128)} %get-tuple-element.70, f32[4,4,176,256]{3,2,1,0:T(8,128)} %get-tuple-element.71, f32[4,4,176,256]{3,2,1,0:T(8,128)} %get-tuple-element.69), kind=kLoop, calls=%fused_computation.14 | loop fusion | flops 1458176 | bytes 11567104 | tf_op jit(solution)/shard_map/add | solution.py:152
  63.9 0.8 copy-done.6
  64.8 0.8 pad_add_fusion.2
  65.5 1.5 slice_multiply_fusion.7
  67.0 0.8 pad_add_fusion.3
  67.9 2.9 %fusion.79 = (bf16[4,6,178,256]{3,2,1,0:T(8,128)(2,1)S(1)}, f32[4,6,178,256]{3,2,1,0:T(8,128)}) fusion(f32[4,4,178,256]{3,2,1,0:T(8,128)S(1)} %pad_add_fusion.1, f32[4,4,178,256]{3,2,1,0:T(8,128)S(1)} %pad_add_fusion.2, f32[4,4,178,256]{3,2,1,0:T(8,128)S(1)} %pad_add_fusion.3), kind=kLoop, calls=%fused_computation.175 | loop fusion | flops 3280896 | bytes 15310848 | tf_op jit(solution)/shard_map/convert.2
  70.7 0.9 fusion.96
  71.7 1.9 collective-permute-start.2
  73.6 3.1 %collective-permute-start.3 = (bf16[4,1,176,256]{3,2,1,0:T(8,128)(2,1)}, bf16[4,1,176,256]{3,2,1,0:T(8,128)(2,1)}, u32[]{:S(2)}, u32[]{:S(2)}) collective-permute-start(bf16[4,1,176,256]{3,2,1,0:T(8,128)(2,1)} %get-tuple-element.75), channel_id=1, source_target_pairs={{2,0},{4,2},{6,4},{8,6},{10,8},{12,10},{14,12},{16,14},{18,16},{20... | collective-permute-start | bytes 1081352 | tf_op jit(solution)/shard_map/ppermute | solution.py:17
  76.7 1.6 pad_maximum_fusion.3
  78.3 1.7 add_convert_fusion
  80.4 2.1 slice.195
  82.6 0.9 collective-permute-done.3
  83.4 1.7 fusion.36
  85.2 1.2 fusion.35
  86.4 2.4 %convert_reduce_fusion.1 = (f32[256]{0:T(256)S(1)}, bf16[4,4,176,256]{3,2,1,0:T(8,128)(2,1)}) fusion(f32[4,4,176,256]{3,2,1,0:T(8,128)S(1)} %copy-done.4, f32[4,4,176,256]{3,2,1,0:T(8,128)S(1)} %fusion.35, bf16[4,4,176,256]{3,2,1,0:T(8,128)(2,1)S(1)} %copy-done.8), kind=kLoop, calls=%fused_computation.36 | loop fusion | flops 10092288 | bytes 8651776 | tf_op jit(solution)/shard_map/reduce_sum | solution.py:124
  88.8 39.9 %all-reduce.13 = (f32[256]{0:T(256)}, f32[256]{0:T(256)}, f32[64]{0:T(128)}, f32[256]{0:T(256)}) all-reduce(f32[256]{0:T(256)S(1)} %get-tuple-element.101, f32[256]{0:T(256)S(1)} %get-tuple-element.72, f32[64]{0:T(128)S(1)} %get-tuple-element.103, f32[256]{0:T(256)S(1)} %convert_reduce_fusion), channel_id=1, replica_groups=mesh['strip'=16,'canvas'=2] {'strip','canvas'}, use_global_device_ids=true, to_apply=%region_2.3 | all-reduce | flops 832 | bytes 6656 | tf_op jit(solution)/shard_map/psum | solution.py:167
  128.7 87.9 %all-reduce.17.cloned.1.call-done = (f32[3,3,256,256]{3,2,1,0:T(8,128)}, f32[256,256]{1,0:T(8,128)}, f32[256,64]{0,1:T(8,128)}, f32[512,64]{0,1:T(8,128)}, f32[64,256]{1,0:T(8,128)}) async-done(((f32[3,3,256,256]{3,2,1,0:T(8,128)}, f32[256,256]{1,0:T(8,128)}, f32[256,64]{0,1:T(8,128)}, f32[512,64]{0,1:T(8,128)}, f32[64,256]{1,0:T(8,128)}), (f32[3,3,256,256]{3,2,1,0:T(8,128)}, f32[256,256]{1,0:T(8,128)}, ...) | async-done | bytes 2883600 | tf_op jit(solution)/shard_map/psum | solution.py:167
  216.7 3.3 %copy.45 = f32[3,3,256,256]{3,2,1,0:T(8,128)} copy(f32[3,3,256,256]{3,2,1,0:T(8,128)} %get-tuple-element.110) | data formatting | bytes 4718592
  220.0 0.7 copy.46
  220.7 0.6 copy.47
  221.3 0.7 copy.48
  222.0 0.6 copy.49
  (66 shorter events, 2.1 us)
Async XLA Ops:
  7.2 25.5 %copy-start = (bf16[256,256]{1,0:T(8,128)(2,1)S(1)}, bf16[256,256]{1,0:T(8,128)(2,1)}, u32[]{:S(2)}) copy-start(bf16[256,256]{1,0:T(8,128)(2,1)} %param.22) | copy-start | bytes 393220
  7.2 9.1 %copy-start.19 = (s32[4,4,176]{2,1,0:T(4,128)S(1)}, s32[4,4,176]{2,1,0:T(4,128)}, u32[]{:S(2)}) copy-start(s32[4,4,176]{2,1,0:T(4,128)} %param.18) | copy-start | bytes 33796
  7.2 9.3 %copy-start.21 = (s32[4,4,176]{2,1,0:T(4,128)S(1)}, s32[4,4,176]{2,1,0:T(4,128)}, u32[]{:S(2)}) copy-start(s32[4,4,176]{2,1,0:T(4,128)} %param.19) | copy-start | bytes 33796
  7.2 9.3 %copy-start.20 = (bf16[512,64]{0,1:T(8,128)(2,1)S(1)}, bf16[512,64]{0,1:T(8,128)(2,1)}, u32[]{:S(2)}) copy-start(bf16[512,64]{0,1:T(8,128)(2,1)} %param.26) | copy-start | bytes 196612
  7.2 11.4 %copy-start.2 = (bf16[4,4,176,256]{3,2,1,0:T(8,128)(2,1)S(1)}, bf16[4,4,176,256]{3,2,1,0:T(8,128)(2,1)}, u32[]{:S(2)}) copy-start(bf16[4,4,176,256]{3,2,1,0:T(8,128)(2,1)} %param.29) | copy-start | bytes 4325380
  7.2 209.4 %all-reduce.17.cloned.1.call-start = ((), (), s32[]{:S(2)}) async-start(), calls=%async_computation | async-start | bytes 5767168 | tf_op jit(solution)/shard_map/psum | solution.py:167
  9.6 10.0 %copy-start.22 = (bf16[64]{0:T(256)(128)(2,1)S(1)}, bf16[64]{0:T(256)(128)(2,1)}, u32[]{:S(2)}) copy-start(bf16[64]{0:T(256)(128)(2,1)} %param.25) | copy-start | bytes 388
  9.6 10.0 %copy-start.23 = (bf16[256]{0:T(256)(128)(2,1)S(1)}, bf16[256]{0:T(256)(128)(2,1)}, u32[]{:S(2)}) copy-start(bf16[256]{0:T(256)(128)(2,1)} %param.21) | copy-start | bytes 1540
  9.6 10.0 %copy-start.24 = (bf16[256]{0:T(256)(128)(2,1)S(1)}, bf16[256]{0:T(256)(128)(2,1)}, u32[]{:S(2)}) copy-start(bf16[256]{0:T(256)(128)(2,1)} %param.23) | copy-start | bytes 1540
  9.7 10.0 %copy-start.25 = (bf16[256]{0:T(256)(128)(2,1)S(1)}, bf16[256]{0:T(256)(128)(2,1)}, u32[]{:S(2)}) copy-start(bf16[256]{0:T(256)(128)(2,1)} %param.28) | copy-start | bytes 1540
  9.7 10.1 %copy-start.9 = (bf16[3,3,256,256]{3,2,1,0:T(8,128)(2,1)S(1)}, bf16[3,3,256,256]{3,2,1,0:T(8,128)(2,1)}, u32[]{:S(2)}) copy-start(bf16[3,3,256,256]{3,2,1,0:T(8,128)(2,1)} %param.20) | copy-start | bytes 3538948
  9.7 10.1 %collective-permute-start = (bf16[4,1,176,256]{3,2,1,0:T(8,128)(2,1)S(1)}, bf16[4,1,176,256]{3,2,1,0:T(8,128)(2,1)S(1)}, u32[]{:S(2)}, u32[]{:S(2)}) collective-permute-start(bf16[4,1,176,256]{3,2,1,0:T(8,128)(2,1)S(1)} %get-tuple-element.84), channel_id=1, source_target_pairs={{0,2},{2,4},{4,6},{6,8},{8,10},{10,12},{12,14},{14,16},{16,18},{18... | collective-permute-start | bytes 1081352 | tf_op jit(solution)/shard_map/ppermute | solution.py:14
  14.4 8.7 %collective-permute-start.1 = (bf16[4,1,176,256]{3,2,1,0:T(8,128)(2,1)S(1)}, bf16[4,1,176,256]{3,2,1,0:T(8,128)(2,1)S(1)}, u32[]{:S(2)}, u32[]{:S(2)}) collective-permute-start(bf16[4,1,176,256]{3,2,1,0:T(8,128)(2,1)S(1)} %get-tuple-element.85), channel_id=1, source_target_pairs={{2,0},{4,2},{6,4},{8,6},{10,8},{12,10},{14,12},{16,14},{18,16},{20... | collective-permute-start | bytes 1081352 | tf_op jit(solution)/shard_map/ppermute | solution.py:17
  31.3 1.4 copy-start.7
  32.7 1.0 copy-start.14
  33.7 3.6 %copy-start.15 = (bf16[64,256]{1,0:T(8,128)(2,1)S(1)}, bf16[64,256]{1,0:T(8,128)(2,1)}, u32[]{:S(2)}) copy-start(bf16[64,256]{1,0:T(8,128)(2,1)} %param.27) | copy-start | bytes 98308
  39.7 1.7 copy-start.3
  59.5 4.4 %copy-start.5 = (f32[4,4,176,256]{3,2,1,0:T(8,128)S(1)}, f32[4,4,176,256]{3,2,1,0:T(8,128)}, u32[]{:S(2)}) copy-start(f32[4,4,176,256]{3,2,1,0:T(8,128)} %get-tuple-element.106) | copy-start | bytes 8650756
  59.5 5.2 %copy-start.6 = (f32[4,4,176,256]{3,2,1,0:T(8,128)S(1)}, f32[4,4,176,256]{3,2,1,0:T(8,128)}, u32[]{:S(2)}) copy-start(f32[4,4,176,256]{3,2,1,0:T(8,128)} %get-tuple-element.107) | copy-start | bytes 8650756
  67.8 8.9 %copy-start.10 = (f32[1,768,256]{2,1,0:T(8,128)S(1)}, f32[1,768,256]{2,1,0:T(8,128)}, u32[]{:S(2)}) copy-start(f32[1,768,256]{2,1,0:T(8,128)} %fusion.30) | copy-start | bytes 2359300
  67.8 8.9 %copy-start.11 = (f32[1,768,256]{2,1,0:T(8,128)S(1)}, f32[1,768,256]{2,1,0:T(8,128)}, u32[]{:S(2)}) copy-start(f32[1,768,256]{2,1,0:T(8,128)} %fusion.29) | copy-start | bytes 2359300
  67.8 8.9 %copy-start.12 = (f32[1,768,256]{2,1,0:T(8,128)S(1)}, f32[1,768,256]{2,1,0:T(8,128)}, u32[]{:S(2)}) copy-start(f32[1,768,256]{2,1,0:T(8,128)} %fusion.28) | copy-start | bytes 2359300
  71.7 10.9 %collective-permute-start.2 = (bf16[4,1,176,256]{3,2,1,0:T(8,128)(2,1)S(1)}, bf16[4,1,176,256]{3,2,1,0:T(8,128)(2,1)}, u32[]{:S(2)}, u32[]{:S(2)}) collective-permute-start(bf16[4,1,176,256]{3,2,1,0:T(8,128)(2,1)S(1)} %get-tuple-element.74), channel_id=1, source_target_pairs={{0,2},{2,4},{4,6},{6,8},{8,10},{10,12},{12,14},{14,16},{16,18},{18... | collective-permute-start | bytes 1081352 | tf_op jit(solution)/shard_map/ppermute | solution.py:14
  73.6 9.9 %collective-permute-start.3 = (bf16[4,1,176,256]{3,2,1,0:T(8,128)(2,1)}, bf16[4,1,176,256]{3,2,1,0:T(8,128)(2,1)}, u32[]{:S(2)}, u32[]{:S(2)}) collective-permute-start(bf16[4,1,176,256]{3,2,1,0:T(8,128)(2,1)} %get-tuple-element.75), channel_id=1, source_target_pairs={{2,0},{4,2},{6,4},{8,6},{10,8},{12,10},{14,12},{16,14},{18,16},{20... | collective-permute-start | bytes 1081352 | tf_op jit(solution)/shard_map/ppermute | solution.py:17
  82.5 3.8 %copy-start.4 = (f32[4,4,176,256]{3,2,1,0:T(8,128)S(1)}, f32[4,4,176,256]{3,2,1,0:T(8,128)}, u32[]{:S(2)}) copy-start(f32[4,4,176,256]{3,2,1,0:T(8,128)} %copy-done.3) | copy-start | bytes 8650756
  82.6 3.8 %copy-start.8 = (bf16[4,4,176,256]{3,2,1,0:T(8,128)(2,1)S(1)}, bf16[4,4,176,256]{3,2,1,0:T(8,128)(2,1)}, u32[]{:S(2)}) copy-start(bf16[4,4,176,256]{3,2,1,0:T(8,128)(2,1)} %param.17) | copy-start | bytes 4325380
  216.7 3.3 %copy-start.13 = (f32[256,256]{1,0:T(8,128)S(1)}, f32[256,256]{1,0:T(8,128)}, u32[]{:S(2)}) copy-start(f32[256,256]{1,0:T(8,128)} %get-tuple-element.112) | copy-start | bytes 786436
  216.7 4.0 %copy-start.18 = (f32[256,64]{0,1:T(8,128)S(1)}, f32[256,64]{0,1:T(8,128)}, u32[]{:S(2)}) copy-start(f32[256,64]{0,1:T(8,128)} %get-tuple-element.114) | copy-start | bytes 196612
  216.7 4.6 %copy-start.16 = (f32[512,64]{0,1:T(8,128)S(1)}, f32[512,64]{0,1:T(8,128)}, u32[]{:S(2)}) copy-start(f32[512,64]{0,1:T(8,128)} %get-tuple-element.116) | copy-start | bytes 393220
  216.7 5.3 %copy-start.17 = (f32[64,256]{1,0:T(8,128)S(1)}, f32[64,256]{1,0:T(8,128)}, u32[]{:S(2)}) copy-start(f32[64,256]{1,0:T(8,128)} %get-tuple-element.117) | copy-start | bytes 196612
  216.7 5.9 %copy-start.1 = (bf16[256,256]{1,0:T(8,128)(2,1)S(1)}, bf16[256,256]{1,0:T(8,128)(2,1)}, u32[]{:S(2)}) copy-start(bf16[256,256]{1,0:T(8,128)(2,1)} %param.22) | copy-start | bytes 393220
Sparse Core Ops, SparseCore 0:
  78.5 138.1 all-reduce.16
where the time goes:
time: 232 us; the launch traced here: 229 us
  waiting for transfers between devices  92.1 us (40%)
  blocking collectives  39.9 us (17%)
  other arithmetic  30.7 us (13%)
  matrix products  30.5 us (13%)
  between operations  14.6 us (6%)
  starting transfers between devices  11.7 us (5%)
  local copies, waits for them, and re-layouts  10.1 us (4%)
    psum x1, waiting for transfers between devices, per_device(): lax.psum((conv_flat, conv_bias_grad, mix_weight_grad, mix_bias_grad, proj...  87.9 us
    psum x1, blocking collectives, per_device(): lax.psum((conv_flat, conv_bias_grad, mix_weight_grad, mix_bias_grad, proj...  39.9 us
    mul x2, other arithmetic, per_device(): spread[:, :, :, col_step * channels:(col_step + 1) * channels]  7.37 us
    dot_general x3, matrix products, per_device(): jnp.einsum('brwk,brwd->kd', slab_list[row_step], conv_grad, preferred_ele...  6.9 us
    unnamed x57, local copies, waits for them, and re-layouts  6.89 us
    ppermute x2, starting transfers between devices, padded(): lax.ppermute(lax.slice_in_dim(block, block.shape[dim] - width, None, axis...  6.58 us
    add x3, other arithmetic, per_device(): row_total = placed if row_total is None else row_total + placed  5.94 us
    ppermute x2, starting transfers between devices, padded(): lax.ppermute(lax.slice_in_dim(block, 0, width, axis=dim), axis, backward)  5.05 us
  transfers between devices with their start and end apart: 5, of which 3 were waited for; matrix products, arithmetic and copies ran while one was open for 6% of the time, Pallas kernels for 0%

commit v1 on v0

v1 whole, which is shorter than its diff:
```python
import functools

import jax
import jax.numpy as jnp
from jax import lax
from jax.experimental import pallas as pl
from jax.experimental.pallas import tpu as pltpu
from jax.sharding import PartitionSpec as P

commit_weight = 0.25
low = jnp.bfloat16
wide = jnp.float32
bit_up, bit_left, bit_right, bit_down = 1, 3, 4, 6
tile_rows = 16
vmem_bytes = 44 * 2**20


def mm(lhs, rhs):
    return jnp.dot(lhs, rhs, preferred_element_type=wide)


def mm_nt(lhs, rhs):
    return lax.dot_general(lhs, rhs, (((1,), (1,)), ((), ())), preferred_element_type=wide)


def mm_tn(lhs, rhs):
    return lax.dot_general(lhs, rhs, (((0,), (0,)), ((), ())), preferred_element_type=wide)


def sigmoid(values):
    return 0.5 * jnp.tanh(0.5 * values) + 0.5


def code_columns(code_ref):
    canvases, rows, across = code_ref.shape
    flat = code_ref[...].reshape(canvases * rows, across)
    extra = -across % 128
    if extra:
        flat = jnp.concatenate([flat, jnp.zeros((canvases * rows, extra), flat.dtype)], axis=1)
    return flat.T[:across]


def row_codes(columns, row, canvases, rows, lanes):
    pieces = [
        jnp.broadcast_to(
            columns[:, n * rows + row : n * rows + row + 1], (columns.shape[0], lanes)
        )
        for n in range(canvases)
    ]
    return jnp.concatenate(pieces, axis=0)


def bit_mask(codes, bit, channels):
    plane = ((codes >> bit) & 1).astype(wide)
    return jnp.concatenate([plane] * (channels // codes.shape[1]), axis=1)


def store_slab(slab_ref, at, values, left, right):
    count, channels = values.shape
    span = pl.ds(at, count)
    slab_ref[span, :channels] = (pltpu.roll(values, 1, 0) * left).astype(low)
    slab_ref[span, channels : 2 * channels] = values.astype(low)
    slab_ref[span, 2 * channels :] = (pltpu.roll(values, count - 1, 0) * right).astype(low)


def decoder_kernel(
    index_ref,
    out_grad_ref,
    codebook_ref,
    decode_weight_ref,
    decode_bias_ref,
    proj_bias_ref,
    decoded_ref,
    code_term_ref,
    weight_grad_ref,
    bias_grad_ref,
):
    canvases, rows, across = index_ref.shape
    entries, size = codebook_ref.shape
    channels = decode_weight_ref.shape[1]
    codebook = codebook_ref[...]
    both = jnp.concatenate([codebook * low(-0.5), codebook * low(2.0)], axis=1)
    blank = jnp.zeros((size, channels), low)
    weight = decode_weight_ref[...]
    weight_top = jnp.concatenate([weight, blank], axis=0)
    weight_end = jnp.concatenate([blank, weight * low(0.5)], axis=0)
    shift = proj_bias_ref[...].astype(wide)
    shift = jnp.concatenate([0.5 * shift, -2.0 * shift], axis=1)
    bias = decode_bias_ref[...].astype(wide)
    columns = code_columns(index_ref)
    weight_sum, bias_sum = None, None
    for row in range(rows):
        codes = row_codes(columns, row, canvases, rows, entries)
        picks = lax.broadcasted_iota(jnp.int32, codes.shape, 1) == codes
        picks = picks.astype(wide).astype(low)
        grad = out_grad_ref[:, row].reshape(canvases * across, channels)
        term = mm(picks, both) + mm_nt(grad, weight_top)
        code_term_ref[row] = term + shift
        code = term.astype(low)
        decoded = (mm(code, weight_end) + bias).astype(low)
        decoded_ref[:, row] = decoded.reshape(canvases, across, channels)
        weight_part = mm_tn(code, grad)
        bias_part = jnp.sum(grad.astype(wide), axis=0, keepdims=True)
        weight_sum = weight_part if weight_sum is None else weight_sum + weight_part
        bias_sum = bias_part if bias_sum is None else bias_sum + bias_part
    weight_grad_ref[...] = 0.5 * weight_sum[size:]
    bias_grad_ref[...] = bias_sum


def block_kernel(
    plan,
    crop_ref,
    index_ref,
    latent_ref,
    mate_ref,
    other_ref,
    code_term_ref,
    conv_weight_ref,
    conv_bias_ref,
    mix_weight_ref,
    mix_bias_ref,
    proj_weight_ref,
    decode_weight_grad_ref,
    decode_bias_grad_ref,
    grad_ref,
    branch_grad_ref,
    edge_mate_ref,
    edge_other_ref,
    keep_ref,
    send_ref,
    slab_ref,
    up_ref,
    down_ref,
    second_ref,
    stream_ref,
    codes_ref,
    picks_ref,
    message_ref,
):
    canvases, rows, across = crop_ref.shape
    channels = latent_ref.shape[3]
    size = proj_weight_ref.shape[1]
    entries = picks_ref.shape[1]
    count = canvases * across
    odd = lax.axis_index("strip") % 2
    columns = code_columns(crop_ref)
    index_columns = code_columns(index_ref)
    codes = [row_codes(columns, row, canvases, rows, 128) for row in range(rows)]

    def silu_low(values):
        values = values.astype(wide)
        return (values * sigmoid(values)).astype(low).astype(wide)

    def sides(row):
        return (bit_mask(codes[row], bit_left, channels), bit_mask(codes[row], bit_right, channels))

    for row in range(rows):
        values = silu_low(latent_ref[:, row].reshape(count, channels))
        store_slab(slab_ref, (row + 1) * count, values, *sides(row))
    above = jnp.where(odd == 1, mate_ref[...], other_ref[...]).reshape(count, channels)
    below = jnp.where(odd == 1, other_ref[...], mate_ref[...]).reshape(count, channels)
    store_slab(slab_ref, 0, silu_low(above), *sides(0))
    store_slab(slab_ref, (rows + 1) * count, silu_low(below), *sides(rows - 1))

    proj = proj_weight_ref[...]
    proj_both = jnp.concatenate([proj * low(2 * commit_weight), proj * low(-2.0)], axis=1)
    proj_top = jnp.concatenate([proj, jnp.zeros_like(proj)], axis=1)
    conv_bias = conv_bias_ref[...].astype(wide)
    mix_bias = mix_bias_ref[...].astype(wide)
    sums = [None, None, None]
    for row in range(rows):
        up = bit_mask(codes[row], bit_up, channels)
        down = bit_mask(codes[row], bit_down, channels)
        at = row * count
        conv = mm(slab_ref[pl.ds(at + count, count)], conv_weight_ref[1])
        conv = conv + up * mm(slab_ref[pl.ds(at, count)], conv_weight_ref[0])
        conv = conv + down * mm(slab_ref[pl.ds(at + 2 * count, count)], conv_weight_ref[2])
        conv = conv + conv_bias
        gate = sigmoid(conv)
        second = (conv * gate).astype(low)
        slope = gate * (1.0 + conv * (1.0 - gate))
        branch = mm(second, mix_weight_ref[...]) + mix_bias
        latent = latent_ref[:, row].reshape(count, channels).astype(wide)
        stream = (latent + branch).astype(low)
        code = (mm(stream, proj_both) + code_term_ref[row]).astype(low)
        branch_grad = mm_nt(code, proj_top).astype(low)
        grad = (mm_nt(branch_grad, mix_weight_ref[...]) * slope).astype(low)
        grad_wide = grad.astype(wide)
        branch_grad_ref[row] = branch_grad
        grad_ref[pl.ds(at, count)] = grad
        up_ref[pl.ds(at, count)] = (grad_wide * up).astype(low)
        down_ref[pl.ds(at, count)] = (grad_wide * down).astype(low)
        second_ref[pl.ds(at, count)] = second
        stream_ref[pl.ds(at, count)] = stream
        codes_ref[pl.ds(at, count)] = code
        picked = row_codes(index_columns, row, canvases, rows, entries)
        picks = lax.broadcasted_iota(jnp.int32, picked.shape, 1) == picked
        picks_ref[pl.ds(at, count)] = picks.astype(wide).astype(low)
        for place, values in enumerate((grad, branch_grad, code)):
            part = jnp.sum(values.astype(wide), axis=0, keepdims=True)
            sums[place] = part if sums[place] is None else sums[place] + part

    first, last = grad_ref[pl.ds(0, count)], grad_ref[pl.ds((rows - 1) * count, count)]
    edge_mate_ref[...] = jnp.where(odd == 1, first, last)
    edge_other_ref[...] = jnp.where(odd == 1, last, first)

    total = rows * count
    triple = 3 * channels
    for row_step, weighted_ref in enumerate((up_ref, grad_ref, down_ref)):
        part = mm_tn(slab_ref[pl.ds(row_step * count, total)], weighted_ref[...])
        message_ref[pl.ds(row_step * triple, triple)] = part.astype(low)
    at = 3 * triple
    mix_part = mm_tn(second_ref[...], branch_grad_ref[...].reshape(total, channels))
    message_ref[pl.ds(at, channels)] = mix_part.astype(low)
    at += channels
    message_ref[pl.ds(at, size)] = decode_weight_grad_ref[...].astype(low)
    at += size
    proj_part = mm_tn(codes_ref[...], stream_ref[...])
    message_ref[pl.ds(at, size)] = proj_part[:size].astype(low)
    at += size
    code_part = mm_tn(codes_ref[...], picks_ref[...])[size:].astype(low)
    for piece in range(entries // channels):
        message_ref[pl.ds(at, size)] = code_part[:, piece * channels : (piece + 1) * channels]
        at += size
    proj_sum = jnp.concatenate([sums[2]] * (channels // sums[2].shape[1]), axis=1)
    biases = [sums[0], sums[1], decode_bias_grad_ref[...], proj_sum]
    biases.append(jnp.zeros((tile_rows - len(biases), channels), wide))
    message_ref[pl.ds(at, tile_rows)] = jnp.concatenate(biases, axis=0).astype(low)
    at += tile_rows
    rest = message_ref.shape[0] - at
    if rest:
        message_ref[pl.ds(at, rest)] = jnp.zeros((rest, channels), low)

    me = plan.index()
    half, piece_rows = plan.shards // 2, plan.piece_rows
    mine, place = me // half, me % half
    for piece in range(half):
        near = pl.multiple_of((mine * half + piece) * piece_rows, piece_rows)
        far = pl.multiple_of(((1 - mine) * half + piece) * piece_rows, piece_rows)
        keep_ref[piece ^ place] = message_ref[pl.ds(near, piece_rows)]
        send_ref[piece ^ place] = message_ref[pl.ds(far, piece_rows)]


def input_kernel(
    crop_ref,
    latent_ref,
    grad_ref,
    mate_ref,
    other_ref,
    branch_grad_ref,
    conv_weight_ref,
    latent_grad_ref,
    slab_ref,
):
    canvases, rows, across = crop_ref.shape
    channels = latent_ref.shape[3]
    count = canvases * across
    odd = lax.axis_index("strip") % 2
    columns = code_columns(crop_ref)
    codes = [row_codes(columns, row, canvases, rows, 128) for row in range(rows)]

    def sides(row):
        return (bit_mask(codes[row], bit_left, channels), bit_mask(codes[row], bit_right, channels))

    for row in range(rows):
        values = grad_ref[pl.ds(row * count, count)].astype(wide)
        store_slab(slab_ref, (row + 1) * count, values, *sides(row))
    above = jnp.where(odd == 1, mate_ref[...], other_ref[...])
    below = jnp.where(odd == 1, other_ref[...], mate_ref[...])
    store_slab(slab_ref, 0, above.astype(wide), *sides(0))
    store_slab(slab_ref, (rows + 1) * count, below.astype(wide), *sides(rows - 1))

    for row in range(rows):
        spread = None
        for row_step, bit in ((1, None), (0, bit_up), (2, bit_down)):
            part = None
            for col_step in range(3):
                weight = conv_weight_ref[
                    2 - row_step, (2 - col_step) * channels : (3 - col_step) * channels
                ]
                span = pl.ds((row + row_step) * count, count)
                term = mm_nt(
                    slab_ref[span, col_step * channels : (col_step + 1) * channels], weight
                )
                part = term if part is None else part + term
            if bit is not None:
                part = part * bit_mask(codes[row], bit, channels)
            spread = part if spread is None else spread + part
        latent = latent_ref[:, row].reshape(count, channels).astype(wide)
        gate = sigmoid(latent)
        slope = gate * (1.0 + latent * (1.0 - gate))
        out = branch_grad_ref[row].astype(wide) + spread * slope
        latent_grad_ref[:, row] = out.astype(low).reshape(canvases, across, channels)


class Plan:
    def __init__(self, sizes, rows):
        self.sizes = sizes
        bits = {axis: [(axis, b) for b in range(size.bit_length() - 1)] for axis, size in sizes.items()}
        strip, canvas = bits["strip"], bits["canvas"]
        self.stages = [strip[:1], [*strip[1:2], *canvas[:1]], strip[2:4]]
        rest = [*strip[4:], *canvas[1:]]
        self.stages += [rest[i : i + 2] for i in range(0, len(rest), 2)]
        self.stages = [stage for stage in self.stages if stage]
        self.shards = sizes["strip"] * sizes["canvas"]
        self.piece_rows = -(-rows // (self.shards * tile_rows)) * tile_rows
        self.rows = self.shards * self.piece_rows

    def index(self):
        number = 0
        for stage in self.stages:
            for axis, bit in stage:
                number = number * 2 + (lax.axis_index(axis) // 2**bit) % 2
        return number

    def partner(self, stage, step):
        change = {"strip": 0, "canvas": 0}
        for place, (axis, bit) in enumerate(reversed(stage)):
            if step >> place & 1:
                change[axis] |= 1 << bit
        width = self.sizes["canvas"]
        return [
            (s * width + c, (s ^ change["strip"]) * width + (c ^ change["canvas"]))
            for s in range(self.sizes["strip"])
            for c in range(width)
        ]

    def swap(self, values, stage, step):
        return lax.ppermute(values, ("strip", "canvas"), self.partner(stage, step))


def add_kernel(count, *refs):
    ins, outs = refs[:count], refs[count:]
    depth = outs[0].shape[0]
    for place, out_ref in enumerate(outs):
        span = pl.ds(place * depth, depth)
        total = ins[0][span].astype(wide)
        for ref in ins[1:]:
            total = total + ref[span].astype(wide)
        out_ref[...] = total.astype(low)


def add_split(arrays, parts):
    depth, rows, channels = arrays[0].shape
    shape = jax.ShapeDtypeStruct((depth // parts, rows, channels), low)
    return pl.pallas_call(
        functools.partial(add_kernel, len(arrays)),
        out_shape=[shape] * parts,
        compiler_params=pltpu.CompilerParams(vmem_limit_bytes=vmem_bytes),
    )(*arrays)


def final_kernel(plan, count, sizes, *refs):
    ins, outs, gathered_ref = refs[:count], refs[count:-1], refs[-1]
    channels, size, entries = sizes
    me = plan.index()
    at = 0
    for ref in ins:
        for piece in range(ref.shape[0]):
            start = pl.multiple_of((me ^ at) * plan.piece_rows, plan.piece_rows)
            gathered_ref[pl.ds(start, plan.piece_rows)] = ref[piece]
            at += 1
    conv_ref, conv_bias_ref, mix_ref, mix_bias_ref, proj_ref, proj_bias_ref = outs[:6]
    codebook_ref, decode_ref, decode_bias_ref = outs[6:]
    at = 9 * channels
    conv_ref[...] = gathered_ref[pl.ds(0, at)].astype(wide)
    mix_ref[...] = gathered_ref[pl.ds(at, channels)].astype(wide)
    at += channels
    decode_ref[...] = gathered_ref[pl.ds(at, size)].astype(wide)
    at += size
    proj_ref[...] = gathered_ref[pl.ds(at, size)].astype(wide).T
    at += size
    for piece in range(entries // channels):
        rows = gathered_ref[pl.ds(at, size)].astype(wide).T
        codebook_ref[pl.ds(piece * channels, channels)] = rows
        at += size
    biases = gathered_ref[pl.ds(at, tile_rows)].astype(wide)
    conv_bias_ref[...] = biases[0:1]
    mix_bias_ref[...] = biases[1:2]
    decode_bias_ref[...] = biases[2:3]
    proj_bias_ref[...] = biases[3:4, :size]


def per_device(
    plan,
    latent_in,
    crop_code,
    code_index,
    conv_weight,
    conv_bias,
    mix_weight,
    mix_bias,
    proj_weight,
    proj_bias,
    codebook,
    decode_weight,
    decode_bias,
    out_grad,
):
    canvases, rows, across, channels = latent_in.shape
    entries, size = codebook.shape
    count = canvases * across
    total = rows * count
    params = pltpu.CompilerParams(vmem_limit_bytes=vmem_bytes)
    strips = plan.sizes["strip"]

    def line(values):
        return values.reshape(1, -1)

    def trade(mate, other):
        near = [(i, i ^ 1) for i in range(strips)]
        far = [(i, i + 1) for i in range(1, strips - 1, 2)]
        far += [(target, source) for source, target in far]
        return lax.ppermute(mate, "strip", near), lax.ppermute(other, "strip", far)

    odd = lax.axis_index("strip") % 2
    edge = (rows - 1) * (1 - odd)
    mate, other = trade(
        lax.dynamic_index_in_dim(latent_in, edge, axis=1, keepdims=False),
        lax.dynamic_index_in_dim(latent_in, rows - 1 - edge, axis=1, keepdims=False),
    )
    decoded, code_term, decode_weight_grad, decode_bias_grad = pl.pallas_call(
        decoder_kernel,
        out_shape=[
            jax.ShapeDtypeStruct(out_grad.shape, low),
            jax.ShapeDtypeStruct((rows, count, 2 * size), wide),
            jax.ShapeDtypeStruct((size, channels), wide),
            jax.ShapeDtypeStruct((1, channels), wide),
        ],
        compiler_params=params,
    )(code_index, out_grad, codebook, decode_weight, line(decode_bias), line(proj_bias))
    flat_weight = conv_weight.reshape(3, 3 * channels, channels)
    half = jax.ShapeDtypeStruct((plan.shards // 2, plan.piece_rows, channels), low)
    edge_shape = jax.ShapeDtypeStruct((count, channels), low)
    flat = pltpu.VMEM((total, channels), low)
    slab = pltpu.VMEM((total + 2 * count, 3 * channels), low)
    grad, branch_grad, edge_mate, edge_other, keep, send = pl.pallas_call(
        functools.partial(block_kernel, plan),
        out_shape=[
            jax.ShapeDtypeStruct((total, channels), low),
            jax.ShapeDtypeStruct((rows, count, channels), low),
            edge_shape,
            edge_shape,
            half,
            half,
        ],
        scratch_shapes=[
            slab,
            flat,
            flat,
            flat,
            flat,
            pltpu.VMEM((total, 2 * size), low),
            pltpu.VMEM((total, entries), low),
            pltpu.VMEM((plan.rows, channels), low),
        ],
        compiler_params=params,
    )(
        crop_code,
        code_index,
        latent_in,
        mate,
        other,
        code_term,
        flat_weight,
        line(conv_bias),
        mix_weight,
        line(mix_bias),
        proj_weight,
        decode_weight_grad,
        decode_bias_grad,
    )

    arrays = [keep, plan.swap(send, plan.stages[0], 1)]
    grad_mate, grad_other = trade(edge_mate, edge_other)
    for stage in plan.stages[1:]:
        parts = add_split(arrays, 2 ** len(stage))
        arrays = [parts[0]]
        arrays += [plan.swap(parts[i], stage, i) for i in range(1, len(parts))]
    gathered = add_split(arrays, 1)[0]
    latent_grad = pl.pallas_call(
        input_kernel,
        out_shape=jax.ShapeDtypeStruct(latent_in.shape, low),
        scratch_shapes=[slab],
        compiler_params=params,
    )(crop_code, latent_in, grad, grad_mate, grad_other, branch_grad, flat_weight)
    for stage in reversed(plan.stages[1:]):
        others = [plan.swap(gathered, stage, i) for i in range(1, 2 ** len(stage))]
        gathered = jnp.concatenate([gathered, *others], axis=0)
    arrays = [gathered, plan.swap(gathered, plan.stages[0], 1)]

    results = pl.pallas_call(
        functools.partial(final_kernel, plan, len(arrays), (channels, size, entries)),
        out_shape=[
            jax.ShapeDtypeStruct((9 * channels, channels), wide),
            jax.ShapeDtypeStruct((1, channels), wide),
            jax.ShapeDtypeStruct((channels, channels), wide),
            jax.ShapeDtypeStruct((1, channels), wide),
            jax.ShapeDtypeStruct((channels, size), wide),
            jax.ShapeDtypeStruct((1, size), wide),
            jax.ShapeDtypeStruct((entries, size), wide),
            jax.ShapeDtypeStruct((size, channels), wide),
            jax.ShapeDtypeStruct((1, channels), wide),
        ],
        scratch_shapes=[pltpu.VMEM((plan.rows, channels), low)],
        compiler_params=params,
    )(*arrays)
    return (
        decoded,
        latent_grad,
        results[0].reshape(3, 3, channels, channels),
        results[1].reshape(-1),
        results[2],
        results[3].reshape(-1),
        results[4],
        results[5].reshape(-1),
        results[6],
        results[7],
        results[8].reshape(-1),
    )


def solution(mesh):
    sizes = {axis: mesh.shape[axis] for axis in ("strip", "canvas")}
    shared = P("canvas", "strip", None, None)
    codes = P("canvas", "strip", None)

    def wrapped(*args):
        channels = args[0].shape[3]
        entries, size = args[9].shape
        rows = 10 * channels + 2 * size + size * (entries // channels) + tile_rows
        plan = Plan(sizes, rows)
        return jax.shard_map(
            functools.partial(per_device, plan),
            mesh=mesh,
            in_specs=(shared, codes, codes, *[P()] * 9, shared),
            out_specs=(shared, shared, *[P()] * 9),
            check_vma=False,
        )(*args)

    return wrapped
```

time: 232 us -> 95.7 us (0.41)
  waiting for transfers between devices: 92.1 us -> 32.4 us
  blocking collectives: 39.9 us -> 0 us
  other arithmetic: 30.7 us -> 0.03 us
  matrix products: 30.5 us -> 0 us
  Pallas kernels: 0 us -> 25.5 us
  between operations: 14.6 us -> 0.9 us
  starting transfers between devices: 11.7 us -> 24.5 us
    psum x1 -> x0, waiting for transfers between devices: 87.9 us -> none  [per_device(): lax.psum((conv_flat, conv_bias_grad, mix_weight_grad, mix_bias_grad, proj...]
    psum x1 -> x0, blocking collectives: 39.9 us -> none  [per_device(): lax.psum((conv_flat, conv_bias_grad, mix_weight_grad, mix_bias_grad, proj...]
    dot_general x20 -> x0, matrix products: 30.5 us -> none  [the longest x3 6.9 us: per_device(): jnp.einsum('brwk,brwd->kd', slab_list[row_step], conv_grad, preferred_ele...]
    ppermute x4 -> x18, waiting for transfers between devices: 4.14 us -> 32.4 us  [the longest x14 24.2 us: swap(): return lax.ppermute(values, ('strip', 'canvas'), self.partner(stage, step))]
    pallas_call x0 -> x7, Pallas kernels: none -> 25.5 us  [the longest x1 13.4 us: per_device(): pl.pallas_call(functools.partial(block_kernel, plan), out_shape=[jax.Shap...]
    ppermute x4 -> x18, starting transfers between devices: 11.6 us -> 24.5 us  [the longest x14 16.9 us: swap(): return lax.ppermute(values, ('strip', 'canvas'), self.partner(stage, step))]
    mul x4 -> x0, other arithmetic: 11.3 us -> none  [the longest x2 7.37 us: per_device(): spread[:, :, :, col_step * channels:(col_step + 1) * channels]]
    add x3 -> x0, other arithmetic: 5.94 us -> none  [per_device(): row_total = placed if row_total is None else row_total + placed]
  transfers between devices with their start and end apart: 5 -> 18, of which waited for: 3 -> 12; matrix products, arithmetic and copies ran while one was open for 6% -> 4% of each run, Pallas kernels for 0% -> 10%
where the time goes in v1:
time: 95.7 us; the launch traced here: 94.8 us
  waiting for transfers between devices  32.4 us (34%)
  Pallas kernels  25.5 us (27%)
  starting transfers between devices  24.5 us (26%)
  local copies, waits for them, and re-layouts  11.4 us (12%)
    ppermute x14, waiting for transfers between devices, swap(): return lax.ppermute(values, ('strip', 'canvas'), self.partner(stage, step))  24.2 us
    ppermute x14, starting transfers between devices, swap(): return lax.ppermute(values, ('strip', 'canvas'), self.partner(stage, step))  16.9 us
    pallas_call x1, Pallas kernels, per_device(): pl.pallas_call(functools.partial(block_kernel, plan), out_shape=[jax.Shap...  13.4 us
    ppermute x2, waiting for transfers between devices, trade(): lax.ppermute(other, 'strip', far)  8.2 us
    unnamed x38, local copies, waits for them, and re-layouts  7.56 us
    ppermute x2, starting transfers between devices, trade(): lax.ppermute(other, 'strip', far)  7.49 us
    pallas_call x1, Pallas kernels, per_device(): pl.pallas_call(input_kernel, out_shape=jax.ShapeDtypeStruct(latent_in.sha...  5.91 us
    pallas_call x1, Pallas kernels, per_device(): pl.pallas_call(decoder_kernel, out_shape=[jax.ShapeDtypeStruct(out_grad.s...  4.04 us
  transfers between devices with their start and end apart: 18, of which 12 were waited for; matrix products, arithmetic and copies ran while one was open for 4% of the time, Pallas kernels for 10%

profile of v1, /device:TPU:1, one launch (start us, length us, event | category | flops | bytes accessed | tf_op | source)
XLA Modules:
  0.0 94.8 jit_solution(2871272455520986985)
XLA Ops:
  0.7 2.2 %dynamic-slice_bitcast_fusion = (bf16[4,176,256]{2,1,0:T(8,128)(2,1)}, bf16[4,176,256]{2,1,0:T(8,128)(2,1)}) fusion(bf16[4,4,176,256]{3,2,1,0:T(8,128)(2,1)} %latent_ref.3, s32[]{:T(128)S(6)} %select_n.16, s32[]{:T(128)S(6)} %select_n.15), kind=kLoop, calls=%fused_computation | loop fusion | bytes 1441800 | tf_op jit(solution)/shard_map/jit(dynamic_index_in_dim)/squeeze | solution.py:420
  2.9 4.5 %collective-permute-start.1 = (bf16[4,176,256]{2,1,0:T(8,128)(2,1)}, bf16[4,176,256]{2,1,0:T(8,128)(2,1)S(1)}, u32[]{:S(2)}, u32[]{:S(2)}) collective-permute-start(bf16[4,176,256]{2,1,0:T(8,128)(2,1)} %get-tuple-element.76), channel_id=1, source_target_pairs={{2,4},{6,8},{10,12},{14,16},{18,20},{22,24},{26,28},{4,2},{8,6},{1... | collective-permute-start | bytes 1081352 | tf_op jit(solution)/shard_map/ppermute | solution.py:414
  7.4 0.1 collective-permute-start
  7.5 0.6 reshape.55.conv_bias_ref
  8.1 0.6 reshape.56.mix_bias_ref
  8.6 0.6 reshape.52.decode_bias_ref
  9.2 0.9 copy.25.proj_weight_ref
  10.1 1.0 %copy.24.codebook_ref = bf16[512,64]{1,0:T(8,128)(2,1)S(1)} copy(bf16[512,64]{0,1:T(8,128)(2,1)} %param.22) | data formatting | bytes 131072 | tf_op args[9]
  11.1 1.4 %copy-done.2 = bf16[4,4,176,256]{3,2,1,0:T(8,128)(2,1)S(1)} copy-done((bf16[4,4,176,256]{3,2,1,0:T(8,128)(2,1)S(1)}, bf16[4,4,176,256]{3,2,1,0:T(8,128)(2,1)}, u32[]{:S(2)}) %copy-start.2) | copy-done | bytes 1441816
  12.4 0.7 copy-done.5
  13.1 0.8 copy-done.6
  13.9 0.7 copy-done.9
  14.6 0.7 copy-done.10
  15.2 4.0 %shard_map.212 = (bf16[4,4,176,256]{3,2,1,0:T(8,128)(2,1)}, f32[4,704,128]{2,1,0:T(8,128)S(1)}, f32[64,256]{1,0:T(8,128)S(1)}, f32[1,256]{1,0:T(1,128)S(1)}) custom-call(s32[4,4,176]{2,1,0:T(4,128)S(1)} %copy-done.5, bf16[4,4,176,256]{3,2,1,0:T(8,128)(2,1)S(1)} %copy-done.2, bf16[512,64]{1,0:T(8,128)(2,1)S(1)} %copy.24.codebook_ref, ...), custom_call_target="tpu_custom_call" | custom-call | tf_op jit(solution)/shard_map/pallas_call | solution.py:422
  19.3 13.4 %shard_map.213 = (bf16[2816,256]{1,0:T(8,128)(2,1)S(1)}, bf16[4,704,256]{2,1,0:T(8,128)(2,1)S(1)}, bf16[704,256]{1,0:T(8,128)(2,1)S(1)}, bf16[704,256]{1,0:T(8,1...) custom-call(s32[4,4,176]{2,1,0:T(4,128)S(1)} %copy-done.4, s32[4,4,176]{2,1,0:T(4,128)S(1)} %copy-done.5, ...), custom_call_target="tpu_custom_call" | custom-call | tf_op jit(solution)/shard_map/pallas_call | solution.py:437
  32.7 0.6 collective-permute-start.4
  33.3 1.9 %collective-permute-done.4.refs_1_ = bf16[16,96,256]{2,1,0:T(8,128)(2,1)S(1)} collective-permute-done((bf16[16,96,256]{2,1,0:T(8,128)(2,1)S(1)}, bf16[16,96,256]{2,1,0:T(8,128)(2,1)S(1)}, u32[]{:S(2)}, u32[]{:S(2)}) %collective-permute-start.4) | collective-permute-done | bytes 786464 | tf_op jit(solution)/shard_map/ppermute | solution.py:329
  35.2 0.2 shard_map.215
  35.4 1.3 %collective-permute-start.5 = (bf16[4,96,256]{2,1,0:T(8,128)(2,1)S(1)}, bf16[4,96,256]{2,1,0:T(8,128)(2,1)S(1)}, u32[]{:S(2)}, u32[]{:S(2)}) collective-permute-start(bf16[4,96,256]{2,1,0:T(8,128)(2,1)S(1)} %get-tuple-element.49), channel_id=1, source_target_pairs={{0,1},{1,0},{2,3},{3,2},{4,5},{5,4},{6,7},{7,6},{8,9},{9,8},{10,11... | collective-permute-start | bytes 589832 | tf_op jit(solution)/shard_map/ppermute | solution.py:329
  36.7 1.2 %collective-permute-start.6 = (bf16[4,96,256]{2,1,0:T(8,128)(2,1)S(1)}, bf16[4,96,256]{2,1,0:T(8,128)(2,1)S(1)}, u32[]{:S(2)}, u32[]{:S(2)}) collective-permute-start(bf16[4,96,256]{2,1,0:T(8,128)(2,1)S(1)} %get-tuple-element.50), channel_id=1, source_target_pairs={{0,4},{1,5},{2,6},{3,7},{4,0},{5,1},{6,2},{7,3},{8,12},{9,13},{10,... | collective-permute-start | bytes 589832 | tf_op jit(solution)/shard_map/ppermute | solution.py:329
  37.9 0.2 collective-permute-start.7
  38.1 3.5 %collective-permute-done.5.refs_1_ = bf16[4,96,256]{2,1,0:T(8,128)(2,1)S(1)} collective-permute-done((bf16[4,96,256]{2,1,0:T(8,128)(2,1)S(1)}, bf16[4,96,256]{2,1,0:T(8,128)(2,1)S(1)}, u32[]{:S(2)}, u32[]{:S(2)}) %collective-permute-start.5) | collective-permute-done | bytes 196640 | tf_op jit(solution)/shard_map/ppermute | solution.py:329
  41.6 0.9 collective-permute-done.6.refs_2_
  42.5 4.3 %collective-permute-done.7.refs_3_ = bf16[4,96,256]{2,1,0:T(8,128)(2,1)S(1)} collective-permute-done((bf16[4,96,256]{2,1,0:T(8,128)(2,1)S(1)}, bf16[4,96,256]{2,1,0:T(8,128)(2,1)S(1)}, u32[]{:S(2)}, u32[]{:S(2)}) %collective-permute-start.7) | collective-permute-done | bytes 196640 | tf_op jit(solution)/shard_map/ppermute | solution.py:329
  46.8 0.1 shard_map.216
  46.9 2.4 %collective-permute-start.8 = (bf16[1,96,256]{2,1,0:T(8,128)(2,1)S(1)}, bf16[1,96,256]{2,1,0:T(8,128)(2,1)S(1)}, u32[]{:S(2)}, u32[]{:S(2)}) collective-permute-start(bf16[1,96,256]{2,1,0:T(8,128)(2,1)S(1)} %get-tuple-element.53), channel_id=1, source_target_pairs={{0,16},{1,17},{2,18},{3,19},{4,20},{5,21},{6,22},{7,23},{8,24},{9,... | collective-permute-start | bytes 147464 | tf_op jit(solution)/shard_map/ppermute | solution.py:329
  49.3 1.2 %collective-permute-start.9 = (bf16[1,96,256]{2,1,0:T(8,128)(2,1)S(1)}, bf16[1,96,256]{2,1,0:T(8,128)(2,1)S(1)}, u32[]{:S(2)}, u32[]{:S(2)}) collective-permute-start(bf16[1,96,256]{2,1,0:T(8,128)(2,1)S(1)} %get-tuple-element.54), channel_id=1, source_target_pairs={{0,8},{1,9},{2,10},{3,11},{4,12},{5,13},{6,14},{7,15},{8,0},{9,1},... | collective-permute-start | bytes 147464 | tf_op jit(solution)/shard_map/ppermute | solution.py:329
  50.5 0.1 collective-permute-start.10
  50.6 0.3 collective-permute-done.8.refs_1_
  50.8 1.7 %collective-permute-done.9.refs_2_ = bf16[1,96,256]{2,1,0:T(8,128)(2,1)S(1)} collective-permute-done((bf16[1,96,256]{2,1,0:T(8,128)(2,1)S(1)}, bf16[1,96,256]{2,1,0:T(8,128)(2,1)S(1)}, u32[]{:S(2)}, u32[]{:S(2)}) %collective-permute-start.9) | collective-permute-done | bytes 49184 | tf_op jit(solution)/shard_map/ppermute | solution.py:329
  52.5 2.7 %collective-permute-done.10.refs_3_ = bf16[1,96,256]{2,1,0:T(8,128)(2,1)S(1)} collective-permute-done((bf16[1,96,256]{2,1,0:T(8,128)(2,1)S(1)}, bf16[1,96,256]{2,1,0:T(8,128)(2,1)S(1)}, u32[]{:S(2)}, u32[]{:S(2)}) %collective-permute-start.10) | collective-permute-done | bytes 49184 | tf_op jit(solution)/shard_map/ppermute | solution.py:329
  55.2 1.1 %collective-permute-start.13 = (bf16[1,96,256]{2,1,0:T(8,128)(2,1)S(1)}, bf16[1,96,256]{2,1,0:T(8,128)(2,1)S(1)}, u32[]{:S(2)}, u32[]{:S(2)}) collective-permute-start(bf16[1,96,256]{2,1,0:T(8,128)(2,1)S(1)} %shard_map.217), channel_id=1, source_target_pairs={{0,24},{1,25},{2,26},{3,27},{4,28},{5,29},{6,30},{7,31},{8,16},{9,... | collective-permute-start | bytes 147464 | tf_op jit(solution)/shard_map/ppermute | solution.py:329
  56.3 2.6 %collective-permute-start.11 = (bf16[1,96,256]{2,1,0:T(8,128)(2,1)S(1)}, bf16[1,96,256]{2,1,0:T(8,128)(2,1)S(1)}, u32[]{:S(2)}, u32[]{:S(2)}) collective-permute-start(bf16[1,96,256]{2,1,0:T(8,128)(2,1)S(1)} %shard_map.217), channel_id=1, source_target_pairs={{0,16},{1,17},{2,18},{3,19},{4,20},{5,21},{6,22},{7,23},{8,24},{9,... | collective-permute-start | bytes 147464 | tf_op jit(solution)/shard_map/ppermute | solution.py:329
  58.9 1.3 %collective-permute-done.13 = bf16[1,96,256]{2,1,0:T(8,128)(2,1)S(1)} collective-permute-done((bf16[1,96,256]{2,1,0:T(8,128)(2,1)S(1)}, bf16[1,96,256]{2,1,0:T(8,128)(2,1)S(1)}, u32[]{:S(2)}, u32[]{:S(2)}) %collective-permute-start.13) | collective-permute-done | bytes 49184 | tf_op jit(solution)/shard_map/ppermute | solution.py:329
  60.2 1.5 %collective-permute-done.11 = bf16[1,96,256]{2,1,0:T(8,128)(2,1)S(1)} collective-permute-done((bf16[1,96,256]{2,1,0:T(8,128)(2,1)S(1)}, bf16[1,96,256]{2,1,0:T(8,128)(2,1)S(1)}, u32[]{:S(2)}, u32[]{:S(2)}) %collective-permute-start.11) | collective-permute-done | bytes 49184 | tf_op jit(solution)/shard_map/ppermute | solution.py:329
  61.7 1.3 %collective-permute-start.16 = (bf16[4,96,256]{2,1,0:T(8,128)(2,1)S(1)}, bf16[4,96,256]{2,1,0:T(8,128)(2,1)S(1)}, u32[]{:S(2)}, u32[]{:S(2)}) collective-permute-start(bf16[4,96,256]{2,1,0:T(8,128)(2,1)S(1)} %pad_maximum_fusion), channel_id=1, source_target_pairs={{0,5},{1,4},{2,7},{3,6},{4,1},{5,0},{6,3},{7,2},{8,13},{9,12},{10,... | collective-permute-start | bytes 589832 | tf_op jit(solution)/shard_map/ppermute | solution.py:329
  62.9 0.5 collective-permute-start.15
  63.4 0.9 collective-permute-start.14
  64.4 5.7 %collective-permute-done.14 = bf16[4,96,256]{2,1,0:T(8,128)(2,1)S(1)} collective-permute-done((bf16[4,96,256]{2,1,0:T(8,128)(2,1)S(1)}, bf16[4,96,256]{2,1,0:T(8,128)(2,1)S(1)}, u32[]{:S(2)}, u32[]{:S(2)}) %collective-permute-start.14) | collective-permute-done | bytes 196640 | tf_op jit(solution)/shard_map/ppermute | solution.py:329
  70.1 0.5 collective-permute-done.15
  70.6 3.6 %collective-permute-start.17 = (bf16[16,96,256]{2,1,0:T(8,128)(2,1)S(1)}, bf16[16,96,256]{2,1,0:T(8,128)(2,1)S(1)}, u32[]{:S(2)}, u32[]{:S(2)}) collective-permute-start(bf16[16,96,256]{2,1,0:T(8,128)(2,1)S(1)} %constant_dynamic-update-slice_fusion.refs_0_), channel_id=1, source_target_pairs={{0,2},{1,3},{2,0},{3,1},{4,6},{5,7},{6,4},{7,5},{8,10},{9,11},{10,... | collective-permute-start | bytes 2359304 | tf_op jit(solution)/shard_map/ppermute | solution.py:329
  74.3 0.1 collective-permute-start.2
  74.3 3.0 %collective-permute-start.3 = (bf16[704,256]{1,0:T(8,128)(2,1)S(1)}, bf16[704,256]{1,0:T(8,128)(2,1)S(1)}, u32[]{:S(2)}, u32[]{:S(2)}) collective-permute-start(bf16[704,256]{1,0:T(8,128)(2,1)S(1)} %get-tuple-element.44), channel_id=1, source_target_pairs={{2,4},{6,8},{10,12},{14,16},{18,20},{22,24},{26,28},{4,2},{8,6},{1... | collective-permute-start | bytes 1081352 | tf_op jit(solution)/shard_map/ppermute | solution.py:414
  77.3 8.2 %collective-permute-done.3.other_ref = bf16[704,256]{1,0:T(8,128)(2,1)S(1)} collective-permute-done((bf16[704,256]{1,0:T(8,128)(2,1)S(1)}, bf16[704,256]{1,0:T(8,128)(2,1)S(1)}, u32[]{:S(2)}, u32[]{:S(2)}) %collective-permute-start.3) | collective-permute-done | bytes 360480 | tf_op jit(solution)/shard_map/ppermute | solution.py:414
  85.5 5.9 %shard_map.214 = bf16[4,4,176,256]{3,2,1,0:T(8,128)(2,1)} custom-call(s32[4,4,176]{2,1,0:T(4,128)S(1)} %copy-done.4, bf16[4,4,176,256]{3,2,1,0:T(8,128)(2,1)S(1)} %copy-done, bf16[2816,256]{1,0:T(8,128)(2,1)S(1)} %get-tuple-element.42.grad_ref, bf16[704,256]{1,0:T(8,128)(2,1)S(1)} %collective-permute-done.2.mate_ref, ...), custom_call_target="tpu_custom_call" | custom-call | tf_op jit(solution)/shard_map/pallas_call | solution.py:481
  91.4 1.9 %shard_map.218 = (f32[2304,256]{1,0:T(8,128)}, f32[1,256]{1,0:T(1,128)}, f32[256,256]{1,0:T(8,128)}, f32[1,256]{1,0:T(1,128)}, f32[256,64]{1,0:T(8,128)S(1)}, /*...) custom-call(bf16[16,96,256]{2,1,0:T(8,128)(2,1)S(1)} %constant_dynamic-update-slice_fusion.refs_0_,, ...), custom_call_target="tpu_custom_call" | custom-call | tf_op jit(solution)/shard_map/pallas_call | solution.py:492
  93.3 0.7 copy.26
  94.0 0.8 copy.27
  (39 shorter events, 0.2 us)
Async XLA Ops:
  0.6 6.8 %copy-start.11 = (bf16[256]{0:T(256)(128)(2,1)S(1)}, bf16[256]{0:T(256)(128)(2,1)}, u32[]{:S(2)}) copy-start(bf16[256]{0:T(256)(128)(2,1)} %param.17) | copy-start | bytes 1540
  0.7 7.4 %copy-start.12 = (bf16[256]{0:T(256)(128)(2,1)S(1)}, bf16[256]{0:T(256)(128)(2,1)}, u32[]{:S(2)}) copy-start(bf16[256]{0:T(256)(128)(2,1)} %param.19) | copy-start | bytes 1540
  0.7 8.0 %copy-start.13 = (bf16[256]{0:T(256)(128)(2,1)S(1)}, bf16[256]{0:T(256)(128)(2,1)}, u32[]{:S(2)}) copy-start(bf16[256]{0:T(256)(128)(2,1)} %param.24) | copy-start | bytes 1540
  0.7 18.6 %copy-start.4 = (s32[4,4,176]{2,1,0:T(4,128)S(1)}, s32[4,4,176]{2,1,0:T(4,128)}, u32[]{:S(2)}) copy-start(s32[4,4,176]{2,1,0:T(4,128)} %crop_ref.3) | copy-start | bytes 33796
  0.7 18.6 %copy-start = (bf16[4,4,176,256]{3,2,1,0:T(8,128)(2,1)S(1)}, bf16[4,4,176,256]{3,2,1,0:T(8,128)(2,1)}, u32[]{:S(2)}) copy-start(bf16[4,4,176,256]{3,2,1,0:T(8,128)(2,1)} %latent_ref.3) | copy-start | bytes 4325380
  0.7 18.6 %copy-start.1 = (bf16[3,3,256,256]{3,2,1,0:T(8,128)(2,1)S(1)}, bf16[3,3,256,256]{3,2,1,0:T(8,128)(2,1)}, u32[]{:S(2)}) copy-start(bf16[3,3,256,256]{3,2,1,0:T(8,128)(2,1)} %param.16) | copy-start | bytes 3538948
  2.9 16.4 %collective-permute-start.1 = (bf16[4,176,256]{2,1,0:T(8,128)(2,1)}, bf16[4,176,256]{2,1,0:T(8,128)(2,1)S(1)}, u32[]{:S(2)}, u32[]{:S(2)}) collective-permute-start(bf16[4,176,256]{2,1,0:T(8,128)(2,1)} %get-tuple-element.76), channel_id=1, source_target_pairs={{2,4},{6,8},{10,12},{14,16},{18,20},{22,24},{26,28},{4,2},{8,6},{1... | collective-permute-start | bytes 1081352 | tf_op jit(solution)/shard_map/ppermute | solution.py:414
  7.4 11.9 %collective-permute-start = (bf16[4,176,256]{2,1,0:T(8,128)(2,1)}, bf16[4,176,256]{2,1,0:T(8,128)(2,1)S(1)}, u32[]{:S(2)}, u32[]{:S(2)}) collective-permute-start(bf16[4,176,256]{2,1,0:T(8,128)(2,1)} %get-tuple-element.77), channel_id=1, source_target_pairs={{0,2},{2,0},{4,6},{6,4},{8,10},{10,8},{12,14},{14,12},{16,18},{18,... | collective-permute-start | bytes 1081352 | tf_op jit(solution)/shard_map/ppermute | solution.py:414
  11.0 1.4 %copy-start.2 = (bf16[4,4,176,256]{3,2,1,0:T(8,128)(2,1)S(1)}, bf16[4,4,176,256]{3,2,1,0:T(8,128)(2,1)}, u32[]{:S(2)}) copy-start(bf16[4,4,176,256]{3,2,1,0:T(8,128)(2,1)} %out_grad_ref.1) | copy-start | bytes 4325380
  12.4 0.7 copy-start.5
  13.1 0.8 copy-start.6
  13.9 0.7 copy-start.9
  14.6 0.7 copy-start.10
  15.2 4.1 %copy-start.3 = (bf16[256,256]{1,0:T(8,128)(2,1)S(1)}, bf16[256,256]{1,0:T(8,128)(2,1)}, u32[]{:S(2)}) copy-start(bf16[256,256]{1,0:T(8,128)(2,1)} %mix_weight_ref.1) | copy-start | bytes 393220
  15.2 4.1 %copy-start.7 = (bf16[1,256]{1,0:T(2,128)(2,1)S(1)}, bf16[1,256]{1,0:T(2,128)(2,1)}, u32[]{:S(2)}) copy-start(bf16[1,256]{1,0:T(2,128)(2,1)} %reshape.55.conv_bias_ref) | copy-start | bytes 1540
  15.2 4.1 %copy-start.8 = (bf16[1,256]{1,0:T(2,128)(2,1)S(1)}, bf16[1,256]{1,0:T(2,128)(2,1)}, u32[]{:S(2)}) copy-start(bf16[1,256]{1,0:T(2,128)(2,1)} %reshape.56.mix_bias_ref) | copy-start | bytes 1540
  32.7 2.5 %collective-permute-start.4 = (bf16[16,96,256]{2,1,0:T(8,128)(2,1)S(1)}, bf16[16,96,256]{2,1,0:T(8,128)(2,1)S(1)}, u32[]{:S(2)}, u32[]{:S(2)}) collective-permute-start(bf16[16,96,256]{2,1,0:T(8,128)(2,1)S(1)} %get-tuple-element.47), channel_id=1, source_target_pairs={{0,2},{1,3},{2,0},{3,1},{4,6},{5,7},{6,4},{7,5},{8,10},{9,11},{10,... | collective-permute-start | bytes 2359304 | tf_op jit(solution)/shard_map/ppermute | solution.py:329
  35.4 6.2 %collective-permute-start.5 = (bf16[4,96,256]{2,1,0:T(8,128)(2,1)S(1)}, bf16[4,96,256]{2,1,0:T(8,128)(2,1)S(1)}, u32[]{:S(2)}, u32[]{:S(2)}) collective-permute-start(bf16[4,96,256]{2,1,0:T(8,128)(2,1)S(1)} %get-tuple-element.49), channel_id=1, source_target_pairs={{0,1},{1,0},{2,3},{3,2},{4,5},{5,4},{6,7},{7,6},{8,9},{9,8},{10,11... | collective-permute-start | bytes 589832 | tf_op jit(solution)/shard_map/ppermute | solution.py:329
  36.7 5.8 %collective-permute-start.6 = (bf16[4,96,256]{2,1,0:T(8,128)(2,1)S(1)}, bf16[4,96,256]{2,1,0:T(8,128)(2,1)S(1)}, u32[]{:S(2)}, u32[]{:S(2)}) collective-permute-start(bf16[4,96,256]{2,1,0:T(8,128)(2,1)S(1)} %get-tuple-element.50), channel_id=1, source_target_pairs={{0,4},{1,5},{2,6},{3,7},{4,0},{5,1},{6,2},{7,3},{8,12},{9,13},{10,... | collective-permute-start | bytes 589832 | tf_op jit(solution)/shard_map/ppermute | solution.py:329
  37.9 8.9 %collective-permute-start.7 = (bf16[4,96,256]{2,1,0:T(8,128)(2,1)S(1)}, bf16[4,96,256]{2,1,0:T(8,128)(2,1)S(1)}, u32[]{:S(2)}, u32[]{:S(2)}) collective-permute-start(bf16[4,96,256]{2,1,0:T(8,128)(2,1)S(1)} %get-tuple-element.51), channel_id=1, source_target_pairs={{0,5},{1,4},{2,7},{3,6},{4,1},{5,0},{6,3},{7,2},{8,13},{9,12},{10,... | collective-permute-start | bytes 589832 | tf_op jit(solution)/shard_map/ppermute | solution.py:329
  46.9 3.9 %collective-permute-start.8 = (bf16[1,96,256]{2,1,0:T(8,128)(2,1)S(1)}, bf16[1,96,256]{2,1,0:T(8,128)(2,1)S(1)}, u32[]{:S(2)}, u32[]{:S(2)}) collective-permute-start(bf16[1,96,256]{2,1,0:T(8,128)(2,1)S(1)} %get-tuple-element.53), channel_id=1, source_target_pairs={{0,16},{1,17},{2,18},{3,19},{4,20},{5,21},{6,22},{7,23},{8,24},{9,... | collective-permute-start | bytes 147464 | tf_op jit(solution)/shard_map/ppermute | solution.py:329
  49.3 3.2 %collective-permute-start.9 = (bf16[1,96,256]{2,1,0:T(8,128)(2,1)S(1)}, bf16[1,96,256]{2,1,0:T(8,128)(2,1)S(1)}, u32[]{:S(2)}, u32[]{:S(2)}) collective-permute-start(bf16[1,96,256]{2,1,0:T(8,128)(2,1)S(1)} %get-tuple-element.54), channel_id=1, source_target_pairs={{0,8},{1,9},{2,10},{3,11},{4,12},{5,13},{6,14},{7,15},{8,0},{9,1},... | collective-permute-start | bytes 147464 | tf_op jit(solution)/shard_map/ppermute | solution.py:329
  50.5 4.7 %collective-permute-start.10 = (bf16[1,96,256]{2,1,0:T(8,128)(2,1)S(1)}, bf16[1,96,256]{2,1,0:T(8,128)(2,1)S(1)}, u32[]{:S(2)}, u32[]{:S(2)}) collective-permute-start(bf16[1,96,256]{2,1,0:T(8,128)(2,1)S(1)} %get-tuple-element.55), channel_id=1, source_target_pairs={{0,24},{1,25},{2,26},{3,27},{4,28},{5,29},{6,30},{7,31},{8,16},{9,... | collective-permute-start | bytes 147464 | tf_op jit(solution)/shard_map/ppermute | solution.py:329
  55.2 4.9 %collective-permute-start.13 = (bf16[1,96,256]{2,1,0:T(8,128)(2,1)S(1)}, bf16[1,96,256]{2,1,0:T(8,128)(2,1)S(1)}, u32[]{:S(2)}, u32[]{:S(2)}) collective-permute-start(bf16[1,96,256]{2,1,0:T(8,128)(2,1)S(1)} %shard_map.217), channel_id=1, source_target_pairs={{0,24},{1,25},{2,26},{3,27},{4,28},{5,29},{6,30},{7,31},{8,16},{9,... | collective-permute-start | bytes 147464 | tf_op jit(solution)/shard_map/ppermute | solution.py:329
  56.3 3.9 %collective-permute-start.12 = (bf16[1,96,256]{2,1,0:T(8,128)(2,1)S(1)}, bf16[1,96,256]{2,1,0:T(8,128)(2,1)S(1)}, u32[]{:S(2)}, u32[]{:S(2)}) collective-permute-start(bf16[1,96,256]{2,1,0:T(8,128)(2,1)S(1)} %shard_map.217), channel_id=1, source_target_pairs={{0,8},{1,9},{2,10},{3,11},{4,12},{5,13},{6,14},{7,15},{8,0},{9,1},... | collective-permute-start | bytes 147464 | tf_op jit(solution)/shard_map/ppermute | solution.py:329
  56.3 5.3 %collective-permute-start.11 = (bf16[1,96,256]{2,1,0:T(8,128)(2,1)S(1)}, bf16[1,96,256]{2,1,0:T(8,128)(2,1)S(1)}, u32[]{:S(2)}, u32[]{:S(2)}) collective-permute-start(bf16[1,96,256]{2,1,0:T(8,128)(2,1)S(1)} %shard_map.217), channel_id=1, source_target_pairs={{0,16},{1,17},{2,18},{3,19},{4,20},{5,21},{6,22},{7,23},{8,24},{9,... | collective-permute-start | bytes 147464 | tf_op jit(solution)/shard_map/ppermute | solution.py:329
  61.7 8.9 %collective-permute-start.16 = (bf16[4,96,256]{2,1,0:T(8,128)(2,1)S(1)}, bf16[4,96,256]{2,1,0:T(8,128)(2,1)S(1)}, u32[]{:S(2)}, u32[]{:S(2)}) collective-permute-start(bf16[4,96,256]{2,1,0:T(8,128)(2,1)S(1)} %pad_maximum_fusion), channel_id=1, source_target_pairs={{0,5},{1,4},{2,7},{3,6},{4,1},{5,0},{6,3},{7,2},{8,13},{9,12},{10,... | collective-permute-start | bytes 589832 | tf_op jit(solution)/shard_map/ppermute | solution.py:329
  62.9 7.7 %collective-permute-start.15 = (bf16[4,96,256]{2,1,0:T(8,128)(2,1)S(1)}, bf16[4,96,256]{2,1,0:T(8,128)(2,1)S(1)}, u32[]{:S(2)}, u32[]{:S(2)}) collective-permute-start(bf16[4,96,256]{2,1,0:T(8,128)(2,1)S(1)} %pad_maximum_fusion), channel_id=1, source_target_pairs={{0,4},{1,5},{2,6},{3,7},{4,0},{5,1},{6,2},{7,3},{8,12},{9,13},{10,... | collective-permute-start | bytes 589832 | tf_op jit(solution)/shard_map/ppermute | solution.py:329
  63.4 6.6 %collective-permute-start.14 = (bf16[4,96,256]{2,1,0:T(8,128)(2,1)S(1)}, bf16[4,96,256]{2,1,0:T(8,128)(2,1)S(1)}, u32[]{:S(2)}, u32[]{:S(2)}) collective-permute-start(bf16[4,96,256]{2,1,0:T(8,128)(2,1)S(1)} %pad_maximum_fusion), channel_id=1, source_target_pairs={{0,1},{1,0},{2,3},{3,2},{4,5},{5,4},{6,7},{7,6},{8,9},{9,8},{10,11... | collective-permute-start | bytes 589832 | tf_op jit(solution)/shard_map/ppermute | solution.py:329
  70.6 20.8 %collective-permute-start.17 = (bf16[16,96,256]{2,1,0:T(8,128)(2,1)S(1)}, bf16[16,96,256]{2,1,0:T(8,128)(2,1)S(1)}, u32[]{:S(2)}, u32[]{:S(2)}) collective-permute-start(bf16[16,96,256]{2,1,0:T(8,128)(2,1)S(1)} %constant_dynamic-update-slice_fusion.refs_0_), channel_id=1, source_target_pairs={{0,2},{1,3},{2,0},{3,1},{4,6},{5,7},{6,4},{7,5},{8,10},{9,11},{10,... | collective-permute-start | bytes 2359304 | tf_op jit(solution)/shard_map/ppermute | solution.py:329
  74.3 3.0 %collective-permute-start.2 = (bf16[704,256]{1,0:T(8,128)(2,1)S(1)}, bf16[704,256]{1,0:T(8,128)(2,1)S(1)}, u32[]{:S(2)}, u32[]{:S(2)}) collective-permute-start(bf16[704,256]{1,0:T(8,128)(2,1)S(1)} %get-tuple-element.43), channel_id=1, source_target_pairs={{0,2},{2,0},{4,6},{6,4},{8,10},{10,8},{12,14},{14,12},{16,18},{18,... | collective-permute-start | bytes 1081352 | tf_op jit(solution)/shard_map/ppermute | solution.py:414
  74.3 11.2 %collective-permute-start.3 = (bf16[704,256]{1,0:T(8,128)(2,1)S(1)}, bf16[704,256]{1,0:T(8,128)(2,1)S(1)}, u32[]{:S(2)}, u32[]{:S(2)}) collective-permute-start(bf16[704,256]{1,0:T(8,128)(2,1)S(1)} %get-tuple-element.44), channel_id=1, source_target_pairs={{2,4},{6,8},{10,12},{14,16},{18,20},{22,24},{26,28},{4,2},{8,6},{1... | collective-permute-start | bytes 1081352 | tf_op jit(solution)/shard_map/ppermute | solution.py:414

commit v2 on v1

v2 whole, which is shorter than its diff:
```python
import functools

import jax
import jax.numpy as jnp
from jax import lax
from jax.experimental import pallas as pl
from jax.experimental.pallas import tpu as pltpu
from jax.sharding import PartitionSpec as P

commit_weight = 0.25
low = jnp.bfloat16
wide = jnp.float32
bit_up, bit_left, bit_right, bit_down = 1, 3, 4, 6
tile_rows = 16
vmem_bytes = 28 * 2**20
in_hbm = pl.BlockSpec(memory_space=pltpu.HBM)
anywhere = pl.BlockSpec(memory_space=pl.ANY)
in_vmem = pl.BlockSpec(memory_space=pltpu.VMEM)


def mm(lhs, rhs):
    return jnp.dot(lhs, rhs, preferred_element_type=wide)


def mm_nt(lhs, rhs):
    return lax.dot_general(lhs, rhs, (((1,), (1,)), ((), ())), preferred_element_type=wide)


def mm_tn(lhs, rhs):
    return lax.dot_general(lhs, rhs, (((0,), (0,)), ((), ())), preferred_element_type=wide)


def sigmoid(values):
    return 0.5 * jnp.tanh(0.5 * values) + 0.5


def code_columns(code_ref):
    canvases, rows, across = code_ref.shape
    flat = code_ref[...].reshape(canvases * rows, across)
    extra = -across % 128
    if extra:
        flat = jnp.concatenate([flat, jnp.zeros((canvases * rows, extra), flat.dtype)], axis=1)
    return flat.T[:across]


def row_codes(columns, row, canvases, rows, lanes):
    pieces = [
        jnp.broadcast_to(
            columns[:, n * rows + row : n * rows + row + 1], (columns.shape[0], lanes)
        )
        for n in range(canvases)
    ]
    return jnp.concatenate(pieces, axis=0)


def chunks(count):
    return [(at, pl.ds(at, tile_rows)) for at in range(0, count, tile_rows)]


def pick(codes, bit, values):
    chosen = (codes & 2**bit) != 0
    parts = []
    for at in range(0, values.shape[1], 128):
        part = values[:, at : at + 128]
        parts.append(jnp.where(chosen, part, jnp.zeros_like(part)))
    return jnp.concatenate(parts, axis=1)


def store_slab(slab_ref, at, codes, values):
    count = codes.shape[0]
    channels = slab_ref.shape[1] // 3
    steps = chunks(count)
    held = [values(start) for start, _ in steps]
    for place, (start, _) in enumerate(steps):
        here = held[place]
        span = pl.ds(at + start, tile_rows)
        spots = codes[start : start + tile_rows]
        before = held[place - 1][tile_rows - 8 :]
        after = held[(place + 1) % len(steps)][:8]
        left = pltpu.roll(jnp.concatenate([before, here], axis=0), 1, 0)[8:]
        right = jnp.concatenate([here, after], axis=0)
        right = pltpu.roll(right, right.shape[0] - 1, 0)[:tile_rows]
        slab_ref[span, :channels] = pick(spots, bit_left, left).astype(low)
        slab_ref[span, channels : 2 * channels] = here.astype(low)
        slab_ref[span, 2 * channels :] = pick(spots, bit_right, right).astype(low)


def edge_kernel(latent_ref, mate_ref, other_ref, sems):
    rows = latent_ref.shape[1]
    odd = lax.axis_index("strip") % 2
    edge = (rows - 1) * (1 - odd)
    near = pltpu.make_async_copy(latent_ref.at[:, edge], mate_ref, sems.at[0])
    far = pltpu.make_async_copy(latent_ref.at[:, rows - 1 - edge], other_ref, sems.at[1])
    near.start()
    far.start()
    near.wait()
    far.wait()


def code_kernel(
    index_hbm,
    codebook_hbm,
    decode_weight_hbm,
    out_grad_hbm,
    latent_hbm,
    crop_hbm,
    conv_weight_hbm,
    mix_weight_hbm,
    term_ref,
    picks_ref,
    weight_grad_ref,
    bias_grad_ref,
    latent_ref,
    crop_ref,
    conv_weight_ref,
    mix_weight_ref,
    index_ref,
    codebook_ref,
    decode_weight_ref,
    out_grad_ref,
    sems,
):
    canvases, rows, across = index_ref.shape
    size, entries = codebook_ref.shape
    channels = decode_weight_ref.shape[1]
    count = canvases * across
    pairs = [
        (index_hbm, index_ref),
        (codebook_hbm, codebook_ref),
        (decode_weight_hbm, decode_weight_ref),
    ]
    pairs += [(out_grad_hbm.at[:, row], out_grad_ref.at[row]) for row in range(rows)]
    pairs += [
        (latent_hbm, latent_ref),
        (crop_hbm, crop_ref),
        (conv_weight_hbm, conv_weight_ref),
        (mix_weight_hbm, mix_weight_ref),
    ]
    copies = [
        pltpu.make_async_copy(source, target, sems.at[place])
        for place, (source, target) in enumerate(pairs)
    ]
    for copy in copies:
        copy.start()
    for copy in copies[:3]:
        copy.wait()
    codebook = codebook_ref[...]
    both = jnp.concatenate([codebook * low(-0.5), codebook * low(2.0)], axis=0)
    weight = decode_weight_ref[...]
    weight_top = jnp.concatenate([weight, jnp.zeros_like(weight)], axis=0)
    columns = code_columns(index_ref)
    weight_sum, bias_sum = None, None
    for row in range(rows):
        codes = row_codes(columns, row, canvases, rows, entries)
        picks = lax.broadcasted_iota(jnp.int32, codes.shape, 1) == codes
        picks = picks.astype(wide).astype(low)
        picks_ref[pl.ds(row * count, count)] = picks
        copies[3 + row].wait()
        grad = out_grad_ref[row].reshape(count, channels)
        term = mm_nt(picks, both) + mm_nt(grad, weight_top)
        term_ref[row] = term
        weight_part = mm_tn(term.astype(low), grad)
        bias_part = jnp.sum(grad.astype(wide), axis=0, keepdims=True)
        weight_sum = weight_part if weight_sum is None else weight_sum + weight_part
        bias_sum = bias_part if bias_sum is None else bias_sum + bias_part
    weight_grad_ref[...] = 0.5 * weight_sum[size:]
    bias_grad_ref[...] = bias_sum
    for copy in copies[3 + rows :]:
        copy.wait()


def decoded_kernel(term_ref, decode_weight_ref, decode_bias_ref, after_ref, decoded_ref):
    canvases, rows, across, channels = decoded_ref.shape
    weight = decode_weight_ref[...] * low(0.5)
    weight = jnp.concatenate([jnp.zeros_like(weight), weight], axis=0)
    bias = decode_bias_ref[...].astype(wide).reshape(1, channels)
    for row in range(rows):
        decoded = (mm(term_ref[row].astype(low), weight) + bias).astype(low)
        decoded_ref[:, row] = decoded.reshape(canvases, across, channels)


def rows_kernel(
    mine,
    crop_ref,
    latent_ref,
    term_ref,
    conv_weight_ref,
    conv_bias_ref,
    mix_weight_ref,
    mix_bias_ref,
    proj_weight_ref,
    proj_bias_ref,
    *refs,
):
    outs = refs[-9:]
    slab_ref, grad_ref, up_ref, down_ref, second_ref, stream_ref, codes_ref = outs[:7]
    branch_grad_ref, sums_ref = outs[7:]
    canvases, rows, across = crop_ref.shape
    channels = latent_ref.shape[3]
    size = proj_weight_ref.shape[0]
    count = canvases * across
    odd = lax.axis_index("strip") % 2
    columns = code_columns(crop_ref)
    codes = [row_codes(columns, row, canvases, rows, 128) for row in range(rows)]

    def silu(values):
        values = values.astype(wide)
        return values * sigmoid(values)

    def own(row):
        def values(at):
            return silu(latent_ref[at // across, row, pl.ds(at % across, tile_rows)])

        return values

    def beside(first_ref, second_ref, swap):
        def values(at):
            span = pl.ds(at % across, tile_rows)
            one, two = first_ref[at // across, span], second_ref[at // across, span]
            return silu(jnp.where(swap, one, two))

        return values

    inner = 0 not in mine or rows == 1
    if inner or rows <= 2:
        for row in range(rows):
            store_slab(slab_ref, (row + 1) * count, codes[row], own(row))
    if 0 in mine:
        mate_ref, other_ref = refs[:2]
        store_slab(slab_ref, 0, codes[0], beside(mate_ref, other_ref, odd == 1))
        end = (rows + 1) * count
        store_slab(slab_ref, end, codes[rows - 1], beside(other_ref, mate_ref, odd == 1))

    proj = proj_weight_ref[...]
    proj_both = jnp.concatenate([proj * low(2 * commit_weight), proj * low(-2.0)], axis=0)
    proj_top = jnp.concatenate([proj, jnp.zeros_like(proj)], axis=0)
    conv_bias = conv_bias_ref[...].astype(wide).reshape(1, channels)
    mix_bias = mix_bias_ref[...].astype(wide).reshape(1, channels)
    proj_bias = proj_bias_ref[...].astype(wide).reshape(1, size)
    proj_bias = jnp.concatenate([2 * commit_weight * proj_bias, -2.0 * proj_bias], axis=1)
    sums = [None, None, None]
    steps = chunks(count)

    def add_to(place, values):
        values = values[:8] + values[8:]
        sums[place] = values if sums[place] is None else sums[place] + values

    held = None
    for row, was in zip((*mine, None), (None, *mine), strict=True):
        if row is not None:
            at = row * count
            conv_mid = mm(slab_ref[pl.ds(at + count, count)], conv_weight_ref[1])
        if was is not None:
            back = was * count
            slope = held
            branch = mm(second_ref[pl.ds(back, count)], mix_weight_ref[...])
            for start, _ in steps:
                span = pl.ds(back + start, tile_rows)
                latent = latent_ref[start // across, was, pl.ds(start % across, tile_rows)]
                part = latent.astype(wide) + (branch[start : start + tile_rows] + mix_bias)
                stream_ref[span] = part.astype(low)
        if row is not None:
            conv_up = mm(slab_ref[pl.ds(at, count)], conv_weight_ref[0])
        if was is not None:
            code = mm_nt(stream_ref[pl.ds(back, count)], proj_both)
            for start, near in steps:
                part = code[start : start + tile_rows] + (term_ref[was, near] + proj_bias)
                codes_ref[pl.ds(back + start, tile_rows)] = part.astype(low)
                add_to(2, part)
        if row is not None:
            conv_down = mm(slab_ref[pl.ds(at + 2 * count, count)], conv_weight_ref[2])
        if was is not None:
            branch_grad = mm(codes_ref[pl.ds(back, count)], proj_top)
            for start, near in steps:
                part = branch_grad[start : start + tile_rows]
                branch_grad_ref[was, near] = part.astype(low)
                add_to(1, part)
        if row is not None:
            held = []
            for start, _ in steps:
                some = slice(start, start + tile_rows)
                conv = pick(codes[row][some], bit_up, conv_up[some])
                conv = conv + pick(codes[row][some], bit_down, conv_down[some])
                conv = (conv + conv_mid[some]) + conv_bias
                gate = sigmoid(conv)
                second_ref[pl.ds(at + start, tile_rows)] = (conv * gate).astype(low)
                held.append(gate * (1.0 + conv * (1.0 - gate)))
        if was is not None:
            grad = mm_nt(branch_grad_ref[was], mix_weight_ref[...])
            for place, (start, _) in enumerate(steps):
                some = slice(start, start + tile_rows)
                span = pl.ds(back + start, tile_rows)
                part = grad[some] * slope[place]
                grad_ref[span] = part.astype(low)
                up_ref[span] = pick(codes[was][some], bit_up, part).astype(low)
                down_ref[span] = pick(codes[was][some], bit_down, part).astype(low)
                add_to(0, part)
    sums = [jnp.sum(values, axis=0, keepdims=True) for values in sums]
    sums[2] = jnp.concatenate([sums[2]] * (channels // sums[2].shape[1]), axis=1)
    blank = jnp.zeros((sums_ref.shape[0] - 3, channels), wide)
    sums = jnp.concatenate([*sums, blank], axis=0)
    if len(refs) > 9 + 2 * (0 in mine):
        sums = sums + refs[-10][...]
    sums_ref[...] = sums


def edge_rows_kernel(grad_ref, mate_ref, other_ref):
    count = mate_ref.shape[0]
    odd = lax.axis_index("strip") % 2
    first, last = grad_ref[pl.ds(0, count)], grad_ref[pl.ds(grad_ref.shape[0] - count, count)]
    mate_ref[...] = jnp.where(odd == 1, first, last)
    other_ref[...] = jnp.where(odd == 1, last, first)


def weight_kernel(
    plan,
    mine,
    slab_ref,
    grad_ref,
    up_ref,
    down_ref,
    second_ref,
    stream_ref,
    codes_ref,
    branch_grad_ref,
    sums_ref,
    picks_ref,
    decode_weight_grad_ref,
    decode_bias_grad_ref,
    after_ref,
    out_ref,
    message_ref,
):
    total, channels = grad_ref.shape
    rows, count, _ = branch_grad_ref.shape
    size = decode_weight_grad_ref.shape[0]
    entries = picks_ref.shape[1]
    triple = 3 * channels
    me = plan.index()
    half = plan.shards // 2
    core, place = me // half, me % half
    wanted = core if mine else 1 - core

    def step(row_step, weighted_ref):
        span = pl.ds(row_step * count, total)
        return mm_tn(slab_ref[span], weighted_ref[...]).astype(low)

    def fill(parts):
        at = 0
        for part in parts:
            message_ref[pl.ds(at, part.shape[0])] = part
            at += part.shape[0]
        rest = message_ref.shape[0] - at
        if rest:
            message_ref[pl.ds(at, rest)] = jnp.zeros((rest, channels), low)

    @pl.when(wanted == 0)
    def _():
        fill([step(0, up_ref), step(1, grad_ref)])

    @pl.when(wanted == 1)
    def _():
        code_part = mm_tn(codes_ref[...], picks_ref[...])[size:].astype(low)
        sums = sums_ref[...]
        biases = [sums[0:1], sums[1:2], decode_bias_grad_ref[...], sums[2:3]]
        biases.append(jnp.zeros((tile_rows - len(biases), channels), wide))
        fill(
            [
                step(2, down_ref),
                mm_tn(second_ref[...], branch_grad_ref[...].reshape(total, channels)).astype(low),
                decode_weight_grad_ref[...].astype(low),
                mm_tn(codes_ref[...], stream_ref[...])[:size].astype(low),
                *[code_part[:, i : i + channels] for i in range(0, entries, channels)],
                jnp.concatenate(biases, axis=0).astype(low),
            ]
        )

    for piece in range(half):
        rows_of = pl.ds(piece * plan.piece_rows, plan.piece_rows)
        out_ref[piece ^ place] = message_ref[rows_of]


def input_kernel(
    mine,
    crop_ref,
    latent_ref,
    grad_ref,
    mate_ref,
    other_ref,
    branch_grad_ref,
    conv_weight_ref,
    after_ref,
    *refs,
):
    latent_grad_ref, slab_ref, out_ref, sems = refs[-4:]
    canvases, rows, across = crop_ref.shape
    channels = latent_ref.shape[3]
    count = canvases * across
    odd = lax.axis_index("strip") % 2
    columns = code_columns(crop_ref)
    codes = [row_codes(columns, row, canvases, rows, 128) for row in range(rows)]

    steps = chunks(count)

    def own(row):
        def values(at):
            return grad_ref[pl.ds(row * count + at, tile_rows)].astype(wide)

        return values

    def beside(first_ref, second_ref, swap):
        def values(at):
            span = pl.ds(at, tile_rows)
            return jnp.where(swap, first_ref[span], second_ref[span]).astype(wide)

        return values

    for row in range(rows):
        if any(abs(row - near) < 2 for near in mine):
            store_slab(slab_ref, (row + 1) * count, codes[row], own(row))
    if 0 in mine:
        store_slab(slab_ref, 0, codes[0], beside(mate_ref, other_ref, odd == 1))
    if rows - 1 in mine:
        end = (rows + 1) * count
        store_slab(slab_ref, end, codes[rows - 1], beside(other_ref, mate_ref, odd == 1))

    copies = []
    for place, row in enumerate(mine):
        spreads = []
        for row_step in range(3):
            part = None
            for col_step in range(3):
                weight = conv_weight_ref[
                    2 - row_step, (2 - col_step) * channels : (3 - col_step) * channels
                ]
                span = pl.ds((row + row_step) * count, count)
                term = mm_nt(
                    slab_ref[span, col_step * channels : (col_step + 1) * channels], weight
                )
                part = term if part is None else part + term
            spreads.append(part)
        for start, near in steps:
            some = slice(start, start + tile_rows)
            spread = pick(codes[row][some], bit_up, spreads[0][some])
            spread = spread + pick(codes[row][some], bit_down, spreads[2][some])
            spread = spread + spreads[1][some]
            inside = pl.ds(start % across, tile_rows)
            latent = latent_ref[start // across, row, inside].astype(wide)
            gate = sigmoid(latent)
            slope = gate * (1.0 + latent * (1.0 - gate))
            out = branch_grad_ref[row, near].astype(wide) + spread * slope
            out_ref[place, start // across, inside] = out.astype(low)
        copies.append(
            pltpu.make_async_copy(out_ref.at[place], latent_grad_ref.at[:, row], sems.at[place])
        )
        copies[-1].start()
    for copy in copies:
        copy.wait()


class Plan:
    def __init__(self, sizes, half_rows):
        self.sizes = sizes
        bits = {axis: [(axis, b) for b in range(size.bit_length() - 1)] for axis, size in sizes.items()}
        strip, canvas = bits["strip"], bits["canvas"]
        self.stages = [strip[:1], [*strip[1:2], *canvas[:1]], strip[2:4]]
        rest = [*strip[4:], *canvas[1:]]
        self.stages += [rest[i : i + 2] for i in range(0, len(rest), 2)]
        self.stages = [stage for stage in self.stages if stage]
        self.shards = sizes["strip"] * sizes["canvas"]
        self.piece_rows = -(-half_rows // (self.shards // 2 * tile_rows)) * tile_rows
        self.half_rows = self.shards // 2 * self.piece_rows

    def index(self):
        number = 0
        for stage in self.stages:
            for axis, bit in stage:
                number = number * 2 + (lax.axis_index(axis) // 2**bit) % 2
        return number

    def partner(self, stage, step):
        change = {"strip": 0, "canvas": 0}
        for place, (axis, bit) in enumerate(reversed(stage)):
            if step >> place & 1:
                change[axis] |= 1 << bit
        width = self.sizes["canvas"]
        return [
            (s * width + c, (s ^ change["strip"]) * width + (c ^ change["canvas"]))
            for s in range(self.sizes["strip"])
            for c in range(width)
        ]

    def swap(self, values, stage, step):
        return lax.ppermute(values, ("strip", "canvas"), self.partner(stage, step))


def add_kernel(count, after, *refs):
    ins, outs = refs[:count], refs[count + after :]
    depth = outs[0].shape[0]
    for place, out_ref in enumerate(outs):
        span = pl.ds(place * depth, depth)
        total = ins[0][span].astype(wide)
        for ref in ins[1:]:
            total = total + ref[span].astype(wide)
        out_ref[...] = total.astype(low)


def add_split(arrays, parts, after=()):
    depth, rows, channels = arrays[0].shape
    shape = jax.ShapeDtypeStruct((depth // parts, rows, channels), low)
    return pl.pallas_call(
        functools.partial(add_kernel, len(arrays), len(after)),
        in_specs=[in_vmem] * len(arrays) + [anywhere] * len(after),
        out_specs=[in_vmem] * parts,
        out_shape=[shape] * parts,
        compiler_params=pltpu.CompilerParams(vmem_limit_bytes=vmem_bytes),
    )(*arrays, *after)


def gate_kernel(*refs):
    pass


def gate(array, *after):
    return pl.pallas_call(
        gate_kernel,
        in_specs=[in_vmem] + [anywhere] * len(after),
        out_specs=in_vmem,
        out_shape=jax.ShapeDtypeStruct(array.shape, array.dtype),
        input_output_aliases={0: 0},
        compiler_params=pltpu.CompilerParams(vmem_limit_bytes=vmem_bytes),
    )(array, *after)


def join_kernel(count, *refs):
    at = 0
    for ref in refs[:count]:
        refs[-1][pl.ds(at, ref.shape[0])] = ref[...]
        at += ref.shape[0]


def join(arrays, *after):
    depth, rows, channels = arrays[0].shape
    return pl.pallas_call(
        functools.partial(join_kernel, len(arrays)),
        in_specs=[in_vmem] * len(arrays) + [anywhere] * len(after),
        out_specs=in_vmem,
        out_shape=jax.ShapeDtypeStruct((depth * len(arrays), rows, channels), low),
        compiler_params=pltpu.CompilerParams(vmem_limit_bytes=vmem_bytes),
    )(*arrays, *after)


def final_kernel(plan, count, sizes, *refs):
    ins, outs, gathered_ref = refs[:count], refs[count:-1], refs[-1]
    channels, size, entries = sizes
    me = plan.index()
    at = 0
    for ref in ins:
        for piece in range(ref.shape[0]):
            start = pl.multiple_of((me ^ at) * plan.piece_rows, plan.piece_rows)
            gathered_ref[pl.ds(start, plan.piece_rows)] = ref[piece]
            at += 1
    conv_ref, conv_bias_ref, mix_ref, mix_bias_ref, proj_ref, proj_bias_ref = outs[:6]
    codebook_ref, decode_ref, decode_bias_ref = outs[6:]
    triple = 3 * channels
    conv_ref[pl.ds(0, 2 * triple)] = gathered_ref[pl.ds(0, 2 * triple)].astype(wide)
    at = plan.half_rows
    conv_ref[pl.ds(2 * triple, triple)] = gathered_ref[pl.ds(at, triple)].astype(wide)
    at += triple
    mix_ref[...] = gathered_ref[pl.ds(at, channels)].astype(wide)
    at += channels
    decode_ref[...] = gathered_ref[pl.ds(at, size)].astype(wide)
    at += size
    proj_ref[...] = gathered_ref[pl.ds(at, size)].astype(wide)
    at += size
    for piece in range(entries // channels):
        part = gathered_ref[pl.ds(at, size)].astype(wide)
        codebook_ref[:, piece * channels : (piece + 1) * channels] = part
        at += size
    biases = gathered_ref[pl.ds(at, tile_rows)].astype(wide)
    conv_bias_ref[...] = biases[0:1]
    mix_bias_ref[...] = biases[1:2]
    decode_bias_ref[...] = biases[2:3]
    proj_bias_ref[...] = biases[3:4, :size]


def per_device(
    plan,
    latent_in,
    crop_code,
    code_index,
    conv_weight,
    conv_bias,
    mix_weight,
    mix_bias,
    proj_weight,
    proj_bias,
    codebook,
    decode_weight,
    decode_bias,
    out_grad,
):
    canvases, rows, across, channels = latent_in.shape
    entries, size = codebook.shape
    count = canvases * across
    total = rows * count
    strips = plan.sizes["strip"]
    struct = jax.ShapeDtypeStruct
    flat_weight = conv_weight.reshape(3, 3 * channels, channels)

    def far_away(*arrays):
        return [pltpu.with_memory_space_constraint(array, pltpu.HBM) for array in arrays]

    def call(kernel, ins, outs, shapes, scratch=(), flops=0, aliases=None):
        return pl.pallas_call(
            kernel,
            in_specs=list(ins),
            out_specs=list(outs),
            out_shape=list(shapes),
            scratch_shapes=list(scratch),
            input_output_aliases=aliases or {},
            compiler_params=pltpu.CompilerParams(vmem_limit_bytes=vmem_bytes),
            cost_estimate=pl.CostEstimate(flops=flops, bytes_accessed=0, transcendentals=0),
        )

    def trade(mate, other):
        near = [(i, i ^ 1) for i in range(strips)]
        far = [(i, i + 1) for i in range(1, strips - 1, 2)]
        far += [(target, source) for source, target in far]
        return lax.ppermute(mate, "strip", near), lax.ppermute(other, "strip", far)

    edge_shape = struct((canvases, across, channels), low)
    edges = call(
        edge_kernel,
        [in_hbm],
        [in_vmem] * 2,
        [edge_shape] * 2,
        [pltpu.SemaphoreType.DMA((2,))],
    )(*far_away(latent_in))
    mate, other = trade(*edges)
    outs = [
        struct((rows, count, 2 * size), wide),
        struct((total, entries), low),
        struct((size, channels), wide),
        struct((1, channels), wide),
        struct(latent_in.shape, low),
        struct(crop_code.shape, crop_code.dtype),
        struct(flat_weight.shape, low),
        struct(mix_weight.shape, low),
    ]
    held = [
        pltpu.VMEM(code_index.shape, code_index.dtype),
        pltpu.VMEM((size, entries), low),
        pltpu.VMEM((size, channels), low),
        pltpu.VMEM((rows, canvases, across, channels), low),
        pltpu.SemaphoreType.DMA((rows + 7,)),
    ]
    term, picks, decode_weight_grad, decode_bias_grad, latent, crop, near_weight, near_mix = call(
        code_kernel,
        [in_hbm] * 8,
        [in_vmem] * 8,
        outs,
        held,
        flops=6 * total * channels * channels,
    )(
        *far_away(
            code_index,
            codebook.T,
            decode_weight,
            out_grad,
            latent_in,
            crop_code,
            flat_weight,
            mix_weight,
        )
    )
    slab_shape = struct((total + 2 * count, 3 * channels), low)
    flat = struct((total, channels), low)
    kept = [slab_shape, flat, flat, flat, flat, flat, struct((total, 2 * size), low)]
    kept += [struct((rows, count, channels), low), struct((8, channels), wide)]
    inner, outer = tuple(range(1, rows - 1)), tuple(sorted({0, rows - 1}))
    shared = [crop, latent, term, near_weight, conv_bias, near_mix, mix_bias, proj_weight.T, proj_bias]

    def block_rows(mine, halo, before):
        ins = [*shared, *halo, *before]
        first = len(ins) - len(before)
        return call(
            functools.partial(rows_kernel, mine),
            [in_vmem] * len(ins),
            [in_vmem] * len(kept),
            kept,
            flops=7 * len(mine) * total * channels * channels,
            aliases={first + i: i for i in range(len(before))},
        )(*ins)

    before = block_rows(inner, (), ()) if inner else ()
    before = block_rows(outer, (mate, other), before)
    slab, grad, up, down, second, stream, codes, branch_grad, sums = before
    edges = call(
        edge_rows_kernel,
        [in_vmem],
        [in_vmem] * 2,
        [struct((count, channels), low)] * 2,
    )(grad)

    def weight_half(mine, after):
        ins = [slab, grad, up, down, second, stream, codes, branch_grad, sums, picks]
        ins += [decode_weight_grad, decode_bias_grad]
        return call(
            functools.partial(weight_kernel, plan, mine),
            [in_vmem] * len(ins) + [anywhere],
            [in_vmem],
            [struct((plan.shards // 2, plan.piece_rows, channels), low)],
            [pltpu.VMEM((plan.half_rows, channels), low)],
            flops=10 * total * channels * channels,
        )(*ins, after)[0]

    send = weight_half(False, edges[0])
    keep = weight_half(True, send)

    def input_rows(mine, halo, after, *before):
        return call(
            functools.partial(input_kernel, mine),
            [in_vmem] * 7 + [anywhere] + [in_hbm] * len(before),
            [in_hbm],
            [pltpu.HBM(latent_in.shape, low)],
            [
                pltpu.VMEM(slab_shape.shape, low),
                pltpu.VMEM((len(mine), canvases, across, channels), low),
                pltpu.SemaphoreType.DMA((len(mine),)),
            ],
            flops=11 * total * channels * channels,
            aliases={8: 0} if before else {},
        )(crop, latent, grad, *halo, branch_grad, near_weight, after, *before)[0]

    arrays = [keep, plan.swap(send, plan.stages[0], 1)]
    after = []
    for place, stage in enumerate(plan.stages[1:]):
        parts = add_split(arrays, 2 ** len(stage), after)
        arrays = [parts[0]]
        arrays += [plan.swap(parts[i], stage, i) for i in reversed(range(1, len(parts)))]
        after = []
        if place == 0:
            latent_grad = input_rows(inner, edges, parts[0])
            after = far_away(latent_grad)
        elif place == 1:
            decoded = call(
                decoded_kernel,
                [in_vmem, in_vmem, in_vmem, anywhere],
                [pl.BlockSpec()],
                [pltpu.HBM(out_grad.shape, low)],
                flops=4 * total * channels * channels,
            )(term, decode_weight, decode_bias, parts[0])[0]
            after = far_away(decoded)
    pieces = add_split(arrays, 1, after)
    halo = trade(*[gate(edge, pieces[0]) for edge in edges])
    for stage in reversed(plan.stages[1:]):
        gathered = join(pieces, *halo) if len(pieces) > 1 else pieces[0]
        others = [plan.swap(gathered, stage, i) for i in range(1, 2 ** len(stage))]
        pieces = [gathered, *others]
    latent_grad = input_rows(outer, halo, gathered, latent_grad)
    done = far_away(latent_grad)
    pieces = [pieces[0], *[gate(piece, *done) for piece in pieces[1:]]]
    arrays = [*pieces, *[plan.swap(piece, plan.stages[0], 1) for piece in pieces]]

    results = call(
        functools.partial(final_kernel, plan, len(arrays), (channels, size, entries)),
        [in_vmem] * len(arrays),
        [pl.BlockSpec()] * 9,
        [
            struct((9 * channels, channels), wide),
            struct((1, channels), wide),
            struct((channels, channels), wide),
            struct((1, channels), wide),
            struct((size, channels), wide),
            struct((1, size), wide),
            struct((size, entries), wide),
            struct((size, channels), wide),
            struct((1, channels), wide),
        ],
        [pltpu.VMEM((2 * plan.half_rows, channels), low)],
    )(*arrays)
    return (
        decoded,
        latent_grad,
        results[0].reshape(3, 3, channels, channels),
        results[1].reshape(-1),
        results[2],
        results[3].reshape(-1),
        results[4].T,
        results[5].reshape(-1),
        results[6].T,
        results[7],
        results[8].reshape(-1),
    )


def solution(mesh):
    sizes = {axis: mesh.shape[axis] for axis in ("strip", "canvas")}
    shared = P("canvas", "strip", None, None)
    codes = P("canvas", "strip", None)

    def wrapped(*args):
        channels = args[0].shape[3]
        entries, size = args[9].shape
        others = 4 * channels + 2 * size + size * (entries // channels) + tile_rows
        plan = Plan(sizes, max(6 * channels, others))
        return jax.shard_map(
            functools.partial(per_device, plan),
            mesh=mesh,
            in_specs=(shared, codes, codes, *[P()] * 9, shared),
            out_specs=(shared, shared, *[P()] * 9),
            check_vma=False,
        )(*args)

    return wrapped
```

time: 95.7 us -> 75.3 us (0.79)
  waiting for transfers between devices: 32.4 us -> 13.7 us
  local copies, waits for them, and re-layouts: 11.4 us -> 0.04 us
  Pallas kernels: 25.5 us -> 30.5 us
  starting transfers between devices: 24.5 us -> 28.9 us
    ppermute x14 -> x17, waiting for transfers between devices: 24.2 us -> 12.2 us  [swap(): return lax.ppermute(values, ('strip', 'canvas'), self.partner(stage, step))]
    unnamed x38 -> x12, local copies, waits for them, and re-layouts: 7.56 us -> 0.04 us
    ppermute x2, waiting for transfers between devices: 8.2 us -> 1.58 us  [trade(): lax.ppermute(other, 'strip', far)]
    pallas_call x7 -> x20, Pallas kernels: 25.5 us -> 30.5 us  [the longest x2 8.46 us: block_rows(): call(functools.partial(rows_kernel, mine), [in_vmem] * len(ins), [in_vmem...]
    ppermute x14 -> x17, starting transfers between devices: 16.9 us -> 19.7 us  [swap(): return lax.ppermute(values, ('strip', 'canvas'), self.partner(stage, step))]
    ppermute x2, starting transfers between devices: 0.15 us -> 2.57 us  [trade(): lax.ppermute(mate, 'strip', near)]
    squeeze x1 -> x0, local copies, waits for them, and re-layouts: 2.15 us -> none  [per_device(): lax.dynamic_index_in_dim(latent_in, rows - 1 - edge, axis=1, keepdims=False)]
    reshape x3 -> x0, local copies, waits for them, and re-layouts: 1.7 us -> none  [line(): return values.reshape(1, -1)]
  transfers between devices with their start and end apart: 18 -> 21, of which waited for: 12 -> 10; matrix products, arithmetic and copies ran while one was open for 4% -> 0% of each run, Pallas kernels for 10% -> 28%
where the time goes in v2:
time: 75.3 us; the launch traced here: 74.1 us
  Pallas kernels  30.5 us (41%)
  starting transfers between devices  28.9 us (38%)
  waiting for transfers between devices  13.7 us (18%)
  between operations  0.93 us (1%)
    ppermute x17, starting transfers between devices, swap(): return lax.ppermute(values, ('strip', 'canvas'), self.partner(stage, step))  19.7 us
    ppermute x17, waiting for transfers between devices, swap(): return lax.ppermute(values, ('strip', 'canvas'), self.partner(stage, step))  12.2 us
    pallas_call x2, Pallas kernels, block_rows(): call(functools.partial(rows_kernel, mine), [in_vmem] * len(ins), [in_vmem...  8.46 us
    pallas_call x2, Pallas kernels, input_rows(): call(functools.partial(input_kernel, mine), [in_vmem] * 7 + [anywhere] +...  6.81 us
    ppermute x2, starting transfers between devices, trade(): lax.ppermute(other, 'strip', far)  6.63 us
    pallas_call x2, Pallas kernels, weight_half(): call(functools.partial(weight_kernel, plan, mine), [in_vmem] * len(ins) +...  5.37 us
    pallas_call x1, Pallas kernels, per_device(): call(code_kernel, [in_hbm] * 8, [in_vmem] * 8, outs, held, flops=6 * tota...  4.86 us
    ppermute x2, starting transfers between devices, trade(): lax.ppermute(mate, 'strip', near)  2.57 us
  transfers between devices with their start and end apart: 21, of which 10 were waited for; matrix products, arithmetic and copies ran while one was open for 0% of the time, Pallas kernels for 28%

profile of v2, /device:TPU:1, one launch (start us, length us, event | category | flops | bytes accessed | tf_op | source)
XLA Modules:
  0.0 74.1 jit_solution(13582248333668448310)
XLA Ops:
  0.6 1.1 %shard_map.213 = (bf16[4,176,256]{2,1,0:T(8,128)(2,1)S(1)}, bf16[4,176,256]{2,1,0:T(8,128)(2,1)S(1)}) custom-call(bf16[4,4,176,256]{3,2,1,0:T(8,128)(2,1)} %latent_ref.1), custom_call_target="tpu_custom_call" | custom-call | tf_op jit(solution)/shard_map/pallas_call | solution.py:633
  1.8 0.1 collective-permute-start
  1.9 4.5 %collective-permute-start.1 = (bf16[4,176,256]{2,1,0:T(8,128)(2,1)S(1)}, bf16[4,176,256]{2,1,0:T(8,128)(2,1)S(1)}, u32[]{:S(2)}, u32[]{:S(2)}) collective-permute-start(bf16[4,176,256]{2,1,0:T(8,128)(2,1)S(1)} %get-tuple-element.64), channel_id=1, source_target_pairs={{2,4},{6,8},{10,12},{14,16},{18,20},{22,24},{26,28},{4,2},{8,6},{1... | collective-permute-start | bytes 1081352 | tf_op jit(solution)/shard_map/ppermute | solution.py:630
  6.4 0.0 copy-start.1
  6.4 0.0 copy-start.2
  6.4 0.0 copy-start.3
  6.4 0.0 copy-start.4
  6.4 4.9 %shard_map.212 = (f32[4,704,128]{2,1,0:T(8,128)S(1)}, bf16[2816,512]{1,0:T(8,128)(2,1)S(1)}, f32[64,256]{1,0:T(8,128)S(1)}, f32[1,256]{1,0:T(1,128)S(1)}, bf16[4...) custom-call(s32[4,4,176]{2,1,0:T(4,128)} %index_hbm.1, ...), custom_call_target="tpu_custom_call" | custom-call | flops 1107296256 | tf_op jit(solution)/shard_map/pallas_call | solution.py:658
  11.4 4.6 %shard_map.214 = (bf16[4224,768]{1,0:T(8,128)(2,1)S(1)}, bf16[2816,256]{1,0:T(8,128)(2,1)S(1)}, bf16[2816,256]{1,0:T(8,128)(2,1)S(1)}, bf16[2816,256]{1,0:T(8,12...) custom-call(s32[4,4,176]{2,1,0:T(4,128)S(1)} %get-tuple-element.59.c, ...), custom_call_target="tpu_custom_call" | custom-call | flops 2583691264 | tf_op jit(solution)/shard_map/pallas_call | solution.py:687
  16.0 3.8 %shard_map.215 = (bf16[4224,768]{1,0:T(8,128)(2,1)S(1)}, bf16[2816,256]{1,0:T(8,128)(2,1)S(1)}, bf16[2816,256]{1,0:T(8,128)(2,1)S(1)}, bf16[2816,256]{1,0:T(8,12...) custom-call(s32[4,4,176]{2,1,0:T(4,128)S(1)} %get-tuple-element.59.c, ...), custom_call_target="tpu_custom_call", output_to_operand_aliasing={{0}: (11, {}), {1}: (12, {}), {2}: (13, {}), {3}: (14, {}),... | custom-call | flops 2583691264 | tf_op jit(solution)/shard_map/pallas_call | solution.py:687
  19.9 0.1 shard_map.216
  20.0 2.7 %shard_map.217.after_ref = bf16[16,96,256]{2,1,0:T(8,128)(2,1)S(1)} custom-call(bf16[4224,768]{1,0:T(8,128)(2,1)S(1)} %get-tuple-element.74.slab_ref, bf16[2816,256]{1,0:T(8,128)(2,1)S(1)} %get-tuple-element.75.grad_ref, bf16[2816,256]{1,0:T(8,128)(2,1)S(1)} %get-tuple-element.76.up_ref, bf16[2816,256]{1,0:T(8,128)(2,1)S(1)} %get-tuple-element.77.down_ref, ...), custom_call_target="tpu_custom_call" | custom-call | flops 1845493760 | tf_op jit(solution)/shard_map/pallas_call | solution.py:709
  22.7 0.1 collective-permute-start.2
  22.8 2.6 %shard_map.218.refs_0_ = bf16[16,96,256]{2,1,0:T(8,128)(2,1)S(1)} custom-call(bf16[4224,768]{1,0:T(8,128)(2,1)S(1)} %get-tuple-element.74.slab_ref, bf16[2816,256]{1,0:T(8,128)(2,1)S(1)} %get-tuple-element.75.grad_ref, bf16[2816,256]{1,0:T(8,128)(2,1)S(1)} %get-tuple-element.76.up_ref, bf16[2816,256]{1,0:T(8,128)(2,1)S(1)} %get-tuple-element.77.down_ref, ...), custom_call_target="tpu_custom_call" | custom-call | flops 1845493760 | tf_op jit(solution)/shard_map/pallas_call | solution.py:709
  25.4 0.2 shard_map.219
  25.6 2.2 %collective-permute-start.3 = (bf16[4,96,256]{2,1,0:T(8,128)(2,1)S(1)}, bf16[4,96,256]{2,1,0:T(8,128)(2,1)S(1)}, u32[]{:S(2)}, u32[]{:S(2)}) collective-permute-start(bf16[4,96,256]{2,1,0:T(8,128)(2,1)S(1)} %get-tuple-element.88), channel_id=1, source_target_pairs={{0,5},{1,4},{2,7},{3,6},{4,1},{5,0},{6,3},{7,2},{8,13},{9,12},{10,... | collective-permute-start | bytes 589832 | tf_op jit(solution)/shard_map/ppermute | solution.py:494
  27.9 0.2 collective-permute-start.4
  28.1 0.3 collective-permute-start.5
  28.4 3.4 %shard_map.220.refs_4_.refs_0_ = bf16[4,4,176,256]{3,2,1,0:T(8,128)(2,1)} custom-call(s32[4,4,176]{2,1,0:T(4,128)S(1)} %get-tuple-element.59.crop_ref, bf16[4,4,176,256]{3,2,1,0:T(8,128)(2,1)S(1)} %get-tuple-element.60.latent_ref, bf16[2816,256]{1,0:T(8,128)(2,1)S(1)} %get-tuple-element.75.grad_ref, ...), custom_call_target="tpu_custom_call" | custom-call | flops 2030043136 | tf_op jit(solution)/shard_map/pallas_call | solution.py:722
  31.7 0.0 copy-start
  31.7 0.0 copy-start.5
  31.8 0.8 %collective-permute-done.3.refs_1_ = bf16[4,96,256]{2,1,0:T(8,128)(2,1)S(1)} collective-permute-done((bf16[4,96,256]{2,1,0:T(8,128)(2,1)S(1)}, bf16[4,96,256]{2,1,0:T(8,128)(2,1)S(1)}, u32[]{:S(2)}, u32[]{:S(2)}) %collective-permute-start.3) | collective-permute-done | bytes 196640 | tf_op jit(solution)/shard_map/ppermute | solution.py:494
  32.5 5.1 %collective-permute-done.4.refs_2_ = bf16[4,96,256]{2,1,0:T(8,128)(2,1)S(1)} collective-permute-done((bf16[4,96,256]{2,1,0:T(8,128)(2,1)S(1)}, bf16[4,96,256]{2,1,0:T(8,128)(2,1)S(1)}, u32[]{:S(2)}, u32[]{:S(2)}) %collective-permute-start.4) | collective-permute-done | bytes 196640 | tf_op jit(solution)/shard_map/ppermute | solution.py:494
  37.6 0.1 shard_map.221
  37.7 3.6 %collective-permute-start.6 = (bf16[1,96,256]{2,1,0:T(8,128)(2,1)S(1)}, bf16[1,96,256]{2,1,0:T(8,128)(2,1)S(1)}, u32[]{:S(2)}, u32[]{:S(2)}) collective-permute-start(bf16[1,96,256]{2,1,0:T(8,128)(2,1)S(1)} %get-tuple-element.93), channel_id=1, source_target_pairs={{0,24},{1,25},{2,26},{3,27},{4,28},{5,29},{6,30},{7,31},{8,16},{9,... | collective-permute-start | bytes 147464 | tf_op jit(solution)/shard_map/ppermute | solution.py:494
  41.3 0.4 collective-permute-start.8
  41.7 1.6 %shard_map.222.refs_4_ = bf16[4,4,176,256]{3,2,1,0:T(8,128)(2,1)} custom-call(f32[4,704,128]{2,1,0:T(8,128)S(1)} %get-tuple-element.58.term_ref, bf16[64,256]{1,0:T(8,128)(2,1)S(1)} %copy-done, bf16[256]{0:T(256)(128)(2,1)S(1)} %copy-done.5, bf16[1,96,256]{2,1,0:T(8,128)(2,1)S(1)} %get-tuple-element.92.after_ref.refs_0_), custom_call_target="tpu_custom_call" | custom-call | flops 738197504 | tf_op jit(solution)/shard_map/pallas_call | solution.py:747
  43.3 1.1 %collective-permute-done.7.refs_2_ = bf16[1,96,256]{2,1,0:T(8,128)(2,1)S(1)} collective-permute-done((bf16[1,96,256]{2,1,0:T(8,128)(2,1)S(1)}, bf16[1,96,256]{2,1,0:T(8,128)(2,1)S(1)}, u32[]{:S(2)}, u32[]{:S(2)}) %collective-permute-start.7) | collective-permute-done | bytes 49184 | tf_op jit(solution)/shard_map/ppermute | solution.py:494
  44.4 0.8 %collective-permute-done.8.refs_3_ = bf16[1,96,256]{2,1,0:T(8,128)(2,1)S(1)} collective-permute-done((bf16[1,96,256]{2,1,0:T(8,128)(2,1)S(1)}, bf16[1,96,256]{2,1,0:T(8,128)(2,1)S(1)}, u32[]{:S(2)}, u32[]{:S(2)}) %collective-permute-start.8) | collective-permute-done | bytes 49184 | tf_op jit(solution)/shard_map/ppermute | solution.py:494
  45.2 2.4 %collective-permute-start.9 = (bf16[704,256]{1,0:T(8,128)(2,1)S(1)}, bf16[704,256]{1,0:T(8,128)(2,1)S(1)}, u32[]{:S(2)}, u32[]{:S(2)}) collective-permute-start(bf16[704,256]{1,0:T(8,128)(2,1)S(1)} %shard_map.224), channel_id=1, source_target_pairs={{0,2},{2,0},{4,6},{6,4},{8,10},{10,8},{12,14},{14,12},{16,18},{18,... | collective-permute-start | bytes 1081352 | tf_op jit(solution)/shard_map/ppermute | solution.py:630
  47.7 2.1 %collective-permute-start.10 = (bf16[704,256]{1,0:T(8,128)(2,1)S(1)}, bf16[704,256]{1,0:T(8,128)(2,1)S(1)}, u32[]{:S(2)}, u32[]{:S(2)}) collective-permute-start(bf16[704,256]{1,0:T(8,128)(2,1)S(1)} %shard_map.225), channel_id=1, source_target_pairs={{2,4},{6,8},{10,12},{14,16},{18,20},{22,24},{26,28},{4,2},{8,6},{1... | collective-permute-start | bytes 1081352 | tf_op jit(solution)/shard_map/ppermute | solution.py:630
  49.8 2.2 %collective-permute-start.13 = (bf16[1,96,256]{2,1,0:T(8,128)(2,1)S(1)}, bf16[1,96,256]{2,1,0:T(8,128)(2,1)S(1)}, u32[]{:S(2)}, u32[]{:S(2)}) collective-permute-start(bf16[1,96,256]{2,1,0:T(8,128)(2,1)S(1)} %shard_map.223.refs_1_.refs_0_), channel_id=1, source_target_pairs={{0,24},{1,25},{2,26},{3,27},{4,28},{5,29},{6,30},{7,31},{8,16},{9,... | collective-permute-start | bytes 147464 | tf_op jit(solution)/shard_map/ppermute | solution.py:494
  52.0 1.4 %collective-permute-start.11 = (bf16[1,96,256]{2,1,0:T(8,128)(2,1)S(1)}, bf16[1,96,256]{2,1,0:T(8,128)(2,1)S(1)}, u32[]{:S(2)}, u32[]{:S(2)}) collective-permute-start(bf16[1,96,256]{2,1,0:T(8,128)(2,1)S(1)} %shard_map.223.refs_1_.refs_0_), channel_id=1, source_target_pairs={{0,16},{1,17},{2,18},{3,19},{4,20},{5,21},{6,22},{7,23},{8,24},{9,... | collective-permute-start | bytes 147464 | tf_op jit(solution)/shard_map/ppermute | solution.py:494
  53.4 1.7 %collective-permute-done.13.refs_3_ = bf16[1,96,256]{2,1,0:T(8,128)(2,1)S(1)} collective-permute-done((bf16[1,96,256]{2,1,0:T(8,128)(2,1)S(1)}, bf16[1,96,256]{2,1,0:T(8,128)(2,1)S(1)}, u32[]{:S(2)}, u32[]{:S(2)}) %collective-permute-start.13) | collective-permute-done | bytes 49184 | tf_op jit(solution)/shard_map/ppermute | solution.py:494
  55.1 1.3 %collective-permute-done.12.refs_2_ = bf16[1,96,256]{2,1,0:T(8,128)(2,1)S(1)} collective-permute-done((bf16[1,96,256]{2,1,0:T(8,128)(2,1)S(1)}, bf16[1,96,256]{2,1,0:T(8,128)(2,1)S(1)}, u32[]{:S(2)}, u32[]{:S(2)}) %collective-permute-start.12) | collective-permute-done | bytes 49184 | tf_op jit(solution)/shard_map/ppermute | solution.py:494
  56.4 0.1 collective-permute-done.11.refs_1_
  56.4 1.6 %collective-permute-done.10.refs_5_.other_ref = bf16[704,256]{1,0:T(8,128)(2,1)S(1)} collective-permute-done((bf16[704,256]{1,0:T(8,128)(2,1)S(1)}, bf16[704,256]{1,0:T(8,128)(2,1)S(1)}, u32[]{:S(2)}, u32[]{:S(2)}) %collective-permute-start.10) | collective-permute-done | bytes 360480 | tf_op jit(solution)/shard_map/ppermute | solution.py:630
  58.0 2.3 %collective-permute-start.16 = (bf16[4,96,256]{2,1,0:T(8,128)(2,1)S(1)}, bf16[4,96,256]{2,1,0:T(8,128)(2,1)S(1)}, u32[]{:S(2)}, u32[]{:S(2)}) collective-permute-start(bf16[4,96,256]{2,1,0:T(8,128)(2,1)S(1)} %shard_map.226.after_ref.refs_0_), channel_id=1, source_target_pairs={{0,5},{1,4},{2,7},{3,6},{4,1},{5,0},{6,3},{7,2},{8,13},{9,12},{10,... | collective-permute-start | bytes 589832 | tf_op jit(solution)/shard_map/ppermute | solution.py:494
  60.3 0.2 collective-permute-start.15
  60.5 0.3 collective-permute-start.14
  60.8 4.9 %collective-permute-start.17 = (bf16[4,96,256]{2,1,0:T(8,128)(2,1)S(1)}, bf16[4,96,256]{2,1,0:T(8,128)(2,1)S(1)}, u32[]{:S(2)}, u32[]{:S(2)}) collective-permute-start(bf16[4,96,256]{2,1,0:T(8,128)(2,1)S(1)} %shard_map.226.after_ref.refs_0_), channel_id=1, source_target_pairs={{0,2},{1,3},{2,0},{3,1},{4,6},{5,7},{6,4},{7,5},{8,10},{9,11},{10,... | collective-permute-start | bytes 589832 | tf_op jit(solution)/shard_map/ppermute | solution.py:494
  65.6 3.4 %shard_map.227.refs_1_ = bf16[4,4,176,256]{3,2,1,0:T(8,128)(2,1)} custom-call(s32[4,4,176]{2,1,0:T(4,128)S(1)} %get-tuple-element.59.crop_ref, bf16[4,4,176,256]{3,2,1,0:T(8,128)(2,1)S(1)} %get-tuple-element.60.latent_ref, bf16[2816,256]{1,0:T(8,128)(2,1)S(1)} %get-tuple-element.75.grad_ref, ...), custom_call_target="tpu_custom_call", output_to_operand_aliasing={{}: (8, {})} | custom-call | flops 2030043136 | tf_op jit(solution)/shard_map/pallas_call | solution.py:722
  69.1 0.1 collective-permute-start.20
  69.2 1.6 %collective-permute-start.19 = (bf16[4,96,256]{2,1,0:T(8,128)(2,1)S(1)}, bf16[4,96,256]{2,1,0:T(8,128)(2,1)S(1)}, u32[]{:S(2)}, u32[]{:S(2)}) collective-permute-start(bf16[4,96,256]{2,1,0:T(8,128)(2,1)S(1)} %shard_map.229.refs_2_), channel_id=1, source_target_pairs={{0,2},{1,3},{2,0},{3,1},{4,6},{5,7},{6,4},{7,5},{8,10},{9,11},{10,... | collective-permute-start | bytes 589832 | tf_op jit(solution)/shard_map/ppermute | solution.py:494
  70.8 0.1 collective-permute-start.18
  70.9 1.0 %collective-permute-done.19.refs_6_ = bf16[4,96,256]{2,1,0:T(8,128)(2,1)S(1)} collective-permute-done((bf16[4,96,256]{2,1,0:T(8,128)(2,1)S(1)}, bf16[4,96,256]{2,1,0:T(8,128)(2,1)S(1)}, u32[]{:S(2)}, u32[]{:S(2)}) %collective-permute-start.19) | collective-permute-done | bytes 196640 | tf_op jit(solution)/shard_map/ppermute | solution.py:494
  71.9 0.4 collective-permute-done.18.refs_5_
  72.3 1.8 %shard_map.231 = (f32[2304,256]{1,0:T(8,128)}, f32[1,256]{1,0:T(1,128)}, f32[256,256]{1,0:T(8,128)}, f32[1,256]{1,0:T(1,128)}, f32[64,256]{1,0:T(8,128)}, /*inde...) custom-call(bf16[4,96,256]{2,1,0:T(8,128)(2,1)S(1)} %shard_map.226.after_ref.refs_0_, ...), custom_call_target="tpu_custom_call" | custom-call | tf_op jit(solution)/shard_map/pallas_call | solution.py:766
  (26 shorter events, 0.1 us)
Async XLA Ops:
  1.8 14.2 %collective-permute-start = (bf16[4,176,256]{2,1,0:T(8,128)(2,1)S(1)}, bf16[4,176,256]{2,1,0:T(8,128)(2,1)S(1)}, u32[]{:S(2)}, u32[]{:S(2)}) collective-permute-start(bf16[4,176,256]{2,1,0:T(8,128)(2,1)S(1)} %get-tuple-element.63), channel_id=1, source_target_pairs={{0,2},{2,0},{4,6},{6,4},{8,10},{10,8},{12,14},{14,12},{16,18},{18,... | collective-permute-start | bytes 1081352 | tf_op jit(solution)/shard_map/ppermute | solution.py:630
  1.9 14.1 %collective-permute-start.1 = (bf16[4,176,256]{2,1,0:T(8,128)(2,1)S(1)}, bf16[4,176,256]{2,1,0:T(8,128)(2,1)S(1)}, u32[]{:S(2)}, u32[]{:S(2)}) collective-permute-start(bf16[4,176,256]{2,1,0:T(8,128)(2,1)S(1)} %get-tuple-element.64), channel_id=1, source_target_pairs={{2,4},{6,8},{10,12},{14,16},{18,20},{22,24},{26,28},{4,2},{8,6},{1... | collective-permute-start | bytes 1081352 | tf_op jit(solution)/shard_map/ppermute | solution.py:630
  6.4 4.9 %copy-start.1 = (bf16[256,64]{0,1:T(8,128)(2,1)S(1)}, bf16[256,64]{0,1:T(8,128)(2,1)}, u32[]{:S(2)}) copy-start(bf16[256,64]{0,1:T(8,128)(2,1)} %param.20) | copy-start | bytes 98308
  6.4 4.9 %copy-start.2 = (bf16[256]{0:T(256)(128)(2,1)S(1)}, bf16[256]{0:T(256)(128)(2,1)}, u32[]{:S(2)}) copy-start(bf16[256]{0:T(256)(128)(2,1)} %conv_bias_ref.3) | copy-start | bytes 1540
  6.4 4.9 %copy-start.3 = (bf16[256]{0:T(256)(128)(2,1)S(1)}, bf16[256]{0:T(256)(128)(2,1)}, u32[]{:S(2)}) copy-start(bf16[256]{0:T(256)(128)(2,1)} %mix_bias_ref.3) | copy-start | bytes 1540
  6.4 4.9 %copy-start.4 = (bf16[64]{0:T(256)(128)(2,1)S(1)}, bf16[64]{0:T(256)(128)(2,1)}, u32[]{:S(2)}) copy-start(bf16[64]{0:T(256)(128)(2,1)} %proj_bias_ref.3) | copy-start | bytes 388
  22.7 2.7 %collective-permute-start.2 = (bf16[16,96,256]{2,1,0:T(8,128)(2,1)S(1)}, bf16[16,96,256]{2,1,0:T(8,128)(2,1)S(1)}, u32[]{:S(2)}, u32[]{:S(2)}) collective-permute-start(bf16[16,96,256]{2,1,0:T(8,128)(2,1)S(1)} %shard_map.217.after_ref), channel_id=1, source_target_pairs={{0,2},{1,3},{2,0},{3,1},{4,6},{5,7},{6,4},{7,5},{8,10},{9,11},{10,... | collective-permute-start | bytes 2359304 | tf_op jit(solution)/shard_map/ppermute | solution.py:494
  25.6 6.9 %collective-permute-start.3 = (bf16[4,96,256]{2,1,0:T(8,128)(2,1)S(1)}, bf16[4,96,256]{2,1,0:T(8,128)(2,1)S(1)}, u32[]{:S(2)}, u32[]{:S(2)}) collective-permute-start(bf16[4,96,256]{2,1,0:T(8,128)(2,1)S(1)} %get-tuple-element.88), channel_id=1, source_target_pairs={{0,5},{1,4},{2,7},{3,6},{4,1},{5,0},{6,3},{7,2},{8,13},{9,12},{10,... | collective-permute-start | bytes 589832 | tf_op jit(solution)/shard_map/ppermute | solution.py:494
  27.9 9.8 %collective-permute-start.4 = (bf16[4,96,256]{2,1,0:T(8,128)(2,1)S(1)}, bf16[4,96,256]{2,1,0:T(8,128)(2,1)S(1)}, u32[]{:S(2)}, u32[]{:S(2)}) collective-permute-start(bf16[4,96,256]{2,1,0:T(8,128)(2,1)S(1)} %get-tuple-element.89), channel_id=1, source_target_pairs={{0,4},{1,5},{2,6},{3,7},{4,0},{5,1},{6,2},{7,3},{8,12},{9,13},{10,... | collective-permute-start | bytes 589832 | tf_op jit(solution)/shard_map/ppermute | solution.py:494
  28.1 9.5 %collective-permute-start.5 = (bf16[4,96,256]{2,1,0:T(8,128)(2,1)S(1)}, bf16[4,96,256]{2,1,0:T(8,128)(2,1)S(1)}, u32[]{:S(2)}, u32[]{:S(2)}) collective-permute-start(bf16[4,96,256]{2,1,0:T(8,128)(2,1)S(1)} %get-tuple-element.90), channel_id=1, source_target_pairs={{0,1},{1,0},{2,3},{3,2},{4,5},{5,4},{6,7},{7,6},{8,9},{9,8},{10,11... | collective-permute-start | bytes 589832 | tf_op jit(solution)/shard_map/ppermute | solution.py:494
  31.7 9.9 %copy-start = (bf16[64,256]{1,0:T(8,128)(2,1)S(1)}, bf16[64,256]{1,0:T(8,128)(2,1)}, u32[]{:S(2)}) copy-start(bf16[64,256]{1,0:T(8,128)(2,1)} %decode_weight_ref.1) | copy-start | bytes 98308
  31.7 9.9 %copy-start.5 = (bf16[256]{0:T(256)(128)(2,1)S(1)}, bf16[256]{0:T(256)(128)(2,1)}, u32[]{:S(2)}) copy-start(bf16[256]{0:T(256)(128)(2,1)} %decode_bias_ref.1) | copy-start | bytes 1540
  37.7 5.5 %collective-permute-start.6 = (bf16[1,96,256]{2,1,0:T(8,128)(2,1)S(1)}, bf16[1,96,256]{2,1,0:T(8,128)(2,1)S(1)}, u32[]{:S(2)}, u32[]{:S(2)}) collective-permute-start(bf16[1,96,256]{2,1,0:T(8,128)(2,1)S(1)} %get-tuple-element.93), channel_id=1, source_target_pairs={{0,24},{1,25},{2,26},{3,27},{4,28},{5,29},{6,30},{7,31},{8,16},{9,... | collective-permute-start | bytes 147464 | tf_op jit(solution)/shard_map/ppermute | solution.py:494
  41.3 3.1 %collective-permute-start.7 = (bf16[1,96,256]{2,1,0:T(8,128)(2,1)S(1)}, bf16[1,96,256]{2,1,0:T(8,128)(2,1)S(1)}, u32[]{:S(2)}, u32[]{:S(2)}) collective-permute-start(bf16[1,96,256]{2,1,0:T(8,128)(2,1)S(1)} %get-tuple-element.94), channel_id=1, source_target_pairs={{0,8},{1,9},{2,10},{3,11},{4,12},{5,13},{6,14},{7,15},{8,0},{9,1},... | collective-permute-start | bytes 147464 | tf_op jit(solution)/shard_map/ppermute | solution.py:494
  41.3 3.9 %collective-permute-start.8 = (bf16[1,96,256]{2,1,0:T(8,128)(2,1)S(1)}, bf16[1,96,256]{2,1,0:T(8,128)(2,1)S(1)}, u32[]{:S(2)}, u32[]{:S(2)}) collective-permute-start(bf16[1,96,256]{2,1,0:T(8,128)(2,1)S(1)} %get-tuple-element.95), channel_id=1, source_target_pairs={{0,16},{1,17},{2,18},{3,19},{4,20},{5,21},{6,22},{7,23},{8,24},{9,... | collective-permute-start | bytes 147464 | tf_op jit(solution)/shard_map/ppermute | solution.py:494
  45.2 11.2 %collective-permute-start.9 = (bf16[704,256]{1,0:T(8,128)(2,1)S(1)}, bf16[704,256]{1,0:T(8,128)(2,1)S(1)}, u32[]{:S(2)}, u32[]{:S(2)}) collective-permute-start(bf16[704,256]{1,0:T(8,128)(2,1)S(1)} %shard_map.224), channel_id=1, source_target_pairs={{0,2},{2,0},{4,6},{6,4},{8,10},{10,8},{12,14},{14,12},{16,18},{18,... | collective-permute-start | bytes 1081352 | tf_op jit(solution)/shard_map/ppermute | solution.py:630
  47.7 10.3 %collective-permute-start.10 = (bf16[704,256]{1,0:T(8,128)(2,1)S(1)}, bf16[704,256]{1,0:T(8,128)(2,1)S(1)}, u32[]{:S(2)}, u32[]{:S(2)}) collective-permute-start(bf16[704,256]{1,0:T(8,128)(2,1)S(1)} %shard_map.225), channel_id=1, source_target_pairs={{2,4},{6,8},{10,12},{14,16},{18,20},{22,24},{26,28},{4,2},{8,6},{1... | collective-permute-start | bytes 1081352 | tf_op jit(solution)/shard_map/ppermute | solution.py:630
  49.8 5.3 %collective-permute-start.13 = (bf16[1,96,256]{2,1,0:T(8,128)(2,1)S(1)}, bf16[1,96,256]{2,1,0:T(8,128)(2,1)S(1)}, u32[]{:S(2)}, u32[]{:S(2)}) collective-permute-start(bf16[1,96,256]{2,1,0:T(8,128)(2,1)S(1)} %shard_map.223.refs_1_.refs_0_), channel_id=1, source_target_pairs={{0,24},{1,25},{2,26},{3,27},{4,28},{5,29},{6,30},{7,31},{8,16},{9,... | collective-permute-start | bytes 147464 | tf_op jit(solution)/shard_map/ppermute | solution.py:494
  52.0 4.4 %collective-permute-start.12 = (bf16[1,96,256]{2,1,0:T(8,128)(2,1)S(1)}, bf16[1,96,256]{2,1,0:T(8,128)(2,1)S(1)}, u32[]{:S(2)}, u32[]{:S(2)}) collective-permute-start(bf16[1,96,256]{2,1,0:T(8,128)(2,1)S(1)} %shard_map.223.refs_1_.refs_0_), channel_id=1, source_target_pairs={{0,8},{1,9},{2,10},{3,11},{4,12},{5,13},{6,14},{7,15},{8,0},{9,1},... | collective-permute-start | bytes 147464 | tf_op jit(solution)/shard_map/ppermute | solution.py:494
  52.0 4.4 %collective-permute-start.11 = (bf16[1,96,256]{2,1,0:T(8,128)(2,1)S(1)}, bf16[1,96,256]{2,1,0:T(8,128)(2,1)S(1)}, u32[]{:S(2)}, u32[]{:S(2)}) collective-permute-start(bf16[1,96,256]{2,1,0:T(8,128)(2,1)S(1)} %shard_map.223.refs_1_.refs_0_), channel_id=1, source_target_pairs={{0,16},{1,17},{2,18},{3,19},{4,20},{5,21},{6,22},{7,23},{8,24},{9,... | collective-permute-start | bytes 147464 | tf_op jit(solution)/shard_map/ppermute | solution.py:494
  58.0 11.0 %collective-permute-start.16 = (bf16[4,96,256]{2,1,0:T(8,128)(2,1)S(1)}, bf16[4,96,256]{2,1,0:T(8,128)(2,1)S(1)}, u32[]{:S(2)}, u32[]{:S(2)}) collective-permute-start(bf16[4,96,256]{2,1,0:T(8,128)(2,1)S(1)} %shard_map.226.after_ref.refs_0_), channel_id=1, source_target_pairs={{0,5},{1,4},{2,7},{3,6},{4,1},{5,0},{6,3},{7,2},{8,13},{9,12},{10,... | collective-permute-start | bytes 589832 | tf_op jit(solution)/shard_map/ppermute | solution.py:494
  60.3 8.9 %collective-permute-start.15 = (bf16[4,96,256]{2,1,0:T(8,128)(2,1)S(1)}, bf16[4,96,256]{2,1,0:T(8,128)(2,1)S(1)}, u32[]{:S(2)}, u32[]{:S(2)}) collective-permute-start(bf16[4,96,256]{2,1,0:T(8,128)(2,1)S(1)} %shard_map.226.after_ref.refs_0_), channel_id=1, source_target_pairs={{0,4},{1,5},{2,6},{3,7},{4,0},{5,1},{6,2},{7,3},{8,12},{9,13},{10,... | collective-permute-start | bytes 589832 | tf_op jit(solution)/shard_map/ppermute | solution.py:494
  60.5 10.3 %collective-permute-start.14 = (bf16[4,96,256]{2,1,0:T(8,128)(2,1)S(1)}, bf16[4,96,256]{2,1,0:T(8,128)(2,1)S(1)}, u32[]{:S(2)}, u32[]{:S(2)}) collective-permute-start(bf16[4,96,256]{2,1,0:T(8,128)(2,1)S(1)} %shard_map.226.after_ref.refs_0_), channel_id=1, source_target_pairs={{0,1},{1,0},{2,3},{3,2},{4,5},{5,4},{6,7},{7,6},{8,9},{9,8},{10,11... | collective-permute-start | bytes 589832 | tf_op jit(solution)/shard_map/ppermute | solution.py:494
  60.8 10.2 %collective-permute-start.17 = (bf16[4,96,256]{2,1,0:T(8,128)(2,1)S(1)}, bf16[4,96,256]{2,1,0:T(8,128)(2,1)S(1)}, u32[]{:S(2)}, u32[]{:S(2)}) collective-permute-start(bf16[4,96,256]{2,1,0:T(8,128)(2,1)S(1)} %shard_map.226.after_ref.refs_0_), channel_id=1, source_target_pairs={{0,2},{1,3},{2,0},{3,1},{4,6},{5,7},{6,4},{7,5},{8,10},{9,11},{10,... | collective-permute-start | bytes 589832 | tf_op jit(solution)/shard_map/ppermute | solution.py:494
  69.1 1.8 %collective-permute-start.20 = (bf16[4,96,256]{2,1,0:T(8,128)(2,1)S(1)}, bf16[4,96,256]{2,1,0:T(8,128)(2,1)S(1)}, u32[]{:S(2)}, u32[]{:S(2)}) collective-permute-start(bf16[4,96,256]{2,1,0:T(8,128)(2,1)S(1)} %shard_map.230.refs_3_), channel_id=1, source_target_pairs={{0,2},{1,3},{2,0},{3,1},{4,6},{5,7},{6,4},{7,5},{8,10},{9,11},{10,... | collective-permute-start | bytes 589832 | tf_op jit(solution)/shard_map/ppermute | solution.py:494
  69.2 2.7 %collective-permute-start.19 = (bf16[4,96,256]{2,1,0:T(8,128)(2,1)S(1)}, bf16[4,96,256]{2,1,0:T(8,128)(2,1)S(1)}, u32[]{:S(2)}, u32[]{:S(2)}) collective-permute-start(bf16[4,96,256]{2,1,0:T(8,128)(2,1)S(1)} %shard_map.229.refs_2_), channel_id=1, source_target_pairs={{0,2},{1,3},{2,0},{3,1},{4,6},{5,7},{6,4},{7,5},{8,10},{9,11},{10,... | collective-permute-start | bytes 589832 | tf_op jit(solution)/shard_map/ppermute | solution.py:494
  70.8 1.4 %collective-permute-start.18 = (bf16[4,96,256]{2,1,0:T(8,128)(2,1)S(1)}, bf16[4,96,256]{2,1,0:T(8,128)(2,1)S(1)}, u32[]{:S(2)}, u32[]{:S(2)}) collective-permute-start(bf16[4,96,256]{2,1,0:T(8,128)(2,1)S(1)} %shard_map.228.refs_1_), channel_id=1, source_target_pairs={{0,2},{1,3},{2,0},{3,1},{4,6},{5,7},{6,4},{7,5},{8,10},{9,11},{10,... | collective-permute-start | bytes 589832 | tf_op jit(solution)/shard_map/ppermute | solution.py:494

commit v3 on v2

--- a/solution.py
+++ b/solution.py
@@ -149,22 +149,28 @@
     weight = decode_weight_ref[...]
     weight_top = jnp.concatenate([weight, jnp.zeros_like(weight)], axis=0)
     columns = code_columns(index_ref)
-    weight_sum, bias_sum = None, None
+    lanes = lax.broadcasted_iota(jnp.int32, (tile_rows, 128), 1)
     for row in range(rows):
-        codes = row_codes(columns, row, canvases, rows, entries)
-        picks = lax.broadcasted_iota(jnp.int32, codes.shape, 1) == codes
-        picks = picks.astype(wide).astype(low)
-        picks_ref[pl.ds(row * count, count)] = picks
-        copies[3 + row].wait()
-        grad = out_grad_ref[row].reshape(count, channels)
-        term = mm_nt(picks, both) + mm_nt(grad, weight_top)
-        term_ref[row] = term
-        weight_part = mm_tn(term.astype(low), grad)
-        bias_part = jnp.sum(grad.astype(wide), axis=0, keepdims=True)
-        weight_sum = weight_part if weight_sum is None else weight_sum + weight_part
-        bias_sum = bias_part if bias_sum is None else bias_sum + bias_part
-    weight_grad_ref[...] = 0.5 * weight_sum[size:]
-    bias_grad_ref[...] = bias_sum
+        codes = row_codes(columns, row, canvases, rows, 128)
+        for start, _ in chunks(count):
+            near = codes[start : start + tile_rows]
+            for at in range(0, entries, 128):
+                chosen = lanes + at == near
+                part = jnp.where(chosen, 1.0, 0.0).astype(low)
+                picks_ref[pl.ds(row * count + start, tile_rows), at : at + 128] = part
+    term = mm_nt(picks_ref[...], both)
+    for copy in copies[3 : 3 + rows]:
+        copy.wait()
+    grad = out_grad_ref[...].reshape(rows * count, channels)
+    term = term + mm_nt(grad, weight_top)
+    term_ref[...] = term.reshape(term_ref.shape)
+    weight_grad_ref[...] = 0.5 * mm_tn(term.astype(low), grad)[size:]
+    bias_sum = None
+    for start, _ in chunks(rows * count):
+        part = grad[start : start + tile_rows].astype(wide)
+        part = part[:8] + part[8:]
+        bias_sum = part if bias_sum is None else bias_sum + part
+    bias_grad_ref[...] = jnp.sum(bias_sum, axis=0, keepdims=True)
     for copy in copies[3 + rows :]:
         copy.wait()
 
@@ -336,10 +342,10 @@
     size = decode_weight_grad_ref.shape[0]
     entries = picks_ref.shape[1]
     triple = 3 * channels
-    me = plan.index()
-    half = plan.shards // 2
-    core, place = me // half, me % half
+    half = plan.half
+    core = lax.axis_index("strip") % 2
     wanted = core if mine else 1 - core
+    place = plan.place(wanted)
 
     def step(row_step, weighted_ref):
         span = pl.ds(row_step * count, total)
@@ -463,35 +469,39 @@
         self.sizes = sizes
         bits = {axis: [(axis, b) for b in range(size.bit_length() - 1)] for axis, size in sizes.items()}
         strip, canvas = bits["strip"], bits["canvas"]
-        self.stages = [strip[:1], [*strip[1:2], *canvas[:1]], strip[2:4]]
+        near, far = [*canvas[:1], *strip[1:2]], strip[2:4][::-1]
         rest = [*strip[4:], *canvas[1:]]
-        self.stages += [rest[i : i + 2] for i in range(0, len(rest), 2)]
-        self.stages = [stage for stage in self.stages if stage]
-        self.shards = sizes["strip"] * sizes["canvas"]
-        self.piece_rows = -(-half_rows // (self.shards // 2 * tile_rows)) * tile_rows
-        self.half_rows = self.shards // 2 * self.piece_rows
-
-    def index(self):
+        rest = [rest[i : i + 2] for i in range(0, len(rest), 2)]
+        even, odd = [near, far, *rest], [far, near, *rest]
+        if len(near) != len(far):
+            odd = even
+        self.stages = [tuple(zip(*pair, strict=True)) for pair in zip(even, odd, strict=True) if pair[0]]
+        self.core = ((("strip", 0), ("strip", 0)),)
+        self.half = sizes["strip"] * sizes["canvas"] // 2
+        self.piece_rows = -(-half_rows // (self.half * tile_rows)) * tile_rows
+        self.half_rows = self.half * self.piece_rows
+
+    def place(self, core):
         number = 0
         for stage in self.stages:
-            for axis, bit in stage:
-                number = number * 2 + (lax.axis_index(axis) // 2**bit) % 2
+            for spots in stage:
+                even, odd = [(lax.axis_index(axis) // 2**bit) % 2 for axis, bit in spots]
+                number = number * 2 + (even if spots[0] == spots[1] else jnp.where(core == 0, even, odd))
         return number
 
-    def partner(self, stage, step):
-        change = {"strip": 0, "canvas": 0}
-        for place, (axis, bit) in enumerate(reversed(stage)):
-            if step >> place & 1:
-                change[axis] |= 1 << bit
+    def swap(self, values, stage, step):
         width = self.sizes["canvas"]
-        return [
-            (s * width + c, (s ^ change["strip"]) * width + (c ^ change["canvas"]))
-            for s in range(self.sizes["strip"])
-            for c in range(width)
-        ]
-
-    def swap(self, values, stage, step):
-        return lax.ppermute(values, ("strip", "canvas"), self.partner(stage, step))
+        pairs = []
+        for strip in range(self.sizes["strip"]):
+            change = {"strip": 0, "canvas": 0}
+            for place, spots in enumerate(reversed(stage)):
+                if step >> place & 1:
+                    axis, bit = spots[strip % 2]
+                    change[axis] |= 1 << bit
+            for canvas in range(width):
+                target = (strip ^ change["strip"]) * width + (canvas ^ change["canvas"])
+                pairs.append((strip * width + canvas, target))
+        return lax.ppermute(values, ("strip", "canvas"), pairs)
 
 
 def add_kernel(count, after, *refs):
@@ -553,11 +563,14 @@
 def final_kernel(plan, count, sizes, *refs):
     ins, outs, gathered_ref = refs[:count], refs[count:-1], refs[-1]
     channels, size, entries = sizes
-    me = plan.index()
+    core = lax.axis_index("strip") % 2
     at = 0
     for ref in ins:
+        half = core if at < plan.half else 1 - core
+        place = plan.place(half)
         for piece in range(ref.shape[0]):
-            start = pl.multiple_of((me ^ at) * plan.piece_rows, plan.piece_rows)
+            shard = half * plan.half + (place ^ at % plan.half)
+            start = pl.multiple_of(shard * plan.piece_rows, plan.piece_rows)
             gathered_ref[pl.ds(start, plan.piece_rows)] = ref[piece]
             at += 1
     conv_ref, conv_bias_ref, mix_ref, mix_bias_ref, proj_ref, proj_bias_ref = outs[:6]
@@ -710,7 +723,7 @@
             functools.partial(weight_kernel, plan, mine),
             [in_vmem] * len(ins) + [anywhere],
             [in_vmem],
-            [struct((plan.shards // 2, plan.piece_rows, channels), low)],
+            [struct((plan.half, plan.piece_rows, channels), low)],
             [pltpu.VMEM((plan.half_rows, channels), low)],
             flops=10 * total * channels * channels,
         )(*ins, after)[0]
@@ -733,9 +746,9 @@
             aliases={8: 0} if before else {},
         )(crop, latent, grad, *halo, branch_grad, near_weight, after, *before)[0]
 
-    arrays = [keep, plan.swap(send, plan.stages[0], 1)]
+    arrays = [keep, plan.swap(send, plan.core, 1)]
     after = []
-    for place, stage in enumerate(plan.stages[1:]):
+    for place, stage in enumerate(plan.stages):
         parts = add_split(arrays, 2 ** len(stage), after)
         arrays = [parts[0]]
         arrays += [plan.swap(parts[i], stage, i) for i in reversed(range(1, len(parts)))]
@@ -744,6 +757,7 @@
             latent_grad = input_rows(inner, edges, parts[0])
             after = far_away(latent_grad)
         elif place == 1:
+            halo = trade(*[gate(edge, parts[0]) for edge in edges])
             decoded = call(
                 decoded_kernel,
                 [in_vmem, in_vmem, in_vmem, anywhere],
@@ -753,15 +767,14 @@
             )(term, decode_weight, decode_bias, parts[0])[0]
             after = far_away(decoded)
     pieces = add_split(arrays, 1, after)
-    halo = trade(*[gate(edge, pieces[0]) for edge in edges])
-    for stage in reversed(plan.stages[1:]):
-        gathered = join(pieces, *halo) if len(pieces) > 1 else pieces[0]
+    for stage in reversed(plan.stages):
+        gathered = join(pieces) if len(pieces) > 1 else pieces[0]
         others = [plan.swap(gathered, stage, i) for i in range(1, 2 ** len(stage))]
         pieces = [gathered, *others]
     latent_grad = input_rows(outer, halo, gathered, latent_grad)
     done = far_away(latent_grad)
     pieces = [pieces[0], *[gate(piece, *done) for piece in pieces[1:]]]
-    arrays = [*pieces, *[plan.swap(piece, plan.stages[0], 1) for piece in pieces]]
+    arrays = [*pieces, *[plan.swap(piece, plan.core, 1) for piece in pieces]]
 
     results = call(
         functools.partial(final_kernel, plan, len(arrays), (channels, size, entries)),

time: 75.3 us -> 70.1 us (0.931); the launches traced: 74.1 us -> 69.8 us
  starting transfers between devices: 28.9 us -> 23.5 us
  waiting for transfers between devices: 13.7 us -> 15.9 us
  Pallas kernels: 30.5 us -> 29.4 us
    ppermute x17, starting transfers between devices: 19.7 us -> 15.5 us  [swap(): return lax.ppermute(values, ('strip', 'canvas'), pairs)]
    ppermute x17, waiting for transfers between devices: 12.2 us -> 15.9 us  [swap(): return lax.ppermute(values, ('strip', 'canvas'), pairs)]
    ppermute x2, starting transfers between devices: 2.57 us -> 0.19 us  [trade(): lax.ppermute(mate, 'strip', near)]
    ppermute x2, waiting for transfers between devices: 1.58 us -> 0.01 us  [trade(): lax.ppermute(other, 'strip', far)]
    ppermute x2, starting transfers between devices: 6.63 us -> 7.83 us  [trade(): lax.ppermute(other, 'strip', far)]
    pallas_call x1, Pallas kernels: 4.86 us -> 3.8 us  [per_device(): call(code_kernel, [in_hbm] * 8, [in_vmem] * 8, outs, held, flops=6 * tota...]
  transfers between devices with their start and end apart: 21 -> 21, of which waited for: 10 -> 8; matrix products, arithmetic and copies ran while one was open for 0% -> 0% of each run, Pallas kernels for 28% -> 28%
where the time goes in v3:
time: 70.1 us; the launch traced here: 69.8 us
  Pallas kernels  29.4 us (42%)
  starting transfers between devices  23.5 us (34%)
  waiting for transfers between devices  15.9 us (23%)
  between operations  0.94 us (1%)
    ppermute x17, waiting for transfers between devices, swap(): return lax.ppermute(values, ('strip', 'canvas'), pairs)  15.9 us
    ppermute x17, starting transfers between devices, swap(): return lax.ppermute(values, ('strip', 'canvas'), pairs)  15.5 us
    pallas_call x2, Pallas kernels, block_rows(): call(functools.partial(rows_kernel, mine), [in_vmem] * len(ins), [in_vmem...  8.46 us
    ppermute x2, starting transfers between devices, trade(): lax.ppermute(other, 'strip', far)  7.83 us
    pallas_call x2, Pallas kernels, input_rows(): call(functools.partial(input_kernel, mine), [in_vmem] * 7 + [anywhere] +...  6.82 us
    pallas_call x2, Pallas kernels, weight_half(): call(functools.partial(weight_kernel, plan, mine), [in_vmem] * len(ins) +...  5.34 us
    pallas_call x1, Pallas kernels, per_device(): call(code_kernel, [in_hbm] * 8, [in_vmem] * 8, outs, held, flops=6 * tota...  3.8 us
    pallas_call x1, Pallas kernels, per_device(): call(functools.partial(final_kernel, plan, len(arrays), (channels, size,...  1.84 us
  transfers between devices with their start and end apart: 21, of which 8 were waited for; matrix products, arithmetic and copies ran while one was open for 0% of the time, Pallas kernels for 28%

profile of v3, /device:TPU:1, one launch (start us, length us, event | category | flops | bytes accessed | tf_op | source)
XLA Modules:
  0.0 69.8 jit_solution(12235148398122658693)
XLA Ops:
  0.6 1.1 %shard_map.213 = (bf16[4,176,256]{2,1,0:T(8,128)(2,1)S(1)}, bf16[4,176,256]{2,1,0:T(8,128)(2,1)S(1)}) custom-call(bf16[4,4,176,256]{3,2,1,0:T(8,128)(2,1)} %latent_ref.1), custom_call_target="tpu_custom_call" | custom-call | tf_op jit(solution)/shard_map/pallas_call | solution.py:646
  1.8 0.1 collective-permute-start
  1.9 4.5 %collective-permute-start.1 = (bf16[4,176,256]{2,1,0:T(8,128)(2,1)S(1)}, bf16[4,176,256]{2,1,0:T(8,128)(2,1)S(1)}, u32[]{:S(2)}, u32[]{:S(2)}) collective-permute-start(bf16[4,176,256]{2,1,0:T(8,128)(2,1)S(1)} %get-tuple-element.64), channel_id=1, source_target_pairs={{2,4},{6,8},{10,12},{14,16},{18,20},{22,24},{26,28},{4,2},{8,6},{1... | collective-permute-start | bytes 1081352 | tf_op jit(solution)/shard_map/ppermute | solution.py:643
  6.4 0.0 copy-start.1
  6.4 0.0 copy-start.2
  6.4 0.0 copy-start.3
  6.4 0.0 copy-start.4
  6.4 3.8 %shard_map.212 = (f32[4,704,128]{2,1,0:T(8,128)S(1)}, bf16[2816,512]{1,0:T(8,128)(2,1)S(1)}, f32[64,256]{1,0:T(8,128)S(1)}, f32[1,256]{1,0:T(1,128)S(1)}, bf16[4...) custom-call(s32[4,4,176]{2,1,0:T(4,128)} %index_hbm.1, ...), custom_call_target="tpu_custom_call" | custom-call | flops 1107296256 | tf_op jit(solution)/shard_map/pallas_call | solution.py:671
  10.3 4.6 %shard_map.214 = (bf16[4224,768]{1,0:T(8,128)(2,1)S(1)}, bf16[2816,256]{1,0:T(8,128)(2,1)S(1)}, bf16[2816,256]{1,0:T(8,128)(2,1)S(1)}, bf16[2816,256]{1,0:T(8,12...) custom-call(s32[4,4,176]{2,1,0:T(4,128)S(1)} %get-tuple-element.59.c, ...), custom_call_target="tpu_custom_call" | custom-call | flops 2583691264 | tf_op jit(solution)/shard_map/pallas_call | solution.py:700
  14.9 0.0 collective-permute-done.refs_0_
  14.9 0.0 collective-permute-done.1.refs_1_
  14.9 3.8 %shard_map.215 = (bf16[4224,768]{1,0:T(8,128)(2,1)S(1)}, bf16[2816,256]{1,0:T(8,128)(2,1)S(1)}, bf16[2816,256]{1,0:T(8,128)(2,1)S(1)}, bf16[2816,256]{1,0:T(8,12...) custom-call(s32[4,4,176]{2,1,0:T(4,128)S(1)} %get-tuple-element.59.c, ...), custom_call_target="tpu_custom_call", output_to_operand_aliasing={{0}: (11, {}), {1}: (12, {}), {2}: (13, {}), {3}: (14, {}),... | custom-call | flops 2583691264 | tf_op jit(solution)/shard_map/pallas_call | solution.py:700
  18.8 0.1 shard_map.216
  18.9 2.7 %shard_map.217.after_ref = bf16[16,96,256]{2,1,0:T(8,128)(2,1)S(1)} custom-call(bf16[4224,768]{1,0:T(8,128)(2,1)S(1)} %get-tuple-element.74.slab_ref, bf16[2816,256]{1,0:T(8,128)(2,1)S(1)} %get-tuple-element.75.grad_ref, bf16[2816,256]{1,0:T(8,128)(2,1)S(1)} %get-tuple-element.76.up_ref, bf16[2816,256]{1,0:T(8,128)(2,1)S(1)} %get-tuple-element.77.down_ref, ...), custom_call_target="tpu_custom_call" | custom-call | flops 1845493760 | tf_op jit(solution)/shard_map/pallas_call | solution.py:722
  21.6 0.1 collective-permute-start.2
  21.7 2.6 %shard_map.218.refs_0_ = bf16[16,96,256]{2,1,0:T(8,128)(2,1)S(1)} custom-call(bf16[4224,768]{1,0:T(8,128)(2,1)S(1)} %get-tuple-element.74.slab_ref, bf16[2816,256]{1,0:T(8,128)(2,1)S(1)} %get-tuple-element.75.grad_ref, bf16[2816,256]{1,0:T(8,128)(2,1)S(1)} %get-tuple-element.76.up_ref, bf16[2816,256]{1,0:T(8,128)(2,1)S(1)} %get-tuple-element.77.down_ref, ...), custom_call_target="tpu_custom_call" | custom-call | flops 1845493760 | tf_op jit(solution)/shard_map/pallas_call | solution.py:722
  24.3 0.2 shard_map.219
  24.5 4.4 %collective-permute-start.3 = (bf16[4,96,256]{2,1,0:T(8,128)(2,1)S(1)}, bf16[4,96,256]{2,1,0:T(8,128)(2,1)S(1)}, u32[]{:S(2)}, u32[]{:S(2)}) collective-permute-start(bf16[4,96,256]{2,1,0:T(8,128)(2,1)S(1)} %get-tuple-element.88), channel_id=1, source_target_pairs={{0,5},{1,4},{2,26},{3,27},{4,1},{5,0},{6,30},{7,31},{8,13},{9,12},... | collective-permute-start | bytes 589832 | tf_op jit(solution)/shard_map/ppermute | solution.py:504
  28.9 0.4 collective-permute-start.5
  29.3 3.4 %shard_map.220.refs_4_.refs_0_ = bf16[4,4,176,256]{3,2,1,0:T(8,128)(2,1)} custom-call(s32[4,4,176]{2,1,0:T(4,128)S(1)} %get-tuple-element.59.crop_ref, bf16[4,4,176,256]{3,2,1,0:T(8,128)(2,1)S(1)} %get-tuple-element.60.latent_ref, bf16[2816,256]{1,0:T(8,128)(2,1)S(1)} %get-tuple-element.75.grad_ref, ...), custom_call_target="tpu_custom_call" | custom-call | flops 2030043136 | tf_op jit(solution)/shard_map/pallas_call | solution.py:735
  32.7 0.0 copy-start
  32.7 0.0 copy-start.5
  32.7 4.7 %collective-permute-done.4.refs_2_ = bf16[4,96,256]{2,1,0:T(8,128)(2,1)S(1)} collective-permute-done((bf16[4,96,256]{2,1,0:T(8,128)(2,1)S(1)}, bf16[4,96,256]{2,1,0:T(8,128)(2,1)S(1)}, u32[]{:S(2)}, u32[]{:S(2)}) %collective-permute-start.4) | collective-permute-done | bytes 196640 | tf_op jit(solution)/shard_map/ppermute | solution.py:504
  37.5 0.1 shard_map.221
  37.6 0.1 collective-permute-start.6
  37.7 3.3 %collective-permute-start.7 = (bf16[704,256]{1,0:T(8,128)(2,1)S(1)}, bf16[704,256]{1,0:T(8,128)(2,1)S(1)}, u32[]{:S(2)}, u32[]{:S(2)}) collective-permute-start(bf16[704,256]{1,0:T(8,128)(2,1)S(1)} %shard_map.224), channel_id=1, source_target_pairs={{2,4},{6,8},{10,12},{14,16},{18,20},{22,24},{26,28},{4,2},{8,6},{1... | collective-permute-start | bytes 1081352 | tf_op jit(solution)/shard_map/ppermute | solution.py:643
  41.0 1.4 %collective-permute-start.8 = (bf16[1,96,256]{2,1,0:T(8,128)(2,1)S(1)}, bf16[1,96,256]{2,1,0:T(8,128)(2,1)S(1)}, u32[]{:S(2)}, u32[]{:S(2)}) collective-permute-start(bf16[1,96,256]{2,1,0:T(8,128)(2,1)S(1)} %get-tuple-element.93), channel_id=1, source_target_pairs={{0,24},{1,25},{2,7},{3,6},{4,28},{5,29},{6,3},{7,2},{8,16},{9,17},... | collective-permute-start | bytes 147464 | tf_op jit(solution)/shard_map/ppermute | solution.py:504
  42.4 0.3 collective-permute-start.9
  42.7 1.1 %collective-permute-start.10 = (bf16[1,96,256]{2,1,0:T(8,128)(2,1)S(1)}, bf16[1,96,256]{2,1,0:T(8,128)(2,1)S(1)}, u32[]{:S(2)}, u32[]{:S(2)}) collective-permute-start(bf16[1,96,256]{2,1,0:T(8,128)(2,1)S(1)} %get-tuple-element.95), channel_id=1, source_target_pairs={{0,8},{1,9},{2,6},{3,7},{4,12},{5,13},{6,2},{7,3},{8,0},{9,1},{10,... | collective-permute-start | bytes 147464 | tf_op jit(solution)/shard_map/ppermute | solution.py:504
  43.7 1.6 %shard_map.222.refs_4_ = bf16[4,4,176,256]{3,2,1,0:T(8,128)(2,1)} custom-call(f32[4,704,128]{2,1,0:T(8,128)S(1)} %get-tuple-element.58.term_ref, bf16[64,256]{1,0:T(8,128)(2,1)S(1)} %copy-done, bf16[256]{0:T(256)(128)(2,1)S(1)} %copy-done.5, bf16[1,96,256]{2,1,0:T(8,128)(2,1)S(1)} %get-tuple-element.92.after_ref.refs_1_.refs_0_), custom_call_target="tpu_custom_call" | custom-call | flops 738197504 | tf_op jit(solution)/shard_map/pallas_call | solution.py:761
  45.3 4.9 %collective-permute-done.10.refs_3_ = bf16[1,96,256]{2,1,0:T(8,128)(2,1)S(1)} collective-permute-done((bf16[1,96,256]{2,1,0:T(8,128)(2,1)S(1)}, bf16[1,96,256]{2,1,0:T(8,128)(2,1)S(1)}, u32[]{:S(2)}, u32[]{:S(2)}) %collective-permute-start.10) | collective-permute-done | bytes 49184 | tf_op jit(solution)/shard_map/ppermute | solution.py:504
  50.3 2.9 %collective-permute-start.13 = (bf16[1,96,256]{2,1,0:T(8,128)(2,1)S(1)}, bf16[1,96,256]{2,1,0:T(8,128)(2,1)S(1)}, u32[]{:S(2)}, u32[]{:S(2)}) collective-permute-start(bf16[1,96,256]{2,1,0:T(8,128)(2,1)S(1)} %shard_map.225.refs_0_), channel_id=1, source_target_pairs={{0,24},{1,25},{2,7},{3,6},{4,28},{5,29},{6,3},{7,2},{8,16},{9,17},... | collective-permute-start | bytes 147464 | tf_op jit(solution)/shard_map/ppermute | solution.py:504
  53.2 0.3 collective-permute-start.12
  53.5 0.1 collective-permute-start.11
  53.6 1.2 %collective-permute-done.13.refs_3_ = bf16[1,96,256]{2,1,0:T(8,128)(2,1)S(1)} collective-permute-done((bf16[1,96,256]{2,1,0:T(8,128)(2,1)S(1)}, bf16[1,96,256]{2,1,0:T(8,128)(2,1)S(1)}, u32[]{:S(2)}, u32[]{:S(2)}) %collective-permute-start.13) | collective-permute-done | bytes 49184 | tf_op jit(solution)/shard_map/ppermute | solution.py:504
  54.8 1.4 %collective-permute-done.12.refs_2_ = bf16[1,96,256]{2,1,0:T(8,128)(2,1)S(1)} collective-permute-done((bf16[1,96,256]{2,1,0:T(8,128)(2,1)S(1)}, bf16[1,96,256]{2,1,0:T(8,128)(2,1)S(1)}, u32[]{:S(2)}, u32[]{:S(2)}) %collective-permute-start.12) | collective-permute-done | bytes 49184 | tf_op jit(solution)/shard_map/ppermute | solution.py:504
  56.2 0.2 collective-permute-done.11.refs_1_
  56.4 0.1 collective-permute-start.14
  56.5 0.1 collective-permute-start.15
  56.6 3.5 %collective-permute-start.16 = (bf16[4,96,256]{2,1,0:T(8,128)(2,1)S(1)}, bf16[4,96,256]{2,1,0:T(8,128)(2,1)S(1)}, u32[]{:S(2)}, u32[]{:S(2)}) collective-permute-start(bf16[4,96,256]{2,1,0:T(8,128)(2,1)S(1)} %shard_map.226.after_ref.refs_0_), channel_id=1, source_target_pairs={{0,5},{1,4},{2,26},{3,27},{4,1},{5,0},{6,30},{7,31},{8,13},{9,12},... | collective-permute-start | bytes 589832 | tf_op jit(solution)/shard_map/ppermute | solution.py:504
  60.0 0.1 collective-permute-start.17
  60.2 3.4 %shard_map.227.refs_1_ = bf16[4,4,176,256]{3,2,1,0:T(8,128)(2,1)} custom-call(s32[4,4,176]{2,1,0:T(4,128)S(1)} %get-tuple-element.59.crop_ref, bf16[4,4,176,256]{3,2,1,0:T(8,128)(2,1)S(1)} %get-tuple-element.60.latent_ref, bf16[2816,256]{1,0:T(8,128)(2,1)S(1)} %get-tuple-element.75.grad_ref, ...), custom_call_target="tpu_custom_call", output_to_operand_aliasing={{}: (8, {})} | custom-call | flops 2030043136 | tf_op jit(solution)/shard_map/pallas_call | solution.py:735
  63.6 0.4 collective-permute-start.18
  64.1 2.2 %collective-permute-done.15.refs_0_ = bf16[4,96,256]{2,1,0:T(8,128)(2,1)S(1)} collective-permute-done((bf16[4,96,256]{2,1,0:T(8,128)(2,1)S(1)}, bf16[4,96,256]{2,1,0:T(8,128)(2,1)S(1)}, u32[]{:S(2)}, u32[]{:S(2)}) %collective-permute-start.15) | collective-permute-done | bytes 196640 | tf_op jit(solution)/shard_map/ppermute | solution.py:504
  66.2 0.5 collective-permute-start.20
  66.8 0.9 %collective-permute-done.19.refs_6_ = bf16[4,96,256]{2,1,0:T(8,128)(2,1)S(1)} collective-permute-done((bf16[4,96,256]{2,1,0:T(8,128)(2,1)S(1)}, bf16[4,96,256]{2,1,0:T(8,128)(2,1)S(1)}, u32[]{:S(2)}, u32[]{:S(2)}) %collective-permute-start.19) | collective-permute-done | bytes 196640 | tf_op jit(solution)/shard_map/ppermute | solution.py:504
  67.7 0.3 collective-permute-done.20.refs_7_
  68.0 1.8 %shard_map.231 = (f32[2304,256]{1,0:T(8,128)}, f32[1,256]{1,0:T(1,128)}, f32[256,256]{1,0:T(8,128)}, f32[1,256]{1,0:T(1,128)}, f32[64,256]{1,0:T(8,128)}, /*inde...) custom-call(bf16[4,96,256]{2,1,0:T(8,128)(2,1)S(1)} %shard_map.226.after_ref.refs_0_, ...), custom_call_target="tpu_custom_call" | custom-call | tf_op jit(solution)/shard_map/pallas_call | solution.py:779
  (26 shorter events, 0.1 us)
Async XLA Ops:
  1.8 13.2 %collective-permute-start = (bf16[4,176,256]{2,1,0:T(8,128)(2,1)S(1)}, bf16[4,176,256]{2,1,0:T(8,128)(2,1)S(1)}, u32[]{:S(2)}, u32[]{:S(2)}) collective-permute-start(bf16[4,176,256]{2,1,0:T(8,128)(2,1)S(1)} %get-tuple-element.63), channel_id=1, source_target_pairs={{0,2},{2,0},{4,6},{6,4},{8,10},{10,8},{12,14},{14,12},{16,18},{18,... | collective-permute-start | bytes 1081352 | tf_op jit(solution)/shard_map/ppermute | solution.py:643
  1.9 13.0 %collective-permute-start.1 = (bf16[4,176,256]{2,1,0:T(8,128)(2,1)S(1)}, bf16[4,176,256]{2,1,0:T(8,128)(2,1)S(1)}, u32[]{:S(2)}, u32[]{:S(2)}) collective-permute-start(bf16[4,176,256]{2,1,0:T(8,128)(2,1)S(1)} %get-tuple-element.64), channel_id=1, source_target_pairs={{2,4},{6,8},{10,12},{14,16},{18,20},{22,24},{26,28},{4,2},{8,6},{1... | collective-permute-start | bytes 1081352 | tf_op jit(solution)/shard_map/ppermute | solution.py:643
  6.4 3.9 %copy-start.1 = (bf16[256,64]{0,1:T(8,128)(2,1)S(1)}, bf16[256,64]{0,1:T(8,128)(2,1)}, u32[]{:S(2)}) copy-start(bf16[256,64]{0,1:T(8,128)(2,1)} %param.20) | copy-start | bytes 98308
  6.4 3.9 %copy-start.2 = (bf16[256]{0:T(256)(128)(2,1)S(1)}, bf16[256]{0:T(256)(128)(2,1)}, u32[]{:S(2)}) copy-start(bf16[256]{0:T(256)(128)(2,1)} %conv_bias_ref.3) | copy-start | bytes 1540
  6.4 3.9 %copy-start.3 = (bf16[256]{0:T(256)(128)(2,1)S(1)}, bf16[256]{0:T(256)(128)(2,1)}, u32[]{:S(2)}) copy-start(bf16[256]{0:T(256)(128)(2,1)} %mix_bias_ref.3) | copy-start | bytes 1540
  6.4 3.9 %copy-start.4 = (bf16[64]{0:T(256)(128)(2,1)S(1)}, bf16[64]{0:T(256)(128)(2,1)}, u32[]{:S(2)}) copy-start(bf16[64]{0:T(256)(128)(2,1)} %proj_bias_ref.3) | copy-start | bytes 388
  21.6 2.7 %collective-permute-start.2 = (bf16[16,96,256]{2,1,0:T(8,128)(2,1)S(1)}, bf16[16,96,256]{2,1,0:T(8,128)(2,1)S(1)}, u32[]{:S(2)}, u32[]{:S(2)}) collective-permute-start(bf16[16,96,256]{2,1,0:T(8,128)(2,1)S(1)} %shard_map.217.after_ref), channel_id=1, source_target_pairs={{0,2},{1,3},{2,0},{3,1},{4,6},{5,7},{6,4},{7,5},{8,10},{9,11},{10,... | collective-permute-start | bytes 2359304 | tf_op jit(solution)/shard_map/ppermute | solution.py:504
  24.5 8.2 %collective-permute-start.3 = (bf16[4,96,256]{2,1,0:T(8,128)(2,1)S(1)}, bf16[4,96,256]{2,1,0:T(8,128)(2,1)S(1)}, u32[]{:S(2)}, u32[]{:S(2)}) collective-permute-start(bf16[4,96,256]{2,1,0:T(8,128)(2,1)S(1)} %get-tuple-element.88), channel_id=1, source_target_pairs={{0,5},{1,4},{2,26},{3,27},{4,1},{5,0},{6,30},{7,31},{8,13},{9,12},... | collective-permute-start | bytes 589832 | tf_op jit(solution)/shard_map/ppermute | solution.py:504
  28.9 8.5 %collective-permute-start.4 = (bf16[4,96,256]{2,1,0:T(8,128)(2,1)S(1)}, bf16[4,96,256]{2,1,0:T(8,128)(2,1)S(1)}, u32[]{:S(2)}, u32[]{:S(2)}) collective-permute-start(bf16[4,96,256]{2,1,0:T(8,128)(2,1)S(1)} %get-tuple-element.89), channel_id=1, source_target_pairs={{0,1},{1,0},{2,18},{3,19},{4,5},{5,4},{6,22},{7,23},{8,9},{9,8},{1... | collective-permute-start | bytes 589832 | tf_op jit(solution)/shard_map/ppermute | solution.py:504
  28.9 8.5 %collective-permute-start.5 = (bf16[4,96,256]{2,1,0:T(8,128)(2,1)S(1)}, bf16[4,96,256]{2,1,0:T(8,128)(2,1)S(1)}, u32[]{:S(2)}, u32[]{:S(2)}) collective-permute-start(bf16[4,96,256]{2,1,0:T(8,128)(2,1)S(1)} %get-tuple-element.90), channel_id=1, source_target_pairs={{0,4},{1,5},{2,10},{3,11},{4,0},{5,1},{6,14},{7,15},{8,12},{9,13},... | collective-permute-start | bytes 589832 | tf_op jit(solution)/shard_map/ppermute | solution.py:504
  32.7 11.1 %copy-start = (bf16[64,256]{1,0:T(8,128)(2,1)S(1)}, bf16[64,256]{1,0:T(8,128)(2,1)}, u32[]{:S(2)}) copy-start(bf16[64,256]{1,0:T(8,128)(2,1)} %decode_weight_ref.1) | copy-start | bytes 98308
  32.7 11.0 %copy-start.5 = (bf16[256]{0:T(256)(128)(2,1)S(1)}, bf16[256]{0:T(256)(128)(2,1)}, u32[]{:S(2)}) copy-start(bf16[256]{0:T(256)(128)(2,1)} %decode_bias_ref.1) | copy-start | bytes 1540
  37.6 22.5 %collective-permute-start.6 = (bf16[704,256]{1,0:T(8,128)(2,1)S(1)}, bf16[704,256]{1,0:T(8,128)(2,1)S(1)}, u32[]{:S(2)}, u32[]{:S(2)}) collective-permute-start(bf16[704,256]{1,0:T(8,128)(2,1)S(1)} %shard_map.223), channel_id=1, source_target_pairs={{0,2},{2,0},{4,6},{6,4},{8,10},{10,8},{12,14},{14,12},{16,18},{18,... | collective-permute-start | bytes 1081352 | tf_op jit(solution)/shard_map/ppermute | solution.py:643
  37.7 22.5 %collective-permute-start.7 = (bf16[704,256]{1,0:T(8,128)(2,1)S(1)}, bf16[704,256]{1,0:T(8,128)(2,1)S(1)}, u32[]{:S(2)}, u32[]{:S(2)}) collective-permute-start(bf16[704,256]{1,0:T(8,128)(2,1)S(1)} %shard_map.224), channel_id=1, source_target_pairs={{2,4},{6,8},{10,12},{14,16},{18,20},{22,24},{26,28},{4,2},{8,6},{1... | collective-permute-start | bytes 1081352 | tf_op jit(solution)/shard_map/ppermute | solution.py:643
  41.0 4.3 %collective-permute-start.8 = (bf16[1,96,256]{2,1,0:T(8,128)(2,1)S(1)}, bf16[1,96,256]{2,1,0:T(8,128)(2,1)S(1)}, u32[]{:S(2)}, u32[]{:S(2)}) collective-permute-start(bf16[1,96,256]{2,1,0:T(8,128)(2,1)S(1)} %get-tuple-element.93), channel_id=1, source_target_pairs={{0,24},{1,25},{2,7},{3,6},{4,28},{5,29},{6,3},{7,2},{8,16},{9,17},... | collective-permute-start | bytes 147464 | tf_op jit(solution)/shard_map/ppermute | solution.py:504
  42.4 2.9 %collective-permute-start.9 = (bf16[1,96,256]{2,1,0:T(8,128)(2,1)S(1)}, bf16[1,96,256]{2,1,0:T(8,128)(2,1)S(1)}, u32[]{:S(2)}, u32[]{:S(2)}) collective-permute-start(bf16[1,96,256]{2,1,0:T(8,128)(2,1)S(1)} %get-tuple-element.94), channel_id=1, source_target_pairs={{0,16},{1,17},{2,3},{3,2},{4,20},{5,21},{6,7},{7,6},{8,24},{9,25},... | collective-permute-start | bytes 147464 | tf_op jit(solution)/shard_map/ppermute | solution.py:504
  42.7 7.6 %collective-permute-start.10 = (bf16[1,96,256]{2,1,0:T(8,128)(2,1)S(1)}, bf16[1,96,256]{2,1,0:T(8,128)(2,1)S(1)}, u32[]{:S(2)}, u32[]{:S(2)}) collective-permute-start(bf16[1,96,256]{2,1,0:T(8,128)(2,1)S(1)} %get-tuple-element.95), channel_id=1, source_target_pairs={{0,8},{1,9},{2,6},{3,7},{4,12},{5,13},{6,2},{7,3},{8,0},{9,1},{10,... | collective-permute-start | bytes 147464 | tf_op jit(solution)/shard_map/ppermute | solution.py:504
  50.3 4.5 %collective-permute-start.13 = (bf16[1,96,256]{2,1,0:T(8,128)(2,1)S(1)}, bf16[1,96,256]{2,1,0:T(8,128)(2,1)S(1)}, u32[]{:S(2)}, u32[]{:S(2)}) collective-permute-start(bf16[1,96,256]{2,1,0:T(8,128)(2,1)S(1)} %shard_map.225.refs_0_), channel_id=1, source_target_pairs={{0,24},{1,25},{2,7},{3,6},{4,28},{5,29},{6,3},{7,2},{8,16},{9,17},... | collective-permute-start | bytes 147464 | tf_op jit(solution)/shard_map/ppermute | solution.py:504
  53.2 3.0 %collective-permute-start.12 = (bf16[1,96,256]{2,1,0:T(8,128)(2,1)S(1)}, bf16[1,96,256]{2,1,0:T(8,128)(2,1)S(1)}, u32[]{:S(2)}, u32[]{:S(2)}) collective-permute-start(bf16[1,96,256]{2,1,0:T(8,128)(2,1)S(1)} %shard_map.225.refs_0_), channel_id=1, source_target_pairs={{0,16},{1,17},{2,3},{3,2},{4,20},{5,21},{6,7},{7,6},{8,24},{9,25},... | collective-permute-start | bytes 147464 | tf_op jit(solution)/shard_map/ppermute | solution.py:504
  53.5 2.9 %collective-permute-start.11 = (bf16[1,96,256]{2,1,0:T(8,128)(2,1)S(1)}, bf16[1,96,256]{2,1,0:T(8,128)(2,1)S(1)}, u32[]{:S(2)}, u32[]{:S(2)}) collective-permute-start(bf16[1,96,256]{2,1,0:T(8,128)(2,1)S(1)} %shard_map.225.refs_0_), channel_id=1, source_target_pairs={{0,8},{1,9},{2,6},{3,7},{4,12},{5,13},{6,2},{7,3},{8,0},{9,1},{10,... | collective-permute-start | bytes 147464 | tf_op jit(solution)/shard_map/ppermute | solution.py:504
  56.4 7.2 %collective-permute-start.14 = (bf16[4,96,256]{2,1,0:T(8,128)(2,1)S(1)}, bf16[4,96,256]{2,1,0:T(8,128)(2,1)S(1)}, u32[]{:S(2)}, u32[]{:S(2)}) collective-permute-start(bf16[4,96,256]{2,1,0:T(8,128)(2,1)S(1)} %shard_map.226.after_ref.refs_0_), channel_id=1, source_target_pairs={{0,4},{1,5},{2,10},{3,11},{4,0},{5,1},{6,14},{7,15},{8,12},{9,13},... | collective-permute-start | bytes 589832 | tf_op jit(solution)/shard_map/ppermute | solution.py:504
  56.5 9.7 %collective-permute-start.15 = (bf16[4,96,256]{2,1,0:T(8,128)(2,1)S(1)}, bf16[4,96,256]{2,1,0:T(8,128)(2,1)S(1)}, u32[]{:S(2)}, u32[]{:S(2)}) collective-permute-start(bf16[4,96,256]{2,1,0:T(8,128)(2,1)S(1)} %shard_map.226.after_ref.refs_0_), channel_id=1, source_target_pairs={{0,1},{1,0},{2,18},{3,19},{4,5},{5,4},{6,22},{7,23},{8,9},{9,8},{1... | collective-permute-start | bytes 589832 | tf_op jit(solution)/shard_map/ppermute | solution.py:504
  56.6 9.7 %collective-permute-start.16 = (bf16[4,96,256]{2,1,0:T(8,128)(2,1)S(1)}, bf16[4,96,256]{2,1,0:T(8,128)(2,1)S(1)}, u32[]{:S(2)}, u32[]{:S(2)}) collective-permute-start(bf16[4,96,256]{2,1,0:T(8,128)(2,1)S(1)} %shard_map.226.after_ref.refs_0_), channel_id=1, source_target_pairs={{0,5},{1,4},{2,26},{3,27},{4,1},{5,0},{6,30},{7,31},{8,13},{9,12},... | collective-permute-start | bytes 589832 | tf_op jit(solution)/shard_map/ppermute | solution.py:504
  60.0 6.7 %collective-permute-start.17 = (bf16[4,96,256]{2,1,0:T(8,128)(2,1)S(1)}, bf16[4,96,256]{2,1,0:T(8,128)(2,1)S(1)}, u32[]{:S(2)}, u32[]{:S(2)}) collective-permute-start(bf16[4,96,256]{2,1,0:T(8,128)(2,1)S(1)} %shard_map.226.after_ref.refs_0_), channel_id=1, source_target_pairs={{0,2},{1,3},{2,0},{3,1},{4,6},{5,7},{6,4},{7,5},{8,10},{9,11},{10,... | collective-permute-start | bytes 589832 | tf_op jit(solution)/shard_map/ppermute | solution.py:504
  63.6 3.1 %collective-permute-start.18 = (bf16[4,96,256]{2,1,0:T(8,128)(2,1)S(1)}, bf16[4,96,256]{2,1,0:T(8,128)(2,1)S(1)}, u32[]{:S(2)}, u32[]{:S(2)}) collective-permute-start(bf16[4,96,256]{2,1,0:T(8,128)(2,1)S(1)} %shard_map.228.refs_1_), channel_id=1, source_target_pairs={{0,2},{1,3},{2,0},{3,1},{4,6},{5,7},{6,4},{7,5},{8,10},{9,11},{10,... | collective-permute-start | bytes 589832 | tf_op jit(solution)/shard_map/ppermute | solution.py:504
  66.2 1.4 %collective-permute-start.19 = (bf16[4,96,256]{2,1,0:T(8,128)(2,1)S(1)}, bf16[4,96,256]{2,1,0:T(8,128)(2,1)S(1)}, u32[]{:S(2)}, u32[]{:S(2)}) collective-permute-start(bf16[4,96,256]{2,1,0:T(8,128)(2,1)S(1)} %shard_map.229.refs_2_), channel_id=1, source_target_pairs={{0,2},{1,3},{2,0},{3,1},{4,6},{5,7},{6,4},{7,5},{8,10},{9,11},{10,... | collective-permute-start | bytes 589832 | tf_op jit(solution)/shard_map/ppermute | solution.py:504
  66.2 1.7 %collective-permute-start.20 = (bf16[4,96,256]{2,1,0:T(8,128)(2,1)S(1)}, bf16[4,96,256]{2,1,0:T(8,128)(2,1)S(1)}, u32[]{:S(2)}, u32[]{:S(2)}) collective-permute-start(bf16[4,96,256]{2,1,0:T(8,128)(2,1)S(1)} %shard_map.230.refs_3_), channel_id=1, source_target_pairs={{0,2},{1,3},{2,0},{3,1},{4,6},{5,7},{6,4},{7,5},{8,10},{9,11},{10,... | collective-permute-start | bytes 589832 | tf_op jit(solution)/shard_map/ppermute | solution.py:504

commit v4 on v3

v4 whole, which is shorter than its diff:
```python
import functools

import jax
import jax.numpy as jnp
from jax import lax
from jax.experimental import pallas as pl
from jax.experimental.pallas import tpu as pltpu
from jax.sharding import PartitionSpec as P

commit_weight = 0.25
low = jnp.bfloat16
wide = jnp.float32
bits = (1, 3, 4, 6)
up_plane, left_plane, right_plane, down_plane = range(4)
tile_rows = 16
vmem_bytes = 20 * 2**20
in_hbm = pl.BlockSpec(memory_space=pltpu.HBM)
anywhere = pl.BlockSpec(memory_space=pl.ANY)
in_vmem = pl.BlockSpec(memory_space=pltpu.VMEM)


def mm(lhs, rhs):
    return jnp.dot(lhs, rhs, preferred_element_type=wide)


def mm_nt(lhs, rhs):
    return lax.dot_general(lhs, rhs, (((1,), (1,)), ((), ())), preferred_element_type=wide)


def mm_tn(lhs, rhs):
    return lax.dot_general(lhs, rhs, (((0,), (0,)), ((), ())), preferred_element_type=wide)


def silu(values):
    half = 0.5 * values.astype(wide)
    return half * (1.0 + jnp.tanh(half))


def silu_slopes(half):
    turn = jnp.tanh(half)
    more = 1.0 + turn
    return half * more, more * (1.0 + half * (1.0 - turn))


def code_columns(code_ref):
    canvases, rows, across = code_ref.shape
    flat = code_ref[...].reshape(canvases * rows, across)
    extra = -across % 128
    if extra:
        flat = jnp.concatenate([flat, jnp.zeros((canvases * rows, extra), flat.dtype)], axis=1)
    return flat.T[:across]


def row_codes(columns, row, canvases, rows, lanes):
    pieces = [
        jnp.broadcast_to(
            columns[:, n * rows + row : n * rows + row + 1], (columns.shape[0], lanes)
        )
        for n in range(canvases)
    ]
    return jnp.concatenate(pieces, axis=0)


def chunks(count):
    return [(at, pl.ds(at, tile_rows)) for at in range(0, count, tile_rows)]


def masked(values, masks):
    return values * jnp.concatenate([masks] * (values.shape[1] // masks.shape[1]), axis=1)


def store_slab(slab_ref, at, left, right, values):
    channels = slab_ref.shape[1] // 3
    eight = tile_rows // 2
    place = lax.broadcasted_iota(jnp.int32, (eight, channels), 0)
    steps = chunks(left.count)

    def part(number):
        here = values(steps[number][0])
        halves = here[:eight], here[eight:]
        later = [pltpu.roll(half, 1, 0) for half in halves]
        sooner = [pltpu.roll(half, eight - 1, 0) for half in halves]
        return here, later, sooner

    now = part(0)
    before = now[1][1]
    for number, (start, _) in enumerate(steps):
        new = part(number + 1) if number + 1 < len(steps) else now
        here, later, sooner = now
        span = pl.ds(at + start, tile_rows)
        shifted = [
            jnp.where(place == 0, before, later[0]),
            jnp.where(place == 0, later[0], later[1]),
        ]
        shifted = jnp.concatenate(shifted, axis=0).astype(low)
        slab_ref[span, :channels] = masked(shifted, left(start))
        slab_ref[span, channels : 2 * channels] = here.astype(low)
        shifted = [
            jnp.where(place == eight - 1, sooner[1], sooner[0]),
            jnp.where(place == eight - 1, new[2][0], sooner[1]),
        ]
        shifted = jnp.concatenate(shifted, axis=0).astype(low)
        slab_ref[span, 2 * channels :] = masked(shifted, right(start))
        before = later[1]
        now = new


class Masks:
    def __init__(self, masks_ref, plane, at, count):
        self.masks_ref, self.plane, self.at, self.count = masks_ref, plane, at, count

    def __call__(self, start):
        at = self.at + start
        if not isinstance(at, int):
            at = pl.multiple_of(at, tile_rows)
        return self.masks_ref[self.plane, pl.ds(at, tile_rows)]


class Tape:
    def __init__(self):
        self.steps = []

    def add(self, unit, cost, after, step):
        self.steps.append((unit, cost, [a for a in after if a is not None], step))
        return len(self.steps) - 1

    def play(self):
        free = {"mxu": 0.0, "vpu": 0.0}
        lag = {"mxu": 0.1, "vpu": 0.02}
        ends = {}
        left = list(range(len(self.steps)))
        while left:
            best = None
            for number in left:
                unit, _, after, _ = self.steps[number]
                if all(a in ends for a in after):
                    start = max([free[unit], *[ends[a] for a in after]])
                    if best is None or (start, number) < best:
                        best = (start, number)
            start, number = best
            unit, cost, _, step = self.steps[number]
            free[unit] = start + cost
            ends[number] = start + cost + lag[unit]
            left.remove(number)
            step()


def edge_kernel(latent_ref, crop_hbm, mate_ref, other_ref, masks_ref, crop_ref, sems):
    canvases, rows, across = crop_ref.shape
    count = canvases * across
    odd = lax.axis_index("strip") % 2
    edge = (rows - 1) * (1 - odd)
    codes = pltpu.make_async_copy(crop_hbm, crop_ref, sems.at[0])
    near = pltpu.make_async_copy(latent_ref.at[:, edge], mate_ref, sems.at[1])
    far = pltpu.make_async_copy(latent_ref.at[:, rows - 1 - edge], other_ref, sems.at[2])
    codes.start()
    near.start()
    far.start()
    codes.wait()
    columns = code_columns(crop_ref)
    for row in range(rows):
        here = row_codes(columns, row, canvases, rows, 128)
        for start, _ in chunks(count):
            some = here[start : start + tile_rows]
            span = pl.ds(row * count + start, tile_rows)
            for plane, bit in enumerate(bits):
                masks_ref[plane, span] = jnp.where((some & 2**bit) != 0, 1.0, 0.0).astype(low)
    near.wait()
    far.wait()


def code_kernel(
    index_hbm,
    codebook_hbm,
    decode_weight_hbm,
    out_grad_hbm,
    latent_hbm,
    conv_weight_hbm,
    mix_weight_hbm,
    term_ref,
    picks_ref,
    weight_grad_ref,
    bias_grad_ref,
    latent_ref,
    conv_weight_ref,
    mix_weight_ref,
    index_ref,
    codebook_ref,
    decode_weight_ref,
    out_grad_ref,
    sems,
):
    canvases, rows, across = index_ref.shape
    size, entries = codebook_ref.shape
    channels = decode_weight_ref.shape[1]
    count = canvases * across
    pairs = [
        (index_hbm, index_ref),
        (codebook_hbm, codebook_ref),
        (decode_weight_hbm, decode_weight_ref),
    ]
    pairs += [(out_grad_hbm.at[:, row], out_grad_ref.at[row]) for row in range(rows)]
    pairs += [
        (conv_weight_hbm, conv_weight_ref),
        (latent_hbm, latent_ref),
        (mix_weight_hbm, mix_weight_ref),
    ]
    copies = [
        pltpu.make_async_copy(source, target, sems.at[place])
        for place, (source, target) in enumerate(pairs)
    ]
    for copy in copies:
        copy.start()
    for copy in copies[:3]:
        copy.wait()
    codebook = codebook_ref[...]
    both = jnp.concatenate([codebook * low(-0.5), codebook * low(2.0)], axis=0)
    weight = decode_weight_ref[...]
    weight_top = jnp.concatenate([weight, jnp.zeros_like(weight)], axis=0)
    columns = code_columns(index_ref)
    lanes = lax.broadcasted_iota(jnp.int32, (tile_rows, 128), 1)
    for row in range(rows):
        codes = row_codes(columns, row, canvases, rows, 128)
        for start, _ in chunks(count):
            near = codes[start : start + tile_rows]
            for at in range(0, entries, 128):
                chosen = lanes + at == near
                part = jnp.where(chosen, 1.0, 0.0).astype(low)
                picks_ref[pl.ds(row * count + start, tile_rows), at : at + 128] = part
    term = mm_nt(picks_ref[...], both)
    for copy in copies[3 : 3 + rows]:
        copy.wait()
    grad = out_grad_ref[...].reshape(rows * count, channels)
    term = term + mm_nt(grad, weight_top)
    term_ref[...] = term.reshape(term_ref.shape)
    weight_grad_ref[...] = 0.5 * mm_tn(term.astype(low), grad)[size:]
    bias_sum = None
    for start, _ in chunks(rows * count):
        part = grad[start : start + tile_rows].astype(wide)
        part = part[:8] + part[8:]
        bias_sum = part if bias_sum is None else bias_sum + part
    bias_grad_ref[...] = jnp.sum(bias_sum, axis=0, keepdims=True)
    for copy in copies[3 + rows :]:
        copy.wait()
    for row_step in range(3):
        for start, span in chunks(3 * channels):
            conv_weight_ref[row_step, span] = conv_weight_ref[row_step, span] * low(0.5)


def decoded_kernel(term_ref, decode_weight_ref, decode_bias_ref, after_ref, decoded_ref):
    canvases, rows, across, channels = decoded_ref.shape
    weight = decode_weight_ref[...] * low(0.5)
    weight = jnp.concatenate([jnp.zeros_like(weight), weight], axis=0)
    bias = decode_bias_ref[...].astype(wide).reshape(1, channels)
    for row in range(rows):
        decoded = (mm(term_ref[row].astype(low), weight) + bias).astype(low)
        decoded_ref[:, row] = decoded.reshape(canvases, across, channels)


class Places:
    mate, other = "mate", "other"

    def __init__(self, rows, count):
        self.rows, self.count = rows, count
        self.odd = lax.axis_index("strip") % 2 == 1
        self.inner = list(range(1, rows - 1))

    def row(self, unit):
        if unit == self.mate:
            return jnp.where(self.odd, 0, self.rows - 1)
        if unit == self.other:
            return jnp.where(self.odd, self.rows - 1, 0)
        return unit

    def halo(self, unit):
        first, last = 0, self.rows + 1
        return jnp.where(self.odd, *((first, last) if unit == self.mate else (last, first)))

    def span(self, number, at=0, size=None):
        start = number * self.count + at
        if not isinstance(start, int):
            start = pl.multiple_of(start, tile_rows)
        return pl.ds(start, size or self.count)

    def masks(self, masks_ref, plane, unit, canvas, across):
        return Masks(masks_ref, plane, self.row(unit) * self.count + canvas * across, across)


def rows_kernel(
    beyond,
    masks_ref,
    latent_ref,
    term_ref,
    conv_weight_ref,
    conv_bias_ref,
    mix_weight_ref,
    mix_bias_ref,
    proj_weight_ref,
    proj_bias_ref,
    halo_ref,
    *refs,
):
    outs = refs[-10:]
    slab_ref, grad_ref, up_ref, down_ref, second_ref, stream_ref, codes_ref = outs[:7]
    branch_grad_ref, sums_ref, edge_ref = outs[7:]
    canvases, rows, across, channels = latent_ref.shape
    size = proj_weight_ref.shape[0]
    count = canvases * across
    places = Places(rows, count)
    first = beyond == places.mate
    units = [*places.inner, places.mate] if first else [places.other]

    def own(row, canvas):
        return lambda at: silu(latent_ref[canvas, row, pl.ds(at, tile_rows)])

    def halo(canvas):
        return lambda at: silu(halo_ref[canvas, pl.ds(at, tile_rows)])

    proj = proj_weight_ref[...]
    proj_both = jnp.concatenate([proj * low(2 * commit_weight), proj * low(-2.0)], axis=0).T
    mix_back = (mix_weight_ref[...] * low(0.5)).T
    proj_top = jnp.concatenate([proj, jnp.zeros_like(proj)], axis=0)
    conv_bias = 0.5 * conv_bias_ref[...].astype(wide).reshape(1, channels)
    mix_bias = mix_bias_ref[...].astype(wide).reshape(1, channels)
    proj_bias = proj_bias_ref[...].astype(wide).reshape(1, size)
    proj_bias = jnp.concatenate([2 * commit_weight * proj_bias, -2.0 * proj_bias], axis=1)
    sums = [None, None, None]
    steps = chunks(across)
    tape = Tape()
    slabs = {}

    def add_to(place, values):
        values = values[:8] + values[8:]
        sums[place] = values if sums[place] is None else sums[place] + values

    def slab_of(row, canvas):
        if row != beyond and (not first or row == places.other):
            return None
        if (row, canvas) not in slabs:
            if row == beyond:
                place, values = places.halo(beyond), halo(canvas)
            else:
                place, values = row + 1, own(row, canvas)
            sides = [
                places.masks(masks_ref, plane, row, canvas, across)
                for plane in (left_plane, right_plane)
            ]
            start = places.span(place, canvas * across).start
            slabs[row, canvas] = tape.add(
                "vpu", 0.08, [], lambda: store_slab(slab_ref, start, *sides, values)
            )
        return slabs[row, canvas]

    group = canvases

    def tile(unit, canvas):
        inside = canvas * across
        there = places.row(unit)
        here = places.span(there, inside, group * across)
        above, below = [
            places.masks(masks_ref, plane, unit, canvas, across) for plane in (up_plane, down_plane)
        ]
        conv, slope, made = [], [], [None] * 4
        steps = chunks(group * across)

        def span(start):
            return places.span(there, inside + start, tile_rows)

        def multiply(place, step):
            def run():
                made[place] = step()

            return run

        def convolve(row_step):
            def run():
                rows_of = places.span(there + row_step, inside, group * across)
                conv.append(mm(slab_ref[rows_of], conv_weight_ref[row_step]))

            return run

        def activate():
            up, mid, down = conv
            for start, _ in steps:
                some = slice(start, start + tile_rows)
                total = masked(up[some], above(start).astype(wide))
                total = total + masked(down[some], below(start).astype(wide))
                second, twice = silu_slopes((total + mid[some]) + conv_bias)
                second_ref[span(start)] = second.astype(low)
                slope.append(twice)

        def add_latent():
            for start, _ in steps:
                latent = latent_ref[canvas + start // across, there, pl.ds(start % across, tile_rows)].astype(wide)
                part = latent + (made[0][start : start + tile_rows] + mix_bias)
                stream_ref[span(start)] = part.astype(low)

        def add_term():
            for start, _ in steps:
                part = made[1][start : start + tile_rows]
                part = part + (term_ref[there, pl.ds(inside + start, tile_rows)] + proj_bias)
                codes_ref[span(start)] = part.astype(low)
                add_to(2, part)

        def keep_branch():
            for start, _ in steps:
                part = made[2][start : start + tile_rows]
                branch_grad_ref[there, pl.ds(inside + start, tile_rows)] = part.astype(low)
                add_to(1, part)

        def keep_grad():
            for place, (start, _) in enumerate(steps):
                some = slice(start, start + tile_rows)
                part = made[3][some] * slope[place]
                rounded = part.astype(low)
                grad_ref[span(start)] = rounded
                up_ref[span(start)] = masked(rounded, above(start))
                down_ref[span(start)] = masked(rounded, below(start))
                if unit == beyond:
                    edge_ref[pl.ds(inside + start, tile_rows)] = rounded
                add_to(0, part)

        if unit == places.mate:
            needs = [*range(rows), unit]
        elif unit == places.other:
            needs = [unit]
        else:
            needs = [unit - 1, unit, unit + 1]
        needs = [slab_of(near, canvas + k) for near in needs for k in range(group)]
        last = [tape.add("mxu", 0.063 * group, needs, convolve(row_step)) for row_step in range(3)]
        last = tape.add("vpu", 0.1 * group, last, activate)
        chain = [
            (0.021, lambda: mm(second_ref[here], mix_weight_ref[...]), 0.04, add_latent),
            (0.021, lambda: mm(stream_ref[here], proj_both), 0.03, add_term),
            (0.021, lambda: mm(codes_ref[here], proj_top), 0.03, keep_branch),
            (
                0.021,
                lambda: mm(branch_grad_ref[there, pl.ds(inside, group * across)], mix_back),
                0.07,
                keep_grad,
            ),
        ]
        for place, (cost, product, later, rest) in enumerate(chain):
            last = tape.add("mxu", cost * group, [last], multiply(place, product))
            last = tape.add("vpu", later * group, [last], rest)

    for unit in units:
        for canvas in range(0, canvases, group):
            tile(unit, canvas)

    tape.play()
    sums = [jnp.sum(values, axis=0, keepdims=True) for values in sums]
    sums[2] = jnp.concatenate([sums[2]] * (channels // sums[2].shape[1]), axis=1)
    blank = jnp.zeros((sums_ref.shape[0] - 3, channels), wide)
    sums = jnp.concatenate([*sums, blank], axis=0)
    sums_ref[...] = sums if first else sums + refs[8][...]


def weight_kernel(
    plan,
    mine,
    slab_ref,
    grad_ref,
    up_ref,
    down_ref,
    second_ref,
    stream_ref,
    codes_ref,
    branch_grad_ref,
    sums_ref,
    picks_ref,
    decode_weight_grad_ref,
    decode_bias_grad_ref,
    after_ref,
    out_ref,
):
    total, channels = grad_ref.shape
    rows, count, _ = branch_grad_ref.shape
    size = decode_weight_grad_ref.shape[0]
    entries = picks_ref.shape[1]
    core = lax.axis_index("strip") % 2
    wanted = core if mine else 1 - core
    place = plan.place(wanted)

    def step(row_step, weighted_ref):
        return mm_tn(slab_ref[pl.ds(row_step * count, total)], weighted_ref[...])

    def fill(parts):
        piece, had = [], 0
        at = 0
        rest = plan.half_rows - sum(depth for depth, _ in parts)
        for depth, part in [*parts, (rest, lambda: jnp.zeros((rest, channels), wide))]:
            values = part() if depth else None
            start = 0
            while start < depth:
                some = min(depth - start, plan.piece_rows - had)
                piece.append(values[start : start + some].astype(low))
                start += some
                had += some
                if had == plan.piece_rows:
                    out_ref[at ^ place] = jnp.concatenate(piece, axis=0)
                    piece, had = [], 0
                    at += 1

    @pl.when(wanted == 0)
    def _():
        triple = 3 * channels
        fill([(triple, lambda: step(0, up_ref)), (triple, lambda: step(1, grad_ref))])

    @pl.when(wanted == 1)
    def _():
        sums = sums_ref[...]
        biases = [sums[0:1], sums[1:2], decode_bias_grad_ref[...], sums[2:3]]
        biases.append(jnp.zeros((tile_rows - len(biases), channels), wide))

        def picked():
            part = mm_tn(codes_ref[...], picks_ref[...])[size:]
            return jnp.concatenate([part[:, i : i + channels] for i in range(0, entries, channels)], axis=0)

        fill(
            [
                (3 * channels, lambda: step(2, down_ref)),
                (channels, lambda: mm_tn(second_ref[...], branch_grad_ref[...].reshape(total, channels))),
                (size, lambda: mm_tn(codes_ref[...], stream_ref[...])[:size]),
                (size * (entries // channels), picked),
                (size, lambda: decode_weight_grad_ref[...]),
                (tile_rows, lambda: jnp.concatenate(biases, axis=0)),
            ]
        )


def input_kernel(
    mine,
    masks_ref,
    latent_ref,
    grad_ref,
    mate_ref,
    other_ref,
    branch_grad_ref,
    conv_weight_ref,
    after_ref,
    *refs,
):
    latent_grad_ref, slab_ref, back_ref, out_ref, sems = refs[-5:]
    canvases, rows, across, channels = latent_ref.shape
    count = canvases * across
    places = Places(rows, count)
    steps = chunks(across)
    tape = Tape()

    def own(row, canvas):
        start = row * count + canvas * across
        return lambda at: grad_ref[pl.ds(start + at, tile_rows)].astype(wide)

    def beside(mate, canvas):
        def values(at):
            span = pl.ds(canvas * across + at, tile_rows)
            return jnp.where(mate, mate_ref[span], other_ref[span]).astype(wide)

        return values

    for row_step in range(3):
        for col_step in range(3):
            lanes = slice((2 - col_step) * channels, (3 - col_step) * channels)
            turned = conv_weight_ref[2 - row_step, lanes].T
            back_ref[row_step, col_step * channels : (col_step + 1) * channels] = turned

    slabs = {}

    def slab_of(row, canvas):
        if (row, canvas) not in slabs:
            if row < 0:
                values = beside(places.odd, canvas)
            elif row == rows:
                values = beside(jnp.logical_not(places.odd), canvas)
            else:
                values = own(row, canvas)
            near = min(max(row, 0), rows - 1)
            sides = [
                places.masks(masks_ref, plane, near, canvas, across)
                for plane in (left_plane, right_plane)
            ]
            start = (row + 1) * count + canvas * across
            slabs[row, canvas] = tape.add(
                "vpu", 0.07, [], lambda: store_slab(slab_ref, start, *sides, values)
            )
        return slabs[row, canvas]

    def tile(place, row, canvas):
        inside = canvas * across
        above, below = [
            places.masks(masks_ref, plane, row, canvas, across) for plane in (up_plane, down_plane)
        ]
        spreads = [None] * 3

        def spread(row_step):
            def run():
                span = pl.ds((row + row_step) * count + inside, across)
                spreads[row_step] = mm(slab_ref[span], back_ref[row_step])

            return run

        def finish():
            for start, _ in steps:
                some = slice(start, start + tile_rows)
                total = masked(spreads[0][some], above(start).astype(wide))
                total = total + masked(spreads[2][some], below(start).astype(wide))
                total = total + spreads[1][some]
                near = pl.ds(start, tile_rows)
                _, twice = silu_slopes(0.5 * latent_ref[canvas, row, near].astype(wide))
                stream = branch_grad_ref[row, pl.ds(inside + start, tile_rows)]
                out_ref[place, canvas, near] = (stream.astype(wide) + total * twice).astype(low)

        needs = [slab_of(near, canvas) for near in (row - 1, row, row + 1)]
        made = [tape.add("mxu", 0.063, needs, spread(row_step)) for row_step in range(3)]
        tape.add("vpu", 0.12, made, finish)

    for canvas in range(canvases):
        for place, row in enumerate(mine):
            tile(place, row, canvas)
    tape.play()
    copies = []
    for place, row in enumerate(mine):
        copies.append(
            pltpu.make_async_copy(out_ref.at[place], latent_grad_ref.at[:, row], sems.at[place])
        )
        copies[-1].start()
    for copy in copies:
        copy.wait()


class Plan:
    def __init__(self, sizes, half_rows):
        self.sizes = sizes
        bits = {axis: [(axis, b) for b in range(size.bit_length() - 1)] for axis, size in sizes.items()}
        strip, canvas = bits["strip"], bits["canvas"]
        near, far = [*canvas[:1], *strip[1:2]], strip[2:4][::-1]
        rest = [*strip[4:], *canvas[1:]]
        rest = [rest[i : i + 2] for i in range(0, len(rest), 2)]
        even, odd = [near, far, *rest], [far, near, *rest]
        if len(near) != len(far):
            odd = even
        self.stages = [tuple(zip(*pair, strict=True)) for pair in zip(even, odd, strict=True) if pair[0]]
        self.core = ((("strip", 0), ("strip", 0)),)
        self.half = sizes["strip"] * sizes["canvas"] // 2
        self.piece_rows = -(-half_rows // (self.half * tile_rows)) * tile_rows
        self.half_rows = self.half * self.piece_rows

    def place(self, core):
        number = 0
        for stage in self.stages:
            for spots in stage:
                even, odd = [(lax.axis_index(axis) // 2**bit) % 2 for axis, bit in spots]
                number = number * 2 + (even if spots[0] == spots[1] else jnp.where(core == 0, even, odd))
        return number

    def swap(self, values, stage, step):
        width = self.sizes["canvas"]
        pairs = []
        for strip in range(self.sizes["strip"]):
            change = {"strip": 0, "canvas": 0}
            for place, spots in enumerate(reversed(stage)):
                if step >> place & 1:
                    axis, bit = spots[strip % 2]
                    change[axis] |= 1 << bit
            for canvas in range(width):
                target = (strip ^ change["strip"]) * width + (canvas ^ change["canvas"])
                pairs.append((strip * width + canvas, target))
        return lax.ppermute(values, ("strip", "canvas"), pairs)


def add_kernel(count, after, *refs):
    ins, outs = refs[:count], refs[count + after :]
    depth = outs[0].shape[0]
    for place, out_ref in enumerate(outs):
        span = pl.ds(place * depth, depth)
        total = ins[0][span].astype(wide)
        for ref in ins[1:]:
            total = total + ref[span].astype(wide)
        out_ref[...] = total.astype(low)


def add_split(arrays, parts, after=()):
    depth, rows, channels = arrays[0].shape
    shape = jax.ShapeDtypeStruct((depth // parts, rows, channels), low)
    return pl.pallas_call(
        functools.partial(add_kernel, len(arrays), len(after)),
        in_specs=[in_vmem] * len(arrays) + [anywhere] * len(after),
        out_specs=[in_vmem] * parts,
        out_shape=[shape] * parts,
        compiler_params=pltpu.CompilerParams(vmem_limit_bytes=vmem_bytes),
    )(*arrays, *after)


def gate_kernel(*refs):
    pass


def gate(array, *after):
    return pl.pallas_call(
        gate_kernel,
        in_specs=[in_vmem] + [anywhere] * len(after),
        out_specs=in_vmem,
        out_shape=jax.ShapeDtypeStruct(array.shape, array.dtype),
        input_output_aliases={0: 0},
        compiler_params=pltpu.CompilerParams(vmem_limit_bytes=vmem_bytes),
    )(array, *after)


def join_kernel(count, *refs):
    at = 0
    for ref in refs[:count]:
        refs[-1][pl.ds(at, ref.shape[0])] = ref[...]
        at += ref.shape[0]


def join(arrays, *after):
    depth, rows, channels = arrays[0].shape
    return pl.pallas_call(
        functools.partial(join_kernel, len(arrays)),
        in_specs=[in_vmem] * len(arrays) + [anywhere] * len(after),
        out_specs=in_vmem,
        out_shape=jax.ShapeDtypeStruct((depth * len(arrays), rows, channels), low),
        compiler_params=pltpu.CompilerParams(vmem_limit_bytes=vmem_bytes),
    )(*arrays, *after)


def final_kernel(plan, count, sizes, *refs):
    ins, outs, gathered_ref = refs[:count], refs[count:-1], refs[-1]
    channels, size, entries = sizes
    core = lax.axis_index("strip") % 2
    at = 0
    for ref in ins:
        half = core if at < plan.half else 1 - core
        place = plan.place(half)
        for piece in range(ref.shape[0]):
            shard = half * plan.half + (place ^ at % plan.half)
            start = pl.multiple_of(shard * plan.piece_rows, plan.piece_rows)
            gathered_ref[pl.ds(start, plan.piece_rows)] = ref[piece]
            at += 1
    conv_ref, conv_bias_ref, mix_ref, mix_bias_ref, proj_ref, proj_bias_ref = outs[:6]
    codebook_ref, decode_ref, decode_bias_ref = outs[6:]
    triple = 3 * channels
    conv_ref[pl.ds(0, 2 * triple)] = gathered_ref[pl.ds(0, 2 * triple)].astype(wide)
    at = plan.half_rows
    conv_ref[pl.ds(2 * triple, triple)] = gathered_ref[pl.ds(at, triple)].astype(wide)
    at += triple
    mix_ref[...] = gathered_ref[pl.ds(at, channels)].astype(wide)
    at += channels
    proj_ref[...] = gathered_ref[pl.ds(at, size)].astype(wide)
    at += size
    for piece in range(entries // channels):
        part = gathered_ref[pl.ds(at, size)].astype(wide)
        codebook_ref[:, piece * channels : (piece + 1) * channels] = part
        at += size
    decode_ref[...] = gathered_ref[pl.ds(at, size)].astype(wide)
    at += size
    biases = gathered_ref[pl.ds(at, tile_rows)].astype(wide)
    conv_bias_ref[...] = biases[0:1]
    mix_bias_ref[...] = biases[1:2]
    decode_bias_ref[...] = biases[2:3]
    proj_bias_ref[...] = biases[3:4, :size]


def per_device(
    plan,
    latent_in,
    crop_code,
    code_index,
    conv_weight,
    conv_bias,
    mix_weight,
    mix_bias,
    proj_weight,
    proj_bias,
    codebook,
    decode_weight,
    decode_bias,
    out_grad,
):
    canvases, rows, across, channels = latent_in.shape
    entries, size = codebook.shape
    count = canvases * across
    total = rows * count
    strips = plan.sizes["strip"]
    struct = jax.ShapeDtypeStruct
    flat_weight = conv_weight.reshape(3, 3 * channels, channels)

    def far_away(*arrays):
        return [pltpu.with_memory_space_constraint(array, pltpu.HBM) for array in arrays]

    def call(kernel, ins, outs, shapes, scratch=(), flops=0, aliases=None):
        return pl.pallas_call(
            kernel,
            in_specs=list(ins),
            out_specs=list(outs),
            out_shape=list(shapes),
            scratch_shapes=list(scratch),
            input_output_aliases=aliases or {},
            compiler_params=pltpu.CompilerParams(vmem_limit_bytes=vmem_bytes),
            cost_estimate=pl.CostEstimate(flops=flops, bytes_accessed=0, transcendentals=0),
        )

    def trade(mate, other, split=True):
        near = [(i, i ^ 1) for i in range(strips)]
        far = [(i, i + 1) for i in range(1, strips - 1, 2)]
        far += [(target, source) for source, target in far]
        if not split:
            return lax.ppermute(mate, "strip", near), lax.ppermute(other, "strip", far)
        half = other.shape[0] // 2
        others = [lax.ppermute(part, "strip", far) for part in (other[:half], other[half:])]
        return (lax.ppermute(mate, "strip", near), *others)

    edge_shape = struct((canvases, across, channels), low)
    *edges, masks = call(
        edge_kernel,
        [in_hbm] * 2,
        [in_vmem] * 3,
        [edge_shape, edge_shape, struct((len(bits), total, 128), low)],
        [pltpu.VMEM(crop_code.shape, crop_code.dtype), pltpu.SemaphoreType.DMA((3,))],
    )(*far_away(latent_in, crop_code))
    mate, other = trade(*edges, split=False)
    outs = [
        struct((rows, count, 2 * size), wide),
        struct((total, entries), low),
        struct((size, channels), wide),
        struct((1, channels), wide),
        struct(latent_in.shape, low),
        struct(flat_weight.shape, low),
        struct(mix_weight.shape, low),
    ]
    held = [
        pltpu.VMEM(code_index.shape, code_index.dtype),
        pltpu.VMEM((size, entries), low),
        pltpu.VMEM((size, channels), low),
        pltpu.VMEM((rows, canvases, across, channels), low),
        pltpu.SemaphoreType.DMA((rows + 6,)),
    ]
    term, picks, decode_weight_grad, decode_bias_grad, latent, near_weight, near_mix = call(
        code_kernel,
        [in_hbm] * 7,
        [in_vmem] * 7,
        outs,
        held,
        flops=6 * total * channels * channels,
    )(
        *far_away(
            code_index,
            codebook.T,
            decode_weight,
            out_grad,
            latent_in,
            flat_weight,
            mix_weight,
        )
    )
    slab_shape = struct((total + 2 * count, 3 * channels), low)
    flat = struct((total, channels), low)
    kept = [slab_shape, flat, flat, flat, flat, flat, struct((total, 2 * size), low)]
    kept += [struct((rows, count, channels), low), struct((8, channels), wide)]
    edge_shape = struct((count, channels), low)
    inner, outer = tuple(range(1, rows - 1)), tuple(sorted({0, rows - 1}))
    shared = [masks, latent, term, near_weight, conv_bias, near_mix, mix_bias, proj_weight.T, proj_bias]

    def block_rows(beyond, halo, before):
        ins = [*shared, halo, *before]
        first = len(ins) - len(before)
        outs = call(
            functools.partial(rows_kernel, beyond),
            [in_vmem] * len(ins),
            [in_vmem] * (len(kept) + 1),
            [*kept, edge_shape],
            flops=20 * total * channels * channels,
            aliases={first + i: i for i in range(len(before))},
        )(*ins)
        return outs[:-1], outs[-1]

    before, edge_mate = block_rows("mate", mate, ())
    before, edge_other = block_rows("other", other, before)
    slab, grad, up, down, second, stream, codes, branch_grad, sums = before
    edges = (edge_mate, edge_other)

    def weight_half(mine, after):
        ins = [slab, grad, up, down, second, stream, codes, branch_grad, sums, picks]
        ins += [decode_weight_grad, decode_bias_grad]
        return call(
            functools.partial(weight_kernel, plan, mine),
            [in_vmem] * len(ins) + [anywhere],
            [in_vmem],
            [struct((plan.half, plan.piece_rows, channels), low)],
            flops=10 * total * channels * channels,
        )(*ins, after)[0]

    send = weight_half(False, edge_other)
    keep = weight_half(True, send)

    def input_rows(mine, halo, after, *before):
        return call(
            functools.partial(input_kernel, mine),
            [in_vmem] * 7 + [anywhere] + [in_hbm] * len(before),
            [in_hbm],
            [pltpu.HBM(latent_in.shape, low)],
            [
                pltpu.VMEM(slab_shape.shape, low),
                pltpu.VMEM(flat_weight.shape, low),
                pltpu.VMEM((len(mine), canvases, across, channels), low),
                pltpu.SemaphoreType.DMA((len(mine),)),
            ],
            flops=11 * total * channels * channels,
            aliases={8: 0} if before else {},
        )(masks, latent, grad, *halo, branch_grad, near_weight, after, *before)[0]

    arrays = [keep, plan.swap(send, plan.core, 1)]
    after = []
    for place, stage in enumerate(plan.stages):
        parts = add_split(arrays, 2 ** len(stage), after)
        arrays = [parts[0]]
        arrays += [plan.swap(parts[i], stage, i) for i in reversed(range(1, len(parts)))]
        after = []
        if place == 0:
            halo = trade(*[gate(edge, parts[0]) for edge in edges])
        elif place == 1:
            decoded = call(
                decoded_kernel,
                [in_vmem, in_vmem, in_vmem, anywhere],
                [pl.BlockSpec()],
                [pltpu.HBM(out_grad.shape, low)],
                flops=4 * total * channels * channels,
            )(term, decode_weight, decode_bias, parts[0])[0]
            after = [*far_away(decoded), *halo]
    halo = (halo[0], jnp.concatenate(halo[1:], axis=0))
    pieces = add_split(arrays, 1, after)
    latent_grad = input_rows(inner, edges, pieces[0])
    after = far_away(latent_grad)
    for stage in reversed(plan.stages):
        gathered = join(pieces, *after) if len(pieces) > 1 else pieces[0]
        others = [plan.swap(gathered, stage, i) for i in range(1, 2 ** len(stage))]
        pieces = [gathered, *others]
    latent_grad = input_rows(outer, halo, gathered, latent_grad)
    done = far_away(latent_grad)
    pieces = [pieces[0], *[gate(piece, *done) for piece in pieces[1:]]]
    arrays = [*pieces, *[plan.swap(piece, plan.core, 1) for piece in pieces]]

    results = call(
        functools.partial(final_kernel, plan, len(arrays), (channels, size, entries)),
        [in_vmem] * len(arrays),
        [pl.BlockSpec()] * 9,
        [
            struct((9 * channels, channels), wide),
            struct((1, channels), wide),
            struct((channels, channels), wide),
            struct((1, channels), wide),
            struct((size, channels), wide),
            struct((1, size), wide),
            struct((size, entries), wide),
            struct((size, channels), wide),
            struct((1, channels), wide),
        ],
        [pltpu.VMEM((2 * plan.half_rows, channels), low)],
    )(*arrays)
    return (
        decoded,
        latent_grad,
        results[0].reshape(3, 3, channels, channels),
        results[1].reshape(-1),
        results[2],
        results[3].reshape(-1),
        results[4].T,
        results[5].reshape(-1),
        results[6].T,
        results[7],
        results[8].reshape(-1),
    )


def solution(mesh):
    sizes = {axis: mesh.shape[axis] for axis in ("strip", "canvas")}
    shared = P("canvas", "strip", None, None)
    codes = P("canvas", "strip", None)

    def wrapped(*args):
        channels = args[0].shape[3]
        entries, size = args[9].shape
        others = 4 * channels + 2 * size + size * (entries // channels) + tile_rows
        plan = Plan(sizes, max(6 * channels, others))
        return jax.shard_map(
            functools.partial(per_device, plan),
            mesh=mesh,
            in_specs=(shared, codes, codes, *[P()] * 9, shared),
            out_specs=(shared, shared, *[P()] * 9),
            check_vma=False,
        )(*args)

    return wrapped
```

time: 70.1 us -> 65.6 us (0.936)
  waiting for transfers between devices: 15.9 us -> 4.42 us
  starting transfers between devices: 23.5 us -> 31.2 us
  Pallas kernels: 29.4 us -> 28.3 us
    ppermute x17, waiting for transfers between devices: 15.9 us -> 4.41 us  [swap(): return lax.ppermute(values, ('strip', 'canvas'), pairs)]
    ppermute x0 -> x3, starting transfers between devices: none -> 6.38 us  [the longest x2 6.38 us: trade(): lax.ppermute(part, 'strip', far)]
    ppermute x17, starting transfers between devices: 15.5 us -> 20.2 us  [swap(): return lax.ppermute(values, ('strip', 'canvas'), pairs)]
    ppermute x2 -> x1, starting transfers between devices: 7.83 us -> 4.49 us  [trade(): lax.ppermute(other, 'strip', far)]
    pallas_call x5 -> x4, Pallas kernels: 13.5 us -> 12.8 us  [the longest x2 7.33 us: block_rows(): call(functools.partial(rows_kernel, beyond), [in_vmem] * len(ins), [in_vm...]
  transfers between devices with their start and end apart: 21 -> 22, of which waited for: 8 -> 5; matrix products, arithmetic and copies ran while one was open for 0% -> 0% of each run, Pallas kernels for 28% -> 30%
where the time goes in v4:
time: 65.6 us; the launch traced here: 65 us
  starting transfers between devices  31.2 us (48%)
  Pallas kernels  28.3 us (43%)
  waiting for transfers between devices  4.42 us (7%)
  between operations  0.97 us (1%)
    ppermute x17, starting transfers between devices, swap(): return lax.ppermute(values, ('strip', 'canvas'), pairs)  20.2 us
    pallas_call x2, Pallas kernels, block_rows(): call(functools.partial(rows_kernel, beyond), [in_vmem] * len(ins), [in_vm...  7.33 us
    pallas_call x2, Pallas kernels, input_rows(): call(functools.partial(input_kernel, mine), [in_vmem] * 7 + [anywhere] +...  6.69 us
    ppermute x2, starting transfers between devices, trade(): lax.ppermute(part, 'strip', far)  6.38 us
    pallas_call x2, Pallas kernels, weight_half(): call(functools.partial(weight_kernel, plan, mine), [in_vmem] * len(ins) +...  5.06 us
    ppermute x1, starting transfers between devices, trade(): lax.ppermute(other, 'strip', far)  4.49 us
    ppermute x17, waiting for transfers between devices, swap(): return lax.ppermute(values, ('strip', 'canvas'), pairs)  4.41 us
    pallas_call x1, Pallas kernels, per_device(): call(code_kernel, [in_hbm] * 7, [in_vmem] * 7, outs, held, flops=6 * tota...  3.89 us
  transfers between devices with their start and end apart: 22, of which 5 were waited for; matrix products, arithmetic and copies ran while one was open for 0% of the time, Pallas kernels for 30%

profile of v4, /device:TPU:1, one launch (start us, length us, event | category | flops | bytes accessed | tf_op | source)
XLA Modules:
  0.0 65.0 jit_solution(6096111932569553565)
XLA Ops:
  0.6 1.5 %shard_map.213 = (bf16[4,176,256]{2,1,0:T(8,128)(2,1)S(1)}, bf16[4,176,256]{2,1,0:T(8,128)(2,1)S(1)}, bf16[4,2816,128]{2,1,0:T(8,128)(2,1)S(1)}) custom-call(bf16[4,4,176,256]{3,2,1,0:T(8,128)(2,1)} %latent_ref.1, s32[4,4,176]{2,1,0:T(4,128)} %crop_hbm.1), custom_call_target="tpu_custom_call" | custom-call | tf_op jit(solution)/shard_map/pallas_call | solution.py:815
  2.2 0.1 collective-permute-start.1
  2.3 4.5 %collective-permute-start = (bf16[4,176,256]{2,1,0:T(8,128)(2,1)S(1)}, bf16[4,176,256]{2,1,0:T(8,128)(2,1)S(1)}, u32[]{:S(2)}, u32[]{:S(2)}) collective-permute-start(bf16[4,176,256]{2,1,0:T(8,128)(2,1)S(1)} %get-tuple-element.63), channel_id=1, source_target_pairs={{2,4},{6,8},{10,12},{14,16},{18,20},{22,24},{26,28},{4,2},{8,6},{1... | collective-permute-start | bytes 1081352 | tf_op jit(solution)/shard_map/ppermute | solution.py:809
  6.8 0.0 copy-start.1
  6.8 0.0 copy-start.2
  6.8 0.0 copy-start.3
  6.8 0.0 copy-start.4
  6.9 3.9 %shard_map.212 = (f32[4,704,128]{2,1,0:T(8,128)S(1)}, bf16[2816,512]{1,0:T(8,128)(2,1)S(1)}, f32[64,256]{1,0:T(8,128)S(1)}, f32[1,256]{1,0:T(1,128)S(1)}, bf16[4...) custom-call(s32[4,4,176]{2,1,0:T(4,128)} %index_hbm.1, ...), custom_call_target="tpu_custom_call" | custom-call | flops 1107296256 | tf_op jit(solution)/shard_map/pallas_call | solution.py:839
  10.8 0.0 collective-permute-done.1.halo_ref
  10.8 5.1 %shard_map.214 = (bf16[4224,768]{1,0:T(8,128)(2,1)S(1)}, bf16[2816,256]{1,0:T(8,128)(2,1)S(1)}, bf16[2816,256]{1,0:T(8,128)(2,1)S(1)}, bf16[2816,256]{1,0:T(8,12...) custom-call(bf16[4,2816,128]{2,1,0:T(8,128)(2,1)S(1)} %get-tuple-ele, ...), custom_call_target="tpu_custom_call" | custom-call | flops 3690987520 | tf_op jit(solution)/shard_map/pallas_call | solution.py:868
  15.9 0.0 collective-permute-done.halo_ref
  15.9 2.2 %shard_map.215 = (bf16[4224,768]{1,0:T(8,128)(2,1)S(1)}, bf16[2816,256]{1,0:T(8,128)(2,1)S(1)}, bf16[2816,256]{1,0:T(8,128)(2,1)S(1)}, bf16[2816,256]{1,0:T(8,12...) custom-call(bf16[4,2816,128]{2,1,0:T(8,128)(2,1)S(1)} %get-tuple-ele, ...), custom_call_target="tpu_custom_call", output_to_operand_aliasing={{0}: (10, {}), {1}: (11, {}), {2}: (12, {}), {3}: (13, {}),... | custom-call | flops 3690987520 | tf_op jit(solution)/shard_map/pallas_call | solution.py:868
  18.2 2.7 %shard_map.216.after_ref = bf16[16,96,256]{2,1,0:T(8,128)(2,1)S(1)} custom-call(bf16[4224,768]{1,0:T(8,128)(2,1)S(1)} %get-tuple-element.74.slab_ref, bf16[2816,256]{1,0:T(8,128)(2,1)S(1)} %get-tuple-element.75.grad_ref, bf16[2816,256]{1,0:T(8,128)(2,1)S(1)} %get-tuple-element.76.up_ref, bf16[2816,256]{1,0:T(8,128)(2,1)S(1)} %get-tuple-element.77.down_ref, ...), custom_call_target="tpu_custom_call" | custom-call | flops 1845493760 | tf_op jit(solution)/shard_map/pallas_call | solution.py:886
  20.8 0.1 collective-permute-start.2
  21.0 2.4 %shard_map.217.refs_0_ = bf16[16,96,256]{2,1,0:T(8,128)(2,1)S(1)} custom-call(bf16[4224,768]{1,0:T(8,128)(2,1)S(1)} %get-tuple-element.74.slab_ref, bf16[2816,256]{1,0:T(8,128)(2,1)S(1)} %get-tuple-element.75.grad_ref, bf16[2816,256]{1,0:T(8,128)(2,1)S(1)} %get-tuple-element.76.up_ref, bf16[2816,256]{1,0:T(8,128)(2,1)S(1)} %get-tuple-element.77.down_ref, ...), custom_call_target="tpu_custom_call" | custom-call | flops 1845493760 | tf_op jit(solution)/shard_map/pallas_call | solution.py:886
  23.4 0.0 collective-permute-done.2.refs_1_
  23.4 0.2 shard_map.218
  23.6 0.0 copy-start
  23.6 0.0 copy-start.5
  23.6 3.8 %collective-permute-start.3 = (bf16[4,96,256]{2,1,0:T(8,128)(2,1)S(1)}, bf16[4,96,256]{2,1,0:T(8,128)(2,1)S(1)}, u32[]{:S(2)}, u32[]{:S(2)}) collective-permute-start(bf16[4,96,256]{2,1,0:T(8,128)(2,1)S(1)} %get-tuple-element.88), channel_id=1, source_target_pairs={{0,5},{1,4},{2,26},{3,27},{4,1},{5,0},{6,30},{7,31},{8,13},{9,12},... | collective-permute-start | bytes 589832 | tf_op jit(solution)/shard_map/ppermute | solution.py:669
  27.4 0.4 collective-permute-start.5
  27.8 0.0 collective-permute-start.6
  27.8 3.3 %collective-permute-start.7 = (bf16[352,256]{1,0:T(8,128)(2,1)S(1)}, bf16[352,256]{1,0:T(8,128)(2,1)S(1)}, u32[]{:S(2)}, u32[]{:S(2)}) collective-permute-start(bf16[352,256]{1,0:T(8,128)(2,1)S(1)} %get-tuple-element.105), channel_id=1, source_target_pairs={{2,4},{6,8},{10,12},{14,16},{18,20},{22,24},{26,28},{4,2},{8,6},{1... | collective-permute-start | bytes 540680 | tf_op jit(solution)/shard_map/ppermute | solution.py:811
  31.1 0.0 collective-permute-done.3.refs_1_
  31.1 3.1 %collective-permute-start.8 = (bf16[352,256]{1,0:T(8,128)(2,1)S(1)}, bf16[352,256]{1,0:T(8,128)(2,1)S(1)}, u32[]{:S(2)}, u32[]{:S(2)}) collective-permute-start(bf16[352,256]{1,0:T(8,128)(2,1)S(1)} %get-tuple-element.106), channel_id=1, source_target_pairs={{2,4},{6,8},{10,12},{14,16},{18,20},{22,24},{26,28},{4,2},{8,6},{1... | collective-permute-start | bytes 540680 | tf_op jit(solution)/shard_map/ppermute | solution.py:811
  34.2 2.9 %collective-permute-done.4.refs_2_ = bf16[4,96,256]{2,1,0:T(8,128)(2,1)S(1)} collective-permute-done((bf16[4,96,256]{2,1,0:T(8,128)(2,1)S(1)}, bf16[4,96,256]{2,1,0:T(8,128)(2,1)S(1)}, u32[]{:S(2)}, u32[]{:S(2)}) %collective-permute-start.4) | collective-permute-done | bytes 196640 | tf_op jit(solution)/shard_map/ppermute | solution.py:669
  37.2 0.0 collective-permute-done.5.refs_3_
  37.2 0.1 shard_map.219
  37.3 0.9 %collective-permute-start.9 = (bf16[1,96,256]{2,1,0:T(8,128)(2,1)S(1)}, bf16[1,96,256]{2,1,0:T(8,128)(2,1)S(1)}, u32[]{:S(2)}, u32[]{:S(2)}) collective-permute-start(bf16[1,96,256]{2,1,0:T(8,128)(2,1)S(1)} %get-tuple-element.93), channel_id=1, source_target_pairs={{0,24},{1,25},{2,7},{3,6},{4,28},{5,29},{6,3},{7,2},{8,16},{9,17},... | collective-permute-start | bytes 147464 | tf_op jit(solution)/shard_map/ppermute | solution.py:669
  38.2 0.4 collective-permute-start.10
  38.6 1.4 %collective-permute-start.11 = (bf16[1,96,256]{2,1,0:T(8,128)(2,1)S(1)}, bf16[1,96,256]{2,1,0:T(8,128)(2,1)S(1)}, u32[]{:S(2)}, u32[]{:S(2)}) collective-permute-start(bf16[1,96,256]{2,1,0:T(8,128)(2,1)S(1)} %get-tuple-element.95), channel_id=1, source_target_pairs={{0,8},{1,9},{2,6},{3,7},{4,12},{5,13},{6,2},{7,3},{8,0},{9,1},{10,... | collective-permute-start | bytes 147464 | tf_op jit(solution)/shard_map/ppermute | solution.py:669
  40.0 1.6 %shard_map.220.refs_4_ = bf16[4,4,176,256]{3,2,1,0:T(8,128)(2,1)} custom-call(f32[4,704,128]{2,1,0:T(8,128)S(1)} %get-tuple-element.58.term_ref, bf16[64,256]{1,0:T(8,128)(2,1)S(1)} %copy-done, bf16[256]{0:T(256)(128)(2,1)S(1)} %copy-done.5, bf16[1,96,256]{2,1,0:T(8,128)(2,1)S(1)} %get-tuple-element.91.after_ref.refs_0_), custom_call_target="tpu_custom_call" | custom-call | flops 738197504 | tf_op jit(solution)/shard_map/pallas_call | solution.py:923
  41.6 0.1 collective-permute-done.11.refs_3_
  41.7 2.3 %collective-permute-start.14 = (bf16[1,96,256]{2,1,0:T(8,128)(2,1)S(1)}, bf16[1,96,256]{2,1,0:T(8,128)(2,1)S(1)}, u32[]{:S(2)}, u32[]{:S(2)}) collective-permute-start(bf16[1,96,256]{2,1,0:T(8,128)(2,1)S(1)} %shard_map.223.after_ref.refs_0_), channel_id=1, source_target_pairs={{0,24},{1,25},{2,7},{3,6},{4,28},{5,29},{6,3},{7,2},{8,16},{9,17},... | collective-permute-start | bytes 147464 | tf_op jit(solution)/shard_map/ppermute | solution.py:669
  44.0 0.3 collective-permute-start.13
  44.3 0.2 collective-permute-start.12
  44.4 3.3 %shard_map.224.refs_4_.refs_0_ = bf16[4,4,176,256]{3,2,1,0:T(8,128)(2,1)} custom-call(bf16[4,2816,128]{2,1,0:T(8,128)(2,1)S(1)} %get-tuple-element.59.masks_ref, bf16[4,4,176,256]{3,2,1,0:T(8,128)(2,1)S(1)} %get-tuple-element.60.latent_ref, bf16[2816,256]{1,0:T(8,128)(2,1)S(1)} %get-tuple-element.75.grad_ref, ...), custom_call_target="tpu_custom_call" | custom-call | flops 2030043136 | tf_op jit(solution)/shard_map/pallas_call | solution.py:898
  47.8 4.0 %collective-permute-start.17 = (bf16[4,96,256]{2,1,0:T(8,128)(2,1)S(1)}, bf16[4,96,256]{2,1,0:T(8,128)(2,1)S(1)}, u32[]{:S(2)}, u32[]{:S(2)}) collective-permute-start(bf16[4,96,256]{2,1,0:T(8,128)(2,1)S(1)} %shard_map.225.after_ref.refs_0_), channel_id=1, source_target_pairs={{0,5},{1,4},{2,26},{3,27},{4,1},{5,0},{6,30},{7,31},{8,13},{9,12},... | collective-permute-start | bytes 589832 | tf_op jit(solution)/shard_map/ppermute | solution.py:669
  51.7 0.4 collective-permute-start.15
  52.1 4.9 %collective-permute-start.18 = (bf16[4,96,256]{2,1,0:T(8,128)(2,1)S(1)}, bf16[4,96,256]{2,1,0:T(8,128)(2,1)S(1)}, u32[]{:S(2)}, u32[]{:S(2)}) collective-permute-start(bf16[4,96,256]{2,1,0:T(8,128)(2,1)S(1)} %shard_map.225.after_ref.refs_0_), channel_id=1, source_target_pairs={{0,2},{1,3},{2,0},{3,1},{4,6},{5,7},{6,4},{7,5},{8,10},{9,11},{10,... | collective-permute-start | bytes 589832 | tf_op jit(solution)/shard_map/ppermute | solution.py:669
  57.0 3.4 %shard_map.226.refs_1_ = bf16[4,4,176,256]{3,2,1,0:T(8,128)(2,1)} custom-call(bf16[4,2816,128]{2,1,0:T(8,128)(2,1)S(1)} %get-tuple-element.59.masks_ref, bf16[4,4,176,256]{3,2,1,0:T(8,128)(2,1)S(1)} %get-tuple-element.60.latent_ref, bf16[2816,256]{1,0:T(8,128)(2,1)S(1)} %get-tuple-element.75.grad_ref, ...), custom_call_target="tpu_custom_call", output_to_operand_aliasing={{}: (8, {})} | custom-call | flops 2030043136 | tf_op jit(solution)/shard_map/pallas_call | solution.py:898
  60.5 0.1 collective-permute-start.21
  60.5 0.3 collective-permute-done.16.refs_0_
  60.8 0.2 collective-permute-start.20
  61.0 1.0 %collective-permute-start.19 = (bf16[4,96,256]{2,1,0:T(8,128)(2,1)S(1)}, bf16[4,96,256]{2,1,0:T(8,128)(2,1)S(1)}, u32[]{:S(2)}, u32[]{:S(2)}) collective-permute-start(bf16[4,96,256]{2,1,0:T(8,128)(2,1)S(1)} %shard_map.227.refs_1_), channel_id=1, source_target_pairs={{0,2},{1,3},{2,0},{3,1},{4,6},{5,7},{6,4},{7,5},{8,10},{9,11},{10,... | collective-permute-start | bytes 589832 | tf_op jit(solution)/shard_map/ppermute | solution.py:669
  62.1 0.2 collective-permute-done.20.refs_6_
  62.3 0.9 %collective-permute-done.19.refs_5_ = bf16[4,96,256]{2,1,0:T(8,128)(2,1)S(1)} collective-permute-done((bf16[4,96,256]{2,1,0:T(8,128)(2,1)S(1)}, bf16[4,96,256]{2,1,0:T(8,128)(2,1)S(1)}, u32[]{:S(2)}, u32[]{:S(2)}) %collective-permute-start.19) | collective-permute-done | bytes 196640 | tf_op jit(solution)/shard_map/ppermute | solution.py:669
  63.2 1.8 %shard_map.230 = (f32[2304,256]{1,0:T(8,128)}, f32[1,256]{1,0:T(1,128)}, f32[256,256]{1,0:T(8,128)}, f32[1,256]{1,0:T(1,128)}, f32[64,256]{1,0:T(8,128)}, /*inde...) custom-call(bf16[4,96,256]{2,1,0:T(8,128)(2,1)S(1)} %shard_map.225.after_ref.refs_0_, ...), custom_call_target="tpu_custom_call" | custom-call | tf_op jit(solution)/shard_map/pallas_call | solution.py:944
  (31 shorter events, 0.2 us)
Async XLA Ops:
  2.2 8.6 %collective-permute-start.1 = (bf16[4,176,256]{2,1,0:T(8,128)(2,1)S(1)}, bf16[4,176,256]{2,1,0:T(8,128)(2,1)S(1)}, u32[]{:S(2)}, u32[]{:S(2)}) collective-permute-start(bf16[4,176,256]{2,1,0:T(8,128)(2,1)S(1)} %get-tuple-element.64), channel_id=1, source_target_pairs={{0,2},{2,0},{4,6},{6,4},{8,10},{10,8},{12,14},{14,12},{16,18},{18,... | collective-permute-start | bytes 1081352 | tf_op jit(solution)/shard_map/ppermute | solution.py:809
  2.3 13.6 %collective-permute-start = (bf16[4,176,256]{2,1,0:T(8,128)(2,1)S(1)}, bf16[4,176,256]{2,1,0:T(8,128)(2,1)S(1)}, u32[]{:S(2)}, u32[]{:S(2)}) collective-permute-start(bf16[4,176,256]{2,1,0:T(8,128)(2,1)S(1)} %get-tuple-element.63), channel_id=1, source_target_pairs={{2,4},{6,8},{10,12},{14,16},{18,20},{22,24},{26,28},{4,2},{8,6},{1... | collective-permute-start | bytes 1081352 | tf_op jit(solution)/shard_map/ppermute | solution.py:809
  6.8 4.0 %copy-start.1 = (bf16[256,64]{0,1:T(8,128)(2,1)S(1)}, bf16[256,64]{0,1:T(8,128)(2,1)}, u32[]{:S(2)}) copy-start(bf16[256,64]{0,1:T(8,128)(2,1)} %param.20) | copy-start | bytes 98308
  6.8 4.0 %copy-start.2 = (bf16[256]{0:T(256)(128)(2,1)S(1)}, bf16[256]{0:T(256)(128)(2,1)}, u32[]{:S(2)}) copy-start(bf16[256]{0:T(256)(128)(2,1)} %conv_bias_ref.3) | copy-start | bytes 1540
  6.8 4.0 %copy-start.3 = (bf16[256]{0:T(256)(128)(2,1)S(1)}, bf16[256]{0:T(256)(128)(2,1)}, u32[]{:S(2)}) copy-start(bf16[256]{0:T(256)(128)(2,1)} %mix_bias_ref.3) | copy-start | bytes 1540
  6.8 4.0 %copy-start.4 = (bf16[64]{0:T(256)(128)(2,1)S(1)}, bf16[64]{0:T(256)(128)(2,1)}, u32[]{:S(2)}) copy-start(bf16[64]{0:T(256)(128)(2,1)} %proj_bias_ref.3) | copy-start | bytes 388
  20.8 2.5 %collective-permute-start.2 = (bf16[16,96,256]{2,1,0:T(8,128)(2,1)S(1)}, bf16[16,96,256]{2,1,0:T(8,128)(2,1)S(1)}, u32[]{:S(2)}, u32[]{:S(2)}) collective-permute-start(bf16[16,96,256]{2,1,0:T(8,128)(2,1)S(1)} %shard_map.216.after_ref), channel_id=1, source_target_pairs={{0,2},{1,3},{2,0},{3,1},{4,6},{5,7},{6,4},{7,5},{8,10},{9,11},{10,... | collective-permute-start | bytes 2359304 | tf_op jit(solution)/shard_map/ppermute | solution.py:669
  23.6 16.4 %copy-start = (bf16[64,256]{1,0:T(8,128)(2,1)S(1)}, bf16[64,256]{1,0:T(8,128)(2,1)}, u32[]{:S(2)}) copy-start(bf16[64,256]{1,0:T(8,128)(2,1)} %decode_weight_ref.1) | copy-start | bytes 98308
  23.6 16.4 %copy-start.5 = (bf16[256]{0:T(256)(128)(2,1)S(1)}, bf16[256]{0:T(256)(128)(2,1)}, u32[]{:S(2)}) copy-start(bf16[256]{0:T(256)(128)(2,1)} %decode_bias_ref.1) | copy-start | bytes 1540
  23.6 7.5 %collective-permute-start.3 = (bf16[4,96,256]{2,1,0:T(8,128)(2,1)S(1)}, bf16[4,96,256]{2,1,0:T(8,128)(2,1)S(1)}, u32[]{:S(2)}, u32[]{:S(2)}) collective-permute-start(bf16[4,96,256]{2,1,0:T(8,128)(2,1)S(1)} %get-tuple-element.88), channel_id=1, source_target_pairs={{0,5},{1,4},{2,26},{3,27},{4,1},{5,0},{6,30},{7,31},{8,13},{9,12},... | collective-permute-start | bytes 589832 | tf_op jit(solution)/shard_map/ppermute | solution.py:669
  27.4 9.7 %collective-permute-start.4 = (bf16[4,96,256]{2,1,0:T(8,128)(2,1)S(1)}, bf16[4,96,256]{2,1,0:T(8,128)(2,1)S(1)}, u32[]{:S(2)}, u32[]{:S(2)}) collective-permute-start(bf16[4,96,256]{2,1,0:T(8,128)(2,1)S(1)} %get-tuple-element.89), channel_id=1, source_target_pairs={{0,1},{1,0},{2,18},{3,19},{4,5},{5,4},{6,22},{7,23},{8,9},{9,8},{1... | collective-permute-start | bytes 589832 | tf_op jit(solution)/shard_map/ppermute | solution.py:669
  27.4 9.7 %collective-permute-start.5 = (bf16[4,96,256]{2,1,0:T(8,128)(2,1)S(1)}, bf16[4,96,256]{2,1,0:T(8,128)(2,1)S(1)}, u32[]{:S(2)}, u32[]{:S(2)}) collective-permute-start(bf16[4,96,256]{2,1,0:T(8,128)(2,1)S(1)} %get-tuple-element.90), channel_id=1, source_target_pairs={{0,4},{1,5},{2,10},{3,11},{4,0},{5,1},{6,14},{7,15},{8,12},{9,13},... | collective-permute-start | bytes 589832 | tf_op jit(solution)/shard_map/ppermute | solution.py:669
  27.8 13.9 %collective-permute-start.6 = (bf16[704,256]{1,0:T(8,128)(2,1)S(1)}, bf16[704,256]{1,0:T(8,128)(2,1)S(1)}, u32[]{:S(2)}, u32[]{:S(2)}) collective-permute-start(bf16[704,256]{1,0:T(8,128)(2,1)S(1)} %shard_map.221), channel_id=1, source_target_pairs={{0,2},{2,0},{4,6},{6,4},{8,10},{10,8},{12,14},{14,12},{16,18},{18,... | collective-permute-start | bytes 1081352 | tf_op jit(solution)/shard_map/ppermute | solution.py:812
  27.8 10.8 %collective-permute-start.7 = (bf16[352,256]{1,0:T(8,128)(2,1)S(1)}, bf16[352,256]{1,0:T(8,128)(2,1)S(1)}, u32[]{:S(2)}, u32[]{:S(2)}) collective-permute-start(bf16[352,256]{1,0:T(8,128)(2,1)S(1)} %get-tuple-element.105), channel_id=1, source_target_pairs={{2,4},{6,8},{10,12},{14,16},{18,20},{22,24},{26,28},{4,2},{8,6},{1... | collective-permute-start | bytes 540680 | tf_op jit(solution)/shard_map/ppermute | solution.py:811
  31.1 10.5 %collective-permute-start.8 = (bf16[352,256]{1,0:T(8,128)(2,1)S(1)}, bf16[352,256]{1,0:T(8,128)(2,1)S(1)}, u32[]{:S(2)}, u32[]{:S(2)}) collective-permute-start(bf16[352,256]{1,0:T(8,128)(2,1)S(1)} %get-tuple-element.106), channel_id=1, source_target_pairs={{2,4},{6,8},{10,12},{14,16},{18,20},{22,24},{26,28},{4,2},{8,6},{1... | collective-permute-start | bytes 540680 | tf_op jit(solution)/shard_map/ppermute | solution.py:811
  37.3 4.4 %collective-permute-start.9 = (bf16[1,96,256]{2,1,0:T(8,128)(2,1)S(1)}, bf16[1,96,256]{2,1,0:T(8,128)(2,1)S(1)}, u32[]{:S(2)}, u32[]{:S(2)}) collective-permute-start(bf16[1,96,256]{2,1,0:T(8,128)(2,1)S(1)} %get-tuple-element.93), channel_id=1, source_target_pairs={{0,24},{1,25},{2,7},{3,6},{4,28},{5,29},{6,3},{7,2},{8,16},{9,17},... | collective-permute-start | bytes 147464 | tf_op jit(solution)/shard_map/ppermute | solution.py:669
  38.2 3.4 %collective-permute-start.10 = (bf16[1,96,256]{2,1,0:T(8,128)(2,1)S(1)}, bf16[1,96,256]{2,1,0:T(8,128)(2,1)S(1)}, u32[]{:S(2)}, u32[]{:S(2)}) collective-permute-start(bf16[1,96,256]{2,1,0:T(8,128)(2,1)S(1)} %get-tuple-element.94), channel_id=1, source_target_pairs={{0,16},{1,17},{2,3},{3,2},{4,20},{5,21},{6,7},{7,6},{8,24},{9,25},... | collective-permute-start | bytes 147464 | tf_op jit(solution)/shard_map/ppermute | solution.py:669
  38.6 3.1 %collective-permute-start.11 = (bf16[1,96,256]{2,1,0:T(8,128)(2,1)S(1)}, bf16[1,96,256]{2,1,0:T(8,128)(2,1)S(1)}, u32[]{:S(2)}, u32[]{:S(2)}) collective-permute-start(bf16[1,96,256]{2,1,0:T(8,128)(2,1)S(1)} %get-tuple-element.95), channel_id=1, source_target_pairs={{0,8},{1,9},{2,6},{3,7},{4,12},{5,13},{6,2},{7,3},{8,0},{9,1},{10,... | collective-permute-start | bytes 147464 | tf_op jit(solution)/shard_map/ppermute | solution.py:669
  41.7 6.0 %collective-permute-start.14 = (bf16[1,96,256]{2,1,0:T(8,128)(2,1)S(1)}, bf16[1,96,256]{2,1,0:T(8,128)(2,1)S(1)}, u32[]{:S(2)}, u32[]{:S(2)}) collective-permute-start(bf16[1,96,256]{2,1,0:T(8,128)(2,1)S(1)} %shard_map.223.after_ref.refs_0_), channel_id=1, source_target_pairs={{0,24},{1,25},{2,7},{3,6},{4,28},{5,29},{6,3},{7,2},{8,16},{9,17},... | collective-permute-start | bytes 147464 | tf_op jit(solution)/shard_map/ppermute | solution.py:669
  44.0 3.7 %collective-permute-start.13 = (bf16[1,96,256]{2,1,0:T(8,128)(2,1)S(1)}, bf16[1,96,256]{2,1,0:T(8,128)(2,1)S(1)}, u32[]{:S(2)}, u32[]{:S(2)}) collective-permute-start(bf16[1,96,256]{2,1,0:T(8,128)(2,1)S(1)} %shard_map.223.after_ref.refs_0_), channel_id=1, source_target_pairs={{0,16},{1,17},{2,3},{3,2},{4,20},{5,21},{6,7},{7,6},{8,24},{9,25},... | collective-permute-start | bytes 147464 | tf_op jit(solution)/shard_map/ppermute | solution.py:669
  44.3 3.5 %collective-permute-start.12 = (bf16[1,96,256]{2,1,0:T(8,128)(2,1)S(1)}, bf16[1,96,256]{2,1,0:T(8,128)(2,1)S(1)}, u32[]{:S(2)}, u32[]{:S(2)}) collective-permute-start(bf16[1,96,256]{2,1,0:T(8,128)(2,1)S(1)} %shard_map.223.after_ref.refs_0_), channel_id=1, source_target_pairs={{0,8},{1,9},{2,6},{3,7},{4,12},{5,13},{6,2},{7,3},{8,0},{9,1},{10,... | collective-permute-start | bytes 147464 | tf_op jit(solution)/shard_map/ppermute | solution.py:669
  47.8 12.7 %collective-permute-start.17 = (bf16[4,96,256]{2,1,0:T(8,128)(2,1)S(1)}, bf16[4,96,256]{2,1,0:T(8,128)(2,1)S(1)}, u32[]{:S(2)}, u32[]{:S(2)}) collective-permute-start(bf16[4,96,256]{2,1,0:T(8,128)(2,1)S(1)} %shard_map.225.after_ref.refs_0_), channel_id=1, source_target_pairs={{0,5},{1,4},{2,26},{3,27},{4,1},{5,0},{6,30},{7,31},{8,13},{9,12},... | collective-permute-start | bytes 589832 | tf_op jit(solution)/shard_map/ppermute | solution.py:669
  51.7 9.1 %collective-permute-start.16 = (bf16[4,96,256]{2,1,0:T(8,128)(2,1)S(1)}, bf16[4,96,256]{2,1,0:T(8,128)(2,1)S(1)}, u32[]{:S(2)}, u32[]{:S(2)}) collective-permute-start(bf16[4,96,256]{2,1,0:T(8,128)(2,1)S(1)} %shard_map.225.after_ref.refs_0_), channel_id=1, source_target_pairs={{0,1},{1,0},{2,18},{3,19},{4,5},{5,4},{6,22},{7,23},{8,9},{9,8},{1... | collective-permute-start | bytes 589832 | tf_op jit(solution)/shard_map/ppermute | solution.py:669
  51.7 9.3 %collective-permute-start.15 = (bf16[4,96,256]{2,1,0:T(8,128)(2,1)S(1)}, bf16[4,96,256]{2,1,0:T(8,128)(2,1)S(1)}, u32[]{:S(2)}, u32[]{:S(2)}) collective-permute-start(bf16[4,96,256]{2,1,0:T(8,128)(2,1)S(1)} %shard_map.225.after_ref.refs_0_), channel_id=1, source_target_pairs={{0,4},{1,5},{2,10},{3,11},{4,0},{5,1},{6,14},{7,15},{8,12},{9,13},... | collective-permute-start | bytes 589832 | tf_op jit(solution)/shard_map/ppermute | solution.py:669
  52.1 10.0 %collective-permute-start.18 = (bf16[4,96,256]{2,1,0:T(8,128)(2,1)S(1)}, bf16[4,96,256]{2,1,0:T(8,128)(2,1)S(1)}, u32[]{:S(2)}, u32[]{:S(2)}) collective-permute-start(bf16[4,96,256]{2,1,0:T(8,128)(2,1)S(1)} %shard_map.225.after_ref.refs_0_), channel_id=1, source_target_pairs={{0,2},{1,3},{2,0},{3,1},{4,6},{5,7},{6,4},{7,5},{8,10},{9,11},{10,... | collective-permute-start | bytes 589832 | tf_op jit(solution)/shard_map/ppermute | solution.py:669
  60.5 1.6 %collective-permute-start.21 = (bf16[4,96,256]{2,1,0:T(8,128)(2,1)S(1)}, bf16[4,96,256]{2,1,0:T(8,128)(2,1)S(1)}, u32[]{:S(2)}, u32[]{:S(2)}) collective-permute-start(bf16[4,96,256]{2,1,0:T(8,128)(2,1)S(1)} %shard_map.229.refs_3_), channel_id=1, source_target_pairs={{0,2},{1,3},{2,0},{3,1},{4,6},{5,7},{6,4},{7,5},{8,10},{9,11},{10,... | collective-permute-start | bytes 589832 | tf_op jit(solution)/shard_map/ppermute | solution.py:669
  60.8 1.4 %collective-permute-start.20 = (bf16[4,96,256]{2,1,0:T(8,128)(2,1)S(1)}, bf16[4,96,256]{2,1,0:T(8,128)(2,1)S(1)}, u32[]{:S(2)}, u32[]{:S(2)}) collective-permute-start(bf16[4,96,256]{2,1,0:T(8,128)(2,1)S(1)} %shard_map.228.refs_2_), channel_id=1, source_target_pairs={{0,2},{1,3},{2,0},{3,1},{4,6},{5,7},{6,4},{7,5},{8,10},{9,11},{10,... | collective-permute-start | bytes 589832 | tf_op jit(solution)/shard_map/ppermute | solution.py:669
  61.0 2.1 %collective-permute-start.19 = (bf16[4,96,256]{2,1,0:T(8,128)(2,1)S(1)}, bf16[4,96,256]{2,1,0:T(8,128)(2,1)S(1)}, u32[]{:S(2)}, u32[]{:S(2)}) collective-permute-start(bf16[4,96,256]{2,1,0:T(8,128)(2,1)S(1)} %shard_map.227.refs_1_), channel_id=1, source_target_pairs={{0,2},{1,3},{2,0},{3,1},{4,6},{5,7},{6,4},{7,5},{8,10},{9,11},{10,... | collective-permute-start | bytes 589832 | tf_op jit(solution)/shard_map/ppermute | solution.py:669

commit v5 on v4

--- a/solution.py
+++ b/solution.py
@@ -145,61 +145,65 @@
             step()
 
 
-def edge_kernel(latent_ref, crop_hbm, mate_ref, other_ref, masks_ref, crop_ref, sems):
-    canvases, rows, across = crop_ref.shape
-    count = canvases * across
-    odd = lax.axis_index("strip") % 2
-    edge = (rows - 1) * (1 - odd)
-    codes = pltpu.make_async_copy(crop_hbm, crop_ref, sems.at[0])
-    near = pltpu.make_async_copy(latent_ref.at[:, edge], mate_ref, sems.at[1])
-    far = pltpu.make_async_copy(latent_ref.at[:, rows - 1 - edge], other_ref, sems.at[2])
-    codes.start()
-    near.start()
-    far.start()
-    codes.wait()
-    columns = code_columns(crop_ref)
-    for row in range(rows):
-        here = row_codes(columns, row, canvases, rows, 128)
-        for start, _ in chunks(count):
-            some = here[start : start + tile_rows]
-            span = pl.ds(row * count + start, tile_rows)
-            for plane, bit in enumerate(bits):
-                masks_ref[plane, span] = jnp.where((some & 2**bit) != 0, 1.0, 0.0).astype(low)
-    near.wait()
-    far.wait()
-
-
-def code_kernel(
+def edge_kernel(
+    latent_hbm,
+    crop_hbm,
     index_hbm,
     codebook_hbm,
     decode_weight_hbm,
+    mate_ref,
+    other_ref,
+    crop_ref,
+    index_ref,
+    codebook_ref,
+    decode_weight_ref,
+    sems,
+):
+    rows = crop_ref.shape[1]
+    odd = lax.axis_index("strip") % 2
+    edge = (rows - 1) * (1 - odd)
+    pairs = [
+        (latent_hbm.at[:, rows - 1 - edge], other_ref),
+        (latent_hbm.at[:, edge], mate_ref),
+        (crop_hbm, crop_ref),
+        (index_hbm, index_ref),
+        (codebook_hbm, codebook_ref),
+        (decode_weight_hbm, decode_weight_ref),
+    ]
+    copies = [
+        pltpu.make_async_copy(source, target, sems.at[place])
+        for place, (source, target) in enumerate(pairs)
+    ]
+    for copy in copies:
+        copy.start()
+    for copy in copies:
+        copy.wait()
+
+
+def code_kernel(
+    crop_ref,
+    index_ref,
+    codebook_ref,
+    decode_weight_ref,
     out_grad_hbm,
     latent_hbm,
     conv_weight_hbm,
     mix_weight_hbm,
     term_ref,
     picks_ref,
-    weight_grad_ref,
+    masks_ref,
     bias_grad_ref,
+    out_grad_ref,
     latent_ref,
     conv_weight_ref,
     mix_weight_ref,
-    index_ref,
-    codebook_ref,
-    decode_weight_ref,
-    out_grad_ref,
     sems,
 ):
     canvases, rows, across = index_ref.shape
     size, entries = codebook_ref.shape
     channels = decode_weight_ref.shape[1]
     count = canvases * across
-    pairs = [
-        (index_hbm, index_ref),
-        (codebook_hbm, codebook_ref),
-        (decode_weight_hbm, decode_weight_ref),
-    ]
-    pairs += [(out_grad_hbm.at[:, row], out_grad_ref.at[row]) for row in range(rows)]
+    pairs = [(out_grad_hbm.at[:, row], out_grad_ref.at[row]) for row in range(rows)]
     pairs += [
         (conv_weight_hbm, conv_weight_ref),
         (latent_hbm, latent_ref),
@@ -211,36 +215,59 @@
     ]
     for copy in copies:
         copy.start()
-    for copy in copies[:3]:
-        copy.wait()
     codebook = codebook_ref[...]
     both = jnp.concatenate([codebook * low(-0.5), codebook * low(2.0)], axis=0)
     weight = decode_weight_ref[...]
-    weight_top = jnp.concatenate([weight, jnp.zeros_like(weight)], axis=0)
-    columns = code_columns(index_ref)
+    weight = jnp.concatenate([weight, jnp.zeros_like(weight)], axis=0)
+    table = jnp.concatenate([both, weight], axis=1).T
     lanes = lax.broadcasted_iota(jnp.int32, (tile_rows, 128), 1)
-    for row in range(rows):
-        codes = row_codes(columns, row, canvases, rows, 128)
+    index_columns, crop_columns = code_columns(index_ref), code_columns(crop_ref)
+    terms = [None] * rows
+
+    def make_picks(row):
+        codes = row_codes(index_columns, row, canvases, rows, 128)
         for start, _ in chunks(count):
             near = codes[start : start + tile_rows]
             for at in range(0, entries, 128):
                 chosen = lanes + at == near
                 part = jnp.where(chosen, 1.0, 0.0).astype(low)
                 picks_ref[pl.ds(row * count + start, tile_rows), at : at + 128] = part
-    term = mm_nt(picks_ref[...], both)
-    for copy in copies[3 : 3 + rows]:
+
+    def make_masks(row):
+        codes = row_codes(crop_columns, row, canvases, rows, 128)
+        for start, _ in chunks(count):
+            near = codes[start : start + tile_rows]
+            span = pl.ds(row * count + start, tile_rows)
+            for plane, bit in enumerate(bits):
+                masks_ref[plane, span] = jnp.where((near & 2**bit) != 0, 1.0, 0.0).astype(low)
+
+    def look_up(row):
+        picks = picks_ref[pl.ds(row * count, count)]
+        terms[row] = mm(jnp.concatenate([picks, grads(row)], axis=1), table)
+
+    def grads(row):
+        return out_grad_ref[row].reshape(count, channels)
+
+    bias_sum = []
+    make_picks(0)
+    make_masks(0)
+    if rows > 1:
+        make_picks(1)
+    for copy in copies[:rows]:
         copy.wait()
-    grad = out_grad_ref[...].reshape(rows * count, channels)
-    term = term + mm_nt(grad, weight_top)
-    term_ref[...] = term.reshape(term_ref.shape)
-    weight_grad_ref[...] = 0.5 * mm_tn(term.astype(low), grad)[size:]
-    bias_sum = None
-    for start, _ in chunks(rows * count):
-        part = grad[start : start + tile_rows].astype(wide)
-        part = part[:8] + part[8:]
-        bias_sum = part if bias_sum is None else bias_sum + part
-    bias_grad_ref[...] = jnp.sum(bias_sum, axis=0, keepdims=True)
-    for copy in copies[3 + rows :]:
+    for row in range(rows):
+        look_up(row)
+        if row + 2 < rows:
+            make_picks(row + 2)
+        if row + 1 < rows:
+            make_masks(row + 1)
+        for start, _ in chunks(count):
+            part = grads(row)[start : start + tile_rows].astype(wide)
+            part = part[:8] + part[8:]
+            bias_sum = [bias_sum[0] + part] if bias_sum else [part]
+        term_ref[row] = terms[row]
+    bias_grad_ref[...] = jnp.sum(bias_sum[0], axis=0, keepdims=True)
+    for copy in copies[rows:]:
         copy.wait()
     for row_step in range(3):
         for start, span in chunks(3 * channels):
@@ -271,6 +298,9 @@
         if unit == self.other:
             return jnp.where(self.odd, self.rows - 1, 0)
         return unit
+
+    def toward(self, unit):
+        return jnp.where(self.odd, *((0, 2) if unit == self.mate else (2, 0)))
 
     def halo(self, unit):
         first, last = 0, self.rows + 1
@@ -298,16 +328,17 @@
     proj_weight_ref,
     proj_bias_ref,
     halo_ref,
+    also_ref,
     *refs,
 ):
-    outs = refs[-10:]
+    first = beyond == Places.mate
+    outs = refs[-12:] if first else refs[-10:]
     slab_ref, grad_ref, up_ref, down_ref, second_ref, stream_ref, codes_ref = outs[:7]
-    branch_grad_ref, sums_ref, edge_ref = outs[7:]
+    branch_grad_ref, sums_ref, edge_ref = outs[7:10]
     canvases, rows, across, channels = latent_ref.shape
     size = proj_weight_ref.shape[0]
     count = canvases * across
     places = Places(rows, count)
-    first = beyond == places.mate
     units = [*places.inner, places.mate] if first else [places.other]
 
     def own(row, canvas):
@@ -351,7 +382,7 @@
             )
         return slabs[row, canvas]
 
-    group = canvases
+    group = canvases if first else 1
 
     def tile(unit, canvas):
         inside = canvas * across
@@ -360,7 +391,10 @@
         above, below = [
             places.masks(masks_ref, plane, unit, canvas, across) for plane in (up_plane, down_plane)
         ]
-        conv, slope, made = [], [], [None] * 4
+        if unit == places.other:
+            plane = jnp.where(places.odd, down_plane, up_plane)
+            halo_masks = places.masks(masks_ref, plane, unit, canvas, across)
+        conv, slope, made = [None] * 3, [], [None] * 4
         steps = chunks(group * across)
 
         def span(start):
@@ -375,17 +409,25 @@
         def convolve(row_step):
             def run():
                 rows_of = places.span(there + row_step, inside, group * across)
-                conv.append(mm(slab_ref[rows_of], conv_weight_ref[row_step]))
+                conv[row_step] = mm(slab_ref[rows_of], conv_weight_ref[row_step])
 
             return run
+
+        def convolve_halo():
+            rows_of = places.span(places.halo(unit), inside, group * across)
+            conv[0] = mm(slab_ref[rows_of], conv_weight_ref[places.toward(unit)])
 
         def activate():
             up, mid, down = conv
             for start, _ in steps:
                 some = slice(start, start + tile_rows)
-                total = masked(up[some], above(start).astype(wide))
-                total = total + masked(down[some], below(start).astype(wide))
-                second, twice = silu_slopes((total + mid[some]) + conv_bias)
+                if unit == places.other:
+                    total = masked(up[some], halo_masks(start).astype(wide))
+                    total = total + also_ref[pl.ds(inside + start, tile_rows)]
+                else:
+                    total = masked(up[some], above(start).astype(wide))
+                    total = total + masked(down[some], below(start).astype(wide)) + mid[some]
+                second, twice = silu_slopes(total + conv_bias)
                 second_ref[span(start)] = second.astype(low)
                 slope.append(twice)
 
@@ -427,7 +469,10 @@
         else:
             needs = [unit - 1, unit, unit + 1]
         needs = [slab_of(near, canvas + k) for near in needs for k in range(group)]
-        last = [tape.add("mxu", 0.063 * group, needs, convolve(row_step)) for row_step in range(3)]
+        if unit == places.other:
+            last = [tape.add("mxu", 0.063 * group, needs, convolve_halo)]
+        else:
+            last = [tape.add("mxu", 0.063 * group, needs, convolve(row_step)) for row_step in range(3)]
         last = tape.add("vpu", 0.1 * group, last, activate)
         chain = [
             (0.021, lambda: mm(second_ref[here], mix_weight_ref[...]), 0.04, add_latent),
@@ -444,10 +489,60 @@
             last = tape.add("mxu", cost * group, [last], multiply(place, product))
             last = tape.add("vpu", later * group, [last], rest)
 
+    def weigh():
+        box = [None]
+
+        def product(row):
+            def run():
+                part = mm_tn(term_ref[row].astype(low), also_ref[row].reshape(count, channels))
+                box[0] = part if box[0] is None else box[0] + part
+
+            return run
+
+        def store():
+            refs[-2][...] = 0.5 * box[0][size:]
+
+        made = [tape.add("mxu", 0.12, [], product(row)) for row in range(rows)]
+        tape.add("vpu", 0.02, made, store)
+
+    def convolve_last(canvas, some):
+        there = places.row(places.other)
+        inward = jnp.where(places.odd, -1, 1)
+        plane = jnp.where(places.odd, up_plane, down_plane)
+        masks = places.masks(masks_ref, plane, places.other, canvas, across)
+        inside = canvas * across
+        made = [None, None]
+
+        def product(place, row, tap):
+            def run():
+                rows_of = places.span(row + 1, inside, some * across)
+                made[place] = mm(slab_ref[rows_of], conv_weight_ref[tap])
+
+            return run
+
+        def store():
+            for start, _ in chunks(some * across):
+                near = slice(start, start + tile_rows)
+                part = made[0][near] + masked(made[1][near], masks(start).astype(wide))
+                refs[-1][pl.ds(inside + start, tile_rows)] = part
+
+        needs = [slab_of(row, canvas + k) for row in range(rows) for k in range(some)]
+        steps = [(there, 1), (there + inward, inward + 1)]
+        needs = [
+            tape.add("mxu", 0.063 * some, needs, product(place, *step))
+            for place, step in enumerate(steps)
+        ]
+        tape.add("vpu", 0.04 * some, needs, store)
+
+    if first:
+        weigh()
     for unit in units:
         for canvas in range(0, canvases, group):
             tile(unit, canvas)
-
+    if first:
+        some = 2 if canvases % 2 == 0 else 1
+        for canvas in range(0, canvases, some):
+            convolve_last(canvas, some)
     tape.play()
     sums = [jnp.sum(values, axis=0, keepdims=True) for values in sums]
     sums[2] = jnp.concatenate([sums[2]] * (channels // sums[2].shape[1]), axis=1)
@@ -725,41 +820,58 @@
     )(*arrays, *after)
 
 
-def final_kernel(plan, count, sizes, *refs):
-    ins, outs, gathered_ref = refs[:count], refs[count:-1], refs[-1]
+def final_kernel(plan, mine, count, sizes, *refs):
+    ins, outs, scratch = refs[:count], refs[-15:-6], refs[-6:]
+    gathered_ref, *line_refs, sems = scratch
     channels, size, entries = sizes
     core = lax.axis_index("strip") % 2
+    half = core if mine else 1 - core
+    place = plan.place(half)
     at = 0
     for ref in ins:
-        half = core if at < plan.half else 1 - core
-        place = plan.place(half)
         for piece in range(ref.shape[0]):
-            shard = half * plan.half + (place ^ at % plan.half)
-            start = pl.multiple_of(shard * plan.piece_rows, plan.piece_rows)
-            gathered_ref[pl.ds(start, plan.piece_rows)] = ref[piece]
+            start = pl.multiple_of((place ^ at) * plan.piece_rows, plan.piece_rows)
+            gathered_ref[pl.ds(start, plan.piece_rows)] = ref[piece].astype(wide)
             at += 1
     conv_ref, conv_bias_ref, mix_ref, mix_bias_ref, proj_ref, proj_bias_ref = outs[:6]
     codebook_ref, decode_ref, decode_bias_ref = outs[6:]
     triple = 3 * channels
-    conv_ref[pl.ds(0, 2 * triple)] = gathered_ref[pl.ds(0, 2 * triple)].astype(wide)
-    at = plan.half_rows
-    conv_ref[pl.ds(2 * triple, triple)] = gathered_ref[pl.ds(at, triple)].astype(wide)
-    at += triple
-    mix_ref[...] = gathered_ref[pl.ds(at, channels)].astype(wide)
-    at += channels
-    proj_ref[...] = gathered_ref[pl.ds(at, size)].astype(wide)
-    at += size
-    for piece in range(entries // channels):
-        part = gathered_ref[pl.ds(at, size)].astype(wide)
-        codebook_ref[:, piece * channels : (piece + 1) * channels] = part
-        at += size
-    decode_ref[...] = gathered_ref[pl.ds(at, size)].astype(wide)
-    at += size
-    biases = gathered_ref[pl.ds(at, tile_rows)].astype(wide)
-    conv_bias_ref[...] = biases[0:1]
-    mix_bias_ref[...] = biases[1:2]
-    decode_bias_ref[...] = biases[2:3]
-    proj_bias_ref[...] = biases[3:4, :size]
+
+    def copy_all(pairs):
+        copies = [
+            pltpu.make_async_copy(source, target, sems.at[number])
+            for number, (source, target) in enumerate(pairs)
+        ]
+        for copy in copies:
+            copy.start()
+        for copy in copies:
+            copy.wait()
+
+    @pl.when(half == 0)
+    def _():
+        spans = [pl.ds(at, channels) for at in range(0, 2 * triple, channels)]
+        copy_all([(gathered_ref.at[span], conv_ref.at[span]) for span in spans])
+
+    @pl.when(half == 1)
+    def _():
+        pairs = []
+        for at in range(0, triple, channels):
+            span = pl.ds(2 * triple + at, channels)
+            pairs.append((gathered_ref.at[pl.ds(at, channels)], conv_ref.at[span]))
+        at = triple
+        targets = [(mix_ref, channels), (proj_ref, size)]
+        for piece in range(0, entries, channels):
+            targets.append((codebook_ref.at[:, pl.ds(piece, channels)], size))
+        targets.append((decode_ref, size))
+        for target, depth in targets:
+            pairs.append((gathered_ref.at[pl.ds(at, depth)], target))
+            at += depth
+        lines = gathered_ref[pl.ds(at, tile_rows)]
+        targets = (conv_bias_ref, mix_bias_ref, decode_bias_ref, proj_bias_ref)
+        for number, (line_ref, target) in enumerate(zip(line_refs, targets, strict=True)):
+            line_ref[...] = lines[number : number + 1, : target.shape[1]]
+            pairs.append((line_ref, target))
+        copy_all(pairs)
 
 
 def per_device(
@@ -812,47 +924,44 @@
         return (lax.ppermute(mate, "strip", near), *others)
 
     edge_shape = struct((canvases, across, channels), low)
-    *edges, masks = call(
+    starts = [
+        struct(crop_code.shape, crop_code.dtype),
+        struct(code_index.shape, code_index.dtype),
+        struct((size, entries), low),
+        struct((size, channels), low),
+    ]
+    *edges, crop, index, near_codebook, near_decode = call(
         edge_kernel,
-        [in_hbm] * 2,
-        [in_vmem] * 3,
-        [edge_shape, edge_shape, struct((len(bits), total, 128), low)],
-        [pltpu.VMEM(crop_code.shape, crop_code.dtype), pltpu.SemaphoreType.DMA((3,))],
-    )(*far_away(latent_in, crop_code))
+        [in_hbm] * 5,
+        [in_vmem] * 6,
+        [edge_shape, edge_shape, *starts],
+        [pltpu.SemaphoreType.DMA((6,))],
+    )(*far_away(latent_in, crop_code, code_index, codebook.T, decode_weight))
     mate, other = trade(*edges, split=False)
     outs = [
         struct((rows, count, 2 * size), wide),
         struct((total, entries), low),
-        struct((size, channels), wide),
+        struct((len(bits), total, 128), low),
         struct((1, channels), wide),
+        struct((rows, canvases, across, channels), low),
         struct(latent_in.shape, low),
         struct(flat_weight.shape, low),
         struct(mix_weight.shape, low),
     ]
-    held = [
-        pltpu.VMEM(code_index.shape, code_index.dtype),
-        pltpu.VMEM((size, entries), low),
-        pltpu.VMEM((size, channels), low),
-        pltpu.VMEM((rows, canvases, across, channels), low),
-        pltpu.SemaphoreType.DMA((rows + 6,)),
-    ]
-    term, picks, decode_weight_grad, decode_bias_grad, latent, near_weight, near_mix = call(
+    held = [pltpu.SemaphoreType.DMA((rows + 3,))]
+    term, picks, masks, decode_bias_grad, near_grad, latent, near_weight, near_mix = call(
         code_kernel,
-        [in_hbm] * 7,
-        [in_vmem] * 7,
+        [in_vmem] * 4 + [in_hbm] * 4,
+        [in_vmem] * 8,
         outs,
         held,
         flops=6 * total * channels * channels,
     )(
-        *far_away(
-            code_index,
-            codebook.T,
-            decode_weight,
-            out_grad,
-            latent_in,
-            flat_weight,
-            mix_weight,
-        )
+        crop,
+        index,
+        near_codebook,
+        near_decode,
+        *far_away(out_grad, latent_in, flat_weight, mix_weight),
     )
     slab_shape = struct((total + 2 * count, 3 * channels), low)
     flat = struct((total, channels), low)
@@ -862,21 +971,21 @@
     inner, outer = tuple(range(1, rows - 1)), tuple(sorted({0, rows - 1}))
     shared = [masks, latent, term, near_weight, conv_bias, near_mix, mix_bias, proj_weight.T, proj_bias]
 
-    def block_rows(beyond, halo, before):
-        ins = [*shared, halo, *before]
+    def block_rows(beyond, halo, also, before, more):
+        ins = [*shared, halo, also, *before]
         first = len(ins) - len(before)
-        outs = call(
+        return call(
             functools.partial(rows_kernel, beyond),
             [in_vmem] * len(ins),
-            [in_vmem] * (len(kept) + 1),
-            [*kept, edge_shape],
+            [in_vmem] * (len(kept) + 1 + len(more)),
+            [*kept, edge_shape, *more],
             flops=20 * total * channels * channels,
             aliases={first + i: i for i in range(len(before))},
         )(*ins)
-        return outs[:-1], outs[-1]
-
-    before, edge_mate = block_rows("mate", mate, ())
-    before, edge_other = block_rows("other", other, before)
+
+    more = [struct((size, channels), wide), struct((count, channels), wide)]
+    *before, edge_mate, decode_weight_grad, partial = block_rows("mate", mate, near_grad, (), more)
+    *before, edge_other = block_rows("other", other, partial, before, ())
     slab, grad, up, down, second, stream, codes, branch_grad, sums = before
     edges = (edge_mate, edge_other)
 
@@ -926,7 +1035,7 @@
                 [pl.BlockSpec()],
                 [pltpu.HBM(out_grad.shape, low)],
                 flops=4 * total * channels * channels,
-            )(term, decode_weight, decode_bias, parts[0])[0]
+            )(term, near_decode, decode_bias, parts[0])[0]
             after = [*far_away(decoded), *halo]
     halo = (halo[0], jnp.concatenate(halo[1:], axis=0))
     pieces = add_split(arrays, 1, after)
@@ -939,25 +1048,37 @@
     latent_grad = input_rows(outer, halo, gathered, latent_grad)
     done = far_away(latent_grad)
     pieces = [pieces[0], *[gate(piece, *done) for piece in pieces[1:]]]
-    arrays = [*pieces, *[plan.swap(piece, plan.core, 1) for piece in pieces]]
-
-    results = call(
-        functools.partial(final_kernel, plan, len(arrays), (channels, size, entries)),
-        [in_vmem] * len(arrays),
-        [pl.BlockSpec()] * 9,
-        [
-            struct((9 * channels, channels), wide),
-            struct((1, channels), wide),
-            struct((channels, channels), wide),
-            struct((1, channels), wide),
-            struct((size, channels), wide),
-            struct((1, size), wide),
-            struct((size, entries), wide),
-            struct((size, channels), wide),
-            struct((1, channels), wide),
-        ],
-        [pltpu.VMEM((2 * plan.half_rows, channels), low)],
-    )(*arrays)
+    swapped = [plan.swap(piece, plan.core, 1) for piece in pieces]
+    shapes = [
+        (9 * channels, channels),
+        (1, channels),
+        (channels, channels),
+        (1, channels),
+        (size, channels),
+        (1, size),
+        (size, entries),
+        (size, channels),
+        (1, channels),
+    ]
+
+    def finish(mine, arrays, *before):
+        count = len(arrays)
+        return call(
+            functools.partial(final_kernel, plan, mine, count, (channels, size, entries)),
+            [in_vmem] * count + [in_hbm] * len(before),
+            [in_hbm] * len(shapes),
+            [pltpu.HBM(shape, wide) for shape in shapes],
+            [
+                pltpu.VMEM((plan.half_rows, channels), wide),
+                *[pltpu.VMEM((1, channels), wide)] * 3,
+                pltpu.VMEM((1, size), wide),
+                pltpu.SemaphoreType.DMA((16,)),
+            ],
+            aliases={count + i: i for i in range(len(before))},
+        )(*arrays, *before)
+
+    results = finish(True, pieces)
+    results = finish(False, swapped, *results)
     return (
         decoded,
         latent_grad,

time: 65.6 us -> 64.2 us (0.979)
  waiting for transfers between devices: 4.42 us -> 3.33 us
    ppermute x17, waiting for transfers between devices: 4.41 us -> 3.32 us  [swap(): return lax.ppermute(values, ('strip', 'canvas'), pairs)]
    pallas_call x3 -> x4, Pallas kernels: 7.27 us -> 7.06 us  [the longest x1 3.11 us: per_device(): call(code_kernel, [in_vmem] * 4 + [in_hbm] * 4, [in_vmem] * 8, outs, held...]
  transfers between devices with their start and end apart: 22 -> 22, of which waited for: 5 -> 3; matrix products, arithmetic and copies ran while one was open for 0% -> 0% of each run, Pallas kernels for 30% -> 33%
where the time goes in v5:
time: 64.2 us; the launch traced here: 64 us
  starting transfers between devices  31.2 us (49%)
  Pallas kernels  28.2 us (44%)
  waiting for transfers between devices  3.33 us (5%)
  between operations  1.18 us (2%)
    ppermute x17, starting transfers between devices, swap(): return lax.ppermute(values, ('strip', 'canvas'), pairs)  20.1 us
    pallas_call x2, Pallas kernels, block_rows(): call(functools.partial(rows_kernel, beyond), [in_vmem] * len(ins), [in_vm...  7.49 us
    pallas_call x2, Pallas kernels, input_rows(): call(functools.partial(input_kernel, mine), [in_vmem] * 7 + [anywhere] +...  6.68 us
    ppermute x2, starting transfers between devices, trade(): lax.ppermute(part, 'strip', far)  6.37 us
    pallas_call x2, Pallas kernels, weight_half(): call(functools.partial(weight_kernel, plan, mine), [in_vmem] * len(ins) +...  5.03 us
    ppermute x1, starting transfers between devices, trade(): lax.ppermute(other, 'strip', far)  4.49 us
    ppermute x17, waiting for transfers between devices, swap(): return lax.ppermute(values, ('strip', 'canvas'), pairs)  3.32 us
    pallas_call x1, Pallas kernels, per_device(): call(code_kernel, [in_vmem] * 4 + [in_hbm] * 4, [in_vmem] * 8, outs, held...  3.11 us
  transfers between devices with their start and end apart: 22, of which 3 were waited for; matrix products, arithmetic and copies ran while one was open for 0% of the time, Pallas kernels for 33%

profile of v5, /device:TPU:1, one launch (start us, length us, event | category | flops | bytes accessed | tf_op | source)
XLA Modules:
  0.0 64.0 jit_solution(13327316929291066720)
XLA Ops:
  0.6 1.2 %shard_map.212 = (bf16[4,176,256]{2,1,0:T(8,128)(2,1)S(1)}, bf16[4,176,256]{2,1,0:T(8,128)(2,1)S(1)}, s32[4,4,176]{2,1,0:T(4,128)S(1)}, s32[4,4,176]{2,1,0:T(4,1...) custom-call(bf16[4,4,176,256]{3,2,1,0:T(8,128)(2,1)} %latent_hbm.3, s32[4,4,176]{2,1,0:T(4,128)} %crop_hbm.1, ...), custom_call_target="tpu_custom_call" | custom-call | tf_op jit(solution)/shard_map/pallas_call | solution.py:933
  1.8 0.1 collective-permute-start.1
  1.9 4.5 %collective-permute-start = (bf16[4,176,256]{2,1,0:T(8,128)(2,1)S(1)}, bf16[4,176,256]{2,1,0:T(8,128)(2,1)S(1)}, u32[]{:S(2)}, u32[]{:S(2)}) collective-permute-start(bf16[4,176,256]{2,1,0:T(8,128)(2,1)S(1)} %get-tuple-element.82), channel_id=1, source_target_pairs={{2,4},{6,8},{10,12},{14,16},{18,20},{22,24},{26,28},{4,2},{8,6},{1... | collective-permute-start | bytes 1081352 | tf_op jit(solution)/shard_map/ppermute | solution.py:921
  6.4 0.0 copy-start
  6.5 0.0 copy-start.1
  6.5 0.0 copy-start.2
  6.5 0.0 copy-start.3
  6.5 3.1 %shard_map.213 = (f32[4,704,128]{2,1,0:T(8,128)S(1)}, bf16[2816,512]{1,0:T(8,128)(2,1)S(1)}, bf16[4,2816,128]{2,1,0:T(8,128)(2,1)S(1)}, f32[1,256]{1,0:T(1,128)S...) custom-call(s32[4,4,176]{2,1,0:T(4,128)S(1)} %get-tuple-element.73.c, ...), custom_call_target="tpu_custom_call" | custom-call | flops 1107296256 | tf_op jit(solution)/shard_map/pallas_call | solution.py:952
  9.6 0.0 collective-permute-done.1.halo_ref
  9.7 5.9 %shard_map.214 = (bf16[4224,768]{1,0:T(8,128)(2,1)S(1)}, bf16[2816,256]{1,0:T(8,128)(2,1)S(1)}, bf16[2816,256]{1,0:T(8,128)(2,1)S(1)}, bf16[2816,256]{1,0:T(8,12...) custom-call(bf16[4,2816,128]{2,1,0:T(8,128)(2,1)S(1)} %get-tuple-ele, ...), custom_call_target="tpu_custom_call" | custom-call | flops 3690987520 | tf_op jit(solution)/shard_map/pallas_call | solution.py:977
  15.6 0.0 collective-permute-done.halo_ref
  15.6 1.6 %shard_map.215 = (bf16[4224,768]{1,0:T(8,128)(2,1)S(1)}, bf16[2816,256]{1,0:T(8,128)(2,1)S(1)}, bf16[2816,256]{1,0:T(8,128)(2,1)S(1)}, bf16[2816,256]{1,0:T(8,12...) custom-call(bf16[4,2816,128]{2,1,0:T(8,128)(2,1)S(1)} %get-tuple-ele, ...), custom_call_target="tpu_custom_call", output_to_operand_aliasing={{0}: (11, {}), {1}: (12, {}), {2}: (13, {}), {3}: (14, {}),... | custom-call | flops 3690987520 | tf_op jit(solution)/shard_map/pallas_call | solution.py:977
  17.2 2.7 %shard_map.216.after_ref = bf16[16,96,256]{2,1,0:T(8,128)(2,1)S(1)} custom-call(bf16[4224,768]{1,0:T(8,128)(2,1)S(1)} %get-tuple-element.95.slab_ref, bf16[2816,256]{1,0:T(8,128)(2,1)S(1)} %get-tuple-element.96.grad_ref, bf16[2816,256]{1,0:T(8,128)(2,1)S(1)} %get-tuple-element.97.up_ref, bf16[2816,256]{1,0:T(8,128)(2,1)S(1)} %get-tuple-element.98.down_ref, ...), custom_call_target="tpu_custom_call" | custom-call | flops 1845493760 | tf_op jit(solution)/shard_map/pallas_call | solution.py:995
  19.9 0.1 collective-permute-start.2
  20.0 2.4 %shard_map.217.refs_0_ = bf16[16,96,256]{2,1,0:T(8,128)(2,1)S(1)} custom-call(bf16[4224,768]{1,0:T(8,128)(2,1)S(1)} %get-tuple-element.95.slab_ref, bf16[2816,256]{1,0:T(8,128)(2,1)S(1)} %get-tuple-element.96.grad_ref, bf16[2816,256]{1,0:T(8,128)(2,1)S(1)} %get-tuple-element.97.up_ref, bf16[2816,256]{1,0:T(8,128)(2,1)S(1)} %get-tuple-element.98.down_ref, ...), custom_call_target="tpu_custom_call" | custom-call | flops 1845493760 | tf_op jit(solution)/shard_map/pallas_call | solution.py:995
  22.4 0.2 shard_map.218
  22.6 0.0 copy-start.4
  22.6 3.8 %collective-permute-start.3 = (bf16[4,96,256]{2,1,0:T(8,128)(2,1)S(1)}, bf16[4,96,256]{2,1,0:T(8,128)(2,1)S(1)}, u32[]{:S(2)}, u32[]{:S(2)}) collective-permute-start(bf16[4,96,256]{2,1,0:T(8,128)(2,1)S(1)} %get-tuple-element.109), channel_id=1, source_target_pairs={{0,5},{1,4},{2,26},{3,27},{4,1},{5,0},{6,30},{7,31},{8,13},{9,12},... | collective-permute-start | bytes 589832 | tf_op jit(solution)/shard_map/ppermute | solution.py:764
  26.4 0.4 collective-permute-start.5
  26.8 0.0 collective-permute-start.6
  26.8 3.3 %collective-permute-start.7 = (bf16[352,256]{1,0:T(8,128)(2,1)S(1)}, bf16[352,256]{1,0:T(8,128)(2,1)S(1)}, u32[]{:S(2)}, u32[]{:S(2)}) collective-permute-start(bf16[352,256]{1,0:T(8,128)(2,1)S(1)} %get-tuple-element.135), channel_id=1, source_target_pairs={{2,4},{6,8},{10,12},{14,16},{18,20},{22,24},{26,28},{4,2},{8,6},{1... | collective-permute-start | bytes 540680 | tf_op jit(solution)/shard_map/ppermute | solution.py:923
  30.1 0.0 collective-permute-done.3.refs_1_
  30.1 3.1 %collective-permute-start.8 = (bf16[352,256]{1,0:T(8,128)(2,1)S(1)}, bf16[352,256]{1,0:T(8,128)(2,1)S(1)}, u32[]{:S(2)}, u32[]{:S(2)}) collective-permute-start(bf16[352,256]{1,0:T(8,128)(2,1)S(1)} %get-tuple-element.136), channel_id=1, source_target_pairs={{2,4},{6,8},{10,12},{14,16},{18,20},{22,24},{26,28},{4,2},{8,6},{1... | collective-permute-start | bytes 540680 | tf_op jit(solution)/shard_map/ppermute | solution.py:923
  33.2 2.9 %collective-permute-done.4.refs_2_ = bf16[4,96,256]{2,1,0:T(8,128)(2,1)S(1)} collective-permute-done((bf16[4,96,256]{2,1,0:T(8,128)(2,1)S(1)}, bf16[4,96,256]{2,1,0:T(8,128)(2,1)S(1)}, u32[]{:S(2)}, u32[]{:S(2)}) %collective-permute-start.4) | collective-permute-done | bytes 196640 | tf_op jit(solution)/shard_map/ppermute | solution.py:764
  36.1 0.0 collective-permute-done.5.refs_3_
  36.1 0.1 shard_map.219
  36.2 0.9 %collective-permute-start.9 = (bf16[1,96,256]{2,1,0:T(8,128)(2,1)S(1)}, bf16[1,96,256]{2,1,0:T(8,128)(2,1)S(1)}, u32[]{:S(2)}, u32[]{:S(2)}) collective-permute-start(bf16[1,96,256]{2,1,0:T(8,128)(2,1)S(1)} %get-tuple-element.114), channel_id=1, source_target_pairs={{0,24},{1,25},{2,7},{3,6},{4,28},{5,29},{6,3},{7,2},{8,16},{9,17},... | collective-permute-start | bytes 147464 | tf_op jit(solution)/shard_map/ppermute | solution.py:764
  37.1 0.4 collective-permute-start.10
  37.6 0.0 collective-permute-done.7.refs_6_
  37.6 1.4 %collective-permute-start.11 = (bf16[1,96,256]{2,1,0:T(8,128)(2,1)S(1)}, bf16[1,96,256]{2,1,0:T(8,128)(2,1)S(1)}, u32[]{:S(2)}, u32[]{:S(2)}) collective-permute-start(bf16[1,96,256]{2,1,0:T(8,128)(2,1)S(1)} %get-tuple-element.116), channel_id=1, source_target_pairs={{0,8},{1,9},{2,6},{3,7},{4,12},{5,13},{6,2},{7,3},{8,0},{9,1},{10,... | collective-permute-start | bytes 147464 | tf_op jit(solution)/shard_map/ppermute | solution.py:764
  38.9 1.6 %shard_map.220.refs_4_ = bf16[4,4,176,256]{3,2,1,0:T(8,128)(2,1)} custom-call(f32[4,704,128]{2,1,0:T(8,128)S(1)} %get-tuple-element.77.term_ref, bf16[64,256]{1,0:T(8,128)(2,1)S(1)} %get-tuple-element.76.decode_weight_ref, bf16[256]{0:T(256)(128)(2,1)S(1)} %copy-done.4, bf16[1,96,256]{2,1,0:T(8,128)(2,1)S(1)} %get-tuple-element.112.after_ref.refs_0_), custom_call_target="tpu_custom_call" | custom-call | flops 738197504 | tf_op jit(solution)/shard_map/pallas_call | solution.py:1032
  40.6 0.0 collective-permute-done.8.refs_7_
  40.6 0.0 collective-permute-done.9.refs_1_
  40.6 0.1 collective-permute-done.11.refs_3_
  40.7 2.3 %collective-permute-start.14 = (bf16[1,96,256]{2,1,0:T(8,128)(2,1)S(1)}, bf16[1,96,256]{2,1,0:T(8,128)(2,1)S(1)}, u32[]{:S(2)}, u32[]{:S(2)}) collective-permute-start(bf16[1,96,256]{2,1,0:T(8,128)(2,1)S(1)} %shard_map.223.after_ref.refs_0_), channel_id=1, source_target_pairs={{0,24},{1,25},{2,7},{3,6},{4,28},{5,29},{6,3},{7,2},{8,16},{9,17},... | collective-permute-start | bytes 147464 | tf_op jit(solution)/shard_map/ppermute | solution.py:764
  43.0 0.3 collective-permute-start.13
  43.3 0.1 collective-permute-start.12
  43.4 3.3 %shard_map.224.refs_4_.refs_0_ = bf16[4,4,176,256]{3,2,1,0:T(8,128)(2,1)} custom-call(bf16[4,2816,128]{2,1,0:T(8,128)(2,1)S(1)} %get-tuple-element.78.masks_ref, bf16[4,4,176,256]{3,2,1,0:T(8,128)(2,1)S(1)} %get-tuple-element.79.latent_ref, bf16[2816,256]{1,0:T(8,128)(2,1)S(1)} %get-tuple-element.96.grad_ref, ...), custom_call_target="tpu_custom_call" | custom-call | flops 2030043136 | tf_op jit(solution)/shard_map/pallas_call | solution.py:1007
  46.7 4.0 %collective-permute-start.20 = (bf16[4,96,256]{2,1,0:T(8,128)(2,1)S(1)}, bf16[4,96,256]{2,1,0:T(8,128)(2,1)S(1)}, u32[]{:S(2)}, u32[]{:S(2)}) collective-permute-start(bf16[4,96,256]{2,1,0:T(8,128)(2,1)S(1)} %shard_map.225.after_ref.refs_0_), channel_id=1, source_target_pairs={{0,5},{1,4},{2,26},{3,27},{4,1},{5,0},{6,30},{7,31},{8,13},{9,12},... | collective-permute-start | bytes 589832 | tf_op jit(solution)/shard_map/ppermute | solution.py:764
  50.8 0.4 collective-permute-start.16
  51.2 4.8 %collective-permute-start.15 = (bf16[4,96,256]{2,1,0:T(8,128)(2,1)S(1)}, bf16[4,96,256]{2,1,0:T(8,128)(2,1)S(1)}, u32[]{:S(2)}, u32[]{:S(2)}) collective-permute-start(bf16[4,96,256]{2,1,0:T(8,128)(2,1)S(1)} %shard_map.225.after_ref.refs_0_), channel_id=1, source_target_pairs={{0,2},{1,3},{2,0},{3,1},{4,6},{5,7},{6,4},{7,5},{8,10},{9,11},{10,... | collective-permute-start | bytes 589832 | tf_op jit(solution)/shard_map/ppermute | solution.py:764
  55.9 3.4 %shard_map.226.refs_1_ = bf16[4,4,176,256]{3,2,1,0:T(8,128)(2,1)} custom-call(bf16[4,2816,128]{2,1,0:T(8,128)(2,1)S(1)} %get-tuple-element.78.masks_ref, bf16[4,4,176,256]{3,2,1,0:T(8,128)(2,1)S(1)} %get-tuple-element.79.latent_ref, bf16[2816,256]{1,0:T(8,128)(2,1)S(1)} %get-tuple-element.96.grad_ref, ...), custom_call_target="tpu_custom_call", output_to_operand_aliasing={{}: (8, {})} | custom-call | flops 2030043136 | tf_op jit(solution)/shard_map/pallas_call | solution.py:1007
  59.4 0.1 collective-permute-start.21
  59.5 0.3 collective-permute-done.18.refs_0_
  59.8 0.2 collective-permute-start.19
  60.0 1.1 %collective-permute-start.17 = (bf16[4,96,256]{2,1,0:T(8,128)(2,1)S(1)}, bf16[4,96,256]{2,1,0:T(8,128)(2,1)S(1)}, u32[]{:S(2)}, u32[]{:S(2)}) collective-permute-start(bf16[4,96,256]{2,1,0:T(8,128)(2,1)S(1)} %shard_map.227.refs_1_), channel_id=1, source_target_pairs={{0,2},{1,3},{2,0},{3,1},{4,6},{5,7},{6,4},{7,5},{8,10},{9,11},{10,... | collective-permute-start | bytes 589832 | tf_op jit(solution)/shard_map/ppermute | solution.py:764
  61.0 1.3 %shard_map.230 = (f32[2304,256]{1,0:T(8,128)}, f32[1,256]{1,0:T(1,128)}, f32[256,256]{1,0:T(8,128)}, f32[1,256]{1,0:T(1,128)}, f32[64,256]{1,0:T(8,128)}, /*inde...) custom-call(bf16[4,96,256]{2,1,0:T(8,128)(2,1)S(1)} %shard_map.225.after_ref.refs_0_, ...), custom_call_target="tpu_custom_call" | custom-call | tf_op jit(solution)/shard_map/pallas_call | solution.py:1066
  62.4 1.4 %shard_map.231 = (f32[2304,256]{1,0:T(8,128)}, f32[1,256]{1,0:T(1,128)}, f32[256,256]{1,0:T(8,128)}, f32[1,256]{1,0:T(1,128)}, f32[64,256]{1,0:T(8,128)}, /*inde...) custom-call(bf16[4,96,256]{2,1,0:T(8,128)(2,1)S(1)} %collective-perm, ...), custom_call_target="tpu_custom_call", output_to_operand_aliasing={{0}: (4, {}), {1}: (5, {}), {2}: (6, {}), {3}: (7, {}), {4}... | custom-call | tf_op jit(solution)/shard_map/pallas_call | solution.py:1066
  (30 shorter events, 0.2 us)
Async XLA Ops:
  1.8 7.8 %collective-permute-start.1 = (bf16[4,176,256]{2,1,0:T(8,128)(2,1)S(1)}, bf16[4,176,256]{2,1,0:T(8,128)(2,1)S(1)}, u32[]{:S(2)}, u32[]{:S(2)}) collective-permute-start(bf16[4,176,256]{2,1,0:T(8,128)(2,1)S(1)} %get-tuple-element.83), channel_id=1, source_target_pairs={{0,2},{2,0},{4,6},{6,4},{8,10},{10,8},{12,14},{14,12},{16,18},{18,... | collective-permute-start | bytes 1081352 | tf_op jit(solution)/shard_map/ppermute | solution.py:921
  1.9 13.6 %collective-permute-start = (bf16[4,176,256]{2,1,0:T(8,128)(2,1)S(1)}, bf16[4,176,256]{2,1,0:T(8,128)(2,1)S(1)}, u32[]{:S(2)}, u32[]{:S(2)}) collective-permute-start(bf16[4,176,256]{2,1,0:T(8,128)(2,1)S(1)} %get-tuple-element.82), channel_id=1, source_target_pairs={{2,4},{6,8},{10,12},{14,16},{18,20},{22,24},{26,28},{4,2},{8,6},{1... | collective-permute-start | bytes 1081352 | tf_op jit(solution)/shard_map/ppermute | solution.py:921
  6.4 3.2 %copy-start = (bf16[256,64]{0,1:T(8,128)(2,1)S(1)}, bf16[256,64]{0,1:T(8,128)(2,1)}, u32[]{:S(2)}) copy-start(bf16[256,64]{0,1:T(8,128)(2,1)} %param.20) | copy-start | bytes 98308
  6.5 3.2 %copy-start.1 = (bf16[256]{0:T(256)(128)(2,1)S(1)}, bf16[256]{0:T(256)(128)(2,1)}, u32[]{:S(2)}) copy-start(bf16[256]{0:T(256)(128)(2,1)} %conv_bias_ref.3) | copy-start | bytes 1540
  6.5 3.2 %copy-start.2 = (bf16[256]{0:T(256)(128)(2,1)S(1)}, bf16[256]{0:T(256)(128)(2,1)}, u32[]{:S(2)}) copy-start(bf16[256]{0:T(256)(128)(2,1)} %mix_bias_ref.3) | copy-start | bytes 1540
  6.5 3.2 %copy-start.3 = (bf16[64]{0:T(256)(128)(2,1)S(1)}, bf16[64]{0:T(256)(128)(2,1)}, u32[]{:S(2)}) copy-start(bf16[64]{0:T(256)(128)(2,1)} %proj_bias_ref.3) | copy-start | bytes 388
  19.9 2.5 %collective-permute-start.2 = (bf16[16,96,256]{2,1,0:T(8,128)(2,1)S(1)}, bf16[16,96,256]{2,1,0:T(8,128)(2,1)S(1)}, u32[]{:S(2)}, u32[]{:S(2)}) collective-permute-start(bf16[16,96,256]{2,1,0:T(8,128)(2,1)S(1)} %shard_map.216.after_ref), channel_id=1, source_target_pairs={{0,2},{1,3},{2,0},{3,1},{4,6},{5,7},{6,4},{7,5},{8,10},{9,11},{10,... | collective-permute-start | bytes 2359304 | tf_op jit(solution)/shard_map/ppermute | solution.py:764
  22.6 16.3 %copy-start.4 = (bf16[256]{0:T(256)(128)(2,1)S(1)}, bf16[256]{0:T(256)(128)(2,1)}, u32[]{:S(2)}) copy-start(bf16[256]{0:T(256)(128)(2,1)} %decode_bias_ref.1) | copy-start | bytes 1540
  22.6 7.5 %collective-permute-start.3 = (bf16[4,96,256]{2,1,0:T(8,128)(2,1)S(1)}, bf16[4,96,256]{2,1,0:T(8,128)(2,1)S(1)}, u32[]{:S(2)}, u32[]{:S(2)}) collective-permute-start(bf16[4,96,256]{2,1,0:T(8,128)(2,1)S(1)} %get-tuple-element.109), channel_id=1, source_target_pairs={{0,5},{1,4},{2,26},{3,27},{4,1},{5,0},{6,30},{7,31},{8,13},{9,12},... | collective-permute-start | bytes 589832 | tf_op jit(solution)/shard_map/ppermute | solution.py:764
  26.4 9.7 %collective-permute-start.4 = (bf16[4,96,256]{2,1,0:T(8,128)(2,1)S(1)}, bf16[4,96,256]{2,1,0:T(8,128)(2,1)S(1)}, u32[]{:S(2)}, u32[]{:S(2)}) collective-permute-start(bf16[4,96,256]{2,1,0:T(8,128)(2,1)S(1)} %get-tuple-element.110), channel_id=1, source_target_pairs={{0,1},{1,0},{2,18},{3,19},{4,5},{5,4},{6,22},{7,23},{8,9},{9,8},{1... | collective-permute-start | bytes 589832 | tf_op jit(solution)/shard_map/ppermute | solution.py:764
  26.4 9.7 %collective-permute-start.5 = (bf16[4,96,256]{2,1,0:T(8,128)(2,1)S(1)}, bf16[4,96,256]{2,1,0:T(8,128)(2,1)S(1)}, u32[]{:S(2)}, u32[]{:S(2)}) collective-permute-start(bf16[4,96,256]{2,1,0:T(8,128)(2,1)S(1)} %get-tuple-element.111), channel_id=1, source_target_pairs={{0,4},{1,5},{2,10},{3,11},{4,0},{5,1},{6,14},{7,15},{8,12},{9,13},... | collective-permute-start | bytes 589832 | tf_op jit(solution)/shard_map/ppermute | solution.py:764
  26.8 13.9 %collective-permute-start.6 = (bf16[704,256]{1,0:T(8,128)(2,1)S(1)}, bf16[704,256]{1,0:T(8,128)(2,1)S(1)}, u32[]{:S(2)}, u32[]{:S(2)}) collective-permute-start(bf16[704,256]{1,0:T(8,128)(2,1)S(1)} %shard_map.221), channel_id=1, source_target_pairs={{0,2},{2,0},{4,6},{6,4},{8,10},{10,8},{12,14},{14,12},{16,18},{18,... | collective-permute-start | bytes 1081352 | tf_op jit(solution)/shard_map/ppermute | solution.py:924
  26.8 10.8 %collective-permute-start.7 = (bf16[352,256]{1,0:T(8,128)(2,1)S(1)}, bf16[352,256]{1,0:T(8,128)(2,1)S(1)}, u32[]{:S(2)}, u32[]{:S(2)}) collective-permute-start(bf16[352,256]{1,0:T(8,128)(2,1)S(1)} %get-tuple-element.135), channel_id=1, source_target_pairs={{2,4},{6,8},{10,12},{14,16},{18,20},{22,24},{26,28},{4,2},{8,6},{1... | collective-permute-start | bytes 540680 | tf_op jit(solution)/shard_map/ppermute | solution.py:923
  30.1 10.5 %collective-permute-start.8 = (bf16[352,256]{1,0:T(8,128)(2,1)S(1)}, bf16[352,256]{1,0:T(8,128)(2,1)S(1)}, u32[]{:S(2)}, u32[]{:S(2)}) collective-permute-start(bf16[352,256]{1,0:T(8,128)(2,1)S(1)} %get-tuple-element.136), channel_id=1, source_target_pairs={{2,4},{6,8},{10,12},{14,16},{18,20},{22,24},{26,28},{4,2},{8,6},{1... | collective-permute-start | bytes 540680 | tf_op jit(solution)/shard_map/ppermute | solution.py:923
  36.2 4.3 %collective-permute-start.9 = (bf16[1,96,256]{2,1,0:T(8,128)(2,1)S(1)}, bf16[1,96,256]{2,1,0:T(8,128)(2,1)S(1)}, u32[]{:S(2)}, u32[]{:S(2)}) collective-permute-start(bf16[1,96,256]{2,1,0:T(8,128)(2,1)S(1)} %get-tuple-element.114), channel_id=1, source_target_pairs={{0,24},{1,25},{2,7},{3,6},{4,28},{5,29},{6,3},{7,2},{8,16},{9,17},... | collective-permute-start | bytes 147464 | tf_op jit(solution)/shard_map/ppermute | solution.py:764
  37.1 3.4 %collective-permute-start.10 = (bf16[1,96,256]{2,1,0:T(8,128)(2,1)S(1)}, bf16[1,96,256]{2,1,0:T(8,128)(2,1)S(1)}, u32[]{:S(2)}, u32[]{:S(2)}) collective-permute-start(bf16[1,96,256]{2,1,0:T(8,128)(2,1)S(1)} %get-tuple-element.115), channel_id=1, source_target_pairs={{0,16},{1,17},{2,3},{3,2},{4,20},{5,21},{6,7},{7,6},{8,24},{9,25},... | collective-permute-start | bytes 147464 | tf_op jit(solution)/shard_map/ppermute | solution.py:764
  37.6 3.1 %collective-permute-start.11 = (bf16[1,96,256]{2,1,0:T(8,128)(2,1)S(1)}, bf16[1,96,256]{2,1,0:T(8,128)(2,1)S(1)}, u32[]{:S(2)}, u32[]{:S(2)}) collective-permute-start(bf16[1,96,256]{2,1,0:T(8,128)(2,1)S(1)} %get-tuple-element.116), channel_id=1, source_target_pairs={{0,8},{1,9},{2,6},{3,7},{4,12},{5,13},{6,2},{7,3},{8,0},{9,1},{10,... | collective-permute-start | bytes 147464 | tf_op jit(solution)/shard_map/ppermute | solution.py:764
  40.7 6.0 %collective-permute-start.14 = (bf16[1,96,256]{2,1,0:T(8,128)(2,1)S(1)}, bf16[1,96,256]{2,1,0:T(8,128)(2,1)S(1)}, u32[]{:S(2)}, u32[]{:S(2)}) collective-permute-start(bf16[1,96,256]{2,1,0:T(8,128)(2,1)S(1)} %shard_map.223.after_ref.refs_0_), channel_id=1, source_target_pairs={{0,24},{1,25},{2,7},{3,6},{4,28},{5,29},{6,3},{7,2},{8,16},{9,17},... | collective-permute-start | bytes 147464 | tf_op jit(solution)/shard_map/ppermute | solution.py:764
  43.0 3.7 %collective-permute-start.13 = (bf16[1,96,256]{2,1,0:T(8,128)(2,1)S(1)}, bf16[1,96,256]{2,1,0:T(8,128)(2,1)S(1)}, u32[]{:S(2)}, u32[]{:S(2)}) collective-permute-start(bf16[1,96,256]{2,1,0:T(8,128)(2,1)S(1)} %shard_map.223.after_ref.refs_0_), channel_id=1, source_target_pairs={{0,16},{1,17},{2,3},{3,2},{4,20},{5,21},{6,7},{7,6},{8,24},{9,25},... | collective-permute-start | bytes 147464 | tf_op jit(solution)/shard_map/ppermute | solution.py:764
  43.3 3.4 %collective-permute-start.12 = (bf16[1,96,256]{2,1,0:T(8,128)(2,1)S(1)}, bf16[1,96,256]{2,1,0:T(8,128)(2,1)S(1)}, u32[]{:S(2)}, u32[]{:S(2)}) collective-permute-start(bf16[1,96,256]{2,1,0:T(8,128)(2,1)S(1)} %shard_map.223.after_ref.refs_0_), channel_id=1, source_target_pairs={{0,8},{1,9},{2,6},{3,7},{4,12},{5,13},{6,2},{7,3},{8,0},{9,1},{10,... | collective-permute-start | bytes 147464 | tf_op jit(solution)/shard_map/ppermute | solution.py:764
  46.7 12.6 %collective-permute-start.20 = (bf16[4,96,256]{2,1,0:T(8,128)(2,1)S(1)}, bf16[4,96,256]{2,1,0:T(8,128)(2,1)S(1)}, u32[]{:S(2)}, u32[]{:S(2)}) collective-permute-start(bf16[4,96,256]{2,1,0:T(8,128)(2,1)S(1)} %shard_map.225.after_ref.refs_0_), channel_id=1, source_target_pairs={{0,5},{1,4},{2,26},{3,27},{4,1},{5,0},{6,30},{7,31},{8,13},{9,12},... | collective-permute-start | bytes 589832 | tf_op jit(solution)/shard_map/ppermute | solution.py:764
  50.8 9.0 %collective-permute-start.18 = (bf16[4,96,256]{2,1,0:T(8,128)(2,1)S(1)}, bf16[4,96,256]{2,1,0:T(8,128)(2,1)S(1)}, u32[]{:S(2)}, u32[]{:S(2)}) collective-permute-start(bf16[4,96,256]{2,1,0:T(8,128)(2,1)S(1)} %shard_map.225.after_ref.refs_0_), channel_id=1, source_target_pairs={{0,1},{1,0},{2,18},{3,19},{4,5},{5,4},{6,22},{7,23},{8,9},{9,8},{1... | collective-permute-start | bytes 589832 | tf_op jit(solution)/shard_map/ppermute | solution.py:764
  50.8 9.2 %collective-permute-start.16 = (bf16[4,96,256]{2,1,0:T(8,128)(2,1)S(1)}, bf16[4,96,256]{2,1,0:T(8,128)(2,1)S(1)}, u32[]{:S(2)}, u32[]{:S(2)}) collective-permute-start(bf16[4,96,256]{2,1,0:T(8,128)(2,1)S(1)} %shard_map.225.after_ref.refs_0_), channel_id=1, source_target_pairs={{0,4},{1,5},{2,10},{3,11},{4,0},{5,1},{6,14},{7,15},{8,12},{9,13},... | collective-permute-start | bytes 589832 | tf_op jit(solution)/shard_map/ppermute | solution.py:764
  51.2 11.2 %collective-permute-start.15 = (bf16[4,96,256]{2,1,0:T(8,128)(2,1)S(1)}, bf16[4,96,256]{2,1,0:T(8,128)(2,1)S(1)}, u32[]{:S(2)}, u32[]{:S(2)}) collective-permute-start(bf16[4,96,256]{2,1,0:T(8,128)(2,1)S(1)} %shard_map.225.after_ref.refs_0_), channel_id=1, source_target_pairs={{0,2},{1,3},{2,0},{3,1},{4,6},{5,7},{6,4},{7,5},{8,10},{9,11},{10,... | collective-permute-start | bytes 589832 | tf_op jit(solution)/shard_map/ppermute | solution.py:764
  59.4 3.0 %collective-permute-start.21 = (bf16[4,96,256]{2,1,0:T(8,128)(2,1)S(1)}, bf16[4,96,256]{2,1,0:T(8,128)(2,1)S(1)}, u32[]{:S(2)}, u32[]{:S(2)}) collective-permute-start(bf16[4,96,256]{2,1,0:T(8,128)(2,1)S(1)} %shard_map.229.refs_3_), channel_id=1, source_target_pairs={{0,2},{1,3},{2,0},{3,1},{4,6},{5,7},{6,4},{7,5},{8,10},{9,11},{10,... | collective-permute-start | bytes 589832 | tf_op jit(solution)/shard_map/ppermute | solution.py:764
  59.8 2.6 %collective-permute-start.19 = (bf16[4,96,256]{2,1,0:T(8,128)(2,1)S(1)}, bf16[4,96,256]{2,1,0:T(8,128)(2,1)S(1)}, u32[]{:S(2)}, u32[]{:S(2)}) collective-permute-start(bf16[4,96,256]{2,1,0:T(8,128)(2,1)S(1)} %shard_map.228.refs_2_), channel_id=1, source_target_pairs={{0,2},{1,3},{2,0},{3,1},{4,6},{5,7},{6,4},{7,5},{8,10},{9,11},{10,... | collective-permute-start | bytes 589832 | tf_op jit(solution)/shard_map/ppermute | solution.py:764
  60.0 2.4 %collective-permute-start.17 = (bf16[4,96,256]{2,1,0:T(8,128)(2,1)S(1)}, bf16[4,96,256]{2,1,0:T(8,128)(2,1)S(1)}, u32[]{:S(2)}, u32[]{:S(2)}) collective-permute-start(bf16[4,96,256]{2,1,0:T(8,128)(2,1)S(1)} %shard_map.227.refs_1_), channel_id=1, source_target_pairs={{0,2},{1,3},{2,0},{3,1},{4,6},{5,7},{6,4},{7,5},{8,10},{9,11},{10,... | collective-permute-start | bytes 589832 | tf_op jit(solution)/shard_map/ppermute | solution.py:764

commit v6 on v5

--- a/solution.py
+++ b/solution.py
@@ -733,20 +733,18 @@
         rest = [*strip[4:], *canvas[1:]]
         rest = [rest[i : i + 2] for i in range(0, len(rest), 2)]
         even, odd = [near, far, *rest], [far, near, *rest]
-        if len(near) != len(far):
-            odd = even
-        self.stages = [tuple(zip(*pair, strict=True)) for pair in zip(even, odd, strict=True) if pair[0]]
+        stages = [tuple(zip(*pair, strict=True)) for pair in zip(even, odd, strict=True) if pair[0]]
+        self.split, self.whole = stages[0], stages[1:]
         self.core = ((("strip", 0), ("strip", 0)),)
-        self.half = sizes["strip"] * sizes["canvas"] // 2
+        self.half = 2 ** len(self.split)
         self.piece_rows = -(-half_rows // (self.half * tile_rows)) * tile_rows
         self.half_rows = self.half * self.piece_rows
 
     def place(self, core):
         number = 0
-        for stage in self.stages:
-            for spots in stage:
-                even, odd = [(lax.axis_index(axis) // 2**bit) % 2 for axis, bit in spots]
-                number = number * 2 + (even if spots[0] == spots[1] else jnp.where(core == 0, even, odd))
+        for spots in self.split:
+            even, odd = [(lax.axis_index(axis) // 2**bit) % 2 for axis, bit in spots]
+            number = number * 2 + jnp.where(core == 0, even, odd)
         return number
 
     def swap(self, values, stage, step):
@@ -769,10 +767,10 @@
     depth = outs[0].shape[0]
     for place, out_ref in enumerate(outs):
         span = pl.ds(place * depth, depth)
-        total = ins[0][span].astype(wide)
-        for ref in ins[1:]:
-            total = total + ref[span].astype(wide)
-        out_ref[...] = total.astype(low)
+        terms = [ref[span].astype(wide) for ref in ins]
+        while len(terms) > 1:
+            terms = [sum(terms[i + 1 : i + 2], terms[i]) for i in range(0, len(terms), 2)]
+        out_ref[...] = terms[0].astype(low)
 
 
 def add_split(arrays, parts, after=()):
@@ -800,24 +798,6 @@
         input_output_aliases={0: 0},
         compiler_params=pltpu.CompilerParams(vmem_limit_bytes=vmem_bytes),
     )(array, *after)
-
-
-def join_kernel(count, *refs):
-    at = 0
-    for ref in refs[:count]:
-        refs[-1][pl.ds(at, ref.shape[0])] = ref[...]
-        at += ref.shape[0]
-
-
-def join(arrays, *after):
-    depth, rows, channels = arrays[0].shape
-    return pl.pallas_call(
-        functools.partial(join_kernel, len(arrays)),
-        in_specs=[in_vmem] * len(arrays) + [anywhere] * len(after),
-        out_specs=in_vmem,
-        out_shape=jax.ShapeDtypeStruct((depth * len(arrays), rows, channels), low),
-        compiler_params=pltpu.CompilerParams(vmem_limit_bytes=vmem_bytes),
-    )(*arrays, *after)
 
 
 def final_kernel(plan, mine, count, sizes, *refs):
@@ -1019,35 +999,28 @@
             aliases={8: 0} if before else {},
         )(masks, latent, grad, *halo, branch_grad, near_weight, after, *before)[0]
 
-    arrays = [keep, plan.swap(send, plan.core, 1)]
-    after = []
-    for place, stage in enumerate(plan.stages):
-        parts = add_split(arrays, 2 ** len(stage), after)
-        arrays = [parts[0]]
-        arrays += [plan.swap(parts[i], stage, i) for i in reversed(range(1, len(parts)))]
+    parts = add_split([keep, plan.swap(send, plan.core, 1)], plan.half)
+    halo = trade(*edges, split=False)
+    swaps = [plan.swap(parts[i], plan.split, i) for i in reversed(range(1, plan.half))]
+    latent_grad = input_rows(inner, edges, parts[0])
+    after = far_away(latent_grad)
+    piece = add_split([parts[0], *swaps], 1, after)[0]
+    decoded = call(
+        decoded_kernel,
+        [in_vmem, in_vmem, in_vmem, anywhere],
+        [pl.BlockSpec()],
+        [pltpu.HBM(out_grad.shape, low)],
+        flops=4 * total * channels * channels,
+    )(term, near_decode, decode_bias, piece)[0]
+    after = far_away(decoded)
+    for stage in plan.whole:
+        swaps = [plan.swap(piece, stage, i) for i in range(1, 2 ** len(stage))]
+        piece = add_split([piece, *swaps], 1, after)[0]
         after = []
-        if place == 0:
-            halo = trade(*[gate(edge, parts[0]) for edge in edges])
-        elif place == 1:
-            decoded = call(
-                decoded_kernel,
-                [in_vmem, in_vmem, in_vmem, anywhere],
-                [pl.BlockSpec()],
-                [pltpu.HBM(out_grad.shape, low)],
-                flops=4 * total * channels * channels,
-            )(term, near_decode, decode_bias, parts[0])[0]
-            after = [*far_away(decoded), *halo]
-    halo = (halo[0], jnp.concatenate(halo[1:], axis=0))
-    pieces = add_split(arrays, 1, after)
-    latent_grad = input_rows(inner, edges, pieces[0])
-    after = far_away(latent_grad)
-    for stage in reversed(plan.stages):
-        gathered = join(pieces, *after) if len(pieces) > 1 else pieces[0]
-        others = [plan.swap(gathered, stage, i) for i in range(1, 2 ** len(stage))]
-        pieces = [gathered, *others]
-    latent_grad = input_rows(outer, halo, gathered, latent_grad)
+    others = [plan.swap(piece, plan.split, i) for i in range(1, plan.half)]
+    latent_grad = input_rows(outer, halo, piece, latent_grad)
     done = far_away(latent_grad)
-    pieces = [pieces[0], *[gate(piece, *done) for piece in pieces[1:]]]
+    pieces = [piece, *[gate(other, *done) for other in others]]
     swapped = [plan.swap(piece, plan.core, 1) for piece in pieces]
     shapes = [
         (9 * channels, channels),

time: 64.2 us -> 59.9 us (0.933)
  starting transfers between devices: 31.2 us -> 22.3 us
  waiting for transfers between devices: 3.33 us -> 7.99 us
    ppermute x3 -> x0, starting transfers between devices: 6.4 us -> none  [the longest x2 6.37 us: trade(): lax.ppermute(part, 'strip', far)]
    ppermute x17 -> x14, starting transfers between devices: 20.1 us -> 14.4 us  [swap(): return lax.ppermute(values, ('strip', 'canvas'), pairs)]
    ppermute x17 -> x14, waiting for transfers between devices: 3.32 us -> 7.97 us  [swap(): return lax.ppermute(values, ('strip', 'canvas'), pairs)]
    ppermute x1 -> x2, starting transfers between devices: 4.49 us -> 7.7 us  [trade(): lax.ppermute(other, 'strip', far)]
  transfers between devices with their start and end apart: 22 -> 18, of which waited for: 3 -> 5; matrix products, arithmetic and copies ran while one was open for 0% -> 0% of each run, Pallas kernels for 33% -> 36%
where the time goes in v6:
time: 59.9 us; the launch traced here: 59.7 us
  Pallas kernels  28.3 us (47%)
  starting transfers between devices  22.3 us (37%)
  waiting for transfers between devices  7.99 us (13%)
  between operations  1.12 us (2%)
    ppermute x14, starting transfers between devices, swap(): return lax.ppermute(values, ('strip', 'canvas'), pairs)  14.4 us
    ppermute x14, waiting for transfers between devices, swap(): return lax.ppermute(values, ('strip', 'canvas'), pairs)  7.97 us
    ppermute x2, starting transfers between devices, trade(): lax.ppermute(other, 'strip', far)  7.7 us
    pallas_call x2, Pallas kernels, block_rows(): call(functools.partial(rows_kernel, beyond), [in_vmem] * len(ins), [in_vm...  7.49 us
    pallas_call x2, Pallas kernels, input_rows(): call(functools.partial(input_kernel, mine), [in_vmem] * 7 + [anywhere] +...  6.69 us
    pallas_call x2, Pallas kernels, weight_half(): call(functools.partial(weight_kernel, plan, mine), [in_vmem] * len(ins) +...  5.06 us
    pallas_call x1, Pallas kernels, per_device(): call(code_kernel, [in_vmem] * 4 + [in_hbm] * 4, [in_vmem] * 8, outs, held...  3.11 us
    pallas_call x2, Pallas kernels, finish(): call(functools.partial(final_kernel, plan, mine, count, (channels, size,...  2.75 us
  transfers between devices with their start and end apart: 18, of which 5 were waited for; matrix products, arithmetic and copies ran while one was open for 0% of the time, Pallas kernels for 36%

profile of v6, /device:TPU:1, one launch (start us, length us, event | category | flops | bytes accessed | tf_op | source)
XLA Modules:
  0.0 59.7 jit_solution(4922811179446796103)
XLA Ops:
  0.6 1.2 %shard_map.212 = (bf16[4,176,256]{2,1,0:T(8,128)(2,1)S(1)}, bf16[4,176,256]{2,1,0:T(8,128)(2,1)S(1)}, s32[4,4,176]{2,1,0:T(4,128)S(1)}, s32[4,4,176]{2,1,0:T(4,1...) custom-call(bf16[4,4,176,256]{3,2,1,0:T(8,128)(2,1)} %latent_hbm.3, s32[4,4,176]{2,1,0:T(4,128)} %crop_hbm.1, ...), custom_call_target="tpu_custom_call" | custom-call | tf_op jit(solution)/shard_map/pallas_call | solution.py:913
  1.8 0.1 collective-permute-start.1
  1.9 4.5 %collective-permute-start = (bf16[4,176,256]{2,1,0:T(8,128)(2,1)S(1)}, bf16[4,176,256]{2,1,0:T(8,128)(2,1)S(1)}, u32[]{:S(2)}, u32[]{:S(2)}) collective-permute-start(bf16[4,176,256]{2,1,0:T(8,128)(2,1)S(1)} %get-tuple-element.78), channel_id=1, source_target_pairs={{2,4},{6,8},{10,12},{14,16},{18,20},{22,24},{26,28},{4,2},{8,6},{1... | collective-permute-start | bytes 1081352 | tf_op jit(solution)/shard_map/ppermute | solution.py:901
  6.4 0.0 copy-start
  6.5 0.0 copy-start.1
  6.5 0.0 copy-start.2
  6.5 0.0 copy-start.3
  6.5 3.1 %shard_map.213 = (f32[4,704,128]{2,1,0:T(8,128)S(1)}, bf16[2816,512]{1,0:T(8,128)(2,1)S(1)}, bf16[4,2816,128]{2,1,0:T(8,128)(2,1)S(1)}, f32[1,256]{1,0:T(1,128)S...) custom-call(s32[4,4,176]{2,1,0:T(4,128)S(1)} %get-tuple-element.69.c, ...), custom_call_target="tpu_custom_call" | custom-call | flops 1107296256 | tf_op jit(solution)/shard_map/pallas_call | solution.py:932
  9.7 5.9 %shard_map.214 = (bf16[4224,768]{1,0:T(8,128)(2,1)S(1)}, bf16[2816,256]{1,0:T(8,128)(2,1)S(1)}, bf16[2816,256]{1,0:T(8,128)(2,1)S(1)}, bf16[2816,256]{1,0:T(8,12...) custom-call(bf16[4,2816,128]{2,1,0:T(8,128)(2,1)S(1)} %get-tuple-ele, ...), custom_call_target="tpu_custom_call" | custom-call | flops 3690987520 | tf_op jit(solution)/shard_map/pallas_call | solution.py:957
  15.6 0.0 collective-permute-done.halo_ref
  15.6 1.6 %shard_map.215 = (bf16[4224,768]{1,0:T(8,128)(2,1)S(1)}, bf16[2816,256]{1,0:T(8,128)(2,1)S(1)}, bf16[2816,256]{1,0:T(8,128)(2,1)S(1)}, bf16[2816,256]{1,0:T(8,12...) custom-call(bf16[4,2816,128]{2,1,0:T(8,128)(2,1)S(1)} %get-tuple-ele, ...), custom_call_target="tpu_custom_call", output_to_operand_aliasing={{0}: (11, {}), {1}: (12, {}), {2}: (13, {}), {3}: (14, {}),... | custom-call | flops 3690987520 | tf_op jit(solution)/shard_map/pallas_call | solution.py:957
  17.2 2.7 %shard_map.216.after_ref = bf16[4,384,256]{2,1,0:T(8,128)(2,1)S(1)} custom-call(bf16[4224,768]{1,0:T(8,128)(2,1)S(1)} %get-tuple-element.91.slab_ref, bf16[2816,256]{1,0:T(8,128)(2,1)S(1)} %get-tuple-element.92.grad_ref, bf16[2816,256]{1,0:T(8,128)(2,1)S(1)} %get-tuple-element.93.up_ref, bf16[2816,256]{1,0:T(8,128)(2,1)S(1)} %get-tuple-element.94.down_ref, ...), custom_call_target="tpu_custom_call" | custom-call | flops 1845493760 | tf_op jit(solution)/shard_map/pallas_call | solution.py:975
  19.9 0.1 collective-permute-start.2
  19.9 2.4 %shard_map.217.refs_0_ = bf16[4,384,256]{2,1,0:T(8,128)(2,1)S(1)} custom-call(bf16[4224,768]{1,0:T(8,128)(2,1)S(1)} %get-tuple-element.91.slab_ref, bf16[2816,256]{1,0:T(8,128)(2,1)S(1)} %get-tuple-element.92.grad_ref, bf16[2816,256]{1,0:T(8,128)(2,1)S(1)} %get-tuple-element.93.up_ref, bf16[2816,256]{1,0:T(8,128)(2,1)S(1)} %get-tuple-element.94.down_ref, ...), custom_call_target="tpu_custom_call" | custom-call | flops 1845493760 | tf_op jit(solution)/shard_map/pallas_call | solution.py:975
  22.3 0.0 collective-permute-done.2.refs_1_
  22.3 0.2 shard_map.218
  22.5 3.8 %collective-permute-start.3 = (bf16[1,384,256]{2,1,0:T(8,128)(2,1)S(1)}, bf16[1,384,256]{2,1,0:T(8,128)(2,1)S(1)}, u32[]{:S(2)}, u32[]{:S(2)}) collective-permute-start(bf16[1,384,256]{2,1,0:T(8,128)(2,1)S(1)} %get-tuple-element.105), channel_id=1, source_target_pairs={{0,5},{1,4},{2,26},{3,27},{4,1},{5,0},{6,30},{7,31},{8,13},{9,12},... | collective-permute-start | bytes 589832 | tf_op jit(solution)/shard_map/ppermute | solution.py:762
  26.3 0.0 collective-permute-start.4
  26.3 0.4 collective-permute-start.5
  26.7 3.2 %collective-permute-start.7 = (bf16[704,256]{1,0:T(8,128)(2,1)S(1)}, bf16[704,256]{1,0:T(8,128)(2,1)S(1)}, u32[]{:S(2)}, u32[]{:S(2)}) collective-permute-start(bf16[704,256]{1,0:T(8,128)(2,1)S(1)} %get-tuple-element.103.after_ref.other_ref), channel_id=1, source_target_pairs={{2,4},{6,8},{10,12},{14,16},{18,20},{22,24},{26,28},{4,2},{8,6},{1... | collective-permute-start | bytes 1081352 | tf_op jit(solution)/shard_map/ppermute | solution.py:901
  29.9 0.1 collective-permute-start.6
  30.0 3.3 %shard_map.219.refs_4_.refs_0_ = bf16[4,4,176,256]{3,2,1,0:T(8,128)(2,1)} custom-call(bf16[4,2816,128]{2,1,0:T(8,128)(2,1)S(1)} %get-tuple-element.74.masks_ref, bf16[4,4,176,256]{3,2,1,0:T(8,128)(2,1)S(1)} %get-tuple-element.75.latent_ref, bf16[2816,256]{1,0:T(8,128)(2,1)S(1)} %get-tuple-element.92.grad_ref, ...), custom_call_target="tpu_custom_call" | custom-call | flops 2030043136 | tf_op jit(solution)/shard_map/pallas_call | solution.py:987
  33.2 0.0 copy-start.4
  33.2 0.0 collective-permute-done.3.refs_1_
  33.3 4.0 %collective-permute-done.4.refs_2_ = bf16[1,384,256]{2,1,0:T(8,128)(2,1)S(1)} collective-permute-done((bf16[1,384,256]{2,1,0:T(8,128)(2,1)S(1)}, bf16[1,384,256]{2,1,0:T(8,128)(2,1)S(1)}, u32[]{:S(2)}, u32[]{:S(2)}) %collective-permute-start.4) | collective-permute-done | bytes 196640 | tf_op jit(solution)/shard_map/ppermute | solution.py:762
  37.2 0.0 collective-permute-done.5.refs_3_
  37.2 0.1 shard_map.220.after_ref.refs_0_
  37.3 0.1 collective-permute-start.10
  37.4 1.3 %collective-permute-start.9 = (bf16[1,384,256]{2,1,0:T(8,128)(2,1)S(1)}, bf16[1,384,256]{2,1,0:T(8,128)(2,1)S(1)}, u32[]{:S(2)}, u32[]{:S(2)}) collective-permute-start(bf16[1,384,256]{2,1,0:T(8,128)(2,1)S(1)} %shard_map.220.after_ref.refs_0_), channel_id=1, source_target_pairs={{0,16},{1,17},{2,3},{3,2},{4,20},{5,21},{6,7},{7,6},{8,24},{9,25},... | collective-permute-start | bytes 589832 | tf_op jit(solution)/shard_map/ppermute | solution.py:762
  38.7 1.4 %collective-permute-start.8 = (bf16[1,384,256]{2,1,0:T(8,128)(2,1)S(1)}, bf16[1,384,256]{2,1,0:T(8,128)(2,1)S(1)}, u32[]{:S(2)}, u32[]{:S(2)}) collective-permute-start(bf16[1,384,256]{2,1,0:T(8,128)(2,1)S(1)} %shard_map.220.after_ref.refs_0_), channel_id=1, source_target_pairs={{0,8},{1,9},{2,6},{3,7},{4,12},{5,13},{6,2},{7,3},{8,0},{9,1},{10,... | collective-permute-start | bytes 589832 | tf_op jit(solution)/shard_map/ppermute | solution.py:762
  40.1 1.6 %shard_map.221.refs_4_ = bf16[4,4,176,256]{3,2,1,0:T(8,128)(2,1)} custom-call(f32[4,704,128]{2,1,0:T(8,128)S(1)} %get-tuple-element.73.term_ref, bf16[64,256]{1,0:T(8,128)(2,1)S(1)} %get-tuple-element.72.decode_weight_ref, bf16[256]{0:T(256)(128)(2,1)S(1)} %copy-done.4, bf16[1,384,256]{2,1,0:T(8,128)(2,1)S(1)} %shard_map.220.after_ref.refs_0_), custom_call_target="tpu_custom_call" | custom-call | flops 738197504 | tf_op jit(solution)/shard_map/pallas_call | solution.py:1008
  41.7 1.3 %collective-permute-done.10.refs_3_ = bf16[1,384,256]{2,1,0:T(8,128)(2,1)S(1)} collective-permute-done((bf16[1,384,256]{2,1,0:T(8,128)(2,1)S(1)}, bf16[1,384,256]{2,1,0:T(8,128)(2,1)S(1)}, u32[]{:S(2)}, u32[]{:S(2)}) %collective-permute-start.10) | collective-permute-done | bytes 196640 | tf_op jit(solution)/shard_map/ppermute | solution.py:762
  42.9 0.9 %collective-permute-done.9.refs_2_ = bf16[1,384,256]{2,1,0:T(8,128)(2,1)S(1)} collective-permute-done((bf16[1,384,256]{2,1,0:T(8,128)(2,1)S(1)}, bf16[1,384,256]{2,1,0:T(8,128)(2,1)S(1)}, u32[]{:S(2)}, u32[]{:S(2)}) %collective-permute-start.9) | collective-permute-done | bytes 196640 | tf_op jit(solution)/shard_map/ppermute | solution.py:762
  43.8 1.1 %collective-permute-done.8.refs_1_ = bf16[1,384,256]{2,1,0:T(8,128)(2,1)S(1)} collective-permute-done((bf16[1,384,256]{2,1,0:T(8,128)(2,1)S(1)}, bf16[1,384,256]{2,1,0:T(8,128)(2,1)S(1)}, u32[]{:S(2)}, u32[]{:S(2)}) %collective-permute-start.8) | collective-permute-done | bytes 196640 | tf_op jit(solution)/shard_map/ppermute | solution.py:762
  44.9 0.1 shard_map.222.after_ref.refs_0_
  45.0 2.2 %collective-permute-start.16 = (bf16[1,384,256]{2,1,0:T(8,128)(2,1)S(1)}, bf16[1,384,256]{2,1,0:T(8,128)(2,1)S(1)}, u32[]{:S(2)}, u32[]{:S(2)}) collective-permute-start(bf16[1,384,256]{2,1,0:T(8,128)(2,1)S(1)} %shard_map.222.after_ref.refs_0_), channel_id=1, source_target_pairs={{0,5},{1,4},{2,26},{3,27},{4,1},{5,0},{6,30},{7,31},{8,13},{9,12},... | collective-permute-start | bytes 589832 | tf_op jit(solution)/shard_map/ppermute | solution.py:762
  47.2 0.0 collective-permute-start.14
  47.3 1.4 %collective-permute-start.12 = (bf16[1,384,256]{2,1,0:T(8,128)(2,1)S(1)}, bf16[1,384,256]{2,1,0:T(8,128)(2,1)S(1)}, u32[]{:S(2)}, u32[]{:S(2)}) collective-permute-start(bf16[1,384,256]{2,1,0:T(8,128)(2,1)S(1)} %shard_map.222.after_ref.refs_0_), channel_id=1, source_target_pairs={{0,4},{1,5},{2,10},{3,11},{4,0},{5,1},{6,14},{7,15},{8,12},{9,13},... | collective-permute-start | bytes 589832 | tf_op jit(solution)/shard_map/ppermute | solution.py:762
  48.7 0.0 collective-permute-done.7.other_ref
  48.7 2.9 %collective-permute-start.11 = (bf16[1,384,256]{2,1,0:T(8,128)(2,1)S(1)}, bf16[1,384,256]{2,1,0:T(8,128)(2,1)S(1)}, u32[]{:S(2)}, u32[]{:S(2)}) collective-permute-start(bf16[1,384,256]{2,1,0:T(8,128)(2,1)S(1)} %shard_map.222.after_ref.refs_0_), channel_id=1, source_target_pairs={{0,2},{1,3},{2,0},{3,1},{4,6},{5,7},{6,4},{7,5},{8,10},{9,11},{10,... | collective-permute-start | bytes 589832 | tf_op jit(solution)/shard_map/ppermute | solution.py:762
  51.5 0.0 collective-permute-done.6.mate_ref
  51.5 3.4 %shard_map.223.refs_1_ = bf16[4,4,176,256]{3,2,1,0:T(8,128)(2,1)} custom-call(bf16[4,2816,128]{2,1,0:T(8,128)(2,1)S(1)} %get-tuple-element.74.masks_ref, bf16[4,4,176,256]{3,2,1,0:T(8,128)(2,1)S(1)} %get-tuple-element.75.latent_ref, bf16[2816,256]{1,0:T(8,128)(2,1)S(1)} %get-tuple-element.92.grad_ref, ...), custom_call_target="tpu_custom_call", output_to_operand_aliasing={{}: (8, {})} | custom-call | flops 2030043136 | tf_op jit(solution)/shard_map/pallas_call | solution.py:987
  55.0 0.1 collective-permute-start.17
  55.1 0.7 %collective-permute-done.14.refs_0_ = bf16[1,384,256]{2,1,0:T(8,128)(2,1)S(1)} collective-permute-done((bf16[1,384,256]{2,1,0:T(8,128)(2,1)S(1)}, bf16[1,384,256]{2,1,0:T(8,128)(2,1)S(1)}, u32[]{:S(2)}, u32[]{:S(2)}) %collective-permute-start.14) | collective-permute-done | bytes 196640 | tf_op jit(solution)/shard_map/ppermute | solution.py:762
  55.8 0.5 collective-permute-start.15
  56.3 0.5 collective-permute-start.13
  56.7 1.3 %shard_map.227 = (f32[2304,256]{1,0:T(8,128)}, f32[1,256]{1,0:T(1,128)}, f32[256,256]{1,0:T(8,128)}, f32[1,256]{1,0:T(1,128)}, f32[64,256]{1,0:T(8,128)}, /*inde...) custom-call(bf16[1,384,256]{2,1,0:T(8,128)(2,1)S(1)} %shard_map.222.after_ref.refs_0_, ...), custom_call_target="tpu_custom_call" | custom-call | tf_op jit(solution)/shard_map/pallas_call | solution.py:1039
  58.1 1.4 %shard_map.228 = (f32[2304,256]{1,0:T(8,128)}, f32[1,256]{1,0:T(1,128)}, f32[256,256]{1,0:T(8,128)}, f32[1,256]{1,0:T(1,128)}, f32[64,256]{1,0:T(8,128)}, /*inde...) custom-call(bf16[1,384,256]{2,1,0:T(8,128)(2,1)S(1)} %collective-per, ...), custom_call_target="tpu_custom_call", output_to_operand_aliasing={{0}: (4, {}), {1}: (5, {}), {2}: (6, {}), {3}: (7, {}), {4}... | custom-call | tf_op jit(solution)/shard_map/pallas_call | solution.py:1039
  (15 shorter events, 0.0 us)
Async XLA Ops:
  1.8 7.8 %collective-permute-start.1 = (bf16[4,176,256]{2,1,0:T(8,128)(2,1)S(1)}, bf16[4,176,256]{2,1,0:T(8,128)(2,1)S(1)}, u32[]{:S(2)}, u32[]{:S(2)}) collective-permute-start(bf16[4,176,256]{2,1,0:T(8,128)(2,1)S(1)} %get-tuple-element.79), channel_id=1, source_target_pairs={{0,2},{2,0},{4,6},{6,4},{8,10},{10,8},{12,14},{14,12},{16,18},{18,... | collective-permute-start | bytes 1081352 | tf_op jit(solution)/shard_map/ppermute | solution.py:901
  1.9 13.6 %collective-permute-start = (bf16[4,176,256]{2,1,0:T(8,128)(2,1)S(1)}, bf16[4,176,256]{2,1,0:T(8,128)(2,1)S(1)}, u32[]{:S(2)}, u32[]{:S(2)}) collective-permute-start(bf16[4,176,256]{2,1,0:T(8,128)(2,1)S(1)} %get-tuple-element.78), channel_id=1, source_target_pairs={{2,4},{6,8},{10,12},{14,16},{18,20},{22,24},{26,28},{4,2},{8,6},{1... | collective-permute-start | bytes 1081352 | tf_op jit(solution)/shard_map/ppermute | solution.py:901
  6.4 3.2 %copy-start = (bf16[256,64]{0,1:T(8,128)(2,1)S(1)}, bf16[256,64]{0,1:T(8,128)(2,1)}, u32[]{:S(2)}) copy-start(bf16[256,64]{0,1:T(8,128)(2,1)} %param.20) | copy-start | bytes 98308
  6.5 3.2 %copy-start.1 = (bf16[256]{0:T(256)(128)(2,1)S(1)}, bf16[256]{0:T(256)(128)(2,1)}, u32[]{:S(2)}) copy-start(bf16[256]{0:T(256)(128)(2,1)} %conv_bias_ref.3) | copy-start | bytes 1540
  6.5 3.2 %copy-start.2 = (bf16[256]{0:T(256)(128)(2,1)S(1)}, bf16[256]{0:T(256)(128)(2,1)}, u32[]{:S(2)}) copy-start(bf16[256]{0:T(256)(128)(2,1)} %mix_bias_ref.3) | copy-start | bytes 1540
  6.5 3.2 %copy-start.3 = (bf16[64]{0:T(256)(128)(2,1)S(1)}, bf16[64]{0:T(256)(128)(2,1)}, u32[]{:S(2)}) copy-start(bf16[64]{0:T(256)(128)(2,1)} %proj_bias_ref.3) | copy-start | bytes 388
  19.9 2.5 %collective-permute-start.2 = (bf16[4,384,256]{2,1,0:T(8,128)(2,1)S(1)}, bf16[4,384,256]{2,1,0:T(8,128)(2,1)S(1)}, u32[]{:S(2)}, u32[]{:S(2)}) collective-permute-start(bf16[4,384,256]{2,1,0:T(8,128)(2,1)S(1)} %shard_map.216.after_ref), channel_id=1, source_target_pairs={{0,2},{1,3},{2,0},{3,1},{4,6},{5,7},{6,4},{7,5},{8,10},{9,11},{10,... | collective-permute-start | bytes 2359304 | tf_op jit(solution)/shard_map/ppermute | solution.py:762
  22.5 10.7 %collective-permute-start.3 = (bf16[1,384,256]{2,1,0:T(8,128)(2,1)S(1)}, bf16[1,384,256]{2,1,0:T(8,128)(2,1)S(1)}, u32[]{:S(2)}, u32[]{:S(2)}) collective-permute-start(bf16[1,384,256]{2,1,0:T(8,128)(2,1)S(1)} %get-tuple-element.105), channel_id=1, source_target_pairs={{0,5},{1,4},{2,26},{3,27},{4,1},{5,0},{6,30},{7,31},{8,13},{9,12},... | collective-permute-start | bytes 589832 | tf_op jit(solution)/shard_map/ppermute | solution.py:762
  26.3 10.9 %collective-permute-start.4 = (bf16[1,384,256]{2,1,0:T(8,128)(2,1)S(1)}, bf16[1,384,256]{2,1,0:T(8,128)(2,1)S(1)}, u32[]{:S(2)}, u32[]{:S(2)}) collective-permute-start(bf16[1,384,256]{2,1,0:T(8,128)(2,1)S(1)} %get-tuple-element.106), channel_id=1, source_target_pairs={{0,1},{1,0},{2,18},{3,19},{4,5},{5,4},{6,22},{7,23},{8,9},{9,8},{1... | collective-permute-start | bytes 589832 | tf_op jit(solution)/shard_map/ppermute | solution.py:762
  26.3 10.9 %collective-permute-start.5 = (bf16[1,384,256]{2,1,0:T(8,128)(2,1)S(1)}, bf16[1,384,256]{2,1,0:T(8,128)(2,1)S(1)}, u32[]{:S(2)}, u32[]{:S(2)}) collective-permute-start(bf16[1,384,256]{2,1,0:T(8,128)(2,1)S(1)} %get-tuple-element.107), channel_id=1, source_target_pairs={{0,4},{1,5},{2,10},{3,11},{4,0},{5,1},{6,14},{7,15},{8,12},{9,13},... | collective-permute-start | bytes 589832 | tf_op jit(solution)/shard_map/ppermute | solution.py:762
  26.7 22.0 %collective-permute-start.7 = (bf16[704,256]{1,0:T(8,128)(2,1)S(1)}, bf16[704,256]{1,0:T(8,128)(2,1)S(1)}, u32[]{:S(2)}, u32[]{:S(2)}) collective-permute-start(bf16[704,256]{1,0:T(8,128)(2,1)S(1)} %get-tuple-element.103.after_ref.other_ref), channel_id=1, source_target_pairs={{2,4},{6,8},{10,12},{14,16},{18,20},{22,24},{26,28},{4,2},{8,6},{1... | collective-permute-start | bytes 1081352 | tf_op jit(solution)/shard_map/ppermute | solution.py:901
  29.9 21.6 %collective-permute-start.6 = (bf16[704,256]{1,0:T(8,128)(2,1)S(1)}, bf16[704,256]{1,0:T(8,128)(2,1)S(1)}, u32[]{:S(2)}, u32[]{:S(2)}) collective-permute-start(bf16[704,256]{1,0:T(8,128)(2,1)S(1)} %get-tuple-element.108.mate_ref), channel_id=1, source_target_pairs={{0,2},{2,0},{4,6},{6,4},{8,10},{10,8},{12,14},{14,12},{16,18},{18,... | collective-permute-start | bytes 1081352 | tf_op jit(solution)/shard_map/ppermute | solution.py:901
  33.2 6.8 %copy-start.4 = (bf16[256]{0:T(256)(128)(2,1)S(1)}, bf16[256]{0:T(256)(128)(2,1)}, u32[]{:S(2)}) copy-start(bf16[256]{0:T(256)(128)(2,1)} %decode_bias_ref.1) | copy-start | bytes 1540
  37.3 5.6 %collective-permute-start.10 = (bf16[1,384,256]{2,1,0:T(8,128)(2,1)S(1)}, bf16[1,384,256]{2,1,0:T(8,128)(2,1)S(1)}, u32[]{:S(2)}, u32[]{:S(2)}) collective-permute-start(bf16[1,384,256]{2,1,0:T(8,128)(2,1)S(1)} %shard_map.220.after_ref.refs_0_), channel_id=1, source_target_pairs={{0,24},{1,25},{2,7},{3,6},{4,28},{5,29},{6,3},{7,2},{8,16},{9,17},... | collective-permute-start | bytes 589832 | tf_op jit(solution)/shard_map/ppermute | solution.py:762
  37.4 6.4 %collective-permute-start.9 = (bf16[1,384,256]{2,1,0:T(8,128)(2,1)S(1)}, bf16[1,384,256]{2,1,0:T(8,128)(2,1)S(1)}, u32[]{:S(2)}, u32[]{:S(2)}) collective-permute-start(bf16[1,384,256]{2,1,0:T(8,128)(2,1)S(1)} %shard_map.220.after_ref.refs_0_), channel_id=1, source_target_pairs={{0,16},{1,17},{2,3},{3,2},{4,20},{5,21},{6,7},{7,6},{8,24},{9,25},... | collective-permute-start | bytes 589832 | tf_op jit(solution)/shard_map/ppermute | solution.py:762
  38.7 6.2 %collective-permute-start.8 = (bf16[1,384,256]{2,1,0:T(8,128)(2,1)S(1)}, bf16[1,384,256]{2,1,0:T(8,128)(2,1)S(1)}, u32[]{:S(2)}, u32[]{:S(2)}) collective-permute-start(bf16[1,384,256]{2,1,0:T(8,128)(2,1)S(1)} %shard_map.220.after_ref.refs_0_), channel_id=1, source_target_pairs={{0,8},{1,9},{2,6},{3,7},{4,12},{5,13},{6,2},{7,3},{8,0},{9,1},{10,... | collective-permute-start | bytes 589832 | tf_op jit(solution)/shard_map/ppermute | solution.py:762
  45.0 9.9 %collective-permute-start.16 = (bf16[1,384,256]{2,1,0:T(8,128)(2,1)S(1)}, bf16[1,384,256]{2,1,0:T(8,128)(2,1)S(1)}, u32[]{:S(2)}, u32[]{:S(2)}) collective-permute-start(bf16[1,384,256]{2,1,0:T(8,128)(2,1)S(1)} %shard_map.222.after_ref.refs_0_), channel_id=1, source_target_pairs={{0,5},{1,4},{2,26},{3,27},{4,1},{5,0},{6,30},{7,31},{8,13},{9,12},... | collective-permute-start | bytes 589832 | tf_op jit(solution)/shard_map/ppermute | solution.py:762
  47.2 8.5 %collective-permute-start.14 = (bf16[1,384,256]{2,1,0:T(8,128)(2,1)S(1)}, bf16[1,384,256]{2,1,0:T(8,128)(2,1)S(1)}, u32[]{:S(2)}, u32[]{:S(2)}) collective-permute-start(bf16[1,384,256]{2,1,0:T(8,128)(2,1)S(1)} %shard_map.222.after_ref.refs_0_), channel_id=1, source_target_pairs={{0,1},{1,0},{2,18},{3,19},{4,5},{5,4},{6,22},{7,23},{8,9},{9,8},{1... | collective-permute-start | bytes 589832 | tf_op jit(solution)/shard_map/ppermute | solution.py:762
  47.3 9.0 %collective-permute-start.12 = (bf16[1,384,256]{2,1,0:T(8,128)(2,1)S(1)}, bf16[1,384,256]{2,1,0:T(8,128)(2,1)S(1)}, u32[]{:S(2)}, u32[]{:S(2)}) collective-permute-start(bf16[1,384,256]{2,1,0:T(8,128)(2,1)S(1)} %shard_map.222.after_ref.refs_0_), channel_id=1, source_target_pairs={{0,4},{1,5},{2,10},{3,11},{4,0},{5,1},{6,14},{7,15},{8,12},{9,13},... | collective-permute-start | bytes 589832 | tf_op jit(solution)/shard_map/ppermute | solution.py:762
  48.7 9.4 %collective-permute-start.11 = (bf16[1,384,256]{2,1,0:T(8,128)(2,1)S(1)}, bf16[1,384,256]{2,1,0:T(8,128)(2,1)S(1)}, u32[]{:S(2)}, u32[]{:S(2)}) collective-permute-start(bf16[1,384,256]{2,1,0:T(8,128)(2,1)S(1)} %shard_map.222.after_ref.refs_0_), channel_id=1, source_target_pairs={{0,2},{1,3},{2,0},{3,1},{4,6},{5,7},{6,4},{7,5},{8,10},{9,11},{10,... | collective-permute-start | bytes 589832 | tf_op jit(solution)/shard_map/ppermute | solution.py:762
  55.0 3.1 %collective-permute-start.17 = (bf16[1,384,256]{2,1,0:T(8,128)(2,1)S(1)}, bf16[1,384,256]{2,1,0:T(8,128)(2,1)S(1)}, u32[]{:S(2)}, u32[]{:S(2)}) collective-permute-start(bf16[1,384,256]{2,1,0:T(8,128)(2,1)S(1)} %shard_map.226.refs_3_), channel_id=1, source_target_pairs={{0,2},{1,3},{2,0},{3,1},{4,6},{5,7},{6,4},{7,5},{8,10},{9,11},{10,... | collective-permute-start | bytes 589832 | tf_op jit(solution)/shard_map/ppermute | solution.py:762
  55.8 2.3 %collective-permute-start.15 = (bf16[1,384,256]{2,1,0:T(8,128)(2,1)S(1)}, bf16[1,384,256]{2,1,0:T(8,128)(2,1)S(1)}, u32[]{:S(2)}, u32[]{:S(2)}) collective-permute-start(bf16[1,384,256]{2,1,0:T(8,128)(2,1)S(1)} %shard_map.225.refs_2_), channel_id=1, source_target_pairs={{0,2},{1,3},{2,0},{3,1},{4,6},{5,7},{6,4},{7,5},{8,10},{9,11},{10,... | collective-permute-start | bytes 589832 | tf_op jit(solution)/shard_map/ppermute | solution.py:762
  56.3 1.8 %collective-permute-start.13 = (bf16[1,384,256]{2,1,0:T(8,128)(2,1)S(1)}, bf16[1,384,256]{2,1,0:T(8,128)(2,1)S(1)}, u32[]{:S(2)}, u32[]{:S(2)}) collective-permute-start(bf16[1,384,256]{2,1,0:T(8,128)(2,1)S(1)} %shard_map.224.refs_1_), channel_id=1, source_target_pairs={{0,2},{1,3},{2,0},{3,1},{4,6},{5,7},{6,4},{7,5},{8,10},{9,11},{10,... | collective-permute-start | bytes 589832 | tf_op jit(solution)/shard_map/ppermute | solution.py:762

commit v7 on v6

--- a/solution.py
+++ b/solution.py
@@ -13,6 +13,7 @@
 bits = (1, 3, 4, 6)
 up_plane, left_plane, right_plane, down_plane = range(4)
 tile_rows = 16
+half_tile = 8
 vmem_bytes = 20 * 2**20
 in_hbm = pl.BlockSpec(memory_space=pltpu.HBM)
 anywhere = pl.BlockSpec(memory_space=pl.ANY)
@@ -577,8 +578,9 @@
     wanted = core if mine else 1 - core
     place = plan.place(wanted)
 
-    def step(row_step, weighted_ref):
-        return mm_tn(slab_ref[pl.ds(row_step * count, total)], weighted_ref[...])
+    def step(row_step, weighted_ref, first, last):
+        span, lanes = pl.ds(row_step * count, total), pl.ds(first * channels, (last - first) * channels)
+        return (last - first) * channels, lambda: mm_tn(slab_ref[span, lanes], weighted_ref[...])
 
     def fill(parts):
         piece, had = [], 0
@@ -589,18 +591,24 @@
             start = 0
             while start < depth:
                 some = min(depth - start, plan.piece_rows - had)
-                piece.append(values[start : start + some].astype(low))
+                piece.append(values[start : start + some])
                 start += some
                 had += some
                 if had == plan.piece_rows:
-                    out_ref[at ^ place] = jnp.concatenate(piece, axis=0)
+                    out_ref[at ^ place] = jnp.concatenate(piece, axis=0).astype(low)
                     piece, had = [], 0
                     at += 1
 
     @pl.when(wanted == 0)
     def _():
-        triple = 3 * channels
-        fill([(triple, lambda: step(0, up_ref)), (triple, lambda: step(1, grad_ref))])
+        fill(
+            [
+                step(0, up_ref, 0, 3),
+                step(1, grad_ref, 0, 2),
+                (size, lambda: mm_tn(codes_ref[...], stream_ref[...])[:size]),
+                (size, lambda: decode_weight_grad_ref[...]),
+            ]
+        )
 
     @pl.when(wanted == 1)
     def _():
@@ -614,11 +622,10 @@
 
         fill(
             [
-                (3 * channels, lambda: step(2, down_ref)),
+                step(1, grad_ref, 2, 3),
+                step(2, down_ref, 0, 3),
                 (channels, lambda: mm_tn(second_ref[...], branch_grad_ref[...].reshape(total, channels))),
-                (size, lambda: mm_tn(codes_ref[...], stream_ref[...])[:size]),
                 (size * (entries // channels), picked),
-                (size, lambda: decode_weight_grad_ref[...]),
                 (tile_rows, lambda: jnp.concatenate(biases, axis=0)),
             ]
         )
@@ -737,7 +744,7 @@
         self.split, self.whole = stages[0], stages[1:]
         self.core = ((("strip", 0), ("strip", 0)),)
         self.half = 2 ** len(self.split)
-        self.piece_rows = -(-half_rows // (self.half * tile_rows)) * tile_rows
+        self.piece_rows = -(-half_rows // (self.half * half_tile)) * half_tile
         self.half_rows = self.half * self.piece_rows
 
     def place(self, core):
@@ -815,7 +822,7 @@
             at += 1
     conv_ref, conv_bias_ref, mix_ref, mix_bias_ref, proj_ref, proj_bias_ref = outs[:6]
     codebook_ref, decode_ref, decode_bias_ref = outs[6:]
-    triple = 3 * channels
+    conv_rows = 5 * channels
 
     def copy_all(pairs):
         copies = [
@@ -827,25 +834,27 @@
         for copy in copies:
             copy.wait()
 
-    @pl.when(half == 0)
-    def _():
-        spans = [pl.ds(at, channels) for at in range(0, 2 * triple, channels)]
-        copy_all([(gathered_ref.at[span], conv_ref.at[span]) for span in spans])
-
-    @pl.when(half == 1)
-    def _():
+    def place_all(first, last, targets):
         pairs = []
-        for at in range(0, triple, channels):
-            span = pl.ds(2 * triple + at, channels)
-            pairs.append((gathered_ref.at[pl.ds(at, channels)], conv_ref.at[span]))
-        at = triple
-        targets = [(mix_ref, channels), (proj_ref, size)]
-        for piece in range(0, entries, channels):
-            targets.append((codebook_ref.at[:, pl.ds(piece, channels)], size))
-        targets.append((decode_ref, size))
+        for start in range(first, last, channels):
+            span = pl.ds(start, channels)
+            pairs.append((gathered_ref.at[pl.ds(start - first, channels)], conv_ref.at[span]))
+        at = last - first
         for target, depth in targets:
             pairs.append((gathered_ref.at[pl.ds(at, depth)], target))
             at += depth
+        return pairs, at
+
+    @pl.when(half == 0)
+    def _():
+        copy_all(place_all(0, conv_rows, [(proj_ref, size), (decode_ref, size)])[0])
+
+    @pl.when(half == 1)
+    def _():
+        targets = [(mix_ref, channels)]
+        for piece in range(0, entries, channels):
+            targets.append((codebook_ref.at[:, pl.ds(piece, channels)], size))
+        pairs, at = place_all(conv_rows, 9 * channels, targets)
         lines = gathered_ref[pl.ds(at, tile_rows)]
         targets = (conv_bias_ref, mix_bias_ref, decode_bias_ref, proj_bias_ref)
         for number, (line_ref, target) in enumerate(zip(line_refs, targets, strict=True)):
@@ -1002,9 +1011,8 @@
     parts = add_split([keep, plan.swap(send, plan.core, 1)], plan.half)
     halo = trade(*edges, split=False)
     swaps = [plan.swap(parts[i], plan.split, i) for i in reversed(range(1, plan.half))]
-    latent_grad = input_rows(inner, edges, parts[0])
-    after = far_away(latent_grad)
-    piece = add_split([parts[0], *swaps], 1, after)[0]
+    piece = add_split([parts[0], *swaps], 1)[0]
+    latent_grad = input_rows(inner, edges, piece)
     decoded = call(
         decoded_kernel,
         [in_vmem, in_vmem, in_vmem, anywhere],
@@ -1012,7 +1020,7 @@
         [pltpu.HBM(out_grad.shape, low)],
         flops=4 * total * channels * channels,
     )(term, near_decode, decode_bias, piece)[0]
-    after = far_away(decoded)
+    after = far_away(decoded, latent_grad)
     for stage in plan.whole:
         swaps = [plan.swap(piece, stage, i) for i in range(1, 2 ** len(stage))]
         piece = add_split([piece, *swaps], 1, after)[0]
@@ -1075,8 +1083,8 @@
     def wrapped(*args):
         channels = args[0].shape[3]
         entries, size = args[9].shape
-        others = 4 * channels + 2 * size + size * (entries // channels) + tile_rows
-        plan = Plan(sizes, max(6 * channels, others))
+        others = 5 * channels + size * (entries // channels) + tile_rows
+        plan = Plan(sizes, max(5 * channels + 2 * size, others))
         return jax.shard_map(
             functools.partial(per_device, plan),
             mesh=mesh,

time: 59.9 us -> 58.6 us (0.978)
  waiting for transfers between devices: 7.99 us -> 7.05 us
    ppermute x14, waiting for transfers between devices: 7.97 us -> 7.04 us  [swap(): return lax.ppermute(values, ('strip', 'canvas'), pairs)]
  transfers between devices with their start and end apart: 18 -> 18, of which waited for: 5 -> 2; matrix products, arithmetic and copies ran while one was open for 0% -> 0% of each run, Pallas kernels for 36% -> 37%
where the time goes in v7:
time: 58.6 us; the launch traced here: 58.5 us
  Pallas kernels  28.3 us (48%)
  starting transfers between devices  21.9 us (37%)
  waiting for transfers between devices  7.05 us (12%)
  between operations  1.14 us (2%)
    ppermute x14, starting transfers between devices, swap(): return lax.ppermute(values, ('strip', 'canvas'), pairs)  14.2 us
    pallas_call x2, Pallas kernels, block_rows(): call(functools.partial(rows_kernel, beyond), [in_vmem] * len(ins), [in_vm...  7.51 us
    ppermute x2, starting transfers between devices, trade(): lax.ppermute(other, 'strip', far)  7.5 us
    ppermute x14, waiting for transfers between devices, swap(): return lax.ppermute(values, ('strip', 'canvas'), pairs)  7.04 us
    pallas_call x2, Pallas kernels, input_rows(): call(functools.partial(input_kernel, mine), [in_vmem] * 7 + [anywhere] +...  6.74 us
    pallas_call x2, Pallas kernels, weight_half(): call(functools.partial(weight_kernel, plan, mine), [in_vmem] * len(ins) +...  5.07 us
    pallas_call x1, Pallas kernels, per_device(): call(code_kernel, [in_vmem] * 4 + [in_hbm] * 4, [in_vmem] * 8, outs, held...  3.1 us
    pallas_call x2, Pallas kernels, finish(): call(functools.partial(final_kernel, plan, mine, count, (channels, size,...  2.73 us
  transfers between devices with their start and end apart: 18, of which 2 were waited for; matrix products, arithmetic and copies ran while one was open for 0% of the time, Pallas kernels for 37%

profile of v7, /device:TPU:1, one launch (start us, length us, event | category | flops | bytes accessed | tf_op | source)
XLA Modules:
  0.0 58.5 jit_solution(11619382242201986651)
XLA Ops:
  0.6 1.2 %shard_map.212 = (bf16[4,176,256]{2,1,0:T(8,128)(2,1)S(1)}, bf16[4,176,256]{2,1,0:T(8,128)(2,1)S(1)}, s32[4,4,176]{2,1,0:T(4,128)S(1)}, s32[4,4,176]{2,1,0:T(4,1...) custom-call(bf16[4,4,176,256]{3,2,1,0:T(8,128)(2,1)} %latent_hbm.3, s32[4,4,176]{2,1,0:T(4,128)} %crop_hbm.1, ...), custom_call_target="tpu_custom_call" | custom-call | tf_op jit(solution)/shard_map/pallas_call | solution.py:922
  1.8 0.1 collective-permute-start.1
  1.9 4.5 %collective-permute-start = (bf16[4,176,256]{2,1,0:T(8,128)(2,1)S(1)}, bf16[4,176,256]{2,1,0:T(8,128)(2,1)S(1)}, u32[]{:S(2)}, u32[]{:S(2)}) collective-permute-start(bf16[4,176,256]{2,1,0:T(8,128)(2,1)S(1)} %get-tuple-element.78), channel_id=1, source_target_pairs={{2,4},{6,8},{10,12},{14,16},{18,20},{22,24},{26,28},{4,2},{8,6},{1... | collective-permute-start | bytes 1081352 | tf_op jit(solution)/shard_map/ppermute | solution.py:910
  6.4 0.0 copy-start
  6.5 0.0 copy-start.1
  6.5 0.0 copy-start.2
  6.5 0.0 copy-start.3
  6.5 3.1 %shard_map.213 = (f32[4,704,128]{2,1,0:T(8,128)S(1)}, bf16[2816,512]{1,0:T(8,128)(2,1)S(1)}, bf16[4,2816,128]{2,1,0:T(8,128)(2,1)S(1)}, f32[1,256]{1,0:T(1,128)S...) custom-call(s32[4,4,176]{2,1,0:T(4,128)S(1)} %get-tuple-element.69.c, ...), custom_call_target="tpu_custom_call" | custom-call | flops 1107296256 | tf_op jit(solution)/shard_map/pallas_call | solution.py:941
  9.6 0.0 collective-permute-done.1.halo_ref
  9.7 5.9 %shard_map.214 = (bf16[4224,768]{1,0:T(8,128)(2,1)S(1)}, bf16[2816,256]{1,0:T(8,128)(2,1)S(1)}, bf16[2816,256]{1,0:T(8,128)(2,1)S(1)}, bf16[2816,256]{1,0:T(8,12...) custom-call(bf16[4,2816,128]{2,1,0:T(8,128)(2,1)S(1)} %get-tuple-ele, ...), custom_call_target="tpu_custom_call" | custom-call | flops 3690987520 | tf_op jit(solution)/shard_map/pallas_call | solution.py:966
  15.6 1.6 %shard_map.215 = (bf16[4224,768]{1,0:T(8,128)(2,1)S(1)}, bf16[2816,256]{1,0:T(8,128)(2,1)S(1)}, bf16[2816,256]{1,0:T(8,128)(2,1)S(1)}, bf16[2816,256]{1,0:T(8,12...) custom-call(bf16[4,2816,128]{2,1,0:T(8,128)(2,1)S(1)} %get-tuple-ele, ...), custom_call_target="tpu_custom_call", output_to_operand_aliasing={{0}: (11, {}), {1}: (12, {}), {2}: (13, {}), {3}: (14, {}),... | custom-call | flops 3690987520 | tf_op jit(solution)/shard_map/pallas_call | solution.py:966
  17.2 2.5 %shard_map.216.after_ref = bf16[4,360,256]{2,1,0:T(8,128)(2,1)S(1)} custom-call(bf16[4224,768]{1,0:T(8,128)(2,1)S(1)} %get-tuple-element.91.slab_ref, bf16[2816,256]{1,0:T(8,128)(2,1)S(1)} %get-tuple-element.92.grad_ref, bf16[2816,256]{1,0:T(8,128)(2,1)S(1)} %get-tuple-element.93.up_ref, bf16[2816,256]{1,0:T(8,128)(2,1)S(1)} %get-tuple-element.94.down_ref, ...), custom_call_target="tpu_custom_call" | custom-call | flops 1845493760 | tf_op jit(solution)/shard_map/pallas_call | solution.py:984
  19.7 0.1 collective-permute-start.2
  19.8 2.5 %shard_map.217.refs_0_ = bf16[4,360,256]{2,1,0:T(8,128)(2,1)S(1)} custom-call(bf16[4224,768]{1,0:T(8,128)(2,1)S(1)} %get-tuple-element.91.slab_ref, bf16[2816,256]{1,0:T(8,128)(2,1)S(1)} %get-tuple-element.92.grad_ref, bf16[2816,256]{1,0:T(8,128)(2,1)S(1)} %get-tuple-element.93.up_ref, bf16[2816,256]{1,0:T(8,128)(2,1)S(1)} %get-tuple-element.94.down_ref, ...), custom_call_target="tpu_custom_call" | custom-call | flops 1845493760 | tf_op jit(solution)/shard_map/pallas_call | solution.py:984
  22.4 0.0 copy-start.4
  22.4 0.0 collective-permute-done.2.refs_1_
  22.4 0.2 shard_map.218
  22.6 3.9 %collective-permute-start.3 = (bf16[1,360,256]{2,1,0:T(8,128)(2,1)S(1)}, bf16[1,360,256]{2,1,0:T(8,128)(2,1)S(1)}, u32[]{:S(2)}, u32[]{:S(2)}) collective-permute-start(bf16[1,360,256]{2,1,0:T(8,128)(2,1)S(1)} %get-tuple-element.105), channel_id=1, source_target_pairs={{0,5},{1,4},{2,26},{3,27},{4,1},{5,0},{6,30},{7,31},{8,13},{9,12},... | collective-permute-start | bytes 552968 | tf_op jit(solution)/shard_map/ppermute | solution.py:769
  26.4 0.4 collective-permute-start.5
  26.8 3.0 %collective-permute-start.7 = (bf16[704,256]{1,0:T(8,128)(2,1)S(1)}, bf16[704,256]{1,0:T(8,128)(2,1)S(1)}, u32[]{:S(2)}, u32[]{:S(2)}) collective-permute-start(bf16[704,256]{1,0:T(8,128)(2,1)S(1)} %get-tuple-element.103.after_ref.other_ref), channel_id=1, source_target_pairs={{2,4},{6,8},{10,12},{14,16},{18,20},{22,24},{26,28},{4,2},{8,6},{1... | collective-permute-start | bytes 1081352 | tf_op jit(solution)/shard_map/ppermute | solution.py:910
  29.8 0.1 collective-permute-start.6
  29.9 0.0 collective-permute-done.3.refs_1_
  29.9 6.2 %collective-permute-done.4.refs_2_ = bf16[1,360,256]{2,1,0:T(8,128)(2,1)S(1)} collective-permute-done((bf16[1,360,256]{2,1,0:T(8,128)(2,1)S(1)}, bf16[1,360,256]{2,1,0:T(8,128)(2,1)S(1)}, u32[]{:S(2)}, u32[]{:S(2)}) %collective-permute-start.4) | collective-permute-done | bytes 184352 | tf_op jit(solution)/shard_map/ppermute | solution.py:769
  36.1 0.0 collective-permute-done.5.refs_3_
  36.1 0.1 shard_map.219.after_ref.refs_0_
  36.2 0.6 collective-permute-start.10
  36.8 0.8 %collective-permute-start.9 = (bf16[1,360,256]{2,1,0:T(8,128)(2,1)S(1)}, bf16[1,360,256]{2,1,0:T(8,128)(2,1)S(1)}, u32[]{:S(2)}, u32[]{:S(2)}) collective-permute-start(bf16[1,360,256]{2,1,0:T(8,128)(2,1)S(1)} %shard_map.219.after_ref.refs_0_), channel_id=1, source_target_pairs={{0,16},{1,17},{2,3},{3,2},{4,20},{5,21},{6,7},{7,6},{8,24},{9,25},... | collective-permute-start | bytes 552968 | tf_op jit(solution)/shard_map/ppermute | solution.py:769
  37.6 1.4 %collective-permute-start.8 = (bf16[1,360,256]{2,1,0:T(8,128)(2,1)S(1)}, bf16[1,360,256]{2,1,0:T(8,128)(2,1)S(1)}, u32[]{:S(2)}, u32[]{:S(2)}) collective-permute-start(bf16[1,360,256]{2,1,0:T(8,128)(2,1)S(1)} %shard_map.219.after_ref.refs_0_), channel_id=1, source_target_pairs={{0,8},{1,9},{2,6},{3,7},{4,12},{5,13},{6,2},{7,3},{8,0},{9,1},{10,... | collective-permute-start | bytes 552968 | tf_op jit(solution)/shard_map/ppermute | solution.py:769
  39.0 1.6 %shard_map.220.refs_4_ = bf16[4,4,176,256]{3,2,1,0:T(8,128)(2,1)} custom-call(f32[4,704,128]{2,1,0:T(8,128)S(1)} %get-tuple-element.73.term_ref, bf16[64,256]{1,0:T(8,128)(2,1)S(1)} %get-tuple-element.72.decode_weight_ref, bf16[256]{0:T(256)(128)(2,1)S(1)} %copy-done.4, bf16[1,360,256]{2,1,0:T(8,128)(2,1)S(1)} %shard_map.219.after_ref.refs_0_), custom_call_target="tpu_custom_call" | custom-call | flops 738197504 | tf_op jit(solution)/shard_map/pallas_call | solution.py:1016
  40.6 3.3 %shard_map.221.refs_5_.refs_0_ = bf16[4,4,176,256]{3,2,1,0:T(8,128)(2,1)} custom-call(bf16[4,2816,128]{2,1,0:T(8,128)(2,1)S(1)} %get-tuple-element.74.masks_ref, bf16[4,4,176,256]{3,2,1,0:T(8,128)(2,1)S(1)} %get-tuple-element.75.latent_ref, bf16[2816,256]{1,0:T(8,128)(2,1)S(1)} %get-tuple-element.92.grad_ref, ...), custom_call_target="tpu_custom_call" | custom-call | flops 2030043136 | tf_op jit(solution)/shard_map/pallas_call | solution.py:996
  43.9 0.0 collective-permute-done.8.refs_1_
  43.9 0.1 shard_map.222.after_ref.refs_0_
  44.0 2.7 %collective-permute-start.16 = (bf16[1,360,256]{2,1,0:T(8,128)(2,1)S(1)}, bf16[1,360,256]{2,1,0:T(8,128)(2,1)S(1)}, u32[]{:S(2)}, u32[]{:S(2)}) collective-permute-start(bf16[1,360,256]{2,1,0:T(8,128)(2,1)S(1)} %shard_map.222.after_ref.refs_0_), channel_id=1, source_target_pairs={{0,5},{1,4},{2,26},{3,27},{4,1},{5,0},{6,30},{7,31},{8,13},{9,12},... | collective-permute-start | bytes 552968 | tf_op jit(solution)/shard_map/ppermute | solution.py:769
  46.7 0.0 collective-permute-start.14
  46.7 0.9 %collective-permute-start.12 = (bf16[1,360,256]{2,1,0:T(8,128)(2,1)S(1)}, bf16[1,360,256]{2,1,0:T(8,128)(2,1)S(1)}, u32[]{:S(2)}, u32[]{:S(2)}) collective-permute-start(bf16[1,360,256]{2,1,0:T(8,128)(2,1)S(1)} %shard_map.222.after_ref.refs_0_), channel_id=1, source_target_pairs={{0,4},{1,5},{2,10},{3,11},{4,0},{5,1},{6,14},{7,15},{8,12},{9,13},... | collective-permute-start | bytes 552968 | tf_op jit(solution)/shard_map/ppermute | solution.py:769
  47.6 3.0 %collective-permute-start.11 = (bf16[1,360,256]{2,1,0:T(8,128)(2,1)S(1)}, bf16[1,360,256]{2,1,0:T(8,128)(2,1)S(1)}, u32[]{:S(2)}, u32[]{:S(2)}) collective-permute-start(bf16[1,360,256]{2,1,0:T(8,128)(2,1)S(1)} %shard_map.222.after_ref.refs_0_), channel_id=1, source_target_pairs={{0,2},{1,3},{2,0},{3,1},{4,6},{5,7},{6,4},{7,5},{8,10},{9,11},{10,... | collective-permute-start | bytes 552968 | tf_op jit(solution)/shard_map/ppermute | solution.py:769
  50.6 0.0 collective-permute-done.6.mate_ref
  50.6 3.5 %shard_map.223.refs_1_ = bf16[4,4,176,256]{3,2,1,0:T(8,128)(2,1)} custom-call(bf16[4,2816,128]{2,1,0:T(8,128)(2,1)S(1)} %get-tuple-element.74.masks_ref, bf16[4,4,176,256]{3,2,1,0:T(8,128)(2,1)S(1)} %get-tuple-element.75.latent_ref, bf16[2816,256]{1,0:T(8,128)(2,1)S(1)} %get-tuple-element.92.grad_ref, ...), custom_call_target="tpu_custom_call", output_to_operand_aliasing={{}: (8, {})} | custom-call | flops 2030043136 | tf_op jit(solution)/shard_map/pallas_call | solution.py:996
  54.1 0.0 collective-permute-done.16.refs_0_
  54.1 0.1 collective-permute-start.17
  54.2 0.8 %collective-permute-done.14.refs_0_ = bf16[1,360,256]{2,1,0:T(8,128)(2,1)S(1)} collective-permute-done((bf16[1,360,256]{2,1,0:T(8,128)(2,1)S(1)}, bf16[1,360,256]{2,1,0:T(8,128)(2,1)S(1)}, u32[]{:S(2)}, u32[]{:S(2)}) %collective-permute-start.14) | collective-permute-done | bytes 184352 | tf_op jit(solution)/shard_map/ppermute | solution.py:769
  54.9 0.0 collective-permute-start.15
  54.9 0.0 collective-permute-done.12.refs_0_
  54.9 0.6 collective-permute-start.13
  55.5 1.4 %shard_map.227 = (f32[2304,256]{1,0:T(8,128)}, f32[1,256]{1,0:T(1,128)}, f32[256,256]{1,0:T(8,128)}, f32[1,256]{1,0:T(1,128)}, f32[64,256]{1,0:T(8,128)}, /*inde...) custom-call(bf16[1,360,256]{2,1,0:T(8,128)(2,1)S(1)} %shard_map.222.after_ref.refs_0_, ...), custom_call_target="tpu_custom_call" | custom-call | tf_op jit(solution)/shard_map/pallas_call | solution.py:1047
  56.9 0.0 collective-permute-done.17.refs_3_
  56.9 0.0 collective-permute-done.15.refs_2_
  56.9 1.4 %shard_map.228 = (f32[2304,256]{1,0:T(8,128)}, f32[1,256]{1,0:T(1,128)}, f32[256,256]{1,0:T(8,128)}, f32[1,256]{1,0:T(1,128)}, f32[64,256]{1,0:T(8,128)}, /*inde...) custom-call(bf16[1,360,256]{2,1,0:T(8,128)(2,1)S(1)} %collective-per, ...), custom_call_target="tpu_custom_call", output_to_operand_aliasing={{0}: (4, {}), {1}: (5, {}), {2}: (6, {}), {3}: (7, {}), {4}... | custom-call | tf_op jit(solution)/shard_map/pallas_call | solution.py:1047
  (15 shorter events, 0.0 us)
Async XLA Ops:
  1.8 7.8 %collective-permute-start.1 = (bf16[4,176,256]{2,1,0:T(8,128)(2,1)S(1)}, bf16[4,176,256]{2,1,0:T(8,128)(2,1)S(1)}, u32[]{:S(2)}, u32[]{:S(2)}) collective-permute-start(bf16[4,176,256]{2,1,0:T(8,128)(2,1)S(1)} %get-tuple-element.79), channel_id=1, source_target_pairs={{0,2},{2,0},{4,6},{6,4},{8,10},{10,8},{12,14},{14,12},{16,18},{18,... | collective-permute-start | bytes 1081352 | tf_op jit(solution)/shard_map/ppermute | solution.py:910
  1.9 13.7 %collective-permute-start = (bf16[4,176,256]{2,1,0:T(8,128)(2,1)S(1)}, bf16[4,176,256]{2,1,0:T(8,128)(2,1)S(1)}, u32[]{:S(2)}, u32[]{:S(2)}) collective-permute-start(bf16[4,176,256]{2,1,0:T(8,128)(2,1)S(1)} %get-tuple-element.78), channel_id=1, source_target_pairs={{2,4},{6,8},{10,12},{14,16},{18,20},{22,24},{26,28},{4,2},{8,6},{1... | collective-permute-start | bytes 1081352 | tf_op jit(solution)/shard_map/ppermute | solution.py:910
  6.4 3.2 %copy-start = (bf16[256,64]{0,1:T(8,128)(2,1)S(1)}, bf16[256,64]{0,1:T(8,128)(2,1)}, u32[]{:S(2)}) copy-start(bf16[256,64]{0,1:T(8,128)(2,1)} %param.20) | copy-start | bytes 98308
  6.5 3.2 %copy-start.1 = (bf16[256]{0:T(256)(128)(2,1)S(1)}, bf16[256]{0:T(256)(128)(2,1)}, u32[]{:S(2)}) copy-start(bf16[256]{0:T(256)(128)(2,1)} %conv_bias_ref.3) | copy-start | bytes 1540
  6.5 3.2 %copy-start.2 = (bf16[256]{0:T(256)(128)(2,1)S(1)}, bf16[256]{0:T(256)(128)(2,1)}, u32[]{:S(2)}) copy-start(bf16[256]{0:T(256)(128)(2,1)} %mix_bias_ref.3) | copy-start | bytes 1540
  6.5 3.2 %copy-start.3 = (bf16[64]{0:T(256)(128)(2,1)S(1)}, bf16[64]{0:T(256)(128)(2,1)}, u32[]{:S(2)}) copy-start(bf16[64]{0:T(256)(128)(2,1)} %proj_bias_ref.3) | copy-start | bytes 388
  19.7 2.6 %collective-permute-start.2 = (bf16[4,360,256]{2,1,0:T(8,128)(2,1)S(1)}, bf16[4,360,256]{2,1,0:T(8,128)(2,1)S(1)}, u32[]{:S(2)}, u32[]{:S(2)}) collective-permute-start(bf16[4,360,256]{2,1,0:T(8,128)(2,1)S(1)} %shard_map.216.after_ref), channel_id=1, source_target_pairs={{0,2},{1,3},{2,0},{3,1},{4,6},{5,7},{6,4},{7,5},{8,10},{9,11},{10,... | collective-permute-start | bytes 2211848 | tf_op jit(solution)/shard_map/ppermute | solution.py:769
  22.4 16.6 %copy-start.4 = (bf16[256]{0:T(256)(128)(2,1)S(1)}, bf16[256]{0:T(256)(128)(2,1)}, u32[]{:S(2)}) copy-start(bf16[256]{0:T(256)(128)(2,1)} %decode_bias_ref.1) | copy-start | bytes 1540
  22.6 7.3 %collective-permute-start.3 = (bf16[1,360,256]{2,1,0:T(8,128)(2,1)S(1)}, bf16[1,360,256]{2,1,0:T(8,128)(2,1)S(1)}, u32[]{:S(2)}, u32[]{:S(2)}) collective-permute-start(bf16[1,360,256]{2,1,0:T(8,128)(2,1)S(1)} %get-tuple-element.105), channel_id=1, source_target_pairs={{0,5},{1,4},{2,26},{3,27},{4,1},{5,0},{6,30},{7,31},{8,13},{9,12},... | collective-permute-start | bytes 552968 | tf_op jit(solution)/shard_map/ppermute | solution.py:769
  26.4 9.7 %collective-permute-start.4 = (bf16[1,360,256]{2,1,0:T(8,128)(2,1)S(1)}, bf16[1,360,256]{2,1,0:T(8,128)(2,1)S(1)}, u32[]{:S(2)}, u32[]{:S(2)}) collective-permute-start(bf16[1,360,256]{2,1,0:T(8,128)(2,1)S(1)} %get-tuple-element.106), channel_id=1, source_target_pairs={{0,1},{1,0},{2,18},{3,19},{4,5},{5,4},{6,22},{7,23},{8,9},{9,8},{1... | collective-permute-start | bytes 552968 | tf_op jit(solution)/shard_map/ppermute | solution.py:769
  26.4 9.7 %collective-permute-start.5 = (bf16[1,360,256]{2,1,0:T(8,128)(2,1)S(1)}, bf16[1,360,256]{2,1,0:T(8,128)(2,1)S(1)}, u32[]{:S(2)}, u32[]{:S(2)}) collective-permute-start(bf16[1,360,256]{2,1,0:T(8,128)(2,1)S(1)} %get-tuple-element.107), channel_id=1, source_target_pairs={{0,4},{1,5},{2,10},{3,11},{4,0},{5,1},{6,14},{7,15},{8,12},{9,13},... | collective-permute-start | bytes 552968 | tf_op jit(solution)/shard_map/ppermute | solution.py:769
  26.8 20.8 %collective-permute-start.7 = (bf16[704,256]{1,0:T(8,128)(2,1)S(1)}, bf16[704,256]{1,0:T(8,128)(2,1)S(1)}, u32[]{:S(2)}, u32[]{:S(2)}) collective-permute-start(bf16[704,256]{1,0:T(8,128)(2,1)S(1)} %get-tuple-element.103.after_ref.other_ref), channel_id=1, source_target_pairs={{2,4},{6,8},{10,12},{14,16},{18,20},{22,24},{26,28},{4,2},{8,6},{1... | collective-permute-start | bytes 1081352 | tf_op jit(solution)/shard_map/ppermute | solution.py:910
  29.8 20.8 %collective-permute-start.6 = (bf16[704,256]{1,0:T(8,128)(2,1)S(1)}, bf16[704,256]{1,0:T(8,128)(2,1)S(1)}, u32[]{:S(2)}, u32[]{:S(2)}) collective-permute-start(bf16[704,256]{1,0:T(8,128)(2,1)S(1)} %get-tuple-element.108.mate_ref), channel_id=1, source_target_pairs={{0,2},{2,0},{4,6},{6,4},{8,10},{10,8},{12,14},{14,12},{16,18},{18,... | collective-permute-start | bytes 1081352 | tf_op jit(solution)/shard_map/ppermute | solution.py:910
  36.2 7.6 %collective-permute-start.10 = (bf16[1,360,256]{2,1,0:T(8,128)(2,1)S(1)}, bf16[1,360,256]{2,1,0:T(8,128)(2,1)S(1)}, u32[]{:S(2)}, u32[]{:S(2)}) collective-permute-start(bf16[1,360,256]{2,1,0:T(8,128)(2,1)S(1)} %shard_map.219.after_ref.refs_0_), channel_id=1, source_target_pairs={{0,24},{1,25},{2,7},{3,6},{4,28},{5,29},{6,3},{7,2},{8,16},{9,17},... | collective-permute-start | bytes 552968 | tf_op jit(solution)/shard_map/ppermute | solution.py:769
  36.8 7.1 %collective-permute-start.9 = (bf16[1,360,256]{2,1,0:T(8,128)(2,1)S(1)}, bf16[1,360,256]{2,1,0:T(8,128)(2,1)S(1)}, u32[]{:S(2)}, u32[]{:S(2)}) collective-permute-start(bf16[1,360,256]{2,1,0:T(8,128)(2,1)S(1)} %shard_map.219.after_ref.refs_0_), channel_id=1, source_target_pairs={{0,16},{1,17},{2,3},{3,2},{4,20},{5,21},{6,7},{7,6},{8,24},{9,25},... | collective-permute-start | bytes 552968 | tf_op jit(solution)/shard_map/ppermute | solution.py:769
  37.6 6.3 %collective-permute-start.8 = (bf16[1,360,256]{2,1,0:T(8,128)(2,1)S(1)}, bf16[1,360,256]{2,1,0:T(8,128)(2,1)S(1)}, u32[]{:S(2)}, u32[]{:S(2)}) collective-permute-start(bf16[1,360,256]{2,1,0:T(8,128)(2,1)S(1)} %shard_map.219.after_ref.refs_0_), channel_id=1, source_target_pairs={{0,8},{1,9},{2,6},{3,7},{4,12},{5,13},{6,2},{7,3},{8,0},{9,1},{10,... | collective-permute-start | bytes 552968 | tf_op jit(solution)/shard_map/ppermute | solution.py:769
  44.0 10.1 %collective-permute-start.16 = (bf16[1,360,256]{2,1,0:T(8,128)(2,1)S(1)}, bf16[1,360,256]{2,1,0:T(8,128)(2,1)S(1)}, u32[]{:S(2)}, u32[]{:S(2)}) collective-permute-start(bf16[1,360,256]{2,1,0:T(8,128)(2,1)S(1)} %shard_map.222.after_ref.refs_0_), channel_id=1, source_target_pairs={{0,5},{1,4},{2,26},{3,27},{4,1},{5,0},{6,30},{7,31},{8,13},{9,12},... | collective-permute-start | bytes 552968 | tf_op jit(solution)/shard_map/ppermute | solution.py:769
  46.7 8.2 %collective-permute-start.14 = (bf16[1,360,256]{2,1,0:T(8,128)(2,1)S(1)}, bf16[1,360,256]{2,1,0:T(8,128)(2,1)S(1)}, u32[]{:S(2)}, u32[]{:S(2)}) collective-permute-start(bf16[1,360,256]{2,1,0:T(8,128)(2,1)S(1)} %shard_map.222.after_ref.refs_0_), channel_id=1, source_target_pairs={{0,1},{1,0},{2,18},{3,19},{4,5},{5,4},{6,22},{7,23},{8,9},{9,8},{1... | collective-permute-start | bytes 552968 | tf_op jit(solution)/shard_map/ppermute | solution.py:769
  46.7 8.2 %collective-permute-start.12 = (bf16[1,360,256]{2,1,0:T(8,128)(2,1)S(1)}, bf16[1,360,256]{2,1,0:T(8,128)(2,1)S(1)}, u32[]{:S(2)}, u32[]{:S(2)}) collective-permute-start(bf16[1,360,256]{2,1,0:T(8,128)(2,1)S(1)} %shard_map.222.after_ref.refs_0_), channel_id=1, source_target_pairs={{0,4},{1,5},{2,10},{3,11},{4,0},{5,1},{6,14},{7,15},{8,12},{9,13},... | collective-permute-start | bytes 552968 | tf_op jit(solution)/shard_map/ppermute | solution.py:769
  47.6 9.3 %collective-permute-start.11 = (bf16[1,360,256]{2,1,0:T(8,128)(2,1)S(1)}, bf16[1,360,256]{2,1,0:T(8,128)(2,1)S(1)}, u32[]{:S(2)}, u32[]{:S(2)}) collective-permute-start(bf16[1,360,256]{2,1,0:T(8,128)(2,1)S(1)} %shard_map.222.after_ref.refs_0_), channel_id=1, source_target_pairs={{0,2},{1,3},{2,0},{3,1},{4,6},{5,7},{6,4},{7,5},{8,10},{9,11},{10,... | collective-permute-start | bytes 552968 | tf_op jit(solution)/shard_map/ppermute | solution.py:769
  54.1 2.8 %collective-permute-start.17 = (bf16[1,360,256]{2,1,0:T(8,128)(2,1)S(1)}, bf16[1,360,256]{2,1,0:T(8,128)(2,1)S(1)}, u32[]{:S(2)}, u32[]{:S(2)}) collective-permute-start(bf16[1,360,256]{2,1,0:T(8,128)(2,1)S(1)} %shard_map.226.refs_3_), channel_id=1, source_target_pairs={{0,2},{1,3},{2,0},{3,1},{4,6},{5,7},{6,4},{7,5},{8,10},{9,11},{10,... | collective-permute-start | bytes 552968 | tf_op jit(solution)/shard_map/ppermute | solution.py:769
  54.9 2.0 %collective-permute-start.15 = (bf16[1,360,256]{2,1,0:T(8,128)(2,1)S(1)}, bf16[1,360,256]{2,1,0:T(8,128)(2,1)S(1)}, u32[]{:S(2)}, u32[]{:S(2)}) collective-permute-start(bf16[1,360,256]{2,1,0:T(8,128)(2,1)S(1)} %shard_map.225.refs_2_), channel_id=1, source_target_pairs={{0,2},{1,3},{2,0},{3,1},{4,6},{5,7},{6,4},{7,5},{8,10},{9,11},{10,... | collective-permute-start | bytes 552968 | tf_op jit(solution)/shard_map/ppermute | solution.py:769
  54.9 2.0 %collective-permute-start.13 = (bf16[1,360,256]{2,1,0:T(8,128)(2,1)S(1)}, bf16[1,360,256]{2,1,0:T(8,128)(2,1)S(1)}, u32[]{:S(2)}, u32[]{:S(2)}) collective-permute-start(bf16[1,360,256]{2,1,0:T(8,128)(2,1)S(1)} %shard_map.224.refs_1_), channel_id=1, source_target_pairs={{0,2},{1,3},{2,0},{3,1},{4,6},{5,7},{6,4},{7,5},{8,10},{9,11},{10,... | collective-permute-start | bytes 552968 | tf_op jit(solution)/shard_map/ppermute | solution.py:769

commit v8 on v7

--- a/solution.py
+++ b/solution.py
@@ -13,7 +13,7 @@
 bits = (1, 3, 4, 6)
 up_plane, left_plane, right_plane, down_plane = range(4)
 tile_rows = 16
-half_tile = 8
+half_tile = 16
 vmem_bytes = 20 * 2**20
 in_hbm = pl.BlockSpec(memory_space=pltpu.HBM)
 anywhere = pl.BlockSpec(memory_space=pl.ANY)

time: 58.6 us -> 59.1 us (level)
  no operation moved by 1% of the time
where the time goes in v8:
time: 59.1 us; the launch traced here: 58.9 us
  Pallas kernels  28.4 us (48%)
  starting transfers between devices  22 us (37%)
  waiting for transfers between devices  7.37 us (12%)
  between operations  1.14 us (2%)
    ppermute x14, starting transfers between devices, swap(): return lax.ppermute(values, ('strip', 'canvas'), pairs)  14.3 us
    pallas_call x2, Pallas kernels, block_rows(): call(functools.partial(rows_kernel, beyond), [in_vmem] * len(ins), [in_vm...  7.53 us
    ppermute x2, starting transfers between devices, trade(): lax.ppermute(other, 'strip', far)  7.48 us
    ppermute x14, waiting for transfers between devices, swap(): return lax.ppermute(values, ('strip', 'canvas'), pairs)  7.36 us
    pallas_call x2, Pallas kernels, input_rows(): call(functools.partial(input_kernel, mine), [in_vmem] * 7 + [anywhere] +...  6.74 us
    pallas_call x2, Pallas kernels, weight_half(): call(functools.partial(weight_kernel, plan, mine), [in_vmem] * len(ins) +...  5.09 us
    pallas_call x1, Pallas kernels, per_device(): call(code_kernel, [in_vmem] * 4 + [in_hbm] * 4, [in_vmem] * 8, outs, held...  3.11 us
    pallas_call x2, Pallas kernels, finish(): call(functools.partial(final_kernel, plan, mine, count, (channels, size,...  2.74 us
  transfers between devices with their start and end apart: 18, of which 2 were waited for; matrix products, arithmetic and copies ran while one was open for 0% of the time, Pallas kernels for 37%

profile of v8, /device:TPU:1, one launch (start us, length us, event | category | flops | bytes accessed | tf_op | source)
XLA Modules:
  0.0 58.9 jit_solution(7990099001149255315)
XLA Ops:
  0.6 1.2 %shard_map.212 = (bf16[4,176,256]{2,1,0:T(8,128)(2,1)S(1)}, bf16[4,176,256]{2,1,0:T(8,128)(2,1)S(1)}, s32[4,4,176]{2,1,0:T(4,128)S(1)}, s32[4,4,176]{2,1,0:T(4,1...) custom-call(bf16[4,4,176,256]{3,2,1,0:T(8,128)(2,1)} %latent_hbm.3, s32[4,4,176]{2,1,0:T(4,128)} %crop_hbm.1, ...), custom_call_target="tpu_custom_call" | custom-call | tf_op jit(solution)/shard_map/pallas_call | solution.py:922
  1.8 0.1 collective-permute-start.1
  1.9 4.5 %collective-permute-start = (bf16[4,176,256]{2,1,0:T(8,128)(2,1)S(1)}, bf16[4,176,256]{2,1,0:T(8,128)(2,1)S(1)}, u32[]{:S(2)}, u32[]{:S(2)}) collective-permute-start(bf16[4,176,256]{2,1,0:T(8,128)(2,1)S(1)} %get-tuple-element.78), channel_id=1, source_target_pairs={{2,4},{6,8},{10,12},{14,16},{18,20},{22,24},{26,28},{4,2},{8,6},{1... | collective-permute-start | bytes 1081352 | tf_op jit(solution)/shard_map/ppermute | solution.py:910
  6.4 0.0 copy-start
  6.5 0.0 copy-start.1
  6.5 0.0 copy-start.2
  6.5 0.0 copy-start.3
  6.5 3.1 %shard_map.213 = (f32[4,704,128]{2,1,0:T(8,128)S(1)}, bf16[2816,512]{1,0:T(8,128)(2,1)S(1)}, bf16[4,2816,128]{2,1,0:T(8,128)(2,1)S(1)}, f32[1,256]{1,0:T(1,128)S...) custom-call(s32[4,4,176]{2,1,0:T(4,128)S(1)} %get-tuple-element.69.c, ...), custom_call_target="tpu_custom_call" | custom-call | flops 1107296256 | tf_op jit(solution)/shard_map/pallas_call | solution.py:941
  9.6 0.0 collective-permute-done.1.halo_ref
  9.7 5.9 %shard_map.214 = (bf16[4224,768]{1,0:T(8,128)(2,1)S(1)}, bf16[2816,256]{1,0:T(8,128)(2,1)S(1)}, bf16[2816,256]{1,0:T(8,128)(2,1)S(1)}, bf16[2816,256]{1,0:T(8,12...) custom-call(bf16[4,2816,128]{2,1,0:T(8,128)(2,1)S(1)} %get-tuple-ele, ...), custom_call_target="tpu_custom_call" | custom-call | flops 3690987520 | tf_op jit(solution)/shard_map/pallas_call | solution.py:966
  15.6 0.0 collective-permute-done.halo_ref
  15.6 1.6 %shard_map.215 = (bf16[4224,768]{1,0:T(8,128)(2,1)S(1)}, bf16[2816,256]{1,0:T(8,128)(2,1)S(1)}, bf16[2816,256]{1,0:T(8,128)(2,1)S(1)}, bf16[2816,256]{1,0:T(8,12...) custom-call(bf16[4,2816,128]{2,1,0:T(8,128)(2,1)S(1)} %get-tuple-ele, ...), custom_call_target="tpu_custom_call", output_to_operand_aliasing={{0}: (11, {}), {1}: (12, {}), {2}: (13, {}), {3}: (14, {}),... | custom-call | flops 3690987520 | tf_op jit(solution)/shard_map/pallas_call | solution.py:966
  17.2 2.6 %shard_map.216.after_ref = bf16[4,368,256]{2,1,0:T(8,128)(2,1)S(1)} custom-call(bf16[4224,768]{1,0:T(8,128)(2,1)S(1)} %get-tuple-element.91.slab_ref, bf16[2816,256]{1,0:T(8,128)(2,1)S(1)} %get-tuple-element.92.grad_ref, bf16[2816,256]{1,0:T(8,128)(2,1)S(1)} %get-tuple-element.93.up_ref, bf16[2816,256]{1,0:T(8,128)(2,1)S(1)} %get-tuple-element.94.down_ref, ...), custom_call_target="tpu_custom_call" | custom-call | flops 1845493760 | tf_op jit(solution)/shard_map/pallas_call | solution.py:984
  19.8 0.1 collective-permute-start.2
  19.9 2.5 %shard_map.217.refs_0_ = bf16[4,368,256]{2,1,0:T(8,128)(2,1)S(1)} custom-call(bf16[4224,768]{1,0:T(8,128)(2,1)S(1)} %get-tuple-element.91.slab_ref, bf16[2816,256]{1,0:T(8,128)(2,1)S(1)} %get-tuple-element.92.grad_ref, bf16[2816,256]{1,0:T(8,128)(2,1)S(1)} %get-tuple-element.93.up_ref, bf16[2816,256]{1,0:T(8,128)(2,1)S(1)} %get-tuple-element.94.down_ref, ...), custom_call_target="tpu_custom_call" | custom-call | flops 1845493760 | tf_op jit(solution)/shard_map/pallas_call | solution.py:984
  22.4 0.0 copy-start.4
  22.4 0.0 collective-permute-done.2.refs_1_
  22.4 0.2 shard_map.218
  22.6 3.8 %collective-permute-start.3 = (bf16[1,368,256]{2,1,0:T(8,128)(2,1)S(1)}, bf16[1,368,256]{2,1,0:T(8,128)(2,1)S(1)}, u32[]{:S(2)}, u32[]{:S(2)}) collective-permute-start(bf16[1,368,256]{2,1,0:T(8,128)(2,1)S(1)} %get-tuple-element.105), channel_id=1, source_target_pairs={{0,5},{1,4},{2,26},{3,27},{4,1},{5,0},{6,30},{7,31},{8,13},{9,12},... | collective-permute-start | bytes 565256 | tf_op jit(solution)/shard_map/ppermute | solution.py:769
  26.4 0.0 collective-permute-start.4
  26.4 0.4 collective-permute-start.5
  26.8 3.0 %collective-permute-start.7 = (bf16[704,256]{1,0:T(8,128)(2,1)S(1)}, bf16[704,256]{1,0:T(8,128)(2,1)S(1)}, u32[]{:S(2)}, u32[]{:S(2)}) collective-permute-start(bf16[704,256]{1,0:T(8,128)(2,1)S(1)} %get-tuple-element.103.after_ref.other_ref), channel_id=1, source_target_pairs={{2,4},{6,8},{10,12},{14,16},{18,20},{22,24},{26,28},{4,2},{8,6},{1... | collective-permute-start | bytes 1081352 | tf_op jit(solution)/shard_map/ppermute | solution.py:910
  29.8 0.1 collective-permute-start.6
  29.9 0.0 collective-permute-done.3.refs_1_
  29.9 6.7 %collective-permute-done.4.refs_2_ = bf16[1,368,256]{2,1,0:T(8,128)(2,1)S(1)} collective-permute-done((bf16[1,368,256]{2,1,0:T(8,128)(2,1)S(1)}, bf16[1,368,256]{2,1,0:T(8,128)(2,1)S(1)}, u32[]{:S(2)}, u32[]{:S(2)}) %collective-permute-start.4) | collective-permute-done | bytes 188448 | tf_op jit(solution)/shard_map/ppermute | solution.py:769
  36.5 0.1 shard_map.219.after_ref.refs_0_
  36.6 0.3 collective-permute-start.10
  37.0 1.0 %collective-permute-start.9 = (bf16[1,368,256]{2,1,0:T(8,128)(2,1)S(1)}, bf16[1,368,256]{2,1,0:T(8,128)(2,1)S(1)}, u32[]{:S(2)}, u32[]{:S(2)}) collective-permute-start(bf16[1,368,256]{2,1,0:T(8,128)(2,1)S(1)} %shard_map.219.after_ref.refs_0_), channel_id=1, source_target_pairs={{0,16},{1,17},{2,3},{3,2},{4,20},{5,21},{6,7},{7,6},{8,24},{9,25},... | collective-permute-start | bytes 565256 | tf_op jit(solution)/shard_map/ppermute | solution.py:769
  38.0 1.4 %collective-permute-start.8 = (bf16[1,368,256]{2,1,0:T(8,128)(2,1)S(1)}, bf16[1,368,256]{2,1,0:T(8,128)(2,1)S(1)}, u32[]{:S(2)}, u32[]{:S(2)}) collective-permute-start(bf16[1,368,256]{2,1,0:T(8,128)(2,1)S(1)} %shard_map.219.after_ref.refs_0_), channel_id=1, source_target_pairs={{0,8},{1,9},{2,6},{3,7},{4,12},{5,13},{6,2},{7,3},{8,0},{9,1},{10,... | collective-permute-start | bytes 565256 | tf_op jit(solution)/shard_map/ppermute | solution.py:769
  39.3 1.6 %shard_map.220.refs_4_ = bf16[4,4,176,256]{3,2,1,0:T(8,128)(2,1)} custom-call(f32[4,704,128]{2,1,0:T(8,128)S(1)} %get-tuple-element.73.term_ref, bf16[64,256]{1,0:T(8,128)(2,1)S(1)} %get-tuple-element.72.decode_weight_ref, bf16[256]{0:T(256)(128)(2,1)S(1)} %copy-done.4, bf16[1,368,256]{2,1,0:T(8,128)(2,1)S(1)} %shard_map.219.after_ref.refs_0_), custom_call_target="tpu_custom_call" | custom-call | flops 738197504 | tf_op jit(solution)/shard_map/pallas_call | solution.py:1016
  41.0 3.3 %shard_map.221.refs_5_.refs_0_ = bf16[4,4,176,256]{3,2,1,0:T(8,128)(2,1)} custom-call(bf16[4,2816,128]{2,1,0:T(8,128)(2,1)S(1)} %get-tuple-element.74.masks_ref, bf16[4,4,176,256]{3,2,1,0:T(8,128)(2,1)S(1)} %get-tuple-element.75.latent_ref, bf16[2816,256]{1,0:T(8,128)(2,1)S(1)} %get-tuple-element.92.grad_ref, ...), custom_call_target="tpu_custom_call" | custom-call | flops 2030043136 | tf_op jit(solution)/shard_map/pallas_call | solution.py:996
  44.2 0.0 collective-permute-done.10.refs_3_
  44.3 0.0 collective-permute-done.9.refs_2_
  44.3 0.1 shard_map.222.after_ref.refs_0_
  44.4 2.4 %collective-permute-start.16 = (bf16[1,368,256]{2,1,0:T(8,128)(2,1)S(1)}, bf16[1,368,256]{2,1,0:T(8,128)(2,1)S(1)}, u32[]{:S(2)}, u32[]{:S(2)}) collective-permute-start(bf16[1,368,256]{2,1,0:T(8,128)(2,1)S(1)} %shard_map.222.after_ref.refs_0_), channel_id=1, source_target_pairs={{0,5},{1,4},{2,26},{3,27},{4,1},{5,0},{6,30},{7,31},{8,13},{9,12},... | collective-permute-start | bytes 565256 | tf_op jit(solution)/shard_map/ppermute | solution.py:769
  46.8 0.0 collective-permute-start.14
  46.8 1.2 %collective-permute-start.12 = (bf16[1,368,256]{2,1,0:T(8,128)(2,1)S(1)}, bf16[1,368,256]{2,1,0:T(8,128)(2,1)S(1)}, u32[]{:S(2)}, u32[]{:S(2)}) collective-permute-start(bf16[1,368,256]{2,1,0:T(8,128)(2,1)S(1)} %shard_map.222.after_ref.refs_0_), channel_id=1, source_target_pairs={{0,4},{1,5},{2,10},{3,11},{4,0},{5,1},{6,14},{7,15},{8,12},{9,13},... | collective-permute-start | bytes 565256 | tf_op jit(solution)/shard_map/ppermute | solution.py:769
  48.0 0.0 collective-permute-done.7.other_ref
  48.0 2.9 %collective-permute-start.11 = (bf16[1,368,256]{2,1,0:T(8,128)(2,1)S(1)}, bf16[1,368,256]{2,1,0:T(8,128)(2,1)S(1)}, u32[]{:S(2)}, u32[]{:S(2)}) collective-permute-start(bf16[1,368,256]{2,1,0:T(8,128)(2,1)S(1)} %shard_map.222.after_ref.refs_0_), channel_id=1, source_target_pairs={{0,2},{1,3},{2,0},{3,1},{4,6},{5,7},{6,4},{7,5},{8,10},{9,11},{10,... | collective-permute-start | bytes 565256 | tf_op jit(solution)/shard_map/ppermute | solution.py:769
  51.0 3.5 %shard_map.223.refs_1_ = bf16[4,4,176,256]{3,2,1,0:T(8,128)(2,1)} custom-call(bf16[4,2816,128]{2,1,0:T(8,128)(2,1)S(1)} %get-tuple-element.74.masks_ref, bf16[4,4,176,256]{3,2,1,0:T(8,128)(2,1)S(1)} %get-tuple-element.75.latent_ref, bf16[2816,256]{1,0:T(8,128)(2,1)S(1)} %get-tuple-element.92.grad_ref, ...), custom_call_target="tpu_custom_call", output_to_operand_aliasing={{}: (8, {})} | custom-call | flops 2030043136 | tf_op jit(solution)/shard_map/pallas_call | solution.py:996
  54.4 0.0 collective-permute-done.16.refs_0_
  54.4 0.1 collective-permute-start.17
  54.5 0.7 %collective-permute-done.14.refs_0_ = bf16[1,368,256]{2,1,0:T(8,128)(2,1)S(1)} collective-permute-done((bf16[1,368,256]{2,1,0:T(8,128)(2,1)S(1)}, bf16[1,368,256]{2,1,0:T(8,128)(2,1)S(1)}, u32[]{:S(2)}, u32[]{:S(2)}) %collective-permute-start.14) | collective-permute-done | bytes 188448 | tf_op jit(solution)/shard_map/ppermute | solution.py:769
  55.2 0.7 %collective-permute-start.13 = (bf16[1,368,256]{2,1,0:T(8,128)(2,1)S(1)}, bf16[1,368,256]{2,1,0:T(8,128)(2,1)S(1)}, u32[]{:S(2)}, u32[]{:S(2)}) collective-permute-start(bf16[1,368,256]{2,1,0:T(8,128)(2,1)S(1)} %shard_map.224.refs_1_), channel_id=1, source_target_pairs={{0,2},{1,3},{2,0},{3,1},{4,6},{5,7},{6,4},{7,5},{8,10},{9,11},{10,... | collective-permute-start | bytes 565256 | tf_op jit(solution)/shard_map/ppermute | solution.py:769
  56.0 1.4 %shard_map.227 = (f32[2304,256]{1,0:T(8,128)}, f32[1,256]{1,0:T(1,128)}, f32[256,256]{1,0:T(8,128)}, f32[1,256]{1,0:T(1,128)}, f32[64,256]{1,0:T(8,128)}, /*inde...) custom-call(bf16[1,368,256]{2,1,0:T(8,128)(2,1)S(1)} %shard_map.222.after_ref.refs_0_, ...), custom_call_target="tpu_custom_call" | custom-call | tf_op jit(solution)/shard_map/pallas_call | solution.py:1047
  57.3 0.0 collective-permute-done.17.refs_3_
  57.4 0.0 collective-permute-done.15.refs_2_
  57.4 1.4 %shard_map.228 = (f32[2304,256]{1,0:T(8,128)}, f32[1,256]{1,0:T(1,128)}, f32[256,256]{1,0:T(8,128)}, f32[1,256]{1,0:T(1,128)}, f32[64,256]{1,0:T(8,128)}, /*inde...) custom-call(bf16[1,368,256]{2,1,0:T(8,128)(2,1)S(1)} %collective-per, ...), custom_call_target="tpu_custom_call", output_to_operand_aliasing={{0}: (4, {}), {1}: (5, {}), {2}: (6, {}), {3}: (7, {}), {4}... | custom-call | tf_op jit(solution)/shard_map/pallas_call | solution.py:1047
  (15 shorter events, 0.0 us)
Async XLA Ops:
  1.8 7.8 %collective-permute-start.1 = (bf16[4,176,256]{2,1,0:T(8,128)(2,1)S(1)}, bf16[4,176,256]{2,1,0:T(8,128)(2,1)S(1)}, u32[]{:S(2)}, u32[]{:S(2)}) collective-permute-start(bf16[4,176,256]{2,1,0:T(8,128)(2,1)S(1)} %get-tuple-element.79), channel_id=1, source_target_pairs={{0,2},{2,0},{4,6},{6,4},{8,10},{10,8},{12,14},{14,12},{16,18},{18,... | collective-permute-start | bytes 1081352 | tf_op jit(solution)/shard_map/ppermute | solution.py:910
  1.9 13.7 %collective-permute-start = (bf16[4,176,256]{2,1,0:T(8,128)(2,1)S(1)}, bf16[4,176,256]{2,1,0:T(8,128)(2,1)S(1)}, u32[]{:S(2)}, u32[]{:S(2)}) collective-permute-start(bf16[4,176,256]{2,1,0:T(8,128)(2,1)S(1)} %get-tuple-element.78), channel_id=1, source_target_pairs={{2,4},{6,8},{10,12},{14,16},{18,20},{22,24},{26,28},{4,2},{8,6},{1... | collective-permute-start | bytes 1081352 | tf_op jit(solution)/shard_map/ppermute | solution.py:910
  6.4 3.2 %copy-start = (bf16[256,64]{0,1:T(8,128)(2,1)S(1)}, bf16[256,64]{0,1:T(8,128)(2,1)}, u32[]{:S(2)}) copy-start(bf16[256,64]{0,1:T(8,128)(2,1)} %param.20) | copy-start | bytes 98308
  6.5 3.2 %copy-start.1 = (bf16[256]{0:T(256)(128)(2,1)S(1)}, bf16[256]{0:T(256)(128)(2,1)}, u32[]{:S(2)}) copy-start(bf16[256]{0:T(256)(128)(2,1)} %conv_bias_ref.3) | copy-start | bytes 1540
  6.5 3.2 %copy-start.2 = (bf16[256]{0:T(256)(128)(2,1)S(1)}, bf16[256]{0:T(256)(128)(2,1)}, u32[]{:S(2)}) copy-start(bf16[256]{0:T(256)(128)(2,1)} %mix_bias_ref.3) | copy-start | bytes 1540
  6.5 3.2 %copy-start.3 = (bf16[64]{0:T(256)(128)(2,1)S(1)}, bf16[64]{0:T(256)(128)(2,1)}, u32[]{:S(2)}) copy-start(bf16[64]{0:T(256)(128)(2,1)} %proj_bias_ref.3) | copy-start | bytes 388
  19.8 2.6 %collective-permute-start.2 = (bf16[4,368,256]{2,1,0:T(8,128)(2,1)S(1)}, bf16[4,368,256]{2,1,0:T(8,128)(2,1)S(1)}, u32[]{:S(2)}, u32[]{:S(2)}) collective-permute-start(bf16[4,368,256]{2,1,0:T(8,128)(2,1)S(1)} %shard_map.216.after_ref), channel_id=1, source_target_pairs={{0,2},{1,3},{2,0},{3,1},{4,6},{5,7},{6,4},{7,5},{8,10},{9,11},{10,... | collective-permute-start | bytes 2261000 | tf_op jit(solution)/shard_map/ppermute | solution.py:769
  22.4 16.9 %copy-start.4 = (bf16[256]{0:T(256)(128)(2,1)S(1)}, bf16[256]{0:T(256)(128)(2,1)}, u32[]{:S(2)}) copy-start(bf16[256]{0:T(256)(128)(2,1)} %decode_bias_ref.1) | copy-start | bytes 1540
  22.6 7.3 %collective-permute-start.3 = (bf16[1,368,256]{2,1,0:T(8,128)(2,1)S(1)}, bf16[1,368,256]{2,1,0:T(8,128)(2,1)S(1)}, u32[]{:S(2)}, u32[]{:S(2)}) collective-permute-start(bf16[1,368,256]{2,1,0:T(8,128)(2,1)S(1)} %get-tuple-element.105), channel_id=1, source_target_pairs={{0,5},{1,4},{2,26},{3,27},{4,1},{5,0},{6,30},{7,31},{8,13},{9,12},... | collective-permute-start | bytes 565256 | tf_op jit(solution)/shard_map/ppermute | solution.py:769
  26.4 10.1 %collective-permute-start.4 = (bf16[1,368,256]{2,1,0:T(8,128)(2,1)S(1)}, bf16[1,368,256]{2,1,0:T(8,128)(2,1)S(1)}, u32[]{:S(2)}, u32[]{:S(2)}) collective-permute-start(bf16[1,368,256]{2,1,0:T(8,128)(2,1)S(1)} %get-tuple-element.106), channel_id=1, source_target_pairs={{0,1},{1,0},{2,18},{3,19},{4,5},{5,4},{6,22},{7,23},{8,9},{9,8},{1... | collective-permute-start | bytes 565256 | tf_op jit(solution)/shard_map/ppermute | solution.py:769
  26.4 10.1 %collective-permute-start.5 = (bf16[1,368,256]{2,1,0:T(8,128)(2,1)S(1)}, bf16[1,368,256]{2,1,0:T(8,128)(2,1)S(1)}, u32[]{:S(2)}, u32[]{:S(2)}) collective-permute-start(bf16[1,368,256]{2,1,0:T(8,128)(2,1)S(1)} %get-tuple-element.107), channel_id=1, source_target_pairs={{0,4},{1,5},{2,10},{3,11},{4,0},{5,1},{6,14},{7,15},{8,12},{9,13},... | collective-permute-start | bytes 565256 | tf_op jit(solution)/shard_map/ppermute | solution.py:769
  26.8 21.2 %collective-permute-start.7 = (bf16[704,256]{1,0:T(8,128)(2,1)S(1)}, bf16[704,256]{1,0:T(8,128)(2,1)S(1)}, u32[]{:S(2)}, u32[]{:S(2)}) collective-permute-start(bf16[704,256]{1,0:T(8,128)(2,1)S(1)} %get-tuple-element.103.after_ref.other_ref), channel_id=1, source_target_pairs={{2,4},{6,8},{10,12},{14,16},{18,20},{22,24},{26,28},{4,2},{8,6},{1... | collective-permute-start | bytes 1081352 | tf_op jit(solution)/shard_map/ppermute | solution.py:910
  29.8 21.2 %collective-permute-start.6 = (bf16[704,256]{1,0:T(8,128)(2,1)S(1)}, bf16[704,256]{1,0:T(8,128)(2,1)S(1)}, u32[]{:S(2)}, u32[]{:S(2)}) collective-permute-start(bf16[704,256]{1,0:T(8,128)(2,1)S(1)} %get-tuple-element.108.mate_ref), channel_id=1, source_target_pairs={{0,2},{2,0},{4,6},{6,4},{8,10},{10,8},{12,14},{14,12},{16,18},{18,... | collective-permute-start | bytes 1081352 | tf_op jit(solution)/shard_map/ppermute | solution.py:910
  36.6 7.6 %collective-permute-start.10 = (bf16[1,368,256]{2,1,0:T(8,128)(2,1)S(1)}, bf16[1,368,256]{2,1,0:T(8,128)(2,1)S(1)}, u32[]{:S(2)}, u32[]{:S(2)}) collective-permute-start(bf16[1,368,256]{2,1,0:T(8,128)(2,1)S(1)} %shard_map.219.after_ref.refs_0_), channel_id=1, source_target_pairs={{0,24},{1,25},{2,7},{3,6},{4,28},{5,29},{6,3},{7,2},{8,16},{9,17},... | collective-permute-start | bytes 565256 | tf_op jit(solution)/shard_map/ppermute | solution.py:769
  37.0 7.3 %collective-permute-start.9 = (bf16[1,368,256]{2,1,0:T(8,128)(2,1)S(1)}, bf16[1,368,256]{2,1,0:T(8,128)(2,1)S(1)}, u32[]{:S(2)}, u32[]{:S(2)}) collective-permute-start(bf16[1,368,256]{2,1,0:T(8,128)(2,1)S(1)} %shard_map.219.after_ref.refs_0_), channel_id=1, source_target_pairs={{0,16},{1,17},{2,3},{3,2},{4,20},{5,21},{6,7},{7,6},{8,24},{9,25},... | collective-permute-start | bytes 565256 | tf_op jit(solution)/shard_map/ppermute | solution.py:769
  38.0 6.3 %collective-permute-start.8 = (bf16[1,368,256]{2,1,0:T(8,128)(2,1)S(1)}, bf16[1,368,256]{2,1,0:T(8,128)(2,1)S(1)}, u32[]{:S(2)}, u32[]{:S(2)}) collective-permute-start(bf16[1,368,256]{2,1,0:T(8,128)(2,1)S(1)} %shard_map.219.after_ref.refs_0_), channel_id=1, source_target_pairs={{0,8},{1,9},{2,6},{3,7},{4,12},{5,13},{6,2},{7,3},{8,0},{9,1},{10,... | collective-permute-start | bytes 565256 | tf_op jit(solution)/shard_map/ppermute | solution.py:769
  44.4 10.0 %collective-permute-start.16 = (bf16[1,368,256]{2,1,0:T(8,128)(2,1)S(1)}, bf16[1,368,256]{2,1,0:T(8,128)(2,1)S(1)}, u32[]{:S(2)}, u32[]{:S(2)}) collective-permute-start(bf16[1,368,256]{2,1,0:T(8,128)(2,1)S(1)} %shard_map.222.after_ref.refs_0_), channel_id=1, source_target_pairs={{0,5},{1,4},{2,26},{3,27},{4,1},{5,0},{6,30},{7,31},{8,13},{9,12},... | collective-permute-start | bytes 565256 | tf_op jit(solution)/shard_map/ppermute | solution.py:769
  46.8 8.4 %collective-permute-start.14 = (bf16[1,368,256]{2,1,0:T(8,128)(2,1)S(1)}, bf16[1,368,256]{2,1,0:T(8,128)(2,1)S(1)}, u32[]{:S(2)}, u32[]{:S(2)}) collective-permute-start(bf16[1,368,256]{2,1,0:T(8,128)(2,1)S(1)} %shard_map.222.after_ref.refs_0_), channel_id=1, source_target_pairs={{0,1},{1,0},{2,18},{3,19},{4,5},{5,4},{6,22},{7,23},{8,9},{9,8},{1... | collective-permute-start | bytes 565256 | tf_op jit(solution)/shard_map/ppermute | solution.py:769
  46.8 8.4 %collective-permute-start.12 = (bf16[1,368,256]{2,1,0:T(8,128)(2,1)S(1)}, bf16[1,368,256]{2,1,0:T(8,128)(2,1)S(1)}, u32[]{:S(2)}, u32[]{:S(2)}) collective-permute-start(bf16[1,368,256]{2,1,0:T(8,128)(2,1)S(1)} %shard_map.222.after_ref.refs_0_), channel_id=1, source_target_pairs={{0,4},{1,5},{2,10},{3,11},{4,0},{5,1},{6,14},{7,15},{8,12},{9,13},... | collective-permute-start | bytes 565256 | tf_op jit(solution)/shard_map/ppermute | solution.py:769
  48.0 9.3 %collective-permute-start.11 = (bf16[1,368,256]{2,1,0:T(8,128)(2,1)S(1)}, bf16[1,368,256]{2,1,0:T(8,128)(2,1)S(1)}, u32[]{:S(2)}, u32[]{:S(2)}) collective-permute-start(bf16[1,368,256]{2,1,0:T(8,128)(2,1)S(1)} %shard_map.222.after_ref.refs_0_), channel_id=1, source_target_pairs={{0,2},{1,3},{2,0},{3,1},{4,6},{5,7},{6,4},{7,5},{8,10},{9,11},{10,... | collective-permute-start | bytes 565256 | tf_op jit(solution)/shard_map/ppermute | solution.py:769
  54.4 2.9 %collective-permute-start.17 = (bf16[1,368,256]{2,1,0:T(8,128)(2,1)S(1)}, bf16[1,368,256]{2,1,0:T(8,128)(2,1)S(1)}, u32[]{:S(2)}, u32[]{:S(2)}) collective-permute-start(bf16[1,368,256]{2,1,0:T(8,128)(2,1)S(1)} %shard_map.226.refs_3_), channel_id=1, source_target_pairs={{0,2},{1,3},{2,0},{3,1},{4,6},{5,7},{6,4},{7,5},{8,10},{9,11},{10,... | collective-permute-start | bytes 565256 | tf_op jit(solution)/shard_map/ppermute | solution.py:769
  55.2 2.2 %collective-permute-start.15 = (bf16[1,368,256]{2,1,0:T(8,128)(2,1)S(1)}, bf16[1,368,256]{2,1,0:T(8,128)(2,1)S(1)}, u32[]{:S(2)}, u32[]{:S(2)}) collective-permute-start(bf16[1,368,256]{2,1,0:T(8,128)(2,1)S(1)} %shard_map.225.refs_2_), channel_id=1, source_target_pairs={{0,2},{1,3},{2,0},{3,1},{4,6},{5,7},{6,4},{7,5},{8,10},{9,11},{10,... | collective-permute-start | bytes 565256 | tf_op jit(solution)/shard_map/ppermute | solution.py:769
  55.2 2.2 %collective-permute-start.13 = (bf16[1,368,256]{2,1,0:T(8,128)(2,1)S(1)}, bf16[1,368,256]{2,1,0:T(8,128)(2,1)S(1)}, u32[]{:S(2)}, u32[]{:S(2)}) collective-permute-start(bf16[1,368,256]{2,1,0:T(8,128)(2,1)S(1)} %shard_map.224.refs_1_), channel_id=1, source_target_pairs={{0,2},{1,3},{2,0},{3,1},{4,6},{5,7},{6,4},{7,5},{8,10},{9,11},{10,... | collective-permute-start | bytes 565256 | tf_op jit(solution)/shard_map/ppermute | solution.py:769

commit v9 on v8

--- a/solution.py
+++ b/solution.py
@@ -814,15 +814,29 @@
     core = lax.axis_index("strip") % 2
     half = core if mine else 1 - core
     place = plan.place(half)
+    conv_ref, conv_bias_ref, mix_ref, mix_bias_ref, proj_ref, proj_bias_ref = outs[:6]
+    codebook_ref, decode_ref, decode_bias_ref = outs[6:]
+    conv_rows = 5 * channels
+    early = min(conv_rows, 9 * channels - conv_rows) // plan.piece_rows
+    sent = []
     at = 0
     for ref in ins:
         for piece in range(ref.shape[0]):
-            start = pl.multiple_of((place ^ at) * plan.piece_rows, plan.piece_rows)
+            shard = place ^ at
+            start = pl.multiple_of(shard * plan.piece_rows, tile_rows)
             gathered_ref[pl.ds(start, plan.piece_rows)] = ref[piece].astype(wide)
+
+            def send(start=start, at=at):
+                target = pl.multiple_of(half * conv_rows + start, tile_rows)
+                return pltpu.make_async_copy(
+                    gathered_ref.at[pl.ds(start, plan.piece_rows)],
+                    conv_ref.at[pl.ds(target, plan.piece_rows)],
+                    sems.at[12 + at],
+                )
+
+            pl.when(shard < early)(lambda send=send: send().start())
+            sent.append((shard, send))
             at += 1
-    conv_ref, conv_bias_ref, mix_ref, mix_bias_ref, proj_ref, proj_bias_ref = outs[:6]
-    codebook_ref, decode_ref, decode_bias_ref = outs[6:]
-    conv_rows = 5 * channels
 
     def copy_all(pairs):
         copies = [
@@ -836,9 +850,11 @@
 
     def place_all(first, last, targets):
         pairs = []
-        for start in range(first, last, channels):
-            span = pl.ds(start, channels)
-            pairs.append((gathered_ref.at[pl.ds(start - first, channels)], conv_ref.at[span]))
+        done = early * plan.piece_rows
+        if last - first > done:
+            rest = last - first - done
+            source = gathered_ref.at[pl.ds(done, rest)]
+            pairs.append((source, conv_ref.at[pl.ds(first + done, rest)]))
         at = last - first
         for target, depth in targets:
             pairs.append((gathered_ref.at[pl.ds(at, depth)], target))
@@ -861,6 +877,9 @@
             line_ref[...] = lines[number : number + 1, : target.shape[1]]
             pairs.append((line_ref, target))
         copy_all(pairs)
+
+    for shard, send in sent:
+        pl.when(shard < early)(lambda send=send: send().wait())
 
 
 def per_device(

time: 59.1 us -> 59 us (level)
  transfers between devices with their start and end apart: 18 -> 18, of which waited for: 2 -> 2; matrix products, arithmetic and copies ran while one was open for 0% -> 0% of each run, Pallas kernels for 37% -> 36%
where the time goes in v9:
time: 59 us; the launch traced here: 58.8 us
  Pallas kernels  28.2 us (48%)
  starting transfers between devices  22 us (37%)
  waiting for transfers between devices  7.37 us (12%)
  between operations  1.14 us (2%)
    ppermute x14, starting transfers between devices, swap(): return lax.ppermute(values, ('strip', 'canvas'), pairs)  14.3 us
    pallas_call x2, Pallas kernels, block_rows(): call(functools.partial(rows_kernel, beyond), [in_vmem] * len(ins), [in_vm...  7.53 us
    ppermute x2, starting transfers between devices, trade(): lax.ppermute(other, 'strip', far)  7.48 us
    ppermute x14, waiting for transfers between devices, swap(): return lax.ppermute(values, ('strip', 'canvas'), pairs)  7.36 us
    pallas_call x2, Pallas kernels, input_rows(): call(functools.partial(input_kernel, mine), [in_vmem] * 7 + [anywhere] +...  6.74 us
    pallas_call x2, Pallas kernels, weight_half(): call(functools.partial(weight_kernel, plan, mine), [in_vmem] * len(ins) +...  5.09 us
    pallas_call x1, Pallas kernels, per_device(): call(code_kernel, [in_vmem] * 4 + [in_hbm] * 4, [in_vmem] * 8, outs, held...  3.11 us
    pallas_call x2, Pallas kernels, finish(): call(functools.partial(final_kernel, plan, mine, count, (channels, size,...  2.58 us
  transfers between devices with their start and end apart: 18, of which 2 were waited for; matrix products, arithmetic and copies ran while one was open for 0% of the time, Pallas kernels for 36%

profile of v9, /device:TPU:1, one launch (start us, length us, event | category | flops | bytes accessed | tf_op | source)
XLA Modules:
  0.0 58.8 jit_solution(1178600922009519907)
XLA Ops:
  0.6 1.2 %shard_map.212 = (bf16[4,176,256]{2,1,0:T(8,128)(2,1)S(1)}, bf16[4,176,256]{2,1,0:T(8,128)(2,1)S(1)}, s32[4,4,176]{2,1,0:T(4,128)S(1)}, s32[4,4,176]{2,1,0:T(4,1...) custom-call(bf16[4,4,176,256]{3,2,1,0:T(8,128)(2,1)} %latent_hbm.3, s32[4,4,176]{2,1,0:T(4,128)} %crop_hbm.1, ...), custom_call_target="tpu_custom_call" | custom-call | tf_op jit(solution)/shard_map/pallas_call | solution.py:941
  1.8 0.1 collective-permute-start.1
  1.9 4.5 %collective-permute-start = (bf16[4,176,256]{2,1,0:T(8,128)(2,1)S(1)}, bf16[4,176,256]{2,1,0:T(8,128)(2,1)S(1)}, u32[]{:S(2)}, u32[]{:S(2)}) collective-permute-start(bf16[4,176,256]{2,1,0:T(8,128)(2,1)S(1)} %get-tuple-element.78), channel_id=1, source_target_pairs={{2,4},{6,8},{10,12},{14,16},{18,20},{22,24},{26,28},{4,2},{8,6},{1... | collective-permute-start | bytes 1081352 | tf_op jit(solution)/shard_map/ppermute | solution.py:929
  6.4 0.0 copy-start
  6.5 0.0 copy-start.1
  6.5 0.0 copy-start.2
  6.5 0.0 copy-start.3
  6.5 3.1 %shard_map.213 = (f32[4,704,128]{2,1,0:T(8,128)S(1)}, bf16[2816,512]{1,0:T(8,128)(2,1)S(1)}, bf16[4,2816,128]{2,1,0:T(8,128)(2,1)S(1)}, f32[1,256]{1,0:T(1,128)S...) custom-call(s32[4,4,176]{2,1,0:T(4,128)S(1)} %get-tuple-element.69.c, ...), custom_call_target="tpu_custom_call" | custom-call | flops 1107296256 | tf_op jit(solution)/shard_map/pallas_call | solution.py:960
  9.6 0.0 collective-permute-done.1.halo_ref
  9.7 5.9 %shard_map.214 = (bf16[4224,768]{1,0:T(8,128)(2,1)S(1)}, bf16[2816,256]{1,0:T(8,128)(2,1)S(1)}, bf16[2816,256]{1,0:T(8,128)(2,1)S(1)}, bf16[2816,256]{1,0:T(8,12...) custom-call(bf16[4,2816,128]{2,1,0:T(8,128)(2,1)S(1)} %get-tuple-ele, ...), custom_call_target="tpu_custom_call" | custom-call | flops 3690987520 | tf_op jit(solution)/shard_map/pallas_call | solution.py:985
  15.6 1.6 %shard_map.215 = (bf16[4224,768]{1,0:T(8,128)(2,1)S(1)}, bf16[2816,256]{1,0:T(8,128)(2,1)S(1)}, bf16[2816,256]{1,0:T(8,128)(2,1)S(1)}, bf16[2816,256]{1,0:T(8,12...) custom-call(bf16[4,2816,128]{2,1,0:T(8,128)(2,1)S(1)} %get-tuple-ele, ...), custom_call_target="tpu_custom_call", output_to_operand_aliasing={{0}: (11, {}), {1}: (12, {}), {2}: (13, {}), {3}: (14, {}),... | custom-call | flops 3690987520 | tf_op jit(solution)/shard_map/pallas_call | solution.py:985
  17.2 2.6 %shard_map.216.after_ref = bf16[4,368,256]{2,1,0:T(8,128)(2,1)S(1)} custom-call(bf16[4224,768]{1,0:T(8,128)(2,1)S(1)} %get-tuple-element.91.slab_ref, bf16[2816,256]{1,0:T(8,128)(2,1)S(1)} %get-tuple-element.92.grad_ref, bf16[2816,256]{1,0:T(8,128)(2,1)S(1)} %get-tuple-element.93.up_ref, bf16[2816,256]{1,0:T(8,128)(2,1)S(1)} %get-tuple-element.94.down_ref, ...), custom_call_target="tpu_custom_call" | custom-call | flops 1845493760 | tf_op jit(solution)/shard_map/pallas_call | solution.py:1003
  19.8 0.1 collective-permute-start.2
  19.9 2.5 %shard_map.217.refs_0_ = bf16[4,368,256]{2,1,0:T(8,128)(2,1)S(1)} custom-call(bf16[4224,768]{1,0:T(8,128)(2,1)S(1)} %get-tuple-element.91.slab_ref, bf16[2816,256]{1,0:T(8,128)(2,1)S(1)} %get-tuple-element.92.grad_ref, bf16[2816,256]{1,0:T(8,128)(2,1)S(1)} %get-tuple-element.93.up_ref, bf16[2816,256]{1,0:T(8,128)(2,1)S(1)} %get-tuple-element.94.down_ref, ...), custom_call_target="tpu_custom_call" | custom-call | flops 1845493760 | tf_op jit(solution)/shard_map/pallas_call | solution.py:1003
  22.4 0.0 copy-start.4
  22.4 0.0 collective-permute-done.2.refs_1_
  22.4 0.2 shard_map.218
  22.6 3.8 %collective-permute-start.3 = (bf16[1,368,256]{2,1,0:T(8,128)(2,1)S(1)}, bf16[1,368,256]{2,1,0:T(8,128)(2,1)S(1)}, u32[]{:S(2)}, u32[]{:S(2)}) collective-permute-start(bf16[1,368,256]{2,1,0:T(8,128)(2,1)S(1)} %get-tuple-element.105), channel_id=1, source_target_pairs={{0,5},{1,4},{2,26},{3,27},{4,1},{5,0},{6,30},{7,31},{8,13},{9,12},... | collective-permute-start | bytes 565256 | tf_op jit(solution)/shard_map/ppermute | solution.py:769
  26.4 0.0 collective-permute-start.4
  26.4 0.4 collective-permute-start.5
  26.8 3.0 %collective-permute-start.7 = (bf16[704,256]{1,0:T(8,128)(2,1)S(1)}, bf16[704,256]{1,0:T(8,128)(2,1)S(1)}, u32[]{:S(2)}, u32[]{:S(2)}) collective-permute-start(bf16[704,256]{1,0:T(8,128)(2,1)S(1)} %get-tuple-element.103.after_ref.other_ref), channel_id=1, source_target_pairs={{2,4},{6,8},{10,12},{14,16},{18,20},{22,24},{26,28},{4,2},{8,6},{1... | collective-permute-start | bytes 1081352 | tf_op jit(solution)/shard_map/ppermute | solution.py:929
  29.8 0.1 collective-permute-start.6
  29.9 0.0 collective-permute-done.3.refs_1_
  29.9 6.7 %collective-permute-done.4.refs_2_ = bf16[1,368,256]{2,1,0:T(8,128)(2,1)S(1)} collective-permute-done((bf16[1,368,256]{2,1,0:T(8,128)(2,1)S(1)}, bf16[1,368,256]{2,1,0:T(8,128)(2,1)S(1)}, u32[]{:S(2)}, u32[]{:S(2)}) %collective-permute-start.4) | collective-permute-done | bytes 188448 | tf_op jit(solution)/shard_map/ppermute | solution.py:769
  36.5 0.1 shard_map.219.after_ref.refs_0_
  36.6 0.3 collective-permute-start.10
  37.0 1.0 %collective-permute-start.9 = (bf16[1,368,256]{2,1,0:T(8,128)(2,1)S(1)}, bf16[1,368,256]{2,1,0:T(8,128)(2,1)S(1)}, u32[]{:S(2)}, u32[]{:S(2)}) collective-permute-start(bf16[1,368,256]{2,1,0:T(8,128)(2,1)S(1)} %shard_map.219.after_ref.refs_0_), channel_id=1, source_target_pairs={{0,16},{1,17},{2,3},{3,2},{4,20},{5,21},{6,7},{7,6},{8,24},{9,25},... | collective-permute-start | bytes 565256 | tf_op jit(solution)/shard_map/ppermute | solution.py:769
  38.0 1.4 %collective-permute-start.8 = (bf16[1,368,256]{2,1,0:T(8,128)(2,1)S(1)}, bf16[1,368,256]{2,1,0:T(8,128)(2,1)S(1)}, u32[]{:S(2)}, u32[]{:S(2)}) collective-permute-start(bf16[1,368,256]{2,1,0:T(8,128)(2,1)S(1)} %shard_map.219.after_ref.refs_0_), channel_id=1, source_target_pairs={{0,8},{1,9},{2,6},{3,7},{4,12},{5,13},{6,2},{7,3},{8,0},{9,1},{10,... | collective-permute-start | bytes 565256 | tf_op jit(solution)/shard_map/ppermute | solution.py:769
  39.3 1.6 %shard_map.220.refs_4_ = bf16[4,4,176,256]{3,2,1,0:T(8,128)(2,1)} custom-call(f32[4,704,128]{2,1,0:T(8,128)S(1)} %get-tuple-element.73.term_ref, bf16[64,256]{1,0:T(8,128)(2,1)S(1)} %get-tuple-element.72.decode_weight_ref, bf16[256]{0:T(256)(128)(2,1)S(1)} %copy-done.4, bf16[1,368,256]{2,1,0:T(8,128)(2,1)S(1)} %shard_map.219.after_ref.refs_0_), custom_call_target="tpu_custom_call" | custom-call | flops 738197504 | tf_op jit(solution)/shard_map/pallas_call | solution.py:1035
  41.0 3.3 %shard_map.221.refs_5_.refs_0_ = bf16[4,4,176,256]{3,2,1,0:T(8,128)(2,1)} custom-call(bf16[4,2816,128]{2,1,0:T(8,128)(2,1)S(1)} %get-tuple-element.74.masks_ref, bf16[4,4,176,256]{3,2,1,0:T(8,128)(2,1)S(1)} %get-tuple-element.75.latent_ref, bf16[2816,256]{1,0:T(8,128)(2,1)S(1)} %get-tuple-element.92.grad_ref, ...), custom_call_target="tpu_custom_call" | custom-call | flops 2030043136 | tf_op jit(solution)/shard_map/pallas_call | solution.py:1015
  44.2 0.0 collective-permute-done.10.refs_3_
  44.3 0.0 collective-permute-done.9.refs_2_
  44.3 0.1 shard_map.222.after_ref.refs_0_
  44.4 2.4 %collective-permute-start.16 = (bf16[1,368,256]{2,1,0:T(8,128)(2,1)S(1)}, bf16[1,368,256]{2,1,0:T(8,128)(2,1)S(1)}, u32[]{:S(2)}, u32[]{:S(2)}) collective-permute-start(bf16[1,368,256]{2,1,0:T(8,128)(2,1)S(1)} %shard_map.222.after_ref.refs_0_), channel_id=1, source_target_pairs={{0,5},{1,4},{2,26},{3,27},{4,1},{5,0},{6,30},{7,31},{8,13},{9,12},... | collective-permute-start | bytes 565256 | tf_op jit(solution)/shard_map/ppermute | solution.py:769
  46.8 0.0 collective-permute-start.14
  46.8 1.2 %collective-permute-start.12 = (bf16[1,368,256]{2,1,0:T(8,128)(2,1)S(1)}, bf16[1,368,256]{2,1,0:T(8,128)(2,1)S(1)}, u32[]{:S(2)}, u32[]{:S(2)}) collective-permute-start(bf16[1,368,256]{2,1,0:T(8,128)(2,1)S(1)} %shard_map.222.after_ref.refs_0_), channel_id=1, source_target_pairs={{0,4},{1,5},{2,10},{3,11},{4,0},{5,1},{6,14},{7,15},{8,12},{9,13},... | collective-permute-start | bytes 565256 | tf_op jit(solution)/shard_map/ppermute | solution.py:769
  48.0 0.0 collective-permute-done.7.other_ref
  48.0 2.9 %collective-permute-start.11 = (bf16[1,368,256]{2,1,0:T(8,128)(2,1)S(1)}, bf16[1,368,256]{2,1,0:T(8,128)(2,1)S(1)}, u32[]{:S(2)}, u32[]{:S(2)}) collective-permute-start(bf16[1,368,256]{2,1,0:T(8,128)(2,1)S(1)} %shard_map.222.after_ref.refs_0_), channel_id=1, source_target_pairs={{0,2},{1,3},{2,0},{3,1},{4,6},{5,7},{6,4},{7,5},{8,10},{9,11},{10,... | collective-permute-start | bytes 565256 | tf_op jit(solution)/shard_map/ppermute | solution.py:769
  51.0 3.5 %shard_map.223.refs_1_ = bf16[4,4,176,256]{3,2,1,0:T(8,128)(2,1)} custom-call(bf16[4,2816,128]{2,1,0:T(8,128)(2,1)S(1)} %get-tuple-element.74.masks_ref, bf16[4,4,176,256]{3,2,1,0:T(8,128)(2,1)S(1)} %get-tuple-element.75.latent_ref, bf16[2816,256]{1,0:T(8,128)(2,1)S(1)} %get-tuple-element.92.grad_ref, ...), custom_call_target="tpu_custom_call", output_to_operand_aliasing={{}: (8, {})} | custom-call | flops 2030043136 | tf_op jit(solution)/shard_map/pallas_call | solution.py:1015
  54.4 0.0 collective-permute-done.16.refs_0_
  54.4 0.1 collective-permute-start.17
  54.5 0.7 %collective-permute-done.14.refs_0_ = bf16[1,368,256]{2,1,0:T(8,128)(2,1)S(1)} collective-permute-done((bf16[1,368,256]{2,1,0:T(8,128)(2,1)S(1)}, bf16[1,368,256]{2,1,0:T(8,128)(2,1)S(1)}, u32[]{:S(2)}, u32[]{:S(2)}) %collective-permute-start.14) | collective-permute-done | bytes 188448 | tf_op jit(solution)/shard_map/ppermute | solution.py:769
  55.2 0.7 %collective-permute-start.13 = (bf16[1,368,256]{2,1,0:T(8,128)(2,1)S(1)}, bf16[1,368,256]{2,1,0:T(8,128)(2,1)S(1)}, u32[]{:S(2)}, u32[]{:S(2)}) collective-permute-start(bf16[1,368,256]{2,1,0:T(8,128)(2,1)S(1)} %shard_map.224.refs_1_), channel_id=1, source_target_pairs={{0,2},{1,3},{2,0},{3,1},{4,6},{5,7},{6,4},{7,5},{8,10},{9,11},{10,... | collective-permute-start | bytes 565256 | tf_op jit(solution)/shard_map/ppermute | solution.py:769
  56.0 1.3 %shard_map.227 = (f32[2304,256]{1,0:T(8,128)}, f32[1,256]{1,0:T(1,128)}, f32[256,256]{1,0:T(8,128)}, f32[1,256]{1,0:T(1,128)}, f32[64,256]{1,0:T(8,128)}, /*inde...) custom-call(bf16[1,368,256]{2,1,0:T(8,128)(2,1)S(1)} %shard_map.222.after_ref.refs_0_, ...), custom_call_target="tpu_custom_call" | custom-call | tf_op jit(solution)/shard_map/pallas_call | solution.py:1066
  57.3 0.0 collective-permute-done.11.refs_0_
  57.3 0.0 collective-permute-done.15.refs_2_
  57.3 0.0 collective-permute-done.13.refs_1_
  57.3 1.3 %shard_map.228 = (f32[2304,256]{1,0:T(8,128)}, f32[1,256]{1,0:T(1,128)}, f32[256,256]{1,0:T(8,128)}, f32[1,256]{1,0:T(1,128)}, f32[64,256]{1,0:T(8,128)}, /*inde...) custom-call(bf16[1,368,256]{2,1,0:T(8,128)(2,1)S(1)} %collective-per, ...), custom_call_target="tpu_custom_call", output_to_operand_aliasing={{0}: (4, {}), {1}: (5, {}), {2}: (6, {}), {3}: (7, {}), {4}... | custom-call | tf_op jit(solution)/shard_map/pallas_call | solution.py:1066
  (15 shorter events, 0.0 us)
Async XLA Ops:
  1.8 7.8 %collective-permute-start.1 = (bf16[4,176,256]{2,1,0:T(8,128)(2,1)S(1)}, bf16[4,176,256]{2,1,0:T(8,128)(2,1)S(1)}, u32[]{:S(2)}, u32[]{:S(2)}) collective-permute-start(bf16[4,176,256]{2,1,0:T(8,128)(2,1)S(1)} %get-tuple-element.79), channel_id=1, source_target_pairs={{0,2},{2,0},{4,6},{6,4},{8,10},{10,8},{12,14},{14,12},{16,18},{18,... | collective-permute-start | bytes 1081352 | tf_op jit(solution)/shard_map/ppermute | solution.py:929
  1.9 13.7 %collective-permute-start = (bf16[4,176,256]{2,1,0:T(8,128)(2,1)S(1)}, bf16[4,176,256]{2,1,0:T(8,128)(2,1)S(1)}, u32[]{:S(2)}, u32[]{:S(2)}) collective-permute-start(bf16[4,176,256]{2,1,0:T(8,128)(2,1)S(1)} %get-tuple-element.78), channel_id=1, source_target_pairs={{2,4},{6,8},{10,12},{14,16},{18,20},{22,24},{26,28},{4,2},{8,6},{1... | collective-permute-start | bytes 1081352 | tf_op jit(solution)/shard_map/ppermute | solution.py:929
  6.4 3.2 %copy-start = (bf16[256,64]{0,1:T(8,128)(2,1)S(1)}, bf16[256,64]{0,1:T(8,128)(2,1)}, u32[]{:S(2)}) copy-start(bf16[256,64]{0,1:T(8,128)(2,1)} %param.20) | copy-start | bytes 98308
  6.5 3.2 %copy-start.1 = (bf16[256]{0:T(256)(128)(2,1)S(1)}, bf16[256]{0:T(256)(128)(2,1)}, u32[]{:S(2)}) copy-start(bf16[256]{0:T(256)(128)(2,1)} %conv_bias_ref.3) | copy-start | bytes 1540
  6.5 3.2 %copy-start.2 = (bf16[256]{0:T(256)(128)(2,1)S(1)}, bf16[256]{0:T(256)(128)(2,1)}, u32[]{:S(2)}) copy-start(bf16[256]{0:T(256)(128)(2,1)} %mix_bias_ref.3) | copy-start | bytes 1540
  6.5 3.2 %copy-start.3 = (bf16[64]{0:T(256)(128)(2,1)S(1)}, bf16[64]{0:T(256)(128)(2,1)}, u32[]{:S(2)}) copy-start(bf16[64]{0:T(256)(128)(2,1)} %proj_bias_ref.3) | copy-start | bytes 388
  19.8 2.6 %collective-permute-start.2 = (bf16[4,368,256]{2,1,0:T(8,128)(2,1)S(1)}, bf16[4,368,256]{2,1,0:T(8,128)(2,1)S(1)}, u32[]{:S(2)}, u32[]{:S(2)}) collective-permute-start(bf16[4,368,256]{2,1,0:T(8,128)(2,1)S(1)} %shard_map.216.after_ref), channel_id=1, source_target_pairs={{0,2},{1,3},{2,0},{3,1},{4,6},{5,7},{6,4},{7,5},{8,10},{9,11},{10,... | collective-permute-start | bytes 2261000 | tf_op jit(solution)/shard_map/ppermute | solution.py:769
  22.4 16.9 %copy-start.4 = (bf16[256]{0:T(256)(128)(2,1)S(1)}, bf16[256]{0:T(256)(128)(2,1)}, u32[]{:S(2)}) copy-start(bf16[256]{0:T(256)(128)(2,1)} %decode_bias_ref.1) | copy-start | bytes 1540
  22.6 7.3 %collective-permute-start.3 = (bf16[1,368,256]{2,1,0:T(8,128)(2,1)S(1)}, bf16[1,368,256]{2,1,0:T(8,128)(2,1)S(1)}, u32[]{:S(2)}, u32[]{:S(2)}) collective-permute-start(bf16[1,368,256]{2,1,0:T(8,128)(2,1)S(1)} %get-tuple-element.105), channel_id=1, source_target_pairs={{0,5},{1,4},{2,26},{3,27},{4,1},{5,0},{6,30},{7,31},{8,13},{9,12},... | collective-permute-start | bytes 565256 | tf_op jit(solution)/shard_map/ppermute | solution.py:769
  26.4 10.1 %collective-permute-start.4 = (bf16[1,368,256]{2,1,0:T(8,128)(2,1)S(1)}, bf16[1,368,256]{2,1,0:T(8,128)(2,1)S(1)}, u32[]{:S(2)}, u32[]{:S(2)}) collective-permute-start(bf16[1,368,256]{2,1,0:T(8,128)(2,1)S(1)} %get-tuple-element.106), channel_id=1, source_target_pairs={{0,1},{1,0},{2,18},{3,19},{4,5},{5,4},{6,22},{7,23},{8,9},{9,8},{1... | collective-permute-start | bytes 565256 | tf_op jit(solution)/shard_map/ppermute | solution.py:769
  26.4 10.1 %collective-permute-start.5 = (bf16[1,368,256]{2,1,0:T(8,128)(2,1)S(1)}, bf16[1,368,256]{2,1,0:T(8,128)(2,1)S(1)}, u32[]{:S(2)}, u32[]{:S(2)}) collective-permute-start(bf16[1,368,256]{2,1,0:T(8,128)(2,1)S(1)} %get-tuple-element.107), channel_id=1, source_target_pairs={{0,4},{1,5},{2,10},{3,11},{4,0},{5,1},{6,14},{7,15},{8,12},{9,13},... | collective-permute-start | bytes 565256 | tf_op jit(solution)/shard_map/ppermute | solution.py:769
  26.8 21.2 %collective-permute-start.7 = (bf16[704,256]{1,0:T(8,128)(2,1)S(1)}, bf16[704,256]{1,0:T(8,128)(2,1)S(1)}, u32[]{:S(2)}, u32[]{:S(2)}) collective-permute-start(bf16[704,256]{1,0:T(8,128)(2,1)S(1)} %get-tuple-element.103.after_ref.other_ref), channel_id=1, source_target_pairs={{2,4},{6,8},{10,12},{14,16},{18,20},{22,24},{26,28},{4,2},{8,6},{1... | collective-permute-start | bytes 1081352 | tf_op jit(solution)/shard_map/ppermute | solution.py:929
  29.8 21.2 %collective-permute-start.6 = (bf16[704,256]{1,0:T(8,128)(2,1)S(1)}, bf16[704,256]{1,0:T(8,128)(2,1)S(1)}, u32[]{:S(2)}, u32[]{:S(2)}) collective-permute-start(bf16[704,256]{1,0:T(8,128)(2,1)S(1)} %get-tuple-element.108.mate_ref), channel_id=1, source_target_pairs={{0,2},{2,0},{4,6},{6,4},{8,10},{10,8},{12,14},{14,12},{16,18},{18,... | collective-permute-start | bytes 1081352 | tf_op jit(solution)/shard_map/ppermute | solution.py:929
  36.6 7.6 %collective-permute-start.10 = (bf16[1,368,256]{2,1,0:T(8,128)(2,1)S(1)}, bf16[1,368,256]{2,1,0:T(8,128)(2,1)S(1)}, u32[]{:S(2)}, u32[]{:S(2)}) collective-permute-start(bf16[1,368,256]{2,1,0:T(8,128)(2,1)S(1)} %shard_map.219.after_ref.refs_0_), channel_id=1, source_target_pairs={{0,24},{1,25},{2,7},{3,6},{4,28},{5,29},{6,3},{7,2},{8,16},{9,17},... | collective-permute-start | bytes 565256 | tf_op jit(solution)/shard_map/ppermute | solution.py:769
  37.0 7.3 %collective-permute-start.9 = (bf16[1,368,256]{2,1,0:T(8,128)(2,1)S(1)}, bf16[1,368,256]{2,1,0:T(8,128)(2,1)S(1)}, u32[]{:S(2)}, u32[]{:S(2)}) collective-permute-start(bf16[1,368,256]{2,1,0:T(8,128)(2,1)S(1)} %shard_map.219.after_ref.refs_0_), channel_id=1, source_target_pairs={{0,16},{1,17},{2,3},{3,2},{4,20},{5,21},{6,7},{7,6},{8,24},{9,25},... | collective-permute-start | bytes 565256 | tf_op jit(solution)/shard_map/ppermute | solution.py:769
  38.0 6.3 %collective-permute-start.8 = (bf16[1,368,256]{2,1,0:T(8,128)(2,1)S(1)}, bf16[1,368,256]{2,1,0:T(8,128)(2,1)S(1)}, u32[]{:S(2)}, u32[]{:S(2)}) collective-permute-start(bf16[1,368,256]{2,1,0:T(8,128)(2,1)S(1)} %shard_map.219.after_ref.refs_0_), channel_id=1, source_target_pairs={{0,8},{1,9},{2,6},{3,7},{4,12},{5,13},{6,2},{7,3},{8,0},{9,1},{10,... | collective-permute-start | bytes 565256 | tf_op jit(solution)/shard_map/ppermute | solution.py:769
  44.4 10.0 %collective-permute-start.16 = (bf16[1,368,256]{2,1,0:T(8,128)(2,1)S(1)}, bf16[1,368,256]{2,1,0:T(8,128)(2,1)S(1)}, u32[]{:S(2)}, u32[]{:S(2)}) collective-permute-start(bf16[1,368,256]{2,1,0:T(8,128)(2,1)S(1)} %shard_map.222.after_ref.refs_0_), channel_id=1, source_target_pairs={{0,5},{1,4},{2,26},{3,27},{4,1},{5,0},{6,30},{7,31},{8,13},{9,12},... | collective-permute-start | bytes 565256 | tf_op jit(solution)/shard_map/ppermute | solution.py:769
  46.8 8.4 %collective-permute-start.14 = (bf16[1,368,256]{2,1,0:T(8,128)(2,1)S(1)}, bf16[1,368,256]{2,1,0:T(8,128)(2,1)S(1)}, u32[]{:S(2)}, u32[]{:S(2)}) collective-permute-start(bf16[1,368,256]{2,1,0:T(8,128)(2,1)S(1)} %shard_map.222.after_ref.refs_0_), channel_id=1, source_target_pairs={{0,1},{1,0},{2,18},{3,19},{4,5},{5,4},{6,22},{7,23},{8,9},{9,8},{1... | collective-permute-start | bytes 565256 | tf_op jit(solution)/shard_map/ppermute | solution.py:769
  46.8 8.4 %collective-permute-start.12 = (bf16[1,368,256]{2,1,0:T(8,128)(2,1)S(1)}, bf16[1,368,256]{2,1,0:T(8,128)(2,1)S(1)}, u32[]{:S(2)}, u32[]{:S(2)}) collective-permute-start(bf16[1,368,256]{2,1,0:T(8,128)(2,1)S(1)} %shard_map.222.after_ref.refs_0_), channel_id=1, source_target_pairs={{0,4},{1,5},{2,10},{3,11},{4,0},{5,1},{6,14},{7,15},{8,12},{9,13},... | collective-permute-start | bytes 565256 | tf_op jit(solution)/shard_map/ppermute | solution.py:769
  48.0 9.3 %collective-permute-start.11 = (bf16[1,368,256]{2,1,0:T(8,128)(2,1)S(1)}, bf16[1,368,256]{2,1,0:T(8,128)(2,1)S(1)}, u32[]{:S(2)}, u32[]{:S(2)}) collective-permute-start(bf16[1,368,256]{2,1,0:T(8,128)(2,1)S(1)} %shard_map.222.after_ref.refs_0_), channel_id=1, source_target_pairs={{0,2},{1,3},{2,0},{3,1},{4,6},{5,7},{6,4},{7,5},{8,10},{9,11},{10,... | collective-permute-start | bytes 565256 | tf_op jit(solution)/shard_map/ppermute | solution.py:769
  54.4 2.8 %collective-permute-start.17 = (bf16[1,368,256]{2,1,0:T(8,128)(2,1)S(1)}, bf16[1,368,256]{2,1,0:T(8,128)(2,1)S(1)}, u32[]{:S(2)}, u32[]{:S(2)}) collective-permute-start(bf16[1,368,256]{2,1,0:T(8,128)(2,1)S(1)} %shard_map.226.refs_3_), channel_id=1, source_target_pairs={{0,2},{1,3},{2,0},{3,1},{4,6},{5,7},{6,4},{7,5},{8,10},{9,11},{10,... | collective-permute-start | bytes 565256 | tf_op jit(solution)/shard_map/ppermute | solution.py:769
  55.2 2.1 %collective-permute-start.15 = (bf16[1,368,256]{2,1,0:T(8,128)(2,1)S(1)}, bf16[1,368,256]{2,1,0:T(8,128)(2,1)S(1)}, u32[]{:S(2)}, u32[]{:S(2)}) collective-permute-start(bf16[1,368,256]{2,1,0:T(8,128)(2,1)S(1)} %shard_map.225.refs_2_), channel_id=1, source_target_pairs={{0,2},{1,3},{2,0},{3,1},{4,6},{5,7},{6,4},{7,5},{8,10},{9,11},{10,... | collective-permute-start | bytes 565256 | tf_op jit(solution)/shard_map/ppermute | solution.py:769
  55.2 2.1 %collective-permute-start.13 = (bf16[1,368,256]{2,1,0:T(8,128)(2,1)S(1)}, bf16[1,368,256]{2,1,0:T(8,128)(2,1)S(1)}, u32[]{:S(2)}, u32[]{:S(2)}) collective-permute-start(bf16[1,368,256]{2,1,0:T(8,128)(2,1)S(1)} %shard_map.224.refs_1_), channel_id=1, source_target_pairs={{0,2},{1,3},{2,0},{3,1},{4,6},{5,7},{6,4},{7,5},{8,10},{9,11},{10,... | collective-permute-start | bytes 565256 | tf_op jit(solution)/shard_map/ppermute | solution.py:769
